TPU v7x, 256 devices: a whole 4x4x8 slice. The times are simulated.
256 devices in a mesh: pipe: 4 (over z_hi), dp: 64 (over z_lo, x, y, core).
Axes of the slice: x: 4, y: 4, z: 8 (z_hi: 4, z_lo: 2; z = z_hi * 2 + z_lo), core: 2. Of those that a mesh axis runs over, the one named last changes fastest.
Arguments:
- saved: bfloat16 [2, 4, 8192, 4096], P(None, 'pipe', 'dp'), may hold values from -16 to 16
- grad_out: bfloat16 [8192, 4096], P('dp'), may hold values from -6 to 6
- gain: float32 [2, 4, 4096], P(None, 'pipe'), may hold values from 0.5 to 1.5
- w_value: bfloat16 [4, 4096, 512], P('pipe', 'dp'), may hold values from -0.09375 to 0.09375
Outputs:
- grad_x: bfloat16 [2, 4, 8192, 4096], P(None, 'pipe', 'dp')
- grad_w: float32 [4, 4096, 512], P('pipe', 'dp')
All inputs are finite; a program needn't handle non-finite values.
Results may differ from a plain program's by a relative error of at most 0.012.
Values may be sent and summed in bfloat16 or wider, within the bound.
No kernel may reach another device: no remote copies, remote signals or barrier semaphores. Data moves between devices by JAX's collectives and lax.ppermute only.
A program may use at most 64 MiB of HBM per device.

v0:
```python
import jax
import jax.numpy as jnp
from jax import lax
from jax.sharding import Mesh
from jax.sharding import PartitionSpec as P

HEAD = 128
DP = ("dp_0", "dp_1", "dp_2", "dp_3")


def copy_for_each(array, axis):
    count = lax.axis_size(axis)
    return lax.all_to_all(
        jnp.broadcast_to(array[None], (count, *array.shape)), axis, 0, 0, tiled=True
    )


def laid_out(tiles, dim):
    lengths = list(tiles.shape[1:])
    lengths[dim] *= tiles.shape[0]
    return jnp.moveaxis(tiles, 0, dim).reshape(lengths)


def gathered_by_axis(array, axes, dim):
    far, near = axes
    first = copy_for_each(array, far)
    tiles = jnp.swapaxes(copy_for_each(first, near), 0, 1)
    return laid_out(tiles.reshape(-1, *array.shape), dim)


def passed_along(value, axis, steps):
    count = lax.axis_size(axis)
    pairs = [(source, (source + steps) % count) for source in range(count)]
    return lax.ppermute(value, axis, pairs)


def cut_along(array, dim, count):
    lengths = array.shape
    tiles = array.reshape(*lengths[:dim], count, lengths[dim] // count, *lengths[dim + 1 :])
    return jnp.moveaxis(tiles, dim, 0)


def sent_and_summed(array, axis, dim):
    tiles = cut_along(array, dim, lax.axis_size(axis))
    arrived = lax.all_to_all(tiles, axis, split_axis=0, concat_axis=0, tiled=True)
    return arrived.sum(axis=0)


def summed_rows(array, axes, dim):
    far, near = axes
    tiles = cut_along(array, dim, lax.axis_size(far))
    nearer = sent_and_summed(tiles, near, dim + 1)
    arrived = lax.all_to_all(nearer, far, split_axis=0, concat_axis=0, tiled=True)
    return arrived.sum(axis=0)


def normalize(x_rows, scale_row):
    x32 = x_rows.astype(jnp.float32)
    rinv = lax.rsqrt(jnp.mean(x32 * x32, axis=-1, keepdims=True) + 1e-05)
    normed = x32 * rinv
    return (rinv, normed, (normed * scale_row).astype(jnp.bfloat16))


def on_device(saved, grad_out, gain, w_value):
    npipe = lax.axis_size("pipe")
    section = lax.axis_index("pipe")
    w_full = gathered_by_axis(w_value, (("dp_0", "dp_1", "dp_2"), "dp_3"), 1)
    w_mat = w_full[0]
    tok = saved.shape[2]
    width = saved.shape[3]
    kv_width = w_mat.shape[1]
    blocks = 2
    rows = tok // blocks
    kv_heads = kv_width // HEAD
    group = width // kv_width

    def one_step(k, carry):
        incoming, grad_buf, dv_buf = carry
        second = k - (npipe - 1) + section
        first = second - npipe
        in_second = (second >= 0) & (second < blocks)
        in_first = (first >= 0) & (first < blocks)
        valid = in_second | in_first
        loop_id = jnp.where(in_second, 1, 0).astype(jnp.int32)
        block = jnp.clip(jnp.where(in_second, second, first), 0, blocks - 1)
        start = block * rows
        zero = jnp.zeros((), jnp.int32)
        x_rows = lax.dynamic_slice(
            saved, (loop_id, zero, start, zero), (1, 1, rows, width)
        ).reshape(rows, width)
        fresh = lax.dynamic_slice_in_dim(grad_out, start, rows, 0)
        dy = jnp.where(in_second & (section == npipe - 1), fresh, incoming)
        dy = jnp.where(valid, dy, jnp.zeros_like(dy))
        scale_row = lax.dynamic_index_in_dim(gain[:, 0], loop_id, 0, keepdims=False)
        rinv, normed, _ = normalize(x_rows, scale_row)
        dv = dy.astype(jnp.float32).reshape(rows, kv_heads, group, HEAD).sum(2)
        dv = dv.reshape(rows, kv_width).astype(jnp.bfloat16)
        dh = lax.dot_general(
            dv, w_mat, (((1,), (1,)), ((), ())), preferred_element_type=jnp.float32
        )
        dhg = dh * scale_row
        dx = dy.astype(jnp.float32) + rinv * (
            dhg - normed * jnp.mean(dhg * normed, axis=-1, keepdims=True)
        )
        dx = dx.astype(jnp.bfloat16)
        old_x = lax.dynamic_slice(grad_buf, (loop_id, start, zero), (1, rows, width))
        grad_buf = lax.dynamic_update_slice(
            grad_buf, jnp.where(valid, dx[None], old_x), (loop_id, start, zero)
        )
        old_v = lax.dynamic_slice(dv_buf, (loop_id, start, zero), (1, rows, kv_width))
        dv_buf = lax.dynamic_update_slice(
            dv_buf, jnp.where(valid, dv[None], old_v), (loop_id, start, zero)
        )
        outgoing = passed_along(dx, "pipe", -1)
        return (outgoing, grad_buf, dv_buf)

    carry = (
        jnp.zeros((rows, width), jnp.bfloat16),
        jnp.zeros((2, tok, width), jnp.bfloat16),
        jnp.zeros((2, tok, kv_width), jnp.bfloat16),
    )
    carry = lax.fori_loop(0, blocks + 2 * npipe - 1, one_step, carry)
    _, _, hidden = normalize(saved[:, 0], gain[:, 0][:, None, :])
    hidden = hidden.reshape(2 * tok, width)
    dv_all = carry[2].reshape(2 * tok, kv_width)
    full_grad = lax.dot_general(
        hidden, dv_all, (((0,), (0,)), ((), ())), preferred_element_type=jnp.float32
    )
    grad_w = summed_rows(full_grad[None], (("dp_0", "dp_1", "dp_2"), "dp_3"), 1)
    grad_x = carry[1][:, None]
    return (grad_x, grad_w)


def solution(mesh):
    finer = Mesh(
        mesh.devices.reshape(mesh.shape["pipe"], 2, 4, 4, 2),
        ("pipe", "dp_0", "dp_1", "dp_2", "dp_3"),
    )
    placed = (P(None, "pipe", DP, None), P(DP, None), P(None, "pipe", None), P("pipe", DP, None))
    return jax.shard_map(
        on_device,
        mesh=finer,
        in_specs=placed,
        out_specs=(P(None, "pipe", DP, None), P("pipe", DP, None)),
        check_vma=False,
    )
```

profile of v0, /device:TPU:1, one launch (start us, length us, event | category | flops | bytes accessed | tf_op | source)
XLA Modules:
  0.0 430.2 jit_solution(6624458431490756222)
XLA Ops:
  0.6 2.4 broadcast_in_dim.49
  3.0 9.5 %all-to-all-start = ((bf16[32,1,64,512]{3,2,1,0:T(8,128)(2,1)}), bf16[32,1,64,512]{3,2,1,0:T(8,128)(2,1)}, u32[]{:S(2)}, u32[]{:S(2)}) async-start(bf16[32,1,64,512]{3,2,1,0:T(8,128)(2,1)} %broadcast_in_dim.49), calls=%async_computation | async-start | bytes 4194304 | tf_op jit(solution)/shard_map/all_to_all | solution.py:13
  13.8 1.9 fusion.10
  15.8 4.1 copy.10
  19.9 18.2 %all-to-all-done = bf16[32,1,64,512]{3,2,1,0:T(8,128)(2,1)} async-done(((bf16[32,1,64,512]{3,2,1,0:T(8,128)(2,1)}), bf16[32,1,64,512]{3,2,1,0:T(8,128)(2,1)}, u32[]{:S(2)}, u32[]{:S(2)}) %all-to-all-start) | async-done | bytes 2097184 | tf_op jit(solution)/shard_map/all_to_all | solution.py:13
  38.0 2.1 broadcast_in_dim.51
  40.1 10.7 %all_to_all.20 = bf16[2,32,1,64,512]{4,3,1,2,0:T(8,128)(2,1)S(1)} all-to-all(bf16[2,32,1,64,512]{4,3,1,2,0:T(8,128)(2,1)S(1)} %broadcast_in_dim.51), channel_id=1, replica_groups=mesh['pipe'=4,'dp_0'=2,'dp_1'=4,'dp_2'=4,'dp_3'=2] {'dp_3'}, dimensions={0} | all-to-all | bytes 8388608 | tf_op jit(solution)/shard_map/all_to_all | solution.py:13
  50.9 2.4 copy.9
  53.3 0.8 broadcast.74
  54.1 1.6 broadcast_in_dim.46
  55.7 265.9 %while.19 = (s32[]{:T(128)}, bf16[64,4096]{1,0:T(8,128)(2,1)}, bf16[2,128,4096]{2,1,0:T(8,128)(2,1)}, bf16[2,128,512]{2,1,0:T(8,128)(2,1)S(1)}, s32[]{:T(128)}, ...) while((s32[]{:T(128)}, bf16[64,4096]{1,0:T(8,128)(2,1)}, ...), condition=%wide.region_4.5_spmd, body=%wide.region_0.4_spmd.sunk | while | flops 274464864 | bytes 24761596 | solution.py:122
  56.6 1.3 convert_bitcast_fusion.2
  58.1 3.8 fusion.21
  62.0 2.3 fusion.22
  64.3 5.0 %collective-permute-start = (bf16[64,4096]{1,0:T(8,128)(2,1)S(1)}, bf16[64,4096]{1,0:T(8,128)(2,1)S(1)}, u32[]{:S(2)}, u32[]{:S(2)}) collective-permute-start(bf16[64,4096]{1,0:T(8,128)(2,1)S(1)} %get-tuple-element.323), channel_id=1, source_target_pairs={{0,192},{64,0},{128,64},{192,128},{1,193},{65,1},{129,65},{193,129... | collective-permute-start | bytes 1572872 | tf_op jit(solution)/shard_map/while/body/eval_jaxpr/ppermute | solution.py:34
  69.3 21.3 %collective-permute-done = bf16[64,4096]{1,0:T(8,128)(2,1)S(1)} collective-permute-done((bf16[64,4096]{1,0:T(8,128)(2,1)S(1)}, bf16[64,4096]{1,0:T(8,128)(2,1)S(1)}, u32[]{:S(2)}, u32[]{:S(2)}) %collective-permute-start) | collective-permute-done | bytes 524320 | tf_op jit(solution)/shard_map/while/body/eval_jaxpr/ppermute | solution.py:34
  90.6 0.8 copy-done.2
  92.3 1.3 convert_bitcast_fusion.2
  93.8 3.8 fusion.21
  97.6 2.3 fusion.22
  100.0 3.2 collective-permute-start
  103.3 20.8 %collective-permute-done = bf16[64,4096]{1,0:T(8,128)(2,1)S(1)} collective-permute-done((bf16[64,4096]{1,0:T(8,128)(2,1)S(1)}, bf16[64,4096]{1,0:T(8,128)(2,1)S(1)}, u32[]{:S(2)}, u32[]{:S(2)}) %collective-permute-start) | collective-permute-done | bytes 524320 | tf_op jit(solution)/shard_map/while/body/eval_jaxpr/ppermute | solution.py:34
  124.1 0.8 copy-done.2
  125.8 1.3 convert_bitcast_fusion.2
  127.3 3.8 fusion.21
  131.1 2.3 fusion.22
  133.5 1.2 collective-permute-start
  134.7 14.5 %collective-permute-done = bf16[64,4096]{1,0:T(8,128)(2,1)S(1)} collective-permute-done((bf16[64,4096]{1,0:T(8,128)(2,1)S(1)}, bf16[64,4096]{1,0:T(8,128)(2,1)S(1)}, u32[]{:S(2)}, u32[]{:S(2)}) %collective-permute-start) | collective-permute-done | bytes 524320 | tf_op jit(solution)/shard_map/while/body/eval_jaxpr/ppermute | solution.py:34
  149.3 0.8 copy-done.2
  151.0 1.3 convert_bitcast_fusion.2
  152.5 3.8 fusion.21
  156.3 2.3 fusion.22
  158.7 12.9 %collective-permute-done = bf16[64,4096]{1,0:T(8,128)(2,1)S(1)} collective-permute-done((bf16[64,4096]{1,0:T(8,128)(2,1)S(1)}, bf16[64,4096]{1,0:T(8,128)(2,1)S(1)}, u32[]{:S(2)}, u32[]{:S(2)}) %collective-permute-start) | collective-permute-done | bytes 524320 | tf_op jit(solution)/shard_map/while/body/eval_jaxpr/ppermute | solution.py:34
  171.7 0.8 copy-done.2
  173.4 1.3 convert_bitcast_fusion.2
  174.9 3.8 fusion.21
  178.7 2.3 fusion.22
  181.1 2.8 collective-permute-start
  184.0 11.9 %collective-permute-done = bf16[64,4096]{1,0:T(8,128)(2,1)S(1)} collective-permute-done((bf16[64,4096]{1,0:T(8,128)(2,1)S(1)}, bf16[64,4096]{1,0:T(8,128)(2,1)S(1)}, u32[]{:S(2)}, u32[]{:S(2)}) %collective-permute-start) | collective-permute-done | bytes 524320 | tf_op jit(solution)/shard_map/while/body/eval_jaxpr/ppermute | solution.py:34
  197.6 1.3 convert_bitcast_fusion.2
  199.1 3.8 fusion.21
  202.9 2.3 fusion.22
  205.3 4.3 %collective-permute-start = (bf16[64,4096]{1,0:T(8,128)(2,1)S(1)}, bf16[64,4096]{1,0:T(8,128)(2,1)S(1)}, u32[]{:S(2)}, u32[]{:S(2)}) collective-permute-start(bf16[64,4096]{1,0:T(8,128)(2,1)S(1)} %get-tuple-element.323), channel_id=1, source_target_pairs={{0,192},{64,0},{128,64},{192,128},{1,193},{65,1},{129,65},{193,129... | collective-permute-start | bytes 1572872 | tf_op jit(solution)/shard_map/while/body/eval_jaxpr/ppermute | solution.py:34
  209.6 12.0 %collective-permute-done = bf16[64,4096]{1,0:T(8,128)(2,1)S(1)} collective-permute-done((bf16[64,4096]{1,0:T(8,128)(2,1)S(1)}, bf16[64,4096]{1,0:T(8,128)(2,1)S(1)}, u32[]{:S(2)}, u32[]{:S(2)}) %collective-permute-start) | collective-permute-done | bytes 524320 | tf_op jit(solution)/shard_map/while/body/eval_jaxpr/ppermute | solution.py:34
  221.6 0.8 copy-done.2
  223.4 1.3 convert_bitcast_fusion.2
  224.8 3.8 fusion.21
  228.7 2.3 fusion.22
  231.1 15.5 %collective-permute-done = bf16[64,4096]{1,0:T(8,128)(2,1)S(1)} collective-permute-done((bf16[64,4096]{1,0:T(8,128)(2,1)S(1)}, bf16[64,4096]{1,0:T(8,128)(2,1)S(1)}, u32[]{:S(2)}, u32[]{:S(2)}) %collective-permute-start) | collective-permute-done | bytes 524320 | tf_op jit(solution)/shard_map/while/body/eval_jaxpr/ppermute | solution.py:34
  246.6 0.8 copy-done.2
  248.4 1.3 convert_bitcast_fusion.2
  249.8 3.8 fusion.21
  253.7 2.3 fusion.22
  256.3 31.0 %collective-permute-done = bf16[64,4096]{1,0:T(8,128)(2,1)S(1)} collective-permute-done((bf16[64,4096]{1,0:T(8,128)(2,1)S(1)}, bf16[64,4096]{1,0:T(8,128)(2,1)S(1)}, u32[]{:S(2)}, u32[]{:S(2)}) %collective-permute-start) | collective-permute-done | bytes 524320 | tf_op jit(solution)/shard_map/while/body/eval_jaxpr/ppermute | solution.py:34
  289.0 1.3 convert_bitcast_fusion.2
  290.5 3.8 fusion.21
  294.4 2.3 fusion.22
  296.8 24.0 %collective-permute-done = bf16[64,4096]{1,0:T(8,128)(2,1)S(1)} collective-permute-done((bf16[64,4096]{1,0:T(8,128)(2,1)S(1)}, bf16[64,4096]{1,0:T(8,128)(2,1)S(1)}, u32[]{:S(2)}, u32[]{:S(2)}) %collective-permute-start) | collective-permute-done | bytes 524320 | tf_op jit(solution)/shard_map/while/body/eval_jaxpr/ppermute | solution.py:34
  321.6 2.8 convolution_bitcast_fusion
  324.4 1.8 copy.11
  326.2 35.1 %all_to_all.21 = f32[2,32,1,64,512]{4,3,1,2,0:T(8,128)} all-to-all(f32[2,32,1,64,512]{4,3,1,2,0:T(8,128)S(1)} %copy.11), channel_id=1, replica_groups=mesh['pipe'=4,'dp_0'=2,'dp_1'=4,'dp_2'=4,'dp_3'=2] {'dp_3'}, dimensions={0} | all-to-all | bytes 16777216 | tf_op jit(solution)/shard_map/all_to_all | solution.py:45
  361.3 6.8 %reduce_sum.80 = f32[32,64,512]{2,1,0:T(8,128)} reduce(f32[2,32,1,64,512]{4,3,1,2,0:T(8,128)} %all_to_all.21, f32[]{:T(128)} %constant.135.clone.1), dimensions={0,2}, to_apply=%region_6.7 | reduce | flops 1048576 | bytes 12582916 | tf_op jit(solution)/shard_map/reduce_sum | solution.py:46
  368.1 59.0 %all_to_all.22 = f32[32,1,64,512]{3,2,1,0:T(8,128)} all-to-all(f32[32,1,64,512]{3,2,1,0:T(8,128)} %bitcast.80), channel_id=1, replica_groups=mesh['pipe'=4,'dp_0'=2,'dp_1'=4,'dp_2'=4,'dp_3'=2] {'dp_0','dp_1','dp_2'}, dimensions={0} | all-to-all | bytes 8388608 | tf_op jit(solution)/shard_map/all_to_all | solution.py:53
  427.1 3.2 reduce_sum.82
  (130 shorter events, 13.9 us)
Async XLA Ops:
  3.0 10.3 %copy-start = (bf16[2,1,128,4096]{3,2,1,0:T(8,128)(2,1)S(1)}, bf16[2,1,128,4096]{3,2,1,0:T(8,128)(2,1)}, u32[]{:S(2)}) copy-start(bf16[2,1,128,4096]{3,2,1,0:T(8,128)(2,1)} %param.6) | copy-start | bytes 6291460
  3.0 35.0 %all-to-all-start = ((bf16[32,1,64,512]{3,2,1,0:T(8,128)(2,1)}), bf16[32,1,64,512]{3,2,1,0:T(8,128)(2,1)}, u32[]{:S(2)}, u32[]{:S(2)}) async-start(bf16[32,1,64,512]{3,2,1,0:T(8,128)(2,1)} %broadcast_in_dim.49), calls=%async_computation | async-start | bytes 4194304 | tf_op jit(solution)/shard_map/all_to_all | solution.py:13
  58.1 3.8 copy-start.1
  58.1 3.8 copy-start.3
  64.3 26.3 %collective-permute-start = (bf16[64,4096]{1,0:T(8,128)(2,1)S(1)}, bf16[64,4096]{1,0:T(8,128)(2,1)S(1)}, u32[]{:S(2)}, u32[]{:S(2)}) collective-permute-start(bf16[64,4096]{1,0:T(8,128)(2,1)S(1)} %get-tuple-element.323), channel_id=1, source_target_pairs={{0,192},{64,0},{128,64},{192,128},{1,193},{65,1},{129,65},{193,129... | collective-permute-start | bytes 1572872 | tf_op jit(solution)/shard_map/while/body/eval_jaxpr/ppermute | solution.py:34
  90.6 0.8 copy-start.2
  93.8 3.8 copy-start.1
  93.8 3.8 copy-start.3
  100.0 24.1 %collective-permute-start = (bf16[64,4096]{1,0:T(8,128)(2,1)S(1)}, bf16[64,4096]{1,0:T(8,128)(2,1)S(1)}, u32[]{:S(2)}, u32[]{:S(2)}) collective-permute-start(bf16[64,4096]{1,0:T(8,128)(2,1)S(1)} %get-tuple-element.323), channel_id=1, source_target_pairs={{0,192},{64,0},{128,64},{192,128},{1,193},{65,1},{129,65},{193,129... | collective-permute-start | bytes 1572872 | tf_op jit(solution)/shard_map/while/body/eval_jaxpr/ppermute | solution.py:34
  124.1 0.8 copy-start.2
  127.3 3.8 copy-start.1
  127.3 3.8 copy-start.3
  133.5 15.8 %collective-permute-start = (bf16[64,4096]{1,0:T(8,128)(2,1)S(1)}, bf16[64,4096]{1,0:T(8,128)(2,1)S(1)}, u32[]{:S(2)}, u32[]{:S(2)}) collective-permute-start(bf16[64,4096]{1,0:T(8,128)(2,1)S(1)} %get-tuple-element.323), channel_id=1, source_target_pairs={{0,192},{64,0},{128,64},{192,128},{1,193},{65,1},{129,65},{193,129... | collective-permute-start | bytes 1572872 | tf_op jit(solution)/shard_map/while/body/eval_jaxpr/ppermute | solution.py:34
  149.3 0.8 copy-start.2
  152.5 3.8 copy-start.1
  152.5 3.8 copy-start.3
  158.7 13.0 %collective-permute-start = (bf16[64,4096]{1,0:T(8,128)(2,1)S(1)}, bf16[64,4096]{1,0:T(8,128)(2,1)S(1)}, u32[]{:S(2)}, u32[]{:S(2)}) collective-permute-start(bf16[64,4096]{1,0:T(8,128)(2,1)S(1)} %get-tuple-element.323), channel_id=1, source_target_pairs={{0,192},{64,0},{128,64},{192,128},{1,193},{65,1},{129,65},{193,129... | collective-permute-start | bytes 1572872 | tf_op jit(solution)/shard_map/while/body/eval_jaxpr/ppermute | solution.py:34
  171.7 0.8 copy-start.2
  174.9 3.8 copy-start.1
  174.9 3.8 copy-start.3
  181.1 14.8 %collective-permute-start = (bf16[64,4096]{1,0:T(8,128)(2,1)S(1)}, bf16[64,4096]{1,0:T(8,128)(2,1)S(1)}, u32[]{:S(2)}, u32[]{:S(2)}) collective-permute-start(bf16[64,4096]{1,0:T(8,128)(2,1)S(1)} %get-tuple-element.323), channel_id=1, source_target_pairs={{0,192},{64,0},{128,64},{192,128},{1,193},{65,1},{129,65},{193,129... | collective-permute-start | bytes 1572872 | tf_op jit(solution)/shard_map/while/body/eval_jaxpr/ppermute | solution.py:34
  195.9 0.8 copy-start.2
  199.1 3.8 copy-start.1
  199.1 3.8 copy-start.3
  205.3 16.3 %collective-permute-start = (bf16[64,4096]{1,0:T(8,128)(2,1)S(1)}, bf16[64,4096]{1,0:T(8,128)(2,1)S(1)}, u32[]{:S(2)}, u32[]{:S(2)}) collective-permute-start(bf16[64,4096]{1,0:T(8,128)(2,1)S(1)} %get-tuple-element.323), channel_id=1, source_target_pairs={{0,192},{64,0},{128,64},{192,128},{1,193},{65,1},{129,65},{193,129... | collective-permute-start | bytes 1572872 | tf_op jit(solution)/shard_map/while/body/eval_jaxpr/ppermute | solution.py:34
  221.6 0.8 copy-start.2
  224.8 3.8 copy-start.1
  224.8 3.8 copy-start.3
  231.0 15.6 %collective-permute-start = (bf16[64,4096]{1,0:T(8,128)(2,1)S(1)}, bf16[64,4096]{1,0:T(8,128)(2,1)S(1)}, u32[]{:S(2)}, u32[]{:S(2)}) collective-permute-start(bf16[64,4096]{1,0:T(8,128)(2,1)S(1)} %get-tuple-element.323), channel_id=1, source_target_pairs={{0,192},{64,0},{128,64},{192,128},{1,193},{65,1},{129,65},{193,129... | collective-permute-start | bytes 1572872 | tf_op jit(solution)/shard_map/while/body/eval_jaxpr/ppermute | solution.py:34
  246.6 0.8 copy-start.2
  249.8 3.8 copy-start.1
  249.8 3.8 copy-start.3
  256.0 31.3 %collective-permute-start = (bf16[64,4096]{1,0:T(8,128)(2,1)S(1)}, bf16[64,4096]{1,0:T(8,128)(2,1)S(1)}, u32[]{:S(2)}, u32[]{:S(2)}) collective-permute-start(bf16[64,4096]{1,0:T(8,128)(2,1)S(1)} %get-tuple-element.323), channel_id=1, source_target_pairs={{0,192},{64,0},{128,64},{192,128},{1,193},{65,1},{129,65},{193,129... | collective-permute-start | bytes 1572872 | tf_op jit(solution)/shard_map/while/body/eval_jaxpr/ppermute | solution.py:34
  287.3 0.8 copy-start.2
  290.5 3.8 copy-start.1
  290.5 3.8 copy-start.3
  296.7 24.1 %collective-permute-start = (bf16[64,4096]{1,0:T(8,128)(2,1)S(1)}, bf16[64,4096]{1,0:T(8,128)(2,1)S(1)}, u32[]{:S(2)}, u32[]{:S(2)}) collective-permute-start(bf16[64,4096]{1,0:T(8,128)(2,1)S(1)} %get-tuple-element.323), channel_id=1, source_target_pairs={{0,192},{64,0},{128,64},{192,128},{1,193},{65,1},{129,65},{193,129... | collective-permute-start | bytes 1572872 | tf_op jit(solution)/shard_map/while/body/eval_jaxpr/ppermute | solution.py:34
  320.8 0.8 copy-start.2
where the time goes:
time: 434 us; the launch traced here: 430 us
  waiting for transfers between devices  182 us (42%)
  blocking collectives  105 us (24%)
  other arithmetic  48.4 us (11%)
  matrix products  37 us (9%)
  local copies, waits for them, and re-layouts  30.4 us (7%)
  starting transfers between devices  26.3 us (6%)
    ppermute x9, waiting for transfers between devices, passed_along(): return lax.ppermute(value, axis, pairs)  164 us
    all_to_all x1, blocking collectives, summed_rows(): lax.all_to_all(nearer, far, split_axis=0, concat_axis=0, tiled=True)  59 us
    all_to_all x1, blocking collectives, sent_and_summed(): lax.all_to_all(tiles, axis, split_axis=0, concat_axis=0, tiled=True)  35.1 us
    dot_general x9, matrix products, one_step(): lax.dot_general(dv, w_mat, (((1,), (1,)), ((), ())), preferred_element_ty...  34.2 us
    dynamic_update_slice x9, other arithmetic, one_step(): lax.dynamic_update_slice(grad_buf, jnp.where(valid, dx[None], old_x), (lo...  21.1 us
    all_to_all x1, waiting for transfers between devices, copy_for_each(): lax.all_to_all(jnp.broadcast_to(array[None], (count, *array.shape)), axis...  18.2 us
    ppermute x9, starting transfers between devices, passed_along(): return lax.ppermute(value, axis, pairs)  16.8 us
    while x18, other arithmetic  12.6 us
  transfers between devices with their start and end apart: 10, of which 10 were waited for; matrix products, arithmetic and copies ran while one was open for 2% of the time, Pallas kernels for 0%

commit v1 on v0

v1 whole, which is shorter than its diff:
```python
import functools

import jax
import jax.numpy as jnp
from jax import lax
from jax.experimental import pallas as pl
from jax.experimental.pallas import tpu as pltpu
from jax.sharding import Mesh
from jax.sharding import PartitionSpec as P

HEAD = 128
ROWS = 16
SLACK = 2
DP = ("dp_0", "dp_1", "dp_2", "dp_3")
IN_VMEM = pl.BlockSpec(memory_space=pltpu.VMEM)
IN_SMEM = pl.BlockSpec(memory_space=pltpu.SMEM)
ANYWHERE = pl.BlockSpec(memory_space=pl.ANY)


def copy_for_each(array, axis):
    count = lax.axis_size(axis)
    return lax.all_to_all(
        jnp.broadcast_to(array[None], (count, *array.shape)), axis, 0, 0, tiled=True
    )


def gathered_rows(array):
    first = copy_for_each(array, DP[:3])
    tiles = jnp.swapaxes(copy_for_each(first, DP[3]), 0, 1)
    return tiles.reshape(-1, array.shape[-1])


def task_of(step, section, npipe):
    return step - SLACK * (npipe - 1 - section)


def step_kernel(step, npipe, blocks, where, w_ref, x_ref, g_ref, fresh_ref, in_ref, dx_ref, dv_ref):
    section = where[0]
    task = task_of(step, section, npipe)

    @pl.when((task >= 0) & (task < 2 * blocks))
    def _():
        later = task < blocks
        loop = jnp.where(later, 1, 0)
        block = jnp.where(later, task, task - blocks)
        row = pl.multiple_of(block * ROWS, ROWS)
        width = dx_ref.shape[1]
        kv_width = dv_ref.shape[1]
        heads = kv_width // HEAD
        group = width // kv_width
        take = later & (section == npipe - 1)
        dy = jnp.where(take, fresh_ref[pl.ds(row, ROWS), :], in_ref[...]).astype(jnp.float32)
        x = x_ref[loop, pl.ds(row, ROWS), :].astype(jnp.float32)
        sums = []
        for head in range(heads):
            base = head * group * HEAD
            total = dy[:, base : base + HEAD]
            for member in range(1, group):
                at = base + member * HEAD
                total = total + dy[:, at : at + HEAD]
            sums.append(total)
        dv = jnp.concatenate(sums, axis=1).astype(jnp.bfloat16)
        dv_ref[...] = dv
        dh = lax.dot_general(
            dv, w_ref[...], (((1,), (1,)), ((), ())), preferred_element_type=jnp.float32
        )
        dhg = dh * g_ref[loop]
        rinv = lax.rsqrt(jnp.mean(x * x, axis=-1, keepdims=True) + 1e-05)
        normed = x * rinv
        along = jnp.mean(dhg * normed, axis=-1, keepdims=True)
        dx_ref[...] = (dy + rinv * (dhg - normed * along)).astype(jnp.bfloat16)


def one_step(step, npipe, blocks, where, w_mat, x, gain, fresh, incoming):
    rows, width = incoming.shape
    kv_width = w_mat.shape[1]
    return pl.pallas_call(
        functools.partial(step_kernel, step, npipe, blocks),
        out_shape=(
            jax.ShapeDtypeStruct((rows, width), jnp.bfloat16),
            jax.ShapeDtypeStruct((rows, kv_width), jnp.bfloat16),
        ),
        in_specs=[IN_SMEM] + [IN_VMEM] * 5,
        out_specs=(IN_VMEM, IN_VMEM),
        compiler_params=pltpu.CompilerParams(vmem_limit_bytes=32 * 2**20),
        name="section_step",
    )(where, w_mat, x, gain, fresh, incoming)


def collect_kernel(npipe, blocks, where, *refs):
    *pieces, out_ref, sems = refs
    section = where[0]

    def each(act):
        for step, piece in enumerate(pieces):
            task = task_of(step, section, npipe)

            @pl.when((task >= 0) & (task < 2 * blocks))
            def _():
                later = task < blocks
                loop = jnp.where(later, 1, 0)
                row = pl.multiple_of((task - jnp.where(later, 0, blocks)) * ROWS, ROWS)
                target = out_ref.at[loop, pl.ds(row, ROWS), :]
                act(pltpu.make_async_copy(piece, target, sems.at[step]))

    each(lambda copy: copy.start())
    each(lambda copy: copy.wait())


def collected(where, pieces, npipe, blocks):
    width = pieces[0].shape[1]
    return pl.pallas_call(
        functools.partial(collect_kernel, npipe, blocks),
        out_shape=jax.ShapeDtypeStruct((2, blocks * ROWS, width), jnp.bfloat16),
        in_specs=[IN_SMEM] + [ANYWHERE] * len(pieces),
        out_specs=ANYWHERE,
        scratch_shapes=[pltpu.SemaphoreType.DMA((len(pieces),))],
        name="collect_rows",
    )(where, *pieces)


def on_device(saved, grad_out, gain, w_value):
    npipe = lax.axis_size("pipe")
    section = lax.axis_index("pipe")
    where = section.astype(jnp.int32).reshape(1)
    x = saved[:, 0]
    scale = gain
    _, tok, width = x.shape
    blocks = tok // ROWS
    w_mat = gathered_rows(w_value[0])
    kv_width = w_mat.shape[1]

    x32 = x.astype(jnp.float32)
    rinv = lax.rsqrt(jnp.mean(x32 * x32, axis=-1, keepdims=True) + 1e-05)
    hidden = (x32 * rinv * scale).astype(jnp.bfloat16)
    far, across = lax.axis_size("dp_0"), lax.axis_size("dp_1")
    near = width // (far * across)
    tiles = hidden.reshape(2, tok, far, across, near).transpose(3, 0, 1, 2, 4)
    tiles = tiles.reshape(across, 2, tok, far * near)
    tiles = lax.all_to_all(tiles, "dp_1", 0, 0, tiled=True)

    steps = 2 * blocks + SLACK * (npipe - 1)
    sent, gx_parts, gv_parts = {}, [], []
    for step in range(steps):
        incoming = sent.pop(step - SLACK, None)
        if incoming is None:
            incoming = jnp.zeros((ROWS, width), jnp.bfloat16)
        dx, dv = one_step(step, npipe, blocks, where, w_mat, x, scale, grad_out, incoming)
        gx_parts.append(dx)
        gv_parts.append(dv)
        pairs = []
        for source in range(npipe):
            task = task_of(step, source, npipe)
            if 0 <= task < (blocks if source == 0 else 2 * blocks):
                pairs.append((source, (source - 1) % npipe))
        if pairs:
            sent[step] = lax.ppermute(dx, "pipe", pairs)

    grad_x = collected(where, gx_parts, npipe, blocks)[:, None]

    offset = SLACK * (npipe - 1 - section) * ROWS
    span = blocks + SLACK * (npipe - 1)
    grad_w = None
    for loop, first in ((1, 0), (0, blocks)):
        stacked = jnp.concatenate(gv_parts[first : first + span], axis=0)
        dv = lax.dynamic_slice_in_dim(stacked, offset, tok, 0)
        everyone = copy_for_each(dv, "dp_1").reshape(across * tok, kv_width)
        rows = tiles[:, loop].reshape(across * tok, far * near)
        part = lax.dot_general(
            rows, everyone, (((0,), (0,)), ((), ())), preferred_element_type=jnp.float32
        )
        grad_w = part if grad_w is None else grad_w + part
    others = ("dp_0", "dp_2", "dp_3")
    count = lax.axis_size(others)
    pieces = grad_w.astype(jnp.bfloat16).reshape(count, -1, kv_width)
    arrived = lax.all_to_all(pieces, others, 0, 0, tiled=True)
    grad_w = arrived.astype(jnp.float32).sum(axis=0)[None]
    return (grad_x, grad_w)


def solution(mesh):
    finer = Mesh(
        mesh.devices.reshape(mesh.shape["pipe"], 2, 4, 4, 2),
        ("pipe", "dp_0", "dp_1", "dp_2", "dp_3"),
    )
    placed = (P(None, "pipe", DP, None), P(DP, None), P(None, "pipe", None), P("pipe", DP, None))
    return jax.shard_map(
        on_device,
        mesh=finer,
        in_specs=placed,
        out_specs=(P(None, "pipe", DP, None), P("pipe", DP, None)),
        check_vma=False,
    )
```

time: 434 us -> 294 us (0.68)
  waiting for transfers between devices: 182 us -> 73.6 us
  blocking collectives: 105 us -> 11.7 us
  Pallas kernels: 0 us -> 87.7 us
  starting transfers between devices: 26.3 us -> 79.4 us
  other arithmetic: 48.4 us -> 2.76 us
  matrix products: 37 us -> 4.88 us
    ppermute x9 -> x20, waiting for transfers between devices: 164 us -> 53.5 us  [on_device(): sent[step] = lax.ppermute(dx, 'pipe', pairs)]
    all_to_all x2 -> x0, blocking collectives: 94 us -> none  [the longest x1 59 us: summed_rows(): lax.all_to_all(nearer, far, split_axis=0, concat_axis=0, tiled=True)]
    pallas_call x0 -> x23, Pallas kernels: none -> 87.7 us  [the longest x1 64.8 us: collected(): pl.pallas_call(functools.partial(collect_kernel, npipe, blocks), out_shap...]
    dot_general x10 -> x2, matrix products: 37 us -> 4.88 us  [on_device(): lax.dot_general(rows, everyone, (((0,), (0,)), ((), ())), preferred_eleme...]
    all_to_all x1 -> x3, starting transfers between devices: 9.48 us -> 35.5 us  [copy_for_each(): lax.all_to_all(jnp.broadcast_to(array[None], (count, *array.shape)), axis...]
    dynamic_update_slice x18 -> x0, other arithmetic: 21.3 us -> none  [the longest x9 21.1 us: one_step(): lax.dynamic_update_slice(grad_buf, jnp.where(valid, dx[None], old_x), (lo...]
    ppermute x9 -> x20, starting transfers between devices: 16.8 us -> 32 us  [on_device(): sent[step] = lax.ppermute(dx, 'pipe', pairs)]
    unnamed x3 -> x74, local copies, waits for them, and re-layouts: 0.79 us -> 14.5 us
  transfers between devices with their start and end apart: 10 -> 25, of which waited for: 10 -> 11; matrix products, arithmetic and copies ran while one was open for 2% -> 9% of each run, Pallas kernels for 0% -> 30%
where the time goes in v1:
time: 294 us; the launch traced here: 293 us
  Pallas kernels  87.7 us (30%)
  starting transfers between devices  79.4 us (27%)
  waiting for transfers between devices  73.6 us (25%)
  local copies, waits for them, and re-layouts  31.4 us (11%)
  blocking collectives  11.7 us (4%)
  matrix products  4.88 us (2%)
    pallas_call x1, Pallas kernels, collected(): pl.pallas_call(functools.partial(collect_kernel, npipe, blocks), out_shap...  64.8 us
    ppermute x20, waiting for transfers between devices, on_device(): sent[step] = lax.ppermute(dx, 'pipe', pairs)  53.5 us
    all_to_all x3, starting transfers between devices, copy_for_each(): lax.all_to_all(jnp.broadcast_to(array[None], (count, *array.shape)), axis...  35.5 us
    ppermute x20, starting transfers between devices, on_device(): sent[step] = lax.ppermute(dx, 'pipe', pairs)  32 us
    pallas_call x22, Pallas kernels, one_step(): pl.pallas_call(functools.partial(step_kernel, step, npipe, blocks), out_s...  22.9 us
    all_to_all x3, waiting for transfers between devices, copy_for_each(): lax.all_to_all(jnp.broadcast_to(array[None], (count, *array.shape)), axis...  20.1 us
    unnamed x74, local copies, waits for them, and re-layouts  14.5 us
    all_to_all x1, blocking collectives, copy_for_each(): lax.all_to_all(jnp.broadcast_to(array[None], (count, *array.shape)), axis...  11.7 us
  transfers between devices with their start and end apart: 25, of which 11 were waited for; matrix products, arithmetic and copies ran while one was open for 9% of the time, Pallas kernels for 30%

profile of v1, /device:TPU:1, one launch (start us, length us, event | category | flops | bytes accessed | tf_op | source)
XLA Modules:
  0.0 293.0 jit_solution(1590362584749942875)
XLA Ops:
  0.6 2.4 broadcast_in_dim.15
  3.0 9.5 %all-to-all-start = ((bf16[32,64,512]{2,1,0:T(8,128)(2,1)}), bf16[32,64,512]{2,1,0:T(8,128)(2,1)}, u32[]{:S(2)}, u32[]{:S(2)}) async-start(bf16[32,64,512]{2,1,0:T(8,128)(2,1)} %broadcast_in_dim.15), calls=%async_computation | async-start | bytes 4194304 | tf_op jit(solution)/shard_map/all_to_all | solution.py:22
  12.6 2.5 copy.15
  15.7 1.1 copy-done.25
  16.7 1.4 fusion.2
  18.1 1.5 copy.16
  19.7 18.4 %all-to-all-done = bf16[32,64,512]{2,1,0:T(8,128)(2,1)} async-done(((bf16[32,64,512]{2,1,0:T(8,128)(2,1)}), bf16[32,64,512]{2,1,0:T(8,128)(2,1)}, u32[]{:S(2)}, u32[]{:S(2)}) %all-to-all-start) | async-done | bytes 2097184 | tf_op jit(solution)/shard_map/all_to_all | solution.py:22
  38.0 2.1 broadcast_in_dim.16
  40.1 11.7 %all_to_all.30 = bf16[2,32,64,512]{3,2,1,0:T(8,128)(2,1)} all-to-all(bf16[2,32,64,512]{3,2,1,0:T(8,128)(2,1)S(1)} %broadcast_in_dim.16), channel_id=1, replica_groups=mesh['pipe'=4,'dp_0'=2,'dp_1'=4,'dp_2'=4,'dp_3'=2] {'dp_3'}, dimensions={0} | all-to-all | bytes 8388608 | tf_op jit(solution)/shard_map/all_to_all | solution.py:22
  51.9 4.5 %all-to-all-start.2 = ((bf16[4,2,128,1024]{2,3,1,0:T(8,128)(2,1)}), bf16[4,2,128,1024]{2,3,1,0:T(8,128)(2,1)}, u32[]{:S(2)}, u32[]{:S(2)}) async-start(bf16[4,2,128,1024]{2,3,1,0:T(8,128)(2,1)} %bitcast.70), calls=%async_computation.2 | async-start | bytes 4194304 | tf_op jit(solution)/shard_map/all_to_all | solution.py:140
  56.4 2.5 copy.14
  62.7 1.3 collective-permute-start.4
  64.0 1.3 collective-permute-start.5
  65.3 33.9 %collective-permute-done.4.in_ref = bf16[16,4096]{1,0:T(8,128)(2,1)S(1)} collective-permute-done((bf16[16,4096]{1,0:T(8,128)(2,1)S(1)}, bf16[16,4096]{1,0:T(8,128)(2,1)S(1)}, u32[]{:S(2)}, u32[]{:S(2)}) %collective-permute-start.4) | collective-permute-done | bytes 131104 | tf_op jit(solution)/shard_map/ppermute | solution.py:157
  99.3 1.3 section_step.28
  100.7 5.2 %collective-permute-start.6 = (bf16[16,4096]{1,0:T(8,128)(2,1)S(1)}, bf16[16,4096]{1,0:T(8,128)(2,1)S(1)}, u32[]{:S(2)}, u32[]{:S(2)}) collective-permute-start(bf16[16,4096]{1,0:T(8,128)(2,1)S(1)} %get-tuple-element.52.refs_6_), channel_id=1, source_target_pairs={{0,192},{64,0},{128,64},{192,128},{1,193},{65,1},{129,65},{193,129... | collective-permute-start | bytes 393224 | tf_op jit(solution)/shard_map/ppermute | solution.py:157
  105.9 1.3 section_step.29
  107.2 3.3 %collective-permute-start.7 = (bf16[16,4096]{1,0:T(8,128)(2,1)S(1)}, bf16[16,4096]{1,0:T(8,128)(2,1)S(1)}, u32[]{:S(2)}, u32[]{:S(2)}) collective-permute-start(bf16[16,4096]{1,0:T(8,128)(2,1)S(1)} %get-tuple-element.53.refs_7_), channel_id=1, source_target_pairs={{0,192},{64,0},{128,64},{192,128},{1,193},{65,1},{129,65},{193,129... | collective-permute-start | bytes 393224 | tf_op jit(solution)/shard_map/ppermute | solution.py:157
  110.5 2.8 collective-permute-done.6.in_ref
  113.4 1.3 section_step.30
  114.7 1.4 collective-permute-start.8
  116.1 1.3 section_step.31
  117.5 3.2 %collective-permute-start.9 = (bf16[16,4096]{1,0:T(8,128)(2,1)S(1)}, bf16[16,4096]{1,0:T(8,128)(2,1)S(1)}, u32[]{:S(2)}, u32[]{:S(2)}) collective-permute-start(bf16[16,4096]{1,0:T(8,128)(2,1)S(1)} %get-tuple-element.55.refs_9_), channel_id=1, source_target_pairs={{0,192},{64,0},{128,64},{192,128},{1,193},{65,1},{129,65},{193,129... | collective-permute-start | bytes 393224 | tf_op jit(solution)/shard_map/ppermute | solution.py:157
  121.9 2.4 collective-permute-done.8.in_ref
  124.3 1.3 section_step.32
  125.6 1.6 collective-permute-start.10
  127.2 1.9 collective-permute-done.9.in_ref
  129.1 1.3 section_step.33
  132.1 1.7 collective-permute-done.10.in_ref
  133.8 1.3 section_step.34
  135.2 1.7 collective-permute-start.12
  136.9 1.3 section_step.35
  138.3 2.3 collective-permute-start.13
  142.4 2.7 collective-permute-done.12.in_ref
  145.1 1.3 section_step.36
  146.4 1.3 collective-permute-start.14
  148.2 1.3 section_step.37
  149.5 1.3 collective-permute-start.15
  152.0 3.4 %collective-permute-done.14.in_ref = bf16[16,4096]{1,0:T(8,128)(2,1)S(1)} collective-permute-done((bf16[16,4096]{1,0:T(8,128)(2,1)S(1)}, bf16[16,4096]{1,0:T(8,128)(2,1)S(1)}, u32[]{:S(2)}, u32[]{:S(2)}) %collective-permute-start.14) | collective-permute-done | bytes 131104 | tf_op jit(solution)/shard_map/ppermute | solution.py:157
  155.5 1.3 section_step.38
  156.8 1.3 collective-permute-start.16
  158.1 1.3 section_step.39
  159.5 1.3 collective-permute-start.17
  162.0 4.2 %collective-permute-done.16.in_ref = bf16[16,4096]{1,0:T(8,128)(2,1)S(1)} collective-permute-done((bf16[16,4096]{1,0:T(8,128)(2,1)S(1)}, bf16[16,4096]{1,0:T(8,128)(2,1)S(1)}, u32[]{:S(2)}, u32[]{:S(2)}) %collective-permute-start.16) | collective-permute-done | bytes 131104 | tf_op jit(solution)/shard_map/ppermute | solution.py:157
  166.2 2.0 section_step.40
  168.2 1.3 collective-permute-start.18
  169.5 2.0 section_step.41
  171.5 1.3 collective-permute-start.19
  173.4 1.7 broadcast_in_dim.36
  175.2 21.8 %all-to-all-start.3 = ((bf16[4,128,512]{2,1,0:T(8,128)(2,1)}), bf16[4,128,512]{2,1,0:T(8,128)(2,1)}, u32[]{:S(2)}, u32[]{:S(2)}) async-start(bf16[4,128,512]{2,1,0:T(8,128)(2,1)} %broadcast_in_dim.36), calls=%async_computation.3 | async-start | bytes 1048576 | tf_op jit(solution)/shard_map/all_to_all | solution.py:22
  197.6 2.2 copy-done.1
  199.8 1.3 section_step.42
  201.1 1.4 section_step.43
  203.8 0.9 constant_dynamic-slice_fusion
  204.7 0.9 broadcast_in_dim.37
  205.6 4.2 %all-to-all-start.4 = ((bf16[4,128,512]{2,1,0:T(8,128)(2,1)}), bf16[4,128,512]{2,1,0:T(8,128)(2,1)}, u32[]{:S(2)}, u32[]{:S(2)}) async-start(bf16[4,128,512]{2,1,0:T(8,128)(2,1)} %broadcast_in_dim.37), calls=%async_computation.4 | async-start | bytes 1048576 | tf_op jit(solution)/shard_map/all_to_all | solution.py:22
  209.8 1.7 fusion.3
  212.0 1.3 copy.18
  213.4 1.8 fusion.4
  215.1 1.7 all-to-all-done.4
  216.8 3.1 %add_convert_fusion = bf16[1024,512]{1,0:T(8,128)(2,1)} fusion(f32[1024,512]{1,0:T(8,128)S(1)} %fusion.4, bf16[512,1024]{1,0:T(8,128)(2,1)} %bitcast.72, bf16[512,512]{1,0:T(8,128)(2,1)} %bitcast.13), kind=kOutput, calls=%fused_computation.6 | convolution fusion | flops 537919488 | bytes 4718592 | tf_op jit(solution)/shard_map/dot_general | solution.py:169
  219.9 7.4 %all-to-all-start.5 = ((bf16[16,64,512]{2,1,0:T(8,128)(2,1)}), bf16[16,64,512]{2,1,0:T(8,128)(2,1)S(1)}, u32[]{:S(2)}, u32[]{:S(2)}) async-start(bf16[16,64,512]{2,1,0:T(8,128)(2,1)} %bitcast.14), calls=%async_computation.5 | async-start | bytes 2097152 | tf_op jit(solution)/shard_map/all_to_all | solution.py:176
  227.3 64.8 %collect_rows.1 = bf16[2,128,4096]{2,1,0:T(8,128)(2,1)} custom-call(s32[1]{0:T(128)} %bitcast.where, bf16[16,4096]{1,0:T(8,128)(2,1)} %copy-done.5, bf16[16,4096]{1,0:T(8,128)(2,1)} %copy-done.6, bf16[16,4096]{1,0:T(8,128)(2,1)} %copy-done.7, bf16[16,4096]{1,0:T(8,128)(2,1)} %copy-done.8, bf16[16,4096]{1,0:T(8,128)(2,1)} %copy-done.9, ...), custom_call_target="tpu_custom_call" | custom-call | tf_op jit(solution)/shard_map/collect_rows/pallas_call | solution.py:112
  292.2 0.8 convert_reduce_fusion
  (105 shorter events, 14.8 us)
Async XLA Ops:
  3.0 9.5 %copy-start.2 = (bf16[2,1,128,4096]{3,2,1,0:T(8,128)(2,1)S(1)}, bf16[2,1,128,4096]{3,2,1,0:T(8,128)(2,1)}, u32[]{:S(2)}) copy-start(bf16[2,1,128,4096]{3,2,1,0:T(8,128)(2,1)} %param.4) | copy-start | bytes 6291460
  3.0 35.0 %all-to-all-start = ((bf16[32,64,512]{2,1,0:T(8,128)(2,1)}), bf16[32,64,512]{2,1,0:T(8,128)(2,1)}, u32[]{:S(2)}, u32[]{:S(2)}) async-start(bf16[32,64,512]{2,1,0:T(8,128)(2,1)} %broadcast_in_dim.15), calls=%async_computation | async-start | bytes 4194304 | tf_op jit(solution)/shard_map/all_to_all | solution.py:22
  12.5 2.5 copy-start.4
  15.2 1.6 copy-start.25
  51.9 121.5 %all-to-all-start.2 = ((bf16[4,2,128,1024]{2,3,1,0:T(8,128)(2,1)}), bf16[4,2,128,1024]{2,3,1,0:T(8,128)(2,1)}, u32[]{:S(2)}, u32[]{:S(2)}) async-start(bf16[4,2,128,1024]{2,3,1,0:T(8,128)(2,1)} %bitcast.70), calls=%async_computation.2 | async-start | bytes 4194304 | tf_op jit(solution)/shard_map/all_to_all | solution.py:140
  56.4 2.6 copy-start.3
  58.9 110.6 %copy-start = (bf16[32,2,64,512]{3,2,1,0:T(8,128)(2,1)}, bf16[32,2,64,512]{3,2,1,0:T(8,128)(2,1)S(1)}, u32[]{:S(2)}) copy-start(bf16[32,2,64,512]{3,2,1,0:T(8,128)(2,1)S(1)} %copy.14) | copy-start | bytes 12582916
  59.0 0.8 copy-start.5
  59.0 2.1 copy-start.6
  59.8 1.4 collective-permute-start
  60.4 1.4 collective-permute-start.1
  61.2 0.7 copy-start.7
  61.2 1.4 collective-permute-start.2
  61.9 0.7 copy-start.8
  61.9 2.1 collective-permute-start.3
  62.7 1.3 copy-start.9
  62.7 36.6 %collective-permute-start.4 = (bf16[16,4096]{1,0:T(8,128)(2,1)S(1)}, bf16[16,4096]{1,0:T(8,128)(2,1)S(1)}, u32[]{:S(2)}, u32[]{:S(2)}) collective-permute-start(bf16[16,4096]{1,0:T(8,128)(2,1)S(1)} %get-tuple-element.50.refs_4_), channel_id=1, source_target_pairs={{64,0},{128,64},{192,128},{65,1},{129,65},{193,129},{66,2},{130,66... | collective-permute-start | bytes 393224 | tf_op jit(solution)/shard_map/ppermute | solution.py:157
  64.0 36.6 %copy-start.10 = (bf16[16,4096]{1,0:T(8,128)(2,1)}, bf16[16,4096]{1,0:T(8,128)(2,1)S(1)}, u32[]{:S(2)}) copy-start(bf16[16,4096]{1,0:T(8,128)(2,1)S(1)} %get-tuple-element.51.refs_5_) | copy-start | bytes 393220
  64.0 41.9 %collective-permute-start.5 = (bf16[16,4096]{1,0:T(8,128)(2,1)S(1)}, bf16[16,4096]{1,0:T(8,128)(2,1)S(1)}, u32[]{:S(2)}, u32[]{:S(2)}) collective-permute-start(bf16[16,4096]{1,0:T(8,128)(2,1)S(1)} %get-tuple-element.51.refs_5_), channel_id=1, source_target_pairs={{64,0},{128,64},{192,128},{65,1},{129,65},{193,129},{66,2},{130,66... | collective-permute-start | bytes 393224 | tf_op jit(solution)/shard_map/ppermute | solution.py:157
  100.6 6.6 %copy-start.11 = (bf16[16,4096]{1,0:T(8,128)(2,1)}, bf16[16,4096]{1,0:T(8,128)(2,1)S(1)}, u32[]{:S(2)}) copy-start(bf16[16,4096]{1,0:T(8,128)(2,1)S(1)} %get-tuple-element.52.refs_6_) | copy-start | bytes 393220
  100.7 12.7 %collective-permute-start.6 = (bf16[16,4096]{1,0:T(8,128)(2,1)S(1)}, bf16[16,4096]{1,0:T(8,128)(2,1)S(1)}, u32[]{:S(2)}, u32[]{:S(2)}) collective-permute-start(bf16[16,4096]{1,0:T(8,128)(2,1)S(1)} %get-tuple-element.52.refs_6_), channel_id=1, source_target_pairs={{0,192},{64,0},{128,64},{192,128},{1,193},{65,1},{129,65},{193,129... | collective-permute-start | bytes 393224 | tf_op jit(solution)/shard_map/ppermute | solution.py:157
  107.2 7.5 %copy-start.12 = (bf16[16,4096]{1,0:T(8,128)(2,1)}, bf16[16,4096]{1,0:T(8,128)(2,1)S(1)}, u32[]{:S(2)}) copy-start(bf16[16,4096]{1,0:T(8,128)(2,1)S(1)} %get-tuple-element.53.refs_7_) | copy-start | bytes 393220
  107.2 8.9 %collective-permute-start.7 = (bf16[16,4096]{1,0:T(8,128)(2,1)S(1)}, bf16[16,4096]{1,0:T(8,128)(2,1)S(1)}, u32[]{:S(2)}, u32[]{:S(2)}) collective-permute-start(bf16[16,4096]{1,0:T(8,128)(2,1)S(1)} %get-tuple-element.53.refs_7_), channel_id=1, source_target_pairs={{0,192},{64,0},{128,64},{192,128},{1,193},{65,1},{129,65},{193,129... | collective-permute-start | bytes 393224 | tf_op jit(solution)/shard_map/ppermute | solution.py:157
  114.7 2.7 copy-start.13
  114.7 9.5 %collective-permute-start.8 = (bf16[16,4096]{1,0:T(8,128)(2,1)S(1)}, bf16[16,4096]{1,0:T(8,128)(2,1)S(1)}, u32[]{:S(2)}, u32[]{:S(2)}) collective-permute-start(bf16[16,4096]{1,0:T(8,128)(2,1)S(1)} %get-tuple-element.54.refs_8_), channel_id=1, source_target_pairs={{0,192},{64,0},{128,64},{192,128},{1,193},{65,1},{129,65},{193,129... | collective-permute-start | bytes 393224 | tf_op jit(solution)/shard_map/ppermute | solution.py:157
  117.5 8.1 %copy-start.14 = (bf16[16,4096]{1,0:T(8,128)(2,1)}, bf16[16,4096]{1,0:T(8,128)(2,1)S(1)}, u32[]{:S(2)}) copy-start(bf16[16,4096]{1,0:T(8,128)(2,1)S(1)} %get-tuple-element.55.refs_9_) | copy-start | bytes 393220
  117.5 11.6 %collective-permute-start.9 = (bf16[16,4096]{1,0:T(8,128)(2,1)S(1)}, bf16[16,4096]{1,0:T(8,128)(2,1)S(1)}, u32[]{:S(2)}, u32[]{:S(2)}) collective-permute-start(bf16[16,4096]{1,0:T(8,128)(2,1)S(1)} %get-tuple-element.55.refs_9_), channel_id=1, source_target_pairs={{0,192},{64,0},{128,64},{192,128},{1,193},{65,1},{129,65},{193,129... | collective-permute-start | bytes 393224 | tf_op jit(solution)/shard_map/ppermute | solution.py:157
  125.6 4.8 %copy-start.15 = (bf16[16,4096]{1,0:T(8,128)(2,1)}, bf16[16,4096]{1,0:T(8,128)(2,1)S(1)}, u32[]{:S(2)}) copy-start(bf16[16,4096]{1,0:T(8,128)(2,1)S(1)} %get-tuple-element.56.refs_10_) | copy-start | bytes 393220
  125.6 8.2 %collective-permute-start.10 = (bf16[16,4096]{1,0:T(8,128)(2,1)S(1)}, bf16[16,4096]{1,0:T(8,128)(2,1)S(1)}, u32[]{:S(2)}, u32[]{:S(2)}) collective-permute-start(bf16[16,4096]{1,0:T(8,128)(2,1)S(1)} %get-tuple-element.56.refs_10_), channel_id=1, source_target_pairs={{0,192},{64,0},{128,64},{192,128},{1,193},{65,1},{129,65},{193,129... | collective-permute-start | bytes 393224 | tf_op jit(solution)/shard_map/ppermute | solution.py:157
  130.4 4.7 %copy-start.16 = (bf16[16,4096]{1,0:T(8,128)(2,1)}, bf16[16,4096]{1,0:T(8,128)(2,1)S(1)}, u32[]{:S(2)}) copy-start(bf16[16,4096]{1,0:T(8,128)(2,1)S(1)} %get-tuple-element.57.refs_11_) | copy-start | bytes 393220
  130.4 6.5 %collective-permute-start.11 = (bf16[16,4096]{1,0:T(8,128)(2,1)S(1)}, bf16[16,4096]{1,0:T(8,128)(2,1)S(1)}, u32[]{:S(2)}, u32[]{:S(2)}) collective-permute-start(bf16[16,4096]{1,0:T(8,128)(2,1)S(1)} %get-tuple-element.57.refs_11_), channel_id=1, source_target_pairs={{0,192},{64,0},{128,64},{192,128},{1,193},{65,1},{129,65},{193,129... | collective-permute-start | bytes 393224 | tf_op jit(solution)/shard_map/ppermute | solution.py:157
  135.2 3.1 %copy-start.17 = (bf16[16,4096]{1,0:T(8,128)(2,1)}, bf16[16,4096]{1,0:T(8,128)(2,1)S(1)}, u32[]{:S(2)}) copy-start(bf16[16,4096]{1,0:T(8,128)(2,1)S(1)} %get-tuple-element.58.refs_12_) | copy-start | bytes 393220
  135.2 9.9 %collective-permute-start.12 = (bf16[16,4096]{1,0:T(8,128)(2,1)S(1)}, bf16[16,4096]{1,0:T(8,128)(2,1)S(1)}, u32[]{:S(2)}, u32[]{:S(2)}) collective-permute-start(bf16[16,4096]{1,0:T(8,128)(2,1)S(1)} %get-tuple-element.58.refs_12_), channel_id=1, source_target_pairs={{0,192},{64,0},{128,64},{192,128},{1,193},{65,1},{129,65},{193,129... | collective-permute-start | bytes 393224 | tf_op jit(solution)/shard_map/ppermute | solution.py:157
  138.3 8.2 %copy-start.18 = (bf16[16,4096]{1,0:T(8,128)(2,1)}, bf16[16,4096]{1,0:T(8,128)(2,1)S(1)}, u32[]{:S(2)}) copy-start(bf16[16,4096]{1,0:T(8,128)(2,1)S(1)} %get-tuple-element.59.refs_13_) | copy-start | bytes 393220
  138.3 9.9 %collective-permute-start.13 = (bf16[16,4096]{1,0:T(8,128)(2,1)S(1)}, bf16[16,4096]{1,0:T(8,128)(2,1)S(1)}, u32[]{:S(2)}, u32[]{:S(2)}) collective-permute-start(bf16[16,4096]{1,0:T(8,128)(2,1)S(1)} %get-tuple-element.59.refs_13_), channel_id=1, source_target_pairs={{0,192},{64,0},{128,64},{192,128},{1,193},{65,1},{129,65},{193,129... | collective-permute-start | bytes 393224 | tf_op jit(solution)/shard_map/ppermute | solution.py:157
  146.4 3.1 %copy-start.19 = (bf16[16,4096]{1,0:T(8,128)(2,1)}, bf16[16,4096]{1,0:T(8,128)(2,1)S(1)}, u32[]{:S(2)}) copy-start(bf16[16,4096]{1,0:T(8,128)(2,1)S(1)} %get-tuple-element.60.refs_14_) | copy-start | bytes 393220
  146.4 9.0 %collective-permute-start.14 = (bf16[16,4096]{1,0:T(8,128)(2,1)S(1)}, bf16[16,4096]{1,0:T(8,128)(2,1)S(1)}, u32[]{:S(2)}, u32[]{:S(2)}) collective-permute-start(bf16[16,4096]{1,0:T(8,128)(2,1)S(1)} %get-tuple-element.60.refs_14_), channel_id=1, source_target_pairs={{64,0},{128,64},{192,128},{65,1},{129,65},{193,129},{66,2},{130,66... | collective-permute-start | bytes 393224 | tf_op jit(solution)/shard_map/ppermute | solution.py:157
  149.5 7.3 %copy-start.20 = (bf16[16,4096]{1,0:T(8,128)(2,1)}, bf16[16,4096]{1,0:T(8,128)(2,1)S(1)}, u32[]{:S(2)}) copy-start(bf16[16,4096]{1,0:T(8,128)(2,1)S(1)} %get-tuple-element.61.refs_15_) | copy-start | bytes 393220
  149.5 8.6 %collective-permute-start.15 = (bf16[16,4096]{1,0:T(8,128)(2,1)S(1)}, bf16[16,4096]{1,0:T(8,128)(2,1)S(1)}, u32[]{:S(2)}, u32[]{:S(2)}) collective-permute-start(bf16[16,4096]{1,0:T(8,128)(2,1)S(1)} %get-tuple-element.61.refs_15_), channel_id=1, source_target_pairs={{64,0},{128,64},{192,128},{65,1},{129,65},{193,129},{66,2},{130,66... | collective-permute-start | bytes 393224 | tf_op jit(solution)/shard_map/ppermute | solution.py:157
  156.8 2.7 copy-start.21
  156.8 9.4 %collective-permute-start.16 = (bf16[16,4096]{1,0:T(8,128)(2,1)S(1)}, bf16[16,4096]{1,0:T(8,128)(2,1)S(1)}, u32[]{:S(2)}, u32[]{:S(2)}) collective-permute-start(bf16[16,4096]{1,0:T(8,128)(2,1)S(1)} %get-tuple-element.62.refs_16_), channel_id=1, source_target_pairs={{64,0},{128,64},{65,1},{129,65},{66,2},{130,66},{67,3},{131,67},{6... | collective-permute-start | bytes 393224 | tf_op jit(solution)/shard_map/ppermute | solution.py:157
  159.5 8.7 %copy-start.22 = (bf16[16,4096]{1,0:T(8,128)(2,1)}, bf16[16,4096]{1,0:T(8,128)(2,1)S(1)}, u32[]{:S(2)}) copy-start(bf16[16,4096]{1,0:T(8,128)(2,1)S(1)} %get-tuple-element.63.refs_17_) | copy-start | bytes 393220
  159.5 10.0 %collective-permute-start.17 = (bf16[16,4096]{1,0:T(8,128)(2,1)S(1)}, bf16[16,4096]{1,0:T(8,128)(2,1)S(1)}, u32[]{:S(2)}, u32[]{:S(2)}) collective-permute-start(bf16[16,4096]{1,0:T(8,128)(2,1)S(1)} %get-tuple-element.63.refs_17_), channel_id=1, source_target_pairs={{64,0},{128,64},{65,1},{129,65},{66,2},{130,66},{67,3},{131,67},{6... | collective-permute-start | bytes 393224 | tf_op jit(solution)/shard_map/ppermute | solution.py:157
  168.2 29.3 %collective-permute-start.18 = (bf16[16,4096]{1,0:T(8,128)(2,1)}, bf16[16,4096]{1,0:T(8,128)(2,1)S(1)}, u32[]{:S(2)}, u32[]{:S(2)}) collective-permute-start(bf16[16,4096]{1,0:T(8,128)(2,1)} %get-tuple-element.64.refs_18_), channel_id=1, source_target_pairs={{64,0},{65,1},{66,2},{67,3},{68,4},{69,5},{70,6},{71,7},{72,8},{73... | collective-permute-start | bytes 393224 | tf_op jit(solution)/shard_map/ppermute | solution.py:157
  171.5 29.6 %collective-permute-start.19 = (bf16[16,4096]{1,0:T(8,128)(2,1)}, bf16[16,4096]{1,0:T(8,128)(2,1)S(1)}, u32[]{:S(2)}, u32[]{:S(2)}) collective-permute-start(bf16[16,4096]{1,0:T(8,128)(2,1)} %get-tuple-element.65.refs_19_), channel_id=1, source_target_pairs={{64,0},{65,1},{66,2},{67,3},{68,4},{69,5},{70,6},{71,7},{72,8},{73... | collective-permute-start | bytes 393224 | tf_op jit(solution)/shard_map/ppermute | solution.py:157
  175.2 29.5 %all-to-all-start.3 = ((bf16[4,128,512]{2,1,0:T(8,128)(2,1)}), bf16[4,128,512]{2,1,0:T(8,128)(2,1)}, u32[]{:S(2)}, u32[]{:S(2)}) async-start(bf16[4,128,512]{2,1,0:T(8,128)(2,1)} %broadcast_in_dim.36), calls=%async_computation.3 | async-start | bytes 1048576 | tf_op jit(solution)/shard_map/all_to_all | solution.py:22
  197.6 2.2 copy-start.1
  201.1 1.4 copy-start.23
  202.5 9.0 %copy-start.24 = (bf16[16,4096]{1,0:T(8,128)(2,1)}, bf16[16,4096]{1,0:T(8,128)(2,1)S(1)}, u32[]{:S(2)}) copy-start(bf16[16,4096]{1,0:T(8,128)(2,1)S(1)} %get-tuple-element.67.refs_21_) | copy-start | bytes 393220
  205.6 11.3 %all-to-all-start.4 = ((bf16[4,128,512]{2,1,0:T(8,128)(2,1)}), bf16[4,128,512]{2,1,0:T(8,128)(2,1)}, u32[]{:S(2)}, u32[]{:S(2)}) async-start(bf16[4,128,512]{2,1,0:T(8,128)(2,1)} %broadcast_in_dim.37), calls=%async_computation.4 | async-start | bytes 1048576 | tf_op jit(solution)/shard_map/all_to_all | solution.py:22
  219.9 72.2 %all-to-all-start.5 = ((bf16[16,64,512]{2,1,0:T(8,128)(2,1)}), bf16[16,64,512]{2,1,0:T(8,128)(2,1)S(1)}, u32[]{:S(2)}, u32[]{:S(2)}) async-start(bf16[16,64,512]{2,1,0:T(8,128)(2,1)} %bitcast.14), calls=%async_computation.5 | async-start | bytes 2097152 | tf_op jit(solution)/shard_map/all_to_all | solution.py:176

commit v2 on v1

--- a/solution.py
+++ b/solution.py
@@ -28,6 +28,17 @@
     first = copy_for_each(array, DP[:3])
     tiles = jnp.swapaxes(copy_for_each(first, DP[3]), 0, 1)
     return tiles.reshape(-1, array.shape[-1])
+
+
+def held_until(value, token):
+    return pl.pallas_call(
+        lambda value_ref, token_ref, out_ref: None,
+        out_shape=jax.ShapeDtypeStruct(value.shape, value.dtype),
+        in_specs=[ANYWHERE, ANYWHERE],
+        out_specs=ANYWHERE,
+        input_output_aliases={0: 0},
+        name="held_until",
+    )(value, token)
 
 
 def task_of(step, section, npipe):
@@ -112,7 +123,7 @@
     return pl.pallas_call(
         functools.partial(collect_kernel, npipe, blocks),
         out_shape=jax.ShapeDtypeStruct((2, blocks * ROWS, width), jnp.bfloat16),
-        in_specs=[IN_SMEM] + [ANYWHERE] * len(pieces),
+        in_specs=[IN_SMEM] + [IN_VMEM] * len(pieces),
         out_specs=ANYWHERE,
         scratch_shapes=[pltpu.SemaphoreType.DMA((len(pieces),))],
         name="collect_rows",
@@ -137,7 +148,6 @@
     near = width // (far * across)
     tiles = hidden.reshape(2, tok, far, across, near).transpose(3, 0, 1, 2, 4)
     tiles = tiles.reshape(across, 2, tok, far * near)
-    tiles = lax.all_to_all(tiles, "dp_1", 0, 0, tiled=True)
 
     steps = 2 * blocks + SLACK * (npipe - 1)
     sent, gx_parts, gv_parts = {}, [], []
@@ -148,6 +158,8 @@
         dx, dv = one_step(step, npipe, blocks, where, w_mat, x, scale, grad_out, incoming)
         gx_parts.append(dx)
         gv_parts.append(dv)
+        if step == SLACK:
+            tiles = lax.all_to_all(held_until(tiles, dv), "dp_1", 0, 0, tiled=True)
         pairs = []
         for source in range(npipe):
             task = task_of(step, source, npipe)

time: 294 us -> 254 us (0.86)
  Pallas kernels: 87.7 us -> 24.7 us
  waiting for transfers between devices: 73.6 us -> 121 us
  starting transfers between devices: 79.4 us -> 57.7 us
  local copies, waits for them, and re-layouts: 31.4 us -> 23.2 us
  other arithmetic: 2.76 us -> 9.5 us
    pallas_call x1, Pallas kernels: 64.8 us -> 3.33 us  [collected(): pl.pallas_call(functools.partial(collect_kernel, npipe, blocks), out_shap...]
    ppermute x20, waiting for transfers between devices: 53.5 us -> 84.9 us  [on_device(): sent[step] = lax.ppermute(dx, 'pipe', pairs)]
    all_to_all x3, starting transfers between devices: 35.5 us -> 17.8 us  [copy_for_each(): lax.all_to_all(jnp.broadcast_to(array[None], (count, *array.shape)), axis...]
    all_to_all x1, waiting for transfers between devices: 0.01 us -> 12.5 us  [on_device(): arrived = lax.all_to_all(pieces, others, 0, 0, tiled=True)]
    unnamed x74 -> x81, local copies, waits for them, and re-layouts: 14.5 us -> 5.59 us
    ppermute x20, starting transfers between devices: 32 us -> 23.6 us  [on_device(): sent[step] = lax.ppermute(dx, 'pipe', pairs)]
    transpose x1, other arithmetic: 1.37 us -> 8.11 us  [on_device(): tiles = hidden.reshape(2, tok, far, across, near).transpose(3, 0, 1, 2, 4)]
    convert_element_type x0 -> x1, local copies, waits for them, and re-layouts: none -> 4.61 us  [on_device(): x32 = x.astype(jnp.float32)]
  transfers between devices with their start and end apart: 25 -> 25, of which waited for: 11 -> 18; matrix products, arithmetic and copies ran while one was open for 9% -> 8% of each run, Pallas kernels for 30% -> 9%
where the time goes in v2:
time: 254 us; the launch traced here: 253 us
  waiting for transfers between devices  121 us (48%)
  starting transfers between devices  57.7 us (23%)
  Pallas kernels  24.7 us (10%)
  local copies, waits for them, and re-layouts  23.2 us (9%)
  blocking collectives  10.7 us (4%)
  other arithmetic  9.5 us (4%)
  matrix products  4.56 us (2%)
    ppermute x20, waiting for transfers between devices, on_device(): sent[step] = lax.ppermute(dx, 'pipe', pairs)  84.9 us
    all_to_all x3, waiting for transfers between devices, copy_for_each(): lax.all_to_all(jnp.broadcast_to(array[None], (count, *array.shape)), axis...  23.7 us
    ppermute x20, starting transfers between devices, on_device(): sent[step] = lax.ppermute(dx, 'pipe', pairs)  23.6 us
    pallas_call x22, Pallas kernels, one_step(): pl.pallas_call(functools.partial(step_kernel, step, npipe, blocks), out_s...  21.4 us
    all_to_all x3, starting transfers between devices, copy_for_each(): lax.all_to_all(jnp.broadcast_to(array[None], (count, *array.shape)), axis...  17.8 us
    all_to_all x1, waiting for transfers between devices, on_device(): arrived = lax.all_to_all(pieces, others, 0, 0, tiled=True)  12.5 us
    all_to_all x1, starting transfers between devices, on_device(): arrived = lax.all_to_all(pieces, others, 0, 0, tiled=True)  11.8 us
    all_to_all x1, blocking collectives, copy_for_each(): lax.all_to_all(jnp.broadcast_to(array[None], (count, *array.shape)), axis...  10.7 us
  transfers between devices with their start and end apart: 25, of which 18 were waited for; matrix products, arithmetic and copies ran while one was open for 8% of the time, Pallas kernels for 9%

profile of v2, /device:TPU:1, one launch (start us, length us, event | category | flops | bytes accessed | tf_op | source)
XLA Modules:
  0.0 253.0 jit_solution(16069314874010783892)
XLA Ops:
  0.6 2.4 broadcast_in_dim.15
  3.0 9.5 %all-to-all-start = ((bf16[32,64,512]{2,1,0:T(8,128)(2,1)}), bf16[32,64,512]{2,1,0:T(8,128)(2,1)}, u32[]{:S(2)}, u32[]{:S(2)}) async-start(bf16[32,64,512]{2,1,0:T(8,128)(2,1)} %broadcast_in_dim.15), calls=%async_computation | async-start | bytes 4194304 | tf_op jit(solution)/shard_map/all_to_all | solution.py:22
  12.7 4.6 %reshape.45 = f32[2,128,2,4,512]{4,3,2,1,0:T(4,128)} reshape(bf16[2,1,128,4096]{3,2,1,0:T(8,128)(2,1)S(1)} %copy-done.2) | data formatting | bytes 6291456 | tf_op jit(solution)/shard_map/convert_element_type | solution.py:144
  17.8 20.2 %all-to-all-done = bf16[32,64,512]{2,1,0:T(8,128)(2,1)} async-done(((bf16[32,64,512]{2,1,0:T(8,128)(2,1)}), bf16[32,64,512]{2,1,0:T(8,128)(2,1)}, u32[]{:S(2)}, u32[]{:S(2)}) %all-to-all-start) | async-done | bytes 2097184 | tf_op jit(solution)/shard_map/all_to_all | solution.py:22
  38.0 2.1 broadcast_in_dim.16
  40.1 10.7 %all_to_all.30 = bf16[2,32,64,512]{3,2,1,0:T(8,128)(2,1)S(1)} all-to-all(bf16[2,32,64,512]{3,2,1,0:T(8,128)(2,1)S(1)} %broadcast_in_dim.16), channel_id=1, replica_groups=mesh['pipe'=4,'dp_0'=2,'dp_1'=4,'dp_2'=4,'dp_3'=2] {'dp_3'}, dimensions={0} | all-to-all | bytes 8388608 | tf_op jit(solution)/shard_map/all_to_all | solution.py:22
  52.1 1.2 copy-done.5
  56.2 1.3 collective-permute-start.4
  57.5 1.3 collective-permute-start.5
  58.8 33.5 %collective-permute-done.4.in_ref = bf16[16,4096]{1,0:T(8,128)(2,1)S(1)} collective-permute-done((bf16[16,4096]{1,0:T(8,128)(2,1)S(1)}, bf16[16,4096]{1,0:T(8,128)(2,1)S(1)}, u32[]{:S(2)}, u32[]{:S(2)}) %collective-permute-start.4) | collective-permute-done | bytes 131104 | tf_op jit(solution)/shard_map/ppermute | solution.py:169
  92.4 1.3 section_step.28
  93.7 5.4 %collective-permute-start.6 = (bf16[16,4096]{1,0:T(8,128)(2,1)S(1)}, bf16[16,4096]{1,0:T(8,128)(2,1)S(1)}, u32[]{:S(2)}, u32[]{:S(2)}) collective-permute-start(bf16[16,4096]{1,0:T(8,128)(2,1)S(1)} %get-tuple-element.52.refs_6_), channel_id=1, source_target_pairs={{0,192},{64,0},{128,64},{192,128},{1,193},{65,1},{129,65},{193,129... | collective-permute-start | bytes 393224 | tf_op jit(solution)/shard_map/ppermute | solution.py:169
  99.1 6.6 %collective-permute-done.5.in_ref = bf16[16,4096]{1,0:T(8,128)(2,1)S(1)} collective-permute-done((bf16[16,4096]{1,0:T(8,128)(2,1)S(1)}, bf16[16,4096]{1,0:T(8,128)(2,1)S(1)}, u32[]{:S(2)}, u32[]{:S(2)}) %collective-permute-start.5) | collective-permute-done | bytes 131104 | tf_op jit(solution)/shard_map/ppermute | solution.py:169
  105.7 1.3 section_step.29
  107.2 2.1 collective-permute-done.6.in_ref
  109.3 1.3 section_step.30
  110.7 5.8 %collective-permute-done.7.in_ref = bf16[16,4096]{1,0:T(8,128)(2,1)S(1)} collective-permute-done((bf16[16,4096]{1,0:T(8,128)(2,1)S(1)}, bf16[16,4096]{1,0:T(8,128)(2,1)S(1)}, u32[]{:S(2)}, u32[]{:S(2)}) %collective-permute-start.7) | collective-permute-done | bytes 131104 | tf_op jit(solution)/shard_map/ppermute | solution.py:169
  116.5 1.3 section_step.31
  118.0 2.4 collective-permute-done.8.in_ref
  120.4 1.3 section_step.32
  121.8 1.3 collective-permute-start.10
  123.0 2.8 %collective-permute-done.9.in_ref = bf16[16,4096]{1,0:T(8,128)(2,1)S(1)} collective-permute-done((bf16[16,4096]{1,0:T(8,128)(2,1)S(1)}, bf16[16,4096]{1,0:T(8,128)(2,1)S(1)}, u32[]{:S(2)}, u32[]{:S(2)}) %collective-permute-start.9) | collective-permute-done | bytes 131104 | tf_op jit(solution)/shard_map/ppermute | solution.py:169
  125.9 1.3 section_step.33
  127.8 1.0 collective-permute-done.10.in_ref
  128.8 1.3 section_step.34
  130.1 4.4 %collective-permute-done.11.in_ref = bf16[16,4096]{1,0:T(8,128)(2,1)S(1)} collective-permute-done((bf16[16,4096]{1,0:T(8,128)(2,1)S(1)}, bf16[16,4096]{1,0:T(8,128)(2,1)S(1)}, u32[]{:S(2)}, u32[]{:S(2)}) %collective-permute-start.11) | collective-permute-done | bytes 131104 | tf_op jit(solution)/shard_map/ppermute | solution.py:169
  134.6 1.3 section_step.35
  136.7 0.9 broadcast_in_dim.36
  137.5 4.1 %all-to-all-start.3 = ((bf16[4,128,512]{2,1,0:T(8,128)(2,1)}), bf16[4,128,512]{2,1,0:T(8,128)(2,1)}, u32[]{:S(2)}, u32[]{:S(2)}) async-start(bf16[4,128,512]{2,1,0:T(8,128)(2,1)} %broadcast_in_dim.36), calls=%async_computation.3 | async-start | bytes 1048576 | tf_op jit(solution)/shard_map/all_to_all | solution.py:22
  141.7 8.1 %fusion.2 = bf16[4,2,128,2,512]{4,3,2,1,0:T(2,128)(2,1)} fusion(f32[2,2,4,512]{3,1,0,2:T(2,128)S(1)} %copy.12, f32[2,128]{1,0:T(2,128)S(1)} %add_rsqrt_fusion, f32[2,128,2,4,512]{4,3,2,1,0:T(4,128)} %reshape.45), kind=kLoop, calls=%fused_computation.6 | loop fusion | flops 3145728 | bytes 6325248 | tf_op jit(solution)/shard_map/transpose | solution.py:149
  149.8 4.5 %reshape.41.value_ref = bf16[4,2,128,1024]{3,2,1,0:T(8,128)(2,1)} reshape(bf16[4,2,128,2,512]{4,3,2,1,0:T(2,128)(2,1)} %fusion.2) | data formatting | bytes 4194304 | tf_op jit(solution)/shard_map/reshape | solution.py:150
  154.3 4.5 %all-to-all-start.2 = ((bf16[4,2,128,1024]{3,2,1,0:T(8,128)(2,1)}), bf16[4,2,128,1024]{3,2,1,0:T(8,128)(2,1)}, u32[]{:S(2)}, u32[]{:S(2)}) async-start(bf16[4,2,128,1024]{3,2,1,0:T(8,128)(2,1)} %held_until.1), calls=%async_computation.2 | async-start | bytes 4194304 | tf_op jit(solution)/shard_map/all_to_all | solution.py:162
  158.9 2.9 %collective-permute-start.13 = (bf16[16,4096]{1,0:T(8,128)(2,1)S(1)}, bf16[16,4096]{1,0:T(8,128)(2,1)S(1)}, u32[]{:S(2)}, u32[]{:S(2)}) collective-permute-start(bf16[16,4096]{1,0:T(8,128)(2,1)S(1)} %get-tuple-element.59.refs_13_), channel_id=1, source_target_pairs={{0,192},{64,0},{128,64},{192,128},{1,193},{65,1},{129,65},{193,129... | collective-permute-start | bytes 393224 | tf_op jit(solution)/shard_map/ppermute | solution.py:169
  161.8 4.9 %collective-permute-done.12.in_ref = bf16[16,4096]{1,0:T(8,128)(2,1)S(1)} collective-permute-done((bf16[16,4096]{1,0:T(8,128)(2,1)S(1)}, bf16[16,4096]{1,0:T(8,128)(2,1)S(1)}, u32[]{:S(2)}, u32[]{:S(2)}) %collective-permute-start.12) | collective-permute-done | bytes 131104 | tf_op jit(solution)/shard_map/ppermute | solution.py:169
  166.7 2.2 copy-done.1
  168.9 1.3 section_step.36
  170.3 1.4 collective-permute-start.14
  171.7 1.3 section_step.37
  173.1 1.3 collective-permute-start.15
  174.4 6.0 %collective-permute-done.14.in_ref = bf16[16,4096]{1,0:T(8,128)(2,1)S(1)} collective-permute-done((bf16[16,4096]{1,0:T(8,128)(2,1)S(1)}, bf16[16,4096]{1,0:T(8,128)(2,1)S(1)}, u32[]{:S(2)}, u32[]{:S(2)}) %collective-permute-start.14) | collective-permute-done | bytes 131104 | tf_op jit(solution)/shard_map/ppermute | solution.py:169
  180.4 1.3 section_step.38
  181.7 1.3 collective-permute-start.16
  183.0 2.7 %collective-permute-done.15.in_ref = bf16[16,4096]{1,0:T(8,128)(2,1)S(1)} collective-permute-done((bf16[16,4096]{1,0:T(8,128)(2,1)S(1)}, bf16[16,4096]{1,0:T(8,128)(2,1)S(1)}, u32[]{:S(2)}, u32[]{:S(2)}) %collective-permute-start.15) | collective-permute-done | bytes 131104 | tf_op jit(solution)/shard_map/ppermute | solution.py:169
  185.7 1.3 section_step.39
  187.1 1.3 collective-permute-start.17
  188.4 1.3 collective-permute-done.16.in_ref
  189.7 1.3 section_step.40
  191.0 1.3 collective-permute-start.18
  192.3 6.8 %collective-permute-done.17.in_ref = bf16[16,4096]{1,0:T(8,128)(2,1)S(1)} collective-permute-done((bf16[16,4096]{1,0:T(8,128)(2,1)S(1)}, bf16[16,4096]{1,0:T(8,128)(2,1)S(1)}, u32[]{:S(2)}, u32[]{:S(2)}) %collective-permute-start.17) | collective-permute-done | bytes 131104 | tf_op jit(solution)/shard_map/ppermute | solution.py:169
  199.2 1.3 section_step.41
  200.5 1.3 collective-permute-start.19
  201.8 1.5 collective-permute-done.18.in_ref
  203.4 1.3 section_step.42
  204.7 3.0 %collective-permute-done.19.in_ref = bf16[16,4096]{1,0:T(8,128)(2,1)S(1)} collective-permute-done((bf16[16,4096]{1,0:T(8,128)(2,1)S(1)}, bf16[16,4096]{1,0:T(8,128)(2,1)S(1)}, u32[]{:S(2)}, u32[]{:S(2)}) %collective-permute-start.19) | collective-permute-done | bytes 131104 | tf_op jit(solution)/shard_map/ppermute | solution.py:169
  207.8 1.3 section_step.43
  209.8 0.8 broadcast_in_dim.37
  210.6 4.1 %all-to-all-start.4 = ((bf16[4,128,512]{2,1,0:T(8,128)(2,1)}), bf16[4,128,512]{2,1,0:T(8,128)(2,1)}, u32[]{:S(2)}, u32[]{:S(2)}) async-start(bf16[4,128,512]{2,1,0:T(8,128)(2,1)} %broadcast_in_dim.37), calls=%async_computation.4 | async-start | bytes 1048576 | tf_op jit(solution)/shard_map/all_to_all | solution.py:22
  214.8 1.7 fusion.3
  216.5 1.8 fusion.4
  218.3 3.5 %all-to-all-done.4 = bf16[4,128,512]{2,1,0:T(8,128)(2,1)} async-done(((bf16[4,128,512]{2,1,0:T(8,128)(2,1)}), bf16[4,128,512]{2,1,0:T(8,128)(2,1)}, u32[]{:S(2)}, u32[]{:S(2)}) %all-to-all-start.4) | async-done | bytes 524320 | tf_op jit(solution)/shard_map/all_to_all | solution.py:22
  221.8 2.8 %add_convert_fusion = bf16[1024,512]{1,0:T(8,128)(2,1)} fusion(f32[1024,512]{1,0:T(8,128)S(1)} %fusion.4, bf16[512,1024]{1,0:T(8,128)(2,1)S(1)} %bitcast.69, bf16[512,512]{1,0:T(8,128)(2,1)} %bitcast.11), kind=kOutput, calls=%fused_computation.5 | convolution fusion | flops 537919488 | bytes 4718592 | tf_op jit(solution)/shard_map/dot_general | solution.py:181
  224.6 11.8 %all-to-all-start.5 = ((bf16[16,64,512]{2,1,0:T(8,128)(2,1)}), bf16[16,64,512]{2,1,0:T(8,128)(2,1)S(1)}, u32[]{:S(2)}, u32[]{:S(2)}) async-start(bf16[16,64,512]{2,1,0:T(8,128)(2,1)} %bitcast.12), calls=%async_computation.5 | async-start | bytes 2097152 | tf_op jit(solution)/shard_map/all_to_all | solution.py:188
  236.4 3.3 %collect_rows.1 = bf16[2,128,4096]{2,1,0:T(8,128)(2,1)} custom-call(s32[1]{0:T(128)} %bitcast.where, bf16[16,4096]{1,0:T(8,128)(2,1)} %copy-done.5, bf16[16,4096]{1,0:T(8,128)(2,1)} %copy-done.6, bf16[16,4096]{1,0:T(8,128)(2,1)} %copy-done.7, bf16[16,4096]{1,0:T(8,128)(2,1)} %copy-done.8, bf16[16,4096]{1,0:T(8,128)(2,1)} %copy-done.9, ...), custom_call_target="tpu_custom_call" | custom-call | tf_op jit(solution)/shard_map/collect_rows/pallas_call | solution.py:123
  239.7 12.5 %all-to-all-done.5 = bf16[16,64,512]{2,1,0:T(8,128)(2,1)S(1)} async-done(((bf16[16,64,512]{2,1,0:T(8,128)(2,1)}), bf16[16,64,512]{2,1,0:T(8,128)(2,1)S(1)}, u32[]{:S(2)}, u32[]{:S(2)}) %all-to-all-start.5) | async-done | bytes 1048608 | tf_op jit(solution)/shard_map/all_to_all | solution.py:188
  (113 shorter events, 7.9 us)
Async XLA Ops:
  3.0 9.5 %copy-start.4 = (f32[2,1,4096]{2,1,0:T(1,128)S(1)}, f32[2,1,4096]{2,1,0:T(1,128)}, u32[]{:S(2)}) copy-start(f32[2,1,4096]{2,1,0:T(1,128)} %g_ref.43) | copy-start | bytes 98308
  3.0 9.7 %copy-start.2 = (bf16[2,1,128,4096]{3,2,1,0:T(8,128)(2,1)S(1)}, bf16[2,1,128,4096]{3,2,1,0:T(8,128)(2,1)}, u32[]{:S(2)}) copy-start(bf16[2,1,128,4096]{3,2,1,0:T(8,128)(2,1)} %param.4) | copy-start | bytes 6291460
  3.0 35.0 %all-to-all-start = ((bf16[32,64,512]{2,1,0:T(8,128)(2,1)}), bf16[32,64,512]{2,1,0:T(8,128)(2,1)}, u32[]{:S(2)}, u32[]{:S(2)}) async-start(bf16[32,64,512]{2,1,0:T(8,128)(2,1)} %broadcast_in_dim.15), calls=%async_computation | async-start | bytes 4194304 | tf_op jit(solution)/shard_map/all_to_all | solution.py:22
  50.9 1.2 copy-start.3
  51.3 83.2 %copy-start = (bf16[32,2,64,512]{3,2,1,0:T(8,128)(2,1)}, bf16[32,2,64,512]{3,2,1,0:T(8,128)(2,1)S(1)}, u32[]{:S(2)}) copy-start(bf16[32,2,64,512]{3,2,1,0:T(8,128)(2,1)S(1)} %copy.10) | copy-start | bytes 12582916
  52.1 1.2 copy-start.5
  52.1 2.6 %copy-start.6 = (bf16[16,4096]{1,0:T(8,128)(2,1)}, bf16[16,4096]{1,0:T(8,128)(2,1)S(1)}, u32[]{:S(2)}) copy-start(bf16[16,4096]{1,0:T(8,128)(2,1)S(1)} %get-tuple-element.47.refs_1_) | copy-start | bytes 393220
  53.2 1.4 collective-permute-start
  53.9 1.4 collective-permute-start.1
  54.6 0.7 copy-start.7
  54.7 1.4 copy-start.27
  54.7 1.4 collective-permute-start.2
  55.4 0.8 copy-start.8
  55.4 2.1 collective-permute-start.3
  56.1 1.3 copy-start.9
  56.2 36.2 %collective-permute-start.4 = (bf16[16,4096]{1,0:T(8,128)(2,1)S(1)}, bf16[16,4096]{1,0:T(8,128)(2,1)S(1)}, u32[]{:S(2)}, u32[]{:S(2)}) collective-permute-start(bf16[16,4096]{1,0:T(8,128)(2,1)S(1)} %get-tuple-element.50.refs_4_), channel_id=1, source_target_pairs={{64,0},{128,64},{192,128},{65,1},{129,65},{193,129},{66,2},{130,66... | collective-permute-start | bytes 393224 | tf_op jit(solution)/shard_map/ppermute | solution.py:169
  57.5 36.2 %copy-start.10 = (bf16[16,4096]{1,0:T(8,128)(2,1)}, bf16[16,4096]{1,0:T(8,128)(2,1)S(1)}, u32[]{:S(2)}) copy-start(bf16[16,4096]{1,0:T(8,128)(2,1)S(1)} %get-tuple-element.51.refs_5_) | copy-start | bytes 393220
  57.5 48.2 %collective-permute-start.5 = (bf16[16,4096]{1,0:T(8,128)(2,1)S(1)}, bf16[16,4096]{1,0:T(8,128)(2,1)S(1)}, u32[]{:S(2)}, u32[]{:S(2)}) collective-permute-start(bf16[16,4096]{1,0:T(8,128)(2,1)S(1)} %get-tuple-element.51.refs_5_), channel_id=1, source_target_pairs={{64,0},{128,64},{192,128},{65,1},{129,65},{193,129},{66,2},{130,66... | collective-permute-start | bytes 393224 | tf_op jit(solution)/shard_map/ppermute | solution.py:169
  93.7 13.3 %copy-start.11 = (bf16[16,4096]{1,0:T(8,128)(2,1)}, bf16[16,4096]{1,0:T(8,128)(2,1)S(1)}, u32[]{:S(2)}) copy-start(bf16[16,4096]{1,0:T(8,128)(2,1)S(1)} %get-tuple-element.52.refs_6_) | copy-start | bytes 393220
  93.7 15.5 %collective-permute-start.6 = (bf16[16,4096]{1,0:T(8,128)(2,1)S(1)}, bf16[16,4096]{1,0:T(8,128)(2,1)S(1)}, u32[]{:S(2)}, u32[]{:S(2)}) collective-permute-start(bf16[16,4096]{1,0:T(8,128)(2,1)S(1)} %get-tuple-element.52.refs_6_), channel_id=1, source_target_pairs={{0,192},{64,0},{128,64},{192,128},{1,193},{65,1},{129,65},{193,129... | collective-permute-start | bytes 393224 | tf_op jit(solution)/shard_map/ppermute | solution.py:169
  107.0 3.5 %copy-start.12 = (bf16[16,4096]{1,0:T(8,128)(2,1)}, bf16[16,4096]{1,0:T(8,128)(2,1)S(1)}, u32[]{:S(2)}) copy-start(bf16[16,4096]{1,0:T(8,128)(2,1)S(1)} %get-tuple-element.53.refs_7_) | copy-start | bytes 393220
  107.1 9.4 %collective-permute-start.7 = (bf16[16,4096]{1,0:T(8,128)(2,1)S(1)}, bf16[16,4096]{1,0:T(8,128)(2,1)S(1)}, u32[]{:S(2)}, u32[]{:S(2)}) collective-permute-start(bf16[16,4096]{1,0:T(8,128)(2,1)S(1)} %get-tuple-element.53.refs_7_), channel_id=1, source_target_pairs={{0,192},{64,0},{128,64},{192,128},{1,193},{65,1},{129,65},{193,129... | collective-permute-start | bytes 393224 | tf_op jit(solution)/shard_map/ppermute | solution.py:169
  110.6 7.2 %copy-start.13 = (bf16[16,4096]{1,0:T(8,128)(2,1)}, bf16[16,4096]{1,0:T(8,128)(2,1)S(1)}, u32[]{:S(2)}) copy-start(bf16[16,4096]{1,0:T(8,128)(2,1)S(1)} %get-tuple-element.54.refs_8_) | copy-start | bytes 393220
  110.6 9.8 %collective-permute-start.8 = (bf16[16,4096]{1,0:T(8,128)(2,1)S(1)}, bf16[16,4096]{1,0:T(8,128)(2,1)S(1)}, u32[]{:S(2)}, u32[]{:S(2)}) collective-permute-start(bf16[16,4096]{1,0:T(8,128)(2,1)S(1)} %get-tuple-element.54.refs_8_), channel_id=1, source_target_pairs={{0,192},{64,0},{128,64},{192,128},{1,193},{65,1},{129,65},{193,129... | collective-permute-start | bytes 393224 | tf_op jit(solution)/shard_map/ppermute | solution.py:169
  117.9 3.9 %copy-start.14 = (bf16[16,4096]{1,0:T(8,128)(2,1)}, bf16[16,4096]{1,0:T(8,128)(2,1)S(1)}, u32[]{:S(2)}) copy-start(bf16[16,4096]{1,0:T(8,128)(2,1)S(1)} %get-tuple-element.55.refs_9_) | copy-start | bytes 393220
  117.9 8.0 %collective-permute-start.9 = (bf16[16,4096]{1,0:T(8,128)(2,1)S(1)}, bf16[16,4096]{1,0:T(8,128)(2,1)S(1)}, u32[]{:S(2)}, u32[]{:S(2)}) collective-permute-start(bf16[16,4096]{1,0:T(8,128)(2,1)S(1)} %get-tuple-element.55.refs_9_), channel_id=1, source_target_pairs={{0,192},{64,0},{128,64},{192,128},{1,193},{65,1},{129,65},{193,129... | collective-permute-start | bytes 393224 | tf_op jit(solution)/shard_map/ppermute | solution.py:169
  121.8 5.4 %copy-start.15 = (bf16[16,4096]{1,0:T(8,128)(2,1)}, bf16[16,4096]{1,0:T(8,128)(2,1)S(1)}, u32[]{:S(2)}) copy-start(bf16[16,4096]{1,0:T(8,128)(2,1)S(1)} %get-tuple-element.56.refs_10_) | copy-start | bytes 393220
  121.8 7.0 %collective-permute-start.10 = (bf16[16,4096]{1,0:T(8,128)(2,1)S(1)}, bf16[16,4096]{1,0:T(8,128)(2,1)S(1)}, u32[]{:S(2)}, u32[]{:S(2)}) collective-permute-start(bf16[16,4096]{1,0:T(8,128)(2,1)S(1)} %get-tuple-element.56.refs_10_), channel_id=1, source_target_pairs={{0,192},{64,0},{128,64},{192,128},{1,193},{65,1},{129,65},{193,129... | collective-permute-start | bytes 393224 | tf_op jit(solution)/shard_map/ppermute | solution.py:169
  127.2 2.9 %copy-start.16 = (bf16[16,4096]{1,0:T(8,128)(2,1)}, bf16[16,4096]{1,0:T(8,128)(2,1)S(1)}, u32[]{:S(2)}) copy-start(bf16[16,4096]{1,0:T(8,128)(2,1)S(1)} %get-tuple-element.57.refs_11_) | copy-start | bytes 393220
  127.2 7.3 %collective-permute-start.11 = (bf16[16,4096]{1,0:T(8,128)(2,1)S(1)}, bf16[16,4096]{1,0:T(8,128)(2,1)S(1)}, u32[]{:S(2)}, u32[]{:S(2)}) collective-permute-start(bf16[16,4096]{1,0:T(8,128)(2,1)S(1)} %get-tuple-element.57.refs_11_), channel_id=1, source_target_pairs={{0,192},{64,0},{128,64},{192,128},{1,193},{65,1},{129,65},{193,129... | collective-permute-start | bytes 393224 | tf_op jit(solution)/shard_map/ppermute | solution.py:169
  130.1 28.6 %copy-start.17 = (bf16[16,4096]{1,0:T(8,128)(2,1)}, bf16[16,4096]{1,0:T(8,128)(2,1)S(1)}, u32[]{:S(2)}) copy-start(bf16[16,4096]{1,0:T(8,128)(2,1)S(1)} %get-tuple-element.58.refs_12_) | copy-start | bytes 393220
  135.9 23.0 %copy-start.18 = (bf16[16,4096]{1,0:T(8,128)(2,1)}, bf16[16,4096]{1,0:T(8,128)(2,1)S(1)}, u32[]{:S(2)}) copy-start(bf16[16,4096]{1,0:T(8,128)(2,1)S(1)} %get-tuple-element.59.refs_13_) | copy-start | bytes 393220
  135.9 0.7 copy-start.28
  137.5 16.7 %all-to-all-start.3 = ((bf16[4,128,512]{2,1,0:T(8,128)(2,1)}), bf16[4,128,512]{2,1,0:T(8,128)(2,1)}, u32[]{:S(2)}, u32[]{:S(2)}) async-start(bf16[4,128,512]{2,1,0:T(8,128)(2,1)} %broadcast_in_dim.36), calls=%async_computation.3 | async-start | bytes 1048576 | tf_op jit(solution)/shard_map/all_to_all | solution.py:22
  154.3 55.6 %all-to-all-start.2 = ((bf16[4,2,128,1024]{3,2,1,0:T(8,128)(2,1)}), bf16[4,2,128,1024]{3,2,1,0:T(8,128)(2,1)}, u32[]{:S(2)}, u32[]{:S(2)}) async-start(bf16[4,2,128,1024]{3,2,1,0:T(8,128)(2,1)} %held_until.1), calls=%async_computation.2 | async-start | bytes 4194304 | tf_op jit(solution)/shard_map/all_to_all | solution.py:162
  158.8 8.0 %collective-permute-start.12 = (bf16[16,4096]{1,0:T(8,128)(2,1)S(1)}, bf16[16,4096]{1,0:T(8,128)(2,1)S(1)}, u32[]{:S(2)}, u32[]{:S(2)}) collective-permute-start(bf16[16,4096]{1,0:T(8,128)(2,1)S(1)} %get-tuple-element.58.refs_12_), channel_id=1, source_target_pairs={{0,192},{64,0},{128,64},{192,128},{1,193},{65,1},{129,65},{193,129... | collective-permute-start | bytes 393224 | tf_op jit(solution)/shard_map/ppermute | solution.py:169
  158.9 12.8 %collective-permute-start.13 = (bf16[16,4096]{1,0:T(8,128)(2,1)S(1)}, bf16[16,4096]{1,0:T(8,128)(2,1)S(1)}, u32[]{:S(2)}, u32[]{:S(2)}) collective-permute-start(bf16[16,4096]{1,0:T(8,128)(2,1)S(1)} %get-tuple-element.59.refs_13_), channel_id=1, source_target_pairs={{0,192},{64,0},{128,64},{192,128},{1,193},{65,1},{129,65},{193,129... | collective-permute-start | bytes 393224 | tf_op jit(solution)/shard_map/ppermute | solution.py:169
  166.7 2.2 copy-start.1
  170.2 2.8 %copy-start.19 = (bf16[16,4096]{1,0:T(8,128)(2,1)}, bf16[16,4096]{1,0:T(8,128)(2,1)S(1)}, u32[]{:S(2)}) copy-start(bf16[16,4096]{1,0:T(8,128)(2,1)S(1)} %get-tuple-element.60.refs_14_) | copy-start | bytes 393220
  170.2 4.1 %copy-start.29 = (bf16[224,512]{1,0:T(8,128)(2,1)S(1)}, bf16[224,512]{1,0:T(8,128)(2,1)}, u32[]{:S(2)}) copy-start(bf16[224,512]{1,0:T(8,128)(2,1)} %copy-done.28) | copy-start | bytes 688132
  170.3 10.1 %collective-permute-start.14 = (bf16[16,4096]{1,0:T(8,128)(2,1)S(1)}, bf16[16,4096]{1,0:T(8,128)(2,1)S(1)}, u32[]{:S(2)}, u32[]{:S(2)}) collective-permute-start(bf16[16,4096]{1,0:T(8,128)(2,1)S(1)} %get-tuple-element.60.refs_14_), channel_id=1, source_target_pairs={{64,0},{128,64},{192,128},{65,1},{129,65},{193,129},{66,2},{130,66... | collective-permute-start | bytes 393224 | tf_op jit(solution)/shard_map/ppermute | solution.py:169
  173.1 8.6 %copy-start.20 = (bf16[16,4096]{1,0:T(8,128)(2,1)}, bf16[16,4096]{1,0:T(8,128)(2,1)S(1)}, u32[]{:S(2)}) copy-start(bf16[16,4096]{1,0:T(8,128)(2,1)S(1)} %get-tuple-element.61.refs_15_) | copy-start | bytes 393220
  173.1 12.6 %collective-permute-start.15 = (bf16[16,4096]{1,0:T(8,128)(2,1)S(1)}, bf16[16,4096]{1,0:T(8,128)(2,1)S(1)}, u32[]{:S(2)}, u32[]{:S(2)}) collective-permute-start(bf16[16,4096]{1,0:T(8,128)(2,1)S(1)} %get-tuple-element.61.refs_15_), channel_id=1, source_target_pairs={{64,0},{128,64},{192,128},{65,1},{129,65},{193,129},{66,2},{130,66... | collective-permute-start | bytes 393224 | tf_op jit(solution)/shard_map/ppermute | solution.py:169
  181.7 5.3 %copy-start.21 = (bf16[16,4096]{1,0:T(8,128)(2,1)}, bf16[16,4096]{1,0:T(8,128)(2,1)S(1)}, u32[]{:S(2)}) copy-start(bf16[16,4096]{1,0:T(8,128)(2,1)S(1)} %get-tuple-element.62.refs_16_) | copy-start | bytes 393220
  181.7 7.9 %collective-permute-start.16 = (bf16[16,4096]{1,0:T(8,128)(2,1)S(1)}, bf16[16,4096]{1,0:T(8,128)(2,1)S(1)}, u32[]{:S(2)}, u32[]{:S(2)}) collective-permute-start(bf16[16,4096]{1,0:T(8,128)(2,1)S(1)} %get-tuple-element.62.refs_16_), channel_id=1, source_target_pairs={{64,0},{128,64},{65,1},{129,65},{66,2},{130,66},{67,3},{131,67},{6... | collective-permute-start | bytes 393224 | tf_op jit(solution)/shard_map/ppermute | solution.py:169
  187.0 4.0 %copy-start.22 = (bf16[16,4096]{1,0:T(8,128)(2,1)}, bf16[16,4096]{1,0:T(8,128)(2,1)S(1)}, u32[]{:S(2)}) copy-start(bf16[16,4096]{1,0:T(8,128)(2,1)S(1)} %get-tuple-element.63.refs_17_) | copy-start | bytes 393220
  187.1 12.1 %collective-permute-start.17 = (bf16[16,4096]{1,0:T(8,128)(2,1)S(1)}, bf16[16,4096]{1,0:T(8,128)(2,1)S(1)}, u32[]{:S(2)}, u32[]{:S(2)}) collective-permute-start(bf16[16,4096]{1,0:T(8,128)(2,1)S(1)} %get-tuple-element.63.refs_17_), channel_id=1, source_target_pairs={{64,0},{128,64},{65,1},{129,65},{66,2},{130,66},{67,3},{131,67},{6... | collective-permute-start | bytes 393224 | tf_op jit(solution)/shard_map/ppermute | solution.py:169
  191.0 9.5 %copy-start.23 = (bf16[16,4096]{1,0:T(8,128)(2,1)}, bf16[16,4096]{1,0:T(8,128)(2,1)S(1)}, u32[]{:S(2)}) copy-start(bf16[16,4096]{1,0:T(8,128)(2,1)S(1)} %get-tuple-element.64.refs_18_) | copy-start | bytes 393220
  191.0 12.4 %collective-permute-start.18 = (bf16[16,4096]{1,0:T(8,128)(2,1)S(1)}, bf16[16,4096]{1,0:T(8,128)(2,1)S(1)}, u32[]{:S(2)}, u32[]{:S(2)}) collective-permute-start(bf16[16,4096]{1,0:T(8,128)(2,1)S(1)} %get-tuple-element.64.refs_18_), channel_id=1, source_target_pairs={{64,0},{65,1},{66,2},{67,3},{68,4},{69,5},{70,6},{71,7},{72,8},{73... | collective-permute-start | bytes 393224 | tf_op jit(solution)/shard_map/ppermute | solution.py:169
  200.5 4.2 %copy-start.24 = (bf16[16,4096]{1,0:T(8,128)(2,1)}, bf16[16,4096]{1,0:T(8,128)(2,1)S(1)}, u32[]{:S(2)}) copy-start(bf16[16,4096]{1,0:T(8,128)(2,1)S(1)} %get-tuple-element.65.refs_19_) | copy-start | bytes 393220
  200.5 7.3 %collective-permute-start.19 = (bf16[16,4096]{1,0:T(8,128)(2,1)S(1)}, bf16[16,4096]{1,0:T(8,128)(2,1)S(1)}, u32[]{:S(2)}, u32[]{:S(2)}) collective-permute-start(bf16[16,4096]{1,0:T(8,128)(2,1)S(1)} %get-tuple-element.65.refs_19_), channel_id=1, source_target_pairs={{64,0},{65,1},{66,2},{67,3},{68,4},{69,5},{70,6},{71,7},{72,8},{73... | collective-permute-start | bytes 393224 | tf_op jit(solution)/shard_map/ppermute | solution.py:169
  204.7 4.4 %copy-start.25 = (bf16[16,4096]{1,0:T(8,128)(2,1)}, bf16[16,4096]{1,0:T(8,128)(2,1)S(1)}, u32[]{:S(2)}) copy-start(bf16[16,4096]{1,0:T(8,128)(2,1)S(1)} %get-tuple-element.66.refs_20_) | copy-start | bytes 393220
  209.1 0.6 copy-start.26
  210.6 11.1 %all-to-all-start.4 = ((bf16[4,128,512]{2,1,0:T(8,128)(2,1)}), bf16[4,128,512]{2,1,0:T(8,128)(2,1)}, u32[]{:S(2)}, u32[]{:S(2)}) async-start(bf16[4,128,512]{2,1,0:T(8,128)(2,1)} %broadcast_in_dim.37), calls=%async_computation.4 | async-start | bytes 1048576 | tf_op jit(solution)/shard_map/all_to_all | solution.py:22
  224.6 27.7 %all-to-all-start.5 = ((bf16[16,64,512]{2,1,0:T(8,128)(2,1)}), bf16[16,64,512]{2,1,0:T(8,128)(2,1)S(1)}, u32[]{:S(2)}, u32[]{:S(2)}) async-start(bf16[16,64,512]{2,1,0:T(8,128)(2,1)} %bitcast.12), calls=%async_computation.5 | async-start | bytes 2097152 | tf_op jit(solution)/shard_map/all_to_all | solution.py:188

commit v3 on v0

v3 whole, which is shorter than its diff:
```python
import functools

import jax
import jax.numpy as jnp
from jax import lax
from jax.experimental import pallas as pl
from jax.experimental.pallas import tpu as pltpu
from jax.sharding import Mesh
from jax.sharding import PartitionSpec as P

HEAD = 128
CHUNK = 16
DP = ("dp_0", "dp_1", "dp_2", "dp_3")
IN_VMEM = pl.BlockSpec(memory_space=pltpu.VMEM)
IN_SMEM = pl.BlockSpec(memory_space=pltpu.SMEM)
ANYWHERE = pl.BlockSpec(memory_space=pl.ANY)
BF16, F32 = jnp.bfloat16, jnp.float32


def copy_for_each(array, axis):
    count = lax.axis_size(axis)
    return lax.all_to_all(
        jnp.broadcast_to(array[None], (count, *array.shape)), axis, 0, 0, tiled=True
    )


def kernel_call(kernel, name, out_shape, specs, operands, scratch=(), out_spec=IN_VMEM, room=8):
    return pl.pallas_call(
        kernel,
        out_shape=out_shape,
        in_specs=specs,
        out_specs=jax.tree.map(lambda _: out_spec, out_shape),
        scratch_shapes=list(scratch),
        compiler_params=pltpu.CompilerParams(vmem_limit_bytes=room * 2**20),
        name=name,
    )(*operands)


def held_until(value, token):
    return pl.pallas_call(
        lambda value_ref, token_ref, out_ref: None,
        out_shape=jax.ShapeDtypeStruct(value.shape, value.dtype),
        in_specs=[ANYWHERE, IN_VMEM],
        out_specs=ANYWHERE,
        input_output_aliases={0: 0},
        compiler_params=pltpu.CompilerParams(vmem_limit_bytes=2**20),
        name="held_until",
    )(value, token)


def folded(values, kv_width):
    group = values.shape[1] // kv_width
    sums = []
    for head in range(kv_width // HEAD):
        base = head * group * HEAD
        total = values[:, base : base + HEAD]
        for member in range(1, group):
            at = base + member * HEAD
            total = total + values[:, at : at + HEAD]
        sums.append(total)
    return jnp.concatenate(sums, axis=1)


def norm_kernel(where, x_ref, g_ref, fresh_ref, tiles_ref, q_ref, rinv_ref, dv_ref):
    _, tok, width = x_ref.shape
    kv_width = dv_ref.shape[1]
    across, _, _, part = tiles_ref.shape
    far = 2
    near = part // far

    def one(index, carry):
        row = pl.multiple_of(index * CHUNK, CHUNK)
        rows = pl.ds(row, CHUNK)
        dv_ref[rows, :] = folded(fresh_ref[rows, :].astype(F32), kv_width).astype(BF16)
        for loop in range(2):
            x = x_ref[loop, rows, :].astype(F32)
            rinv = lax.rsqrt(jnp.mean(x * x, axis=-1, keepdims=True) + 1e-05)
            normed = x * rinv
            rinv_ref[loop, rows, :] = jnp.broadcast_to(rinv, (CHUNK, HEAD))
            q_ref[loop, rows, :] = folded(normed, kv_width)
            hidden = (normed * g_ref[loop]).astype(BF16)
            for place in range(across):
                for half in range(far):
                    at = (half * across + place) * near
                    tiles_ref[lax.rem(place + across - where[1], across), loop, rows, half * near : (half + 1) * near] = hidden[
                        :, at : at + near
                    ]
        return carry

    lax.fori_loop(0, tok // CHUNK, one, 0)


def fold_kernel(where, mine_ref, other_ref, gcol_ref, tiles_ref, w_ref, f_ref, z_ref):
    width, kv_width = w_ref.shape
    count, piece, _ = mine_ref.shape
    for index in range(count):
        for ref, core in ((mine_ref, where[2]), (other_ref, 1 - where[2])):
            at = pl.multiple_of((2 * index + core) * piece, piece)
            w_ref[pl.ds(at, piece), :] = ref[index]
    across, _, tok, part = tiles_ref.shape
    far = 2
    near = part // far
    group = width // kv_width
    for head in range(kv_width // HEAD):
        for row in range(0, HEAD, CHUNK):
            totals = [None, None]
            for member in range(group):
                at = (head * group + member) * HEAD + row
                rows = w_ref[at : at + CHUNK, :].astype(F32)
                for loop in range(2):
                    term = rows * gcol_ref[at : at + CHUNK, loop : loop + 1]
                    totals[loop] = term if member == 0 else totals[loop] + term
            for loop in range(2):
                f_ref[loop, head * HEAD + row : head * HEAD + row + CHUNK, :] = totals[loop].astype(BF16)
    for loop in range(2):
        total = None
        for place in range(across):
            for half in range(far):
                at = (half * across + place) * near
                term = jnp.dot(
                    tiles_ref[
                        lax.rem(place + across - where[1], across),
                        loop,
                        :,
                        half * near : (half + 1) * near,
                    ],
                    w_ref[at : at + near, :],
                    preferred_element_type=F32,
                )
                total = term if total is None else total + term
        z_ref[loop] = total * (1.0 / width)


def chain_kernel(owner, loop, where, f_ref, z_ref, q_ref, rinv_ref, dv_ref, *refs):
    out_ref = refs[-1]

    @pl.when(where[0] == owner)
    def _():
        dv = dv_ref[...]
        wide = dv.astype(F32)
        pulled = lax.dot_general(dv, f_ref[loop], (((1,), (1,)), ((), ())), preferred_element_type=F32)
        along = jnp.sum(wide * z_ref[loop], axis=-1, keepdims=True)
        rinv = rinv_ref[loop][:, :1]
        out_ref[...] = (wide + rinv * (pulled - q_ref[loop] * along)).astype(BF16)


def change_kernel(loop, where, w_ref, x_ref, g_ref, *refs):
    dv_ref, dh_ref = refs[-2:]
    npipe = x_ref.shape[1] // refs[-3].shape[0]
    given = refs[:npipe]
    pieces = refs[-2 - npipe : -2]
    tok = x_ref.shape[1]
    if dv_ref.shape[0] > tok:
        dv_ref[tok:, :] = refs[npipe][...]
    section = where[0]
    for place in range(npipe):

        @pl.when(section == place)
        def _():
            dv_ref[:tok, :] = given[place][...]

    dh_ref[...] = lax.dot_general(
        dv_ref[:tok, :], w_ref[...], (((1,), (1,)), ((), ())), preferred_element_type=F32
    )
    share = tok // npipe
    for shift in range(npipe):
        start = lax.rem(section + shift, npipe) * share
        for at in range(0, share, CHUNK):
            rows = pl.ds(pl.multiple_of(start + at, CHUNK), CHUNK)
            x = x_ref[loop, rows, :].astype(F32)
            dhg = dh_ref[rows, :] * g_ref[loop]
            rinv = lax.rsqrt(jnp.mean(x * x, axis=-1, keepdims=True) + 1e-05)
            normed = x * rinv
            along = jnp.mean(dhg * normed, axis=-1, keepdims=True)
            pieces[shift][at : at + CHUNK, :] = (rinv * (dhg - normed * along)).astype(BF16)


def part_kernel(*refs):
    part_ref = refs[-1]
    count = (len(refs) - 2) // 2
    total = None
    for tiles_ref, dv_ref in zip(refs[:count], refs[count:-2], strict=True):
        tok = tiles_ref.shape[1]
        for loop in range(2):
            at = 0 if loop == 0 else tok
            term = lax.dot_general(
                tiles_ref[loop],
                dv_ref[at : at + tok, :],
                (((0,), (0,)), ((), ())),
                preferred_element_type=F32,
            )
            total = term if total is None else total + term
    part_ref[...] = total.astype(BF16)


def total_kernel(first, npipe, where, start_ref, *refs):
    given = refs[:npipe]
    run_ref, mark_ref = refs[-2:]
    results = refs[-2 - npipe : -2]
    mark_ref[...] = jnp.zeros_like(mark_ref)
    owner = where[0]
    share = run_ref.shape[0]
    for place in range(npipe):

        @pl.when(owner == place)
        def _():
            for at in range(0, share, CHUNK):
                base = place * share + at if first else at
                total = start_ref[base : base + CHUNK, :].astype(F32)
                for source in reversed(range(npipe)):
                    total = total + given[(place - source) % npipe][at : at + CHUNK, :].astype(F32)
                    results[(source - place) % npipe][at : at + CHUNK, :] = total.astype(BF16)
                run_ref[at : at + CHUNK, :] = total


def collect_kernel(npipe, where, *refs):
    *pieces, out_ref, sems = refs
    section = where[0]
    share = pieces[0].shape[0]
    copies = []
    for index, piece in enumerate(pieces):
        loop, shift = divmod(index, npipe)
        row = pl.multiple_of(lax.rem(section + npipe - shift, npipe) * share, share)
        target = out_ref.at[loop, pl.ds(row, share), :]
        copies.append(pltpu.make_async_copy(piece, target, sems.at[index]))
    for copy in copies:
        copy.start()
    for copy in copies:
        copy.wait()


def exchanged(pieces, axis):
    count = lax.axis_size(axis)
    moved = [pieces[0]]
    for shift in range(1, count):
        pairs = [(source, (source + shift) % count) for source in range(count)]
        moved.append(lax.ppermute(pieces[shift], axis, pairs))
    return moved


def on_device(saved, grad_out, gain, w_value):
    npipe = lax.axis_size("pipe")
    where = jnp.stack([lax.axis_index(name) for name in ("pipe", "dp_1", "dp_3")]).astype(jnp.int32)
    x = saved[:, 0]
    _, tok, width = x.shape
    kv_width = w_value.shape[2]
    share = tok // npipe
    far, across = lax.axis_size("dp_0"), lax.axis_size("dp_1")
    shape = jax.ShapeDtypeStruct

    mine = copy_for_each(w_value[0], DP[:3])
    other = lax.ppermute(mine, DP[3], [(0, 1), (1, 0)])
    tiles, fold_x, rinv, dv_first = kernel_call(
        norm_kernel,
        "normalize",
        (
            shape((across, 2, tok, width // across), BF16),
            shape((2, tok, kv_width), F32),
            shape((2, tok, HEAD), F32),
            shape((tok, kv_width), BF16),
        ),
        [IN_SMEM] + [IN_VMEM] * 3,
        (where, x, gain, grad_out),
    )
    gain_col = gain[:, 0].T
    w_mat, fold_w, along = kernel_call(
        fold_kernel,
        "fold_weights",
        (
            shape((width, kv_width), BF16),
            shape((2, kv_width, kv_width), BF16),
            shape((2, tok, kv_width), F32),
        ),
        [IN_SMEM] + [IN_VMEM] * 4,
        (where, mine, other, gain_col, tiles),
    )

    def changes(loop, given, after):
        out = kernel_call(
            functools.partial(change_kernel, loop),
            "changes",
            (shape((share, width), BF16),) * npipe
            + (shape(((2 - loop) * tok, kv_width), BF16),),
            [IN_SMEM] + [IN_VMEM] * (3 + npipe + len(after)),
            (where, w_mat, x, gain, *given, *after),
            scratch=(pltpu.VMEM((tok, width), F32),),
        )
        return out[:npipe], out[npipe]

    def totals(first, start, pieces, after):
        out = kernel_call(
            functools.partial(total_kernel, first, npipe),
            "totals",
            (shape((share, width), BF16),) * npipe
            + (shape((share, width), F32), shape((8, HEAD), F32)),
            [IN_SMEM] + [IN_VMEM] * (1 + npipe + len(after)),
            (where, start, *pieces, *after),
        )
        return out[:npipe], out[npipe], out[npipe + 1]

    arrived = [dv_first]
    dvs = [None, None]
    made = [None, None]
    back = [None, None]
    run = grad_out
    after, mark, behind = (), (), ()
    for hop in range(2 * npipe):
        owner, loop = npipe - 1 - hop % npipe, 1 - hop // npipe
        if hop < 2 * npipe - 1:
            following = kernel_call(
                functools.partial(chain_kernel, owner, loop),
                "chain",
                shape((tok, kv_width), BF16),
                [IN_SMEM] + [IN_VMEM] * (5 + len(after)),
                (where, fold_w, along, fold_x, rinv, arrived[hop], *after),
            )
            if hop == 0:
                hidden = exchanged(held_until(tiles, following), "dp_1")
            arrived.append(lax.ppermute(following, "pipe", [(owner, (owner - 1) % npipe)]))
        if owner == 0:
            given = [arrived[hop - place] for place in range(npipe)]
            made[loop], dvs[loop] = changes(loop, given, mark)
            behind = () if loop == 1 else tuple(back[1][1:])
            sums, run, sign = totals(loop == 1, run, exchanged(made[loop], "pipe"), behind)
            if loop == 0:
                spread = exchanged([dvs[0]] * across, "dp_1")
                part = kernel_call(
                    part_kernel,
                    "part",
                    shape((width // across, kv_width), BF16),
                    [IN_VMEM] * (2 * across + 1),
                    (*hidden, *spread, sign),
                )
            after, mark = (dvs[loop],), (dvs[loop], sign)
            back[loop] = exchanged(sums, "pipe")

    grad_x = kernel_call(
        functools.partial(collect_kernel, npipe),
        "collect_rows",
        shape((2, tok, width), BF16),
        [IN_SMEM] + [IN_VMEM] * (2 * npipe),
        (where, *back[0], *back[1]),
        scratch=(pltpu.SemaphoreType.DMA((2 * npipe,)),),
        out_spec=ANYWHERE,
    )[:, None]

    others = ("dp_0", "dp_2", "dp_3")
    pieces = part.reshape(lax.axis_size(others), -1, kv_width)
    landed = lax.all_to_all(pieces, others, 0, 0, tiled=True)
    grad_w = landed.astype(F32).sum(axis=0)[None]
    return (grad_x, grad_w)


def solution(mesh):
    finer = Mesh(
        mesh.devices.reshape(mesh.shape["pipe"], 2, 4, 4, 2),
        ("pipe", "dp_0", "dp_1", "dp_2", "dp_3"),
    )
    placed = (P(None, "pipe", DP, None), P(DP, None), P(None, "pipe", None), P("pipe", DP, None))
    return jax.shard_map(
        on_device,
        mesh=finer,
        in_specs=placed,
        out_specs=(P(None, "pipe", DP, None), P("pipe", DP, None)),
        check_vma=False,
    )
```

time: 434 us -> 237 us (0.55)
  blocking collectives: 105 us -> 35.4 us
  waiting for transfers between devices: 182 us -> 127 us
  other arithmetic: 48.4 us -> 0.88 us
  matrix products: 37 us -> 0 us
  local copies, waits for them, and re-layouts: 30.4 us -> 3.22 us
  Pallas kernels: 0 us -> 24.1 us
  starting transfers between devices: 26.3 us -> 45.3 us
    all_to_all x2 -> x0, blocking collectives: 94 us -> none  [the longest x1 59 us: summed_rows(): lax.all_to_all(nearer, far, split_axis=0, concat_axis=0, tiled=True)]
    ppermute x9 -> x26, waiting for transfers between devices: 164 us -> 127 us  [the longest x18 66.5 us: exchanged(): moved.append(lax.ppermute(pieces[shift], axis, pairs))]
    dot_general x10 -> x0, matrix products: 37 us -> none  [the longest x9 34.2 us: one_step(): lax.dot_general(dv, w_mat, (((1,), (1,)), ((), ())), preferred_element_ty...]
    all_to_all x1, blocking collectives: 10.7 us -> 35.4 us  [copy_for_each(): lax.all_to_all(jnp.broadcast_to(array[None], (count, *array.shape)), axis...]
    pallas_call x0 -> x16, Pallas kernels: none -> 24.1 us  [the longest x15 24.1 us: kernel_call(): pl.pallas_call(kernel, out_shape=out_shape, in_specs=specs, out_specs=jax...]
    dynamic_update_slice x18 -> x0, other arithmetic: 21.3 us -> none  [the longest x9 21.1 us: one_step(): lax.dynamic_update_slice(grad_buf, jnp.where(valid, dx[None], old_x), (lo...]
    ppermute x9 -> x26, starting transfers between devices: 16.8 us -> 36.1 us  [the longest x18 27.1 us: exchanged(): moved.append(lax.ppermute(pieces[shift], axis, pairs))]
    all_to_all x1, waiting for transfers between devices: 18.2 us -> 0.01 us  [on_device(): landed = lax.all_to_all(pieces, others, 0, 0, tiled=True)]
  transfers between devices with their start and end apart: 10 -> 27, of which waited for: 10 -> 9; matrix products, arithmetic and copies ran while one was open for 2% -> 1% of each run, Pallas kernels for 0% -> 6%
where the time goes in v3:
time: 237 us
  waiting for transfers between devices  127 us (54%)
  starting transfers between devices  45.3 us (19%)
  blocking collectives  35.4 us (15%)
  Pallas kernels  24.1 us (10%)
  local copies, waits for them, and re-layouts  3.22 us (1%)
    ppermute x18, waiting for transfers between devices, exchanged(): moved.append(lax.ppermute(pieces[shift], axis, pairs))  66.5 us
    ppermute x7, waiting for transfers between devices, on_device(): lax.ppermute(following, 'pipe', [(owner, (owner - 1) % npipe)])  60.3 us
    all_to_all x1, blocking collectives, copy_for_each(): lax.all_to_all(jnp.broadcast_to(array[None], (count, *array.shape)), axis...  35.4 us
    ppermute x18, starting transfers between devices, exchanged(): moved.append(lax.ppermute(pieces[shift], axis, pairs))  27.1 us
    pallas_call x15, Pallas kernels, kernel_call(): pl.pallas_call(kernel, out_shape=out_shape, in_specs=specs, out_specs=jax...  24.1 us
    all_to_all x1, starting transfers between devices, on_device(): landed = lax.all_to_all(pieces, others, 0, 0, tiled=True)  9.11 us
    ppermute x7, starting transfers between devices, on_device(): lax.ppermute(following, 'pipe', [(owner, (owner - 1) % npipe)])  6.56 us
  transfers between devices with their start and end apart: 27, of which 9 were waited for; matrix products, arithmetic and copies ran while one was open for 1% of the time, Pallas kernels for 6%

profile of v3, /device:TPU:1, one launch (start us, length us, event | category | flops | bytes accessed | tf_op | source)
XLA Modules:
  0.0 236.8 jit_solution(3747170699519305656)
XLA Ops:
  0.6 1.1 broadcast_in_dim.14
  1.7 0.0 copy-start.3
  1.7 0.0 copy-start.2
  1.7 35.4 %all_to_all.10.mine_ref = bf16[32,64,512]{2,1,0:T(8,128)(2,1)} all-to-all(bf16[32,64,512]{2,1,0:T(8,128)(2,1)S(1)} %broadcast_in_dim.14), channel_id=1, replica_groups=mesh['pipe'=4,'dp_0'=2,'dp_1'=4,'dp_2'=4,'dp_3'=2] {'dp_0','dp_1','dp_2'}, dimensions={0} | all-to-all | bytes 4194304 | tf_op jit(solution)/shard_map/all_to_all | solution.py:22
  37.2 2.5 %collective-permute-start = (bf16[32,64,512]{2,1,0:T(8,128)(2,1)}, bf16[32,64,512]{2,1,0:T(8,128)(2,1)}, u32[]{:S(2)}, u32[]{:S(2)}) collective-permute-start(bf16[32,64,512]{2,1,0:T(8,128)(2,1)} %all_to_all.10.mine_ref), channel_id=1, source_target_pairs={{0,1},{1,0},{2,3},{3,2},{4,5},{5,4},{6,7},{7,6},{8,9},{9,8},{10,11... | collective-permute-start | bytes 6291464 | tf_op jit(solution)/shard_map/ppermute | solution.py:252
  39.7 2.0 copy.7
  41.7 0.1 pad_add_fusion.where
  41.7 2.2 normalize.1
  43.9 4.8 %fold_weights.1 = (bf16[4096,512]{1,0:T(8,128)(2,1)S(1)}, bf16[2,512,512]{2,1,0:T(8,128)(2,1)S(1)}, f32[2,128,512]{2,1,0:T(8,128)S(1)}) custom-call(s32[3]{0:T(128)S(1)} %pad_add_fusion.where, bf16[32,64,512]{2,1,0:T(8,128)(2,1)} %all_to_all.10.mine_ref, bf16[32,64,512]{2,1,0:T(8,128)(2,1)} %collective-permute-done.other_ref, f32[4096,2]{1,0:T(8,128)S(1)} %bitcast.24, ...), custom_call_target="tpu_custom_call" | custom-call | tf_op jit(solution)/shard_map/fold_weights/pallas_call | solution.py:28
  48.8 0.6 chain.7.token_ref
  49.3 0.7 collective-permute-start.1
  50.0 0.6 chain.8
  50.6 0.7 collective-permute-start.2
  51.3 0.0 collective-permute-done.2.dv_ref.refs_1_
  51.3 0.6 chain.9
  51.8 1.3 collective-permute-start.3
  53.1 25.0 %collective-permute-done.3.refs_0_.dv_ref = bf16[128,512]{1,0:T(8,128)(2,1)S(1)} collective-permute-done((bf16[128,512]{1,0:T(8,128)(2,1)S(1)}, bf16[128,512]{1,0:T(8,128)(2,1)S(1)}, u32[]{:S(2)}, u32[]{:S(2)}) %collective-permute-start.3) | collective-permute-done | bytes 131104 | tf_op jit(solution)/shard_map/ppermute | solution.py:319
  78.1 0.9 chain.10
  79.0 1.3 collective-permute-start.7
  80.3 0.2 slice_bitcast_fusion
  80.5 2.7 %changes.2 = (bf16[32,4096]{1,0:T(8,128)(2,1)S(1)}, bf16[32,4096]{1,0:T(8,128)(2,1)S(1)}, bf16[32,4096]{1,0:T(8,128)(2,1)S(1)}, bf16[32,4096]{1,0:T(8,128)(2,1)S(1)}, bf16[128,512]{1,0:T(8,128)(2,1)S(1)}) custom-call(s32[3]{0:T(128)S(1)} %pad_add_fusion.where, bf16[4096,512]{1,0:T(8,128)(2,1)S(1)} %get-tuple-element.31.w_ref, ...), custom_call_target="tpu_custom_call" | custom-call | tf_op jit(solution)/shard_map/changes/pallas_call | solution.py:28
  83.2 0.1 collective-permute-start.4
  83.3 0.1 collective-permute-start.5
  83.4 3.5 %collective-permute-start.6 = (bf16[32,4096]{1,0:T(8,128)(2,1)S(1)}, bf16[32,4096]{1,0:T(8,128)(2,1)S(1)}, u32[]{:S(2)}, u32[]{:S(2)}) collective-permute-start(bf16[32,4096]{1,0:T(8,128)(2,1)S(1)} %get-tuple-element.40), channel_id=1, source_target_pairs={{0,192},{64,0},{128,64},{192,128},{1,193},{65,1},{129,65},{193,129... | collective-permute-start | bytes 786440 | tf_op jit(solution)/shard_map/ppermute | solution.py:237
  86.9 0.4 collective-permute-start.22
  87.3 13.2 %collective-permute-done.7.dv_ref.refs_3_ = bf16[128,512]{1,0:T(8,128)(2,1)S(1)} collective-permute-done((bf16[128,512]{1,0:T(8,128)(2,1)S(1)}, bf16[128,512]{1,0:T(8,128)(2,1)S(1)}, u32[]{:S(2)}, u32[]{:S(2)}) %collective-permute-start.7) | collective-permute-done | bytes 131104 | tf_op jit(solution)/shard_map/ppermute | solution.py:319
  100.5 0.5 chain.11
  101.1 0.7 collective-permute-start.8
  101.7 0.6 chain.12
  102.3 0.7 collective-permute-start.9
  103.0 0.0 collective-permute-done.4.refs_1_
  103.0 0.0 collective-permute-done.5.refs_2_
  103.0 5.4 %collective-permute-done.6.refs_3_ = bf16[32,4096]{1,0:T(8,128)(2,1)S(1)} collective-permute-done((bf16[32,4096]{1,0:T(8,128)(2,1)S(1)}, bf16[32,4096]{1,0:T(8,128)(2,1)S(1)}, u32[]{:S(2)}, u32[]{:S(2)}) %collective-permute-start.6) | collective-permute-done | bytes 262176 | tf_op jit(solution)/shard_map/ppermute | solution.py:237
  108.4 0.8 totals.2
  109.1 0.5 collective-permute-start.14
  109.6 6.0 %collective-permute-start.15 = (bf16[32,4096]{1,0:T(8,128)(2,1)S(1)}, bf16[32,4096]{1,0:T(8,128)(2,1)S(1)}, u32[]{:S(2)}, u32[]{:S(2)}) collective-permute-start(bf16[32,4096]{1,0:T(8,128)(2,1)S(1)} %get-tuple-element.49), channel_id=1, source_target_pairs={{0,128},{64,192},{128,0},{192,64},{1,129},{65,193},{129,1},{193,65... | collective-permute-start | bytes 786440 | tf_op jit(solution)/shard_map/ppermute | solution.py:237
  115.7 3.5 %collective-permute-start.16 = (bf16[32,4096]{1,0:T(8,128)(2,1)S(1)}, bf16[32,4096]{1,0:T(8,128)(2,1)S(1)}, u32[]{:S(2)}, u32[]{:S(2)}) collective-permute-start(bf16[32,4096]{1,0:T(8,128)(2,1)S(1)} %get-tuple-element.50), channel_id=1, source_target_pairs={{0,192},{64,0},{128,64},{192,128},{1,193},{65,1},{129,65},{193,129... | collective-permute-start | bytes 786440 | tf_op jit(solution)/shard_map/ppermute | solution.py:237
  119.1 0.0 collective-permute-done.9.dv_ref.refs_1_
  119.1 0.5 chain.13
  119.7 1.3 collective-permute-start.10
  121.0 22.1 %collective-permute-done.10.refs_0_ = bf16[128,512]{1,0:T(8,128)(2,1)S(1)} collective-permute-done((bf16[128,512]{1,0:T(8,128)(2,1)S(1)}, bf16[128,512]{1,0:T(8,128)(2,1)S(1)}, u32[]{:S(2)}, u32[]{:S(2)}) %collective-permute-start.10) | collective-permute-done | bytes 131104 | tf_op jit(solution)/shard_map/ppermute | solution.py:319
  143.1 3.8 %collective-permute-start.21 = (bf16[2,128,1024]{2,1,0:T(8,128)(2,1)S(1)}, bf16[2,128,1024]{2,1,0:T(8,128)(2,1)S(1)}, u32[]{:S(2)}, u32[]{:S(2)}) collective-permute-start(bf16[2,128,1024]{2,1,0:T(8,128)(2,1)S(1)} %get-tuple-element.61), channel_id=1, source_target_pairs={{0,16},{8,24},{16,0},{24,8},{1,17},{9,25},{17,1},{25,9},{2,18},{10... | collective-permute-start | bytes 1572872 | tf_op jit(solution)/shard_map/ppermute | solution.py:237
  146.9 2.7 %changes.3 = (bf16[32,4096]{1,0:T(8,128)(2,1)S(1)}, bf16[32,4096]{1,0:T(8,128)(2,1)S(1)}, bf16[32,4096]{1,0:T(8,128)(2,1)S(1)}, bf16[32,4096]{1,0:T(8,128)(2,1)S(1)}, bf16[256,512]{1,0:T(8,128)(2,1)S(1)}) custom-call(s32[3]{0:T(128)S(1)} %pad_add_fusion.where, bf16[4096,512]{1,0:T(8,128)(2,1)S(1)} %get-tuple-element.31.w_ref, ...), custom_call_target="tpu_custom_call" | custom-call | tf_op jit(solution)/shard_map/changes/pallas_call | solution.py:28
  149.6 0.0 collective-permute-done.22.refs_3_
  149.7 0.1 collective-permute-start.20
  149.7 0.0 collective-permute-done.14.refs_4_.refs_5_
  149.8 0.1 collective-permute-start.11
  149.8 0.0 collective-permute-done.15.refs_5_.refs_6_
  149.9 0.1 collective-permute-start.12
  150.0 0.0 collective-permute-done.16.refs_6_.refs_7_
  150.0 3.5 %collective-permute-start.13 = (bf16[32,4096]{1,0:T(8,128)(2,1)S(1)}, bf16[32,4096]{1,0:T(8,128)(2,1)S(1)}, u32[]{:S(2)}, u32[]{:S(2)}) collective-permute-start(bf16[32,4096]{1,0:T(8,128)(2,1)S(1)} %get-tuple-element.47), channel_id=1, source_target_pairs={{0,192},{64,0},{128,64},{192,128},{1,193},{65,1},{129,65},{193,129... | collective-permute-start | bytes 786440 | tf_op jit(solution)/shard_map/ppermute | solution.py:237
  153.5 8.9 %collective-permute-done.11.refs_1_ = bf16[32,4096]{1,0:T(8,128)(2,1)S(1)} collective-permute-done((bf16[32,4096]{1,0:T(8,128)(2,1)S(1)}, bf16[32,4096]{1,0:T(8,128)(2,1)S(1)}, u32[]{:S(2)}, u32[]{:S(2)}) %collective-permute-start.11) | collective-permute-done | bytes 262176 | tf_op jit(solution)/shard_map/ppermute | solution.py:237
  162.4 1.8 collective-permute-start.24
  164.2 14.7 %collective-permute-done.13.refs_3_ = bf16[32,4096]{1,0:T(8,128)(2,1)S(1)} collective-permute-done((bf16[32,4096]{1,0:T(8,128)(2,1)S(1)}, bf16[32,4096]{1,0:T(8,128)(2,1)S(1)}, u32[]{:S(2)}, u32[]{:S(2)}) %collective-permute-start.13) | collective-permute-done | bytes 262176 | tf_op jit(solution)/shard_map/ppermute | solution.py:237
  178.9 1.5 totals.3
  180.5 6.9 %collective-permute-done.23.refs_5_ = bf16[256,512]{1,0:T(8,128)(2,1)S(1)} collective-permute-done((bf16[256,512]{1,0:T(8,128)(2,1)S(1)}, bf16[256,512]{1,0:T(8,128)(2,1)S(1)}, u32[]{:S(2)}, u32[]{:S(2)}) %collective-permute-start.23) | collective-permute-done | bytes 262176 | tf_op jit(solution)/shard_map/ppermute | solution.py:237
  187.3 3.3 %part.1 = bf16[1024,512]{1,0:T(8,128)(2,1)} custom-call(bf16[2,128,1024]{2,1,0:T(8,128)(2,1)S(1)} %get-tuple-element.63.refs_0_, bf16[2,128,1024]{2,1,0:T(8,128)(2,1)S(1)} %collective-permute-done.20.refs_1_, bf16[2,128,1024]{2,1,0:T(8,128)(2,1)S(1)} %collective-permute-done.21.refs_2_, bf16[2,128,1024]{2,1,0:T(8,128)(2,1)S(1)} %collective-permute-done.22.refs_3_, ...), custom_call_target="tpu_custom_call" | custom-call | tf_op jit(solution)/shard_map/part/pallas_call | solution.py:28
  190.6 9.1 %all-to-all-start.1 = ((bf16[16,64,512]{2,1,0:T(8,128)(2,1)}), bf16[16,64,512]{2,1,0:T(8,128)(2,1)S(1)}, u32[]{:S(2)}, u32[]{:S(2)}) async-start(bf16[16,64,512]{2,1,0:T(8,128)(2,1)} %bitcast.13), calls=%async_computation.1 | async-start | bytes 2097152 | tf_op jit(solution)/shard_map/all_to_all | solution.py:349
  199.8 1.3 collective-permute-start.18
  201.1 2.2 collective-permute-start.19
  203.3 19.5 %collective-permute-done.17.refs_1_ = bf16[32,4096]{1,0:T(8,128)(2,1)S(1)} collective-permute-done((bf16[32,4096]{1,0:T(8,128)(2,1)S(1)}, bf16[32,4096]{1,0:T(8,128)(2,1)S(1)}, u32[]{:S(2)}, u32[]{:S(2)}) %collective-permute-start.17) | collective-permute-done | bytes 262176 | tf_op jit(solution)/shard_map/ppermute | solution.py:237
  222.8 11.2 %collective-permute-done.18.refs_2_ = bf16[32,4096]{1,0:T(8,128)(2,1)S(1)} collective-permute-done((bf16[32,4096]{1,0:T(8,128)(2,1)S(1)}, bf16[32,4096]{1,0:T(8,128)(2,1)S(1)}, u32[]{:S(2)}, u32[]{:S(2)}) %collective-permute-start.18) | collective-permute-done | bytes 262176 | tf_op jit(solution)/shard_map/ppermute | solution.py:237
  234.0 1.9 collect_rows.1
  236.0 0.8 convert_reduce_fusion
  (20 shorter events, 0.0 us)
Async XLA Ops:
  1.7 38.0 %copy-start.3 = (f32[2,1,4096]{2,1,0:T(1,128)S(1)}, f32[2,1,4096]{2,1,0:T(1,128)}, u32[]{:S(2)}) copy-start(f32[2,1,4096]{2,1,0:T(1,128)} %g_ref.5) | copy-start | bytes 98308
  1.7 40.0 %copy-start.2 = (bf16[128,4096]{1,0:T(8,128)(2,1)S(1)}, bf16[128,4096]{1,0:T(8,128)(2,1)}, u32[]{:S(2)}) copy-start(bf16[128,4096]{1,0:T(8,128)(2,1)} %start_ref.1) | copy-start | bytes 3145732
  37.2 4.6 %copy-start = (bf16[2,1,128,4096]{3,2,1,0:T(8,128)(2,1)S(1)}, bf16[2,1,128,4096]{3,2,1,0:T(8,128)(2,1)}, u32[]{:S(2)}) copy-start(bf16[2,1,128,4096]{3,2,1,0:T(8,128)(2,1)} %param.4) | copy-start | bytes 6291460
  37.2 6.7 %collective-permute-start = (bf16[32,64,512]{2,1,0:T(8,128)(2,1)}, bf16[32,64,512]{2,1,0:T(8,128)(2,1)}, u32[]{:S(2)}, u32[]{:S(2)}) collective-permute-start(bf16[32,64,512]{2,1,0:T(8,128)(2,1)} %all_to_all.10.mine_ref), channel_id=1, source_target_pairs={{0,1},{1,0},{2,3},{3,2},{4,5},{5,4},{6,7},{7,6},{8,9},{9,8},{10,11... | collective-permute-start | bytes 6291464 | tf_op jit(solution)/shard_map/ppermute | solution.py:252
  41.7 2.3 copy-start.1
  49.3 0.7 collective-permute-start.1
  50.6 0.7 collective-permute-start.2
  51.8 26.3 %collective-permute-start.3 = (bf16[128,512]{1,0:T(8,128)(2,1)S(1)}, bf16[128,512]{1,0:T(8,128)(2,1)S(1)}, u32[]{:S(2)}, u32[]{:S(2)}) collective-permute-start(bf16[128,512]{1,0:T(8,128)(2,1)S(1)} %chain.9), channel_id=1, source_target_pairs={{64,0},{65,1},{66,2},{67,3},{68,4},{69,5},{70,6},{71,7},{72,8},{73... | collective-permute-start | bytes 393224 | tf_op jit(solution)/shard_map/ppermute | solution.py:319
  79.0 21.5 %collective-permute-start.7 = (bf16[128,512]{1,0:T(8,128)(2,1)S(1)}, bf16[128,512]{1,0:T(8,128)(2,1)S(1)}, u32[]{:S(2)}, u32[]{:S(2)}) collective-permute-start(bf16[128,512]{1,0:T(8,128)(2,1)S(1)} %chain.10), channel_id=1, source_target_pairs={{0,192},{1,193},{2,194},{3,195},{4,196},{5,197},{6,198},{7,199},{8... | collective-permute-start | bytes 393224 | tf_op jit(solution)/shard_map/ppermute | solution.py:319
  83.2 19.8 %collective-permute-start.4 = (bf16[32,4096]{1,0:T(8,128)(2,1)S(1)}, bf16[32,4096]{1,0:T(8,128)(2,1)S(1)}, u32[]{:S(2)}, u32[]{:S(2)}) collective-permute-start(bf16[32,4096]{1,0:T(8,128)(2,1)S(1)} %get-tuple-element.38), channel_id=1, source_target_pairs={{0,64},{64,128},{128,192},{192,0},{1,65},{65,129},{129,193},{193,1... | collective-permute-start | bytes 786440 | tf_op jit(solution)/shard_map/ppermute | solution.py:237
  83.3 19.7 %collective-permute-start.5 = (bf16[32,4096]{1,0:T(8,128)(2,1)S(1)}, bf16[32,4096]{1,0:T(8,128)(2,1)S(1)}, u32[]{:S(2)}, u32[]{:S(2)}) collective-permute-start(bf16[32,4096]{1,0:T(8,128)(2,1)S(1)} %get-tuple-element.39), channel_id=1, source_target_pairs={{0,128},{64,192},{128,0},{192,64},{1,129},{65,193},{129,1},{193,65... | collective-permute-start | bytes 786440 | tf_op jit(solution)/shard_map/ppermute | solution.py:237
  83.4 25.0 %collective-permute-start.6 = (bf16[32,4096]{1,0:T(8,128)(2,1)S(1)}, bf16[32,4096]{1,0:T(8,128)(2,1)S(1)}, u32[]{:S(2)}, u32[]{:S(2)}) collective-permute-start(bf16[32,4096]{1,0:T(8,128)(2,1)S(1)} %get-tuple-element.40), channel_id=1, source_target_pairs={{0,192},{64,0},{128,64},{192,128},{1,193},{65,1},{129,65},{193,129... | collective-permute-start | bytes 786440 | tf_op jit(solution)/shard_map/ppermute | solution.py:237
  86.9 62.8 %collective-permute-start.22 = (bf16[2,128,1024]{2,1,0:T(8,128)(2,1)S(1)}, bf16[2,128,1024]{2,1,0:T(8,128)(2,1)S(1)}, u32[]{:S(2)}, u32[]{:S(2)}) collective-permute-start(bf16[2,128,1024]{2,1,0:T(8,128)(2,1)S(1)} %get-tuple-element.60), channel_id=1, source_target_pairs={{0,24},{8,0},{16,8},{24,16},{1,25},{9,1},{17,9},{25,17},{2,26},{10... | collective-permute-start | bytes 1572872 | tf_op jit(solution)/shard_map/ppermute | solution.py:237
  101.1 0.7 collective-permute-start.8
  102.3 16.8 %collective-permute-start.9 = (bf16[128,512]{1,0:T(8,128)(2,1)S(1)}, bf16[128,512]{1,0:T(8,128)(2,1)S(1)}, u32[]{:S(2)}, u32[]{:S(2)}) collective-permute-start(bf16[128,512]{1,0:T(8,128)(2,1)S(1)} %chain.12), channel_id=1, source_target_pairs={{128,64},{129,65},{130,66},{131,67},{132,68},{133,69},{134,70},{13... | collective-permute-start | bytes 393224 | tf_op jit(solution)/shard_map/ppermute | solution.py:319
  109.1 40.6 %collective-permute-start.14 = (bf16[32,4096]{1,0:T(8,128)(2,1)S(1)}, bf16[32,4096]{1,0:T(8,128)(2,1)S(1)}, u32[]{:S(2)}, u32[]{:S(2)}) collective-permute-start(bf16[32,4096]{1,0:T(8,128)(2,1)S(1)} %get-tuple-element.48), channel_id=1, source_target_pairs={{0,64},{64,128},{128,192},{192,0},{1,65},{65,129},{129,193},{193,1... | collective-permute-start | bytes 786440 | tf_op jit(solution)/shard_map/ppermute | solution.py:237
  109.6 40.2 %collective-permute-start.15 = (bf16[32,4096]{1,0:T(8,128)(2,1)S(1)}, bf16[32,4096]{1,0:T(8,128)(2,1)S(1)}, u32[]{:S(2)}, u32[]{:S(2)}) collective-permute-start(bf16[32,4096]{1,0:T(8,128)(2,1)S(1)} %get-tuple-element.49), channel_id=1, source_target_pairs={{0,128},{64,192},{128,0},{192,64},{1,129},{65,193},{129,1},{193,65... | collective-permute-start | bytes 786440 | tf_op jit(solution)/shard_map/ppermute | solution.py:237
  115.7 34.3 %collective-permute-start.16 = (bf16[32,4096]{1,0:T(8,128)(2,1)S(1)}, bf16[32,4096]{1,0:T(8,128)(2,1)S(1)}, u32[]{:S(2)}, u32[]{:S(2)}) collective-permute-start(bf16[32,4096]{1,0:T(8,128)(2,1)S(1)} %get-tuple-element.50), channel_id=1, source_target_pairs={{0,192},{64,0},{128,64},{192,128},{1,193},{65,1},{129,65},{193,129... | collective-permute-start | bytes 786440 | tf_op jit(solution)/shard_map/ppermute | solution.py:237
  119.7 23.4 %collective-permute-start.10 = (bf16[128,512]{1,0:T(8,128)(2,1)S(1)}, bf16[128,512]{1,0:T(8,128)(2,1)S(1)}, u32[]{:S(2)}, u32[]{:S(2)}) collective-permute-start(bf16[128,512]{1,0:T(8,128)(2,1)S(1)} %chain.13), channel_id=1, source_target_pairs={{64,0},{65,1},{66,2},{67,3},{68,4},{69,5},{70,6},{71,7},{72,8},{73... | collective-permute-start | bytes 393224 | tf_op jit(solution)/shard_map/ppermute | solution.py:319
  143.1 37.3 %collective-permute-start.21 = (bf16[2,128,1024]{2,1,0:T(8,128)(2,1)S(1)}, bf16[2,128,1024]{2,1,0:T(8,128)(2,1)S(1)}, u32[]{:S(2)}, u32[]{:S(2)}) collective-permute-start(bf16[2,128,1024]{2,1,0:T(8,128)(2,1)S(1)} %get-tuple-element.61), channel_id=1, source_target_pairs={{0,16},{8,24},{16,0},{24,8},{1,17},{9,25},{17,1},{25,9},{2,18},{10... | collective-permute-start | bytes 1572872 | tf_op jit(solution)/shard_map/ppermute | solution.py:237
  149.7 30.8 %collective-permute-start.20 = (bf16[2,128,1024]{2,1,0:T(8,128)(2,1)S(1)}, bf16[2,128,1024]{2,1,0:T(8,128)(2,1)S(1)}, u32[]{:S(2)}, u32[]{:S(2)}) collective-permute-start(bf16[2,128,1024]{2,1,0:T(8,128)(2,1)S(1)} %get-tuple-element.62), channel_id=1, source_target_pairs={{0,8},{8,16},{16,24},{24,0},{1,9},{9,17},{17,25},{25,1},{2,10},{10... | collective-permute-start | bytes 1572872 | tf_op jit(solution)/shard_map/ppermute | solution.py:237
  149.8 12.6 %collective-permute-start.11 = (bf16[32,4096]{1,0:T(8,128)(2,1)S(1)}, bf16[32,4096]{1,0:T(8,128)(2,1)S(1)}, u32[]{:S(2)}, u32[]{:S(2)}) collective-permute-start(bf16[32,4096]{1,0:T(8,128)(2,1)S(1)} %get-tuple-element.45), channel_id=1, source_target_pairs={{0,64},{64,128},{128,192},{192,0},{1,65},{65,129},{129,193},{193,1... | collective-permute-start | bytes 786440 | tf_op jit(solution)/shard_map/ppermute | solution.py:237
  149.9 12.5 %collective-permute-start.12 = (bf16[32,4096]{1,0:T(8,128)(2,1)S(1)}, bf16[32,4096]{1,0:T(8,128)(2,1)S(1)}, u32[]{:S(2)}, u32[]{:S(2)}) collective-permute-start(bf16[32,4096]{1,0:T(8,128)(2,1)S(1)} %get-tuple-element.46), channel_id=1, source_target_pairs={{0,128},{64,192},{128,0},{192,64},{1,129},{65,193},{129,1},{193,65... | collective-permute-start | bytes 786440 | tf_op jit(solution)/shard_map/ppermute | solution.py:237
  150.0 28.9 %collective-permute-start.13 = (bf16[32,4096]{1,0:T(8,128)(2,1)S(1)}, bf16[32,4096]{1,0:T(8,128)(2,1)S(1)}, u32[]{:S(2)}, u32[]{:S(2)}) collective-permute-start(bf16[32,4096]{1,0:T(8,128)(2,1)S(1)} %get-tuple-element.47), channel_id=1, source_target_pairs={{0,192},{64,0},{128,64},{192,128},{1,193},{65,1},{129,65},{193,129... | collective-permute-start | bytes 786440 | tf_op jit(solution)/shard_map/ppermute | solution.py:237
  162.4 18.1 %collective-permute-start.25 = (bf16[256,512]{1,0:T(8,128)(2,1)S(1)}, bf16[256,512]{1,0:T(8,128)(2,1)S(1)}, u32[]{:S(2)}, u32[]{:S(2)}) collective-permute-start(bf16[256,512]{1,0:T(8,128)(2,1)S(1)} %get-tuple-element.56.refs_4_), channel_id=1, source_target_pairs={{0,24},{8,0},{16,8},{24,16},{1,25},{9,1},{17,9},{25,17},{2,26},{10... | collective-permute-start | bytes 786440 | tf_op jit(solution)/shard_map/ppermute | solution.py:237
  162.4 18.1 %collective-permute-start.24 = (bf16[256,512]{1,0:T(8,128)(2,1)S(1)}, bf16[256,512]{1,0:T(8,128)(2,1)S(1)}, u32[]{:S(2)}, u32[]{:S(2)}) collective-permute-start(bf16[256,512]{1,0:T(8,128)(2,1)S(1)} %get-tuple-element.56.refs_4_), channel_id=1, source_target_pairs={{0,16},{8,24},{16,0},{24,8},{1,17},{9,25},{17,1},{25,9},{2,18},{10... | collective-permute-start | bytes 786440 | tf_op jit(solution)/shard_map/ppermute | solution.py:237
  178.9 8.4 %collective-permute-start.23 = (bf16[256,512]{1,0:T(8,128)(2,1)S(1)}, bf16[256,512]{1,0:T(8,128)(2,1)S(1)}, u32[]{:S(2)}, u32[]{:S(2)}) collective-permute-start(bf16[256,512]{1,0:T(8,128)(2,1)S(1)} %get-tuple-element.56.refs_4_), channel_id=1, source_target_pairs={{0,8},{8,16},{16,24},{24,0},{1,9},{9,17},{17,25},{25,1},{2,10},{10... | collective-permute-start | bytes 786440 | tf_op jit(solution)/shard_map/ppermute | solution.py:237
  190.6 45.3 %all-to-all-start.1 = ((bf16[16,64,512]{2,1,0:T(8,128)(2,1)}), bf16[16,64,512]{2,1,0:T(8,128)(2,1)S(1)}, u32[]{:S(2)}, u32[]{:S(2)}) async-start(bf16[16,64,512]{2,1,0:T(8,128)(2,1)} %bitcast.13), calls=%async_computation.1 | async-start | bytes 2097152 | tf_op jit(solution)/shard_map/all_to_all | solution.py:349
  199.7 23.1 %collective-permute-start.17 = (bf16[32,4096]{1,0:T(8,128)(2,1)S(1)}, bf16[32,4096]{1,0:T(8,128)(2,1)S(1)}, u32[]{:S(2)}, u32[]{:S(2)}) collective-permute-start(bf16[32,4096]{1,0:T(8,128)(2,1)S(1)} %get-tuple-element.52), channel_id=1, source_target_pairs={{0,64},{64,128},{128,192},{192,0},{1,65},{65,129},{129,193},{193,1... | collective-permute-start | bytes 786440 | tf_op jit(solution)/shard_map/ppermute | solution.py:237
  199.8 34.3 %collective-permute-start.18 = (bf16[32,4096]{1,0:T(8,128)(2,1)S(1)}, bf16[32,4096]{1,0:T(8,128)(2,1)S(1)}, u32[]{:S(2)}, u32[]{:S(2)}) collective-permute-start(bf16[32,4096]{1,0:T(8,128)(2,1)S(1)} %get-tuple-element.53), channel_id=1, source_target_pairs={{0,128},{64,192},{128,0},{192,64},{1,129},{65,193},{129,1},{193,65... | collective-permute-start | bytes 786440 | tf_op jit(solution)/shard_map/ppermute | solution.py:237
  201.1 32.9 %collective-permute-start.19 = (bf16[32,4096]{1,0:T(8,128)(2,1)S(1)}, bf16[32,4096]{1,0:T(8,128)(2,1)S(1)}, u32[]{:S(2)}, u32[]{:S(2)}) collective-permute-start(bf16[32,4096]{1,0:T(8,128)(2,1)S(1)} %get-tuple-element.54), channel_id=1, source_target_pairs={{0,192},{64,0},{128,64},{192,128},{1,193},{65,1},{129,65},{193,129... | collective-permute-start | bytes 786440 | tf_op jit(solution)/shard_map/ppermute | solution.py:237

commit v4 on v3

--- a/solution.py
+++ b/solution.py
@@ -193,36 +193,35 @@
     part_ref[...] = total.astype(BF16)
 
 
-def total_kernel(first, npipe, where, start_ref, *refs):
-    given = refs[:npipe]
-    run_ref, mark_ref = refs[-2:]
-    results = refs[-2 - npipe : -2]
-    mark_ref[...] = jnp.zeros_like(mark_ref)
+def total_kernel(npipe, where, start_ref, *refs):
+    given, results = refs[: 2 * npipe], refs[2 * npipe :]
     owner = where[0]
-    share = run_ref.shape[0]
+    share = given[0].shape[0]
     for place in range(npipe):
 
         @pl.when(owner == place)
         def _():
             for at in range(0, share, CHUNK):
-                base = place * share + at if first else at
+                base = place * share + at
+                rows = slice(at, at + CHUNK)
                 total = start_ref[base : base + CHUNK, :].astype(F32)
-                for source in reversed(range(npipe)):
-                    total = total + given[(place - source) % npipe][at : at + CHUNK, :].astype(F32)
-                    results[(source - place) % npipe][at : at + CHUNK, :] = total.astype(BF16)
-                run_ref[at : at + CHUNK, :] = total
+                for loop in (1, 0):
+                    for source in reversed(range(npipe)):
+                        piece = given[(1 - loop) * npipe + (place - source) % npipe]
+                        total = total + piece[rows, :].astype(F32)
+                        results[(source - place) % npipe][loop, rows, :] = total.astype(BF16)
 
 
 def collect_kernel(npipe, where, *refs):
     *pieces, out_ref, sems = refs
     section = where[0]
-    share = pieces[0].shape[0]
+    share = pieces[0].shape[1]
     copies = []
-    for index, piece in enumerate(pieces):
-        loop, shift = divmod(index, npipe)
+    for shift, piece in enumerate(pieces):
         row = pl.multiple_of(lax.rem(section + npipe - shift, npipe) * share, share)
-        target = out_ref.at[loop, pl.ds(row, share), :]
-        copies.append(pltpu.make_async_copy(piece, target, sems.at[index]))
+        for loop in range(2):
+            target = out_ref.at[loop, pl.ds(row, share), :]
+            copies.append(pltpu.make_async_copy(piece.at[loop], target, sems.at[2 * shift + loop]))
     for copy in copies:
         copy.start()
     for copy in copies:
@@ -275,37 +274,28 @@
         (where, mine, other, gain_col, tiles),
     )
 
-    def changes(loop, given, after):
+    def changes(loop, given, after, later):
         out = kernel_call(
             functools.partial(change_kernel, loop),
             "changes",
             (shape((share, width), BF16),) * npipe
             + (shape(((2 - loop) * tok, kv_width), BF16),),
-            [IN_SMEM] + [IN_VMEM] * (3 + npipe + len(after)),
-            (where, w_mat, x, gain, *given, *after),
+            [IN_SMEM] + [IN_VMEM] * (3 + npipe + len(after)) + [ANYWHERE] * len(later),
+            (where, w_mat, x, gain, *given, *after, *later),
             scratch=(pltpu.VMEM((tok, width), F32),),
         )
         return out[:npipe], out[npipe]
 
-    def totals(first, start, pieces, after):
-        out = kernel_call(
-            functools.partial(total_kernel, first, npipe),
-            "totals",
-            (shape((share, width), BF16),) * npipe
-            + (shape((share, width), F32), shape((8, HEAD), F32)),
-            [IN_SMEM] + [IN_VMEM] * (1 + npipe + len(after)),
-            (where, start, *pieces, *after),
-        )
-        return out[:npipe], out[npipe], out[npipe + 1]
-
     arrived = [dv_first]
     dvs = [None, None]
-    made = [None, None]
-    back = [None, None]
-    run = grad_out
-    after, mark, behind = (), (), ()
+    moved = [None, None]
     for hop in range(2 * npipe):
         owner, loop = npipe - 1 - hop % npipe, 1 - hop // npipe
+        after = ()
+        if hop == npipe:
+            after = (dvs[1],)
+        elif hop == 2 * npipe - 2:
+            after = tuple(moved[1][1:])
         if hop < 2 * npipe - 1:
             following = kernel_call(
                 functools.partial(chain_kernel, owner, loop),
@@ -319,31 +309,35 @@
             arrived.append(lax.ppermute(following, "pipe", [(owner, (owner - 1) % npipe)]))
         if owner == 0:
             given = [arrived[hop - place] for place in range(npipe)]
-            made[loop], dvs[loop] = changes(loop, given, mark)
-            behind = () if loop == 1 else tuple(back[1][1:])
-            sums, run, sign = totals(loop == 1, run, exchanged(made[loop], "pipe"), behind)
-            if loop == 0:
-                spread = exchanged([dvs[0]] * across, "dp_1")
-                part = kernel_call(
-                    part_kernel,
-                    "part",
-                    shape((width // across, kv_width), BF16),
-                    [IN_VMEM] * (2 * across + 1),
-                    (*hidden, *spread, sign),
-                )
-            after, mark = (dvs[loop],), (dvs[loop], sign)
-            back[loop] = exchanged(sums, "pipe")
-
+            before = () if loop == 1 else (dvs[1],)
+            made, dvs[loop] = changes(loop, given, before, hidden[1:] if loop == 1 else ())
+            moved[loop] = exchanged(made, "pipe")
+    sums = kernel_call(
+        functools.partial(total_kernel, npipe),
+        "totals",
+        (shape((2, share, width), BF16),) * npipe,
+        [IN_SMEM] + [IN_VMEM] * (1 + 2 * npipe),
+        (where, grad_out, *moved[1], *moved[0]),
+    )
+    back = exchanged(sums, "pipe")
     grad_x = kernel_call(
         functools.partial(collect_kernel, npipe),
         "collect_rows",
         shape((2, tok, width), BF16),
-        [IN_SMEM] + [IN_VMEM] * (2 * npipe),
-        (where, *back[0], *back[1]),
+        [IN_SMEM] + [IN_VMEM] * npipe,
+        (where, *back),
         scratch=(pltpu.SemaphoreType.DMA((2 * npipe,)),),
         out_spec=ANYWHERE,
     )[:, None]
 
+    spread = exchanged([dvs[0]] * across, "dp_1")
+    part = kernel_call(
+        part_kernel,
+        "part",
+        shape((width // across, kv_width), BF16),
+        [IN_VMEM] * (2 * across + 1),
+        (*hidden, *spread, sums[0]),
+    )
     others = ("dp_0", "dp_2", "dp_3")
     pieces = part.reshape(lax.axis_size(others), -1, kv_width)
     landed = lax.all_to_all(pieces, others, 0, 0, tiled=True)

time: 237 us -> 230 us (0.970)
  starting transfers between devices: 45.3 us -> 41.5 us
    ppermute x7, waiting for transfers between devices: 60.3 us -> 31.7 us  [on_device(): lax.ppermute(following, 'pipe', [(owner, (owner - 1) % npipe)])]
    ppermute x18 -> x15, waiting for transfers between devices: 66.5 us -> 92.9 us  [exchanged(): moved.append(lax.ppermute(pieces[shift], axis, pairs))]
    ppermute x18 -> x15, starting transfers between devices: 27.1 us -> 22.3 us  [exchanged(): moved.append(lax.ppermute(pieces[shift], axis, pairs))]
    pallas_call x15 -> x14, Pallas kernels: 24.1 us -> 22.8 us  [kernel_call(): pl.pallas_call(kernel, out_shape=out_shape, in_specs=specs, out_specs=jax...]
  transfers between devices with their start and end apart: 27 -> 24, of which waited for: 9 -> 9; matrix products, arithmetic and copies ran while one was open for 1% -> 1% of each run, Pallas kernels for 6% -> 4%
where the time goes in v4:
time: 230 us; the launch traced here: 229 us
  waiting for transfers between devices  125 us (54%)
  starting transfers between devices  41.5 us (18%)
  blocking collectives  35.4 us (15%)
  Pallas kernels  22.8 us (10%)
  local copies, waits for them, and re-layouts  3.23 us (1%)
    ppermute x15, waiting for transfers between devices, exchanged(): moved.append(lax.ppermute(pieces[shift], axis, pairs))  92.9 us
    all_to_all x1, blocking collectives, copy_for_each(): lax.all_to_all(jnp.broadcast_to(array[None], (count, *array.shape)), axis...  35.4 us
    ppermute x7, waiting for transfers between devices, on_device(): lax.ppermute(following, 'pipe', [(owner, (owner - 1) % npipe)])  31.7 us
    pallas_call x14, Pallas kernels, kernel_call(): pl.pallas_call(kernel, out_shape=out_shape, in_specs=specs, out_specs=jax...  22.8 us
    ppermute x15, starting transfers between devices, exchanged(): moved.append(lax.ppermute(pieces[shift], axis, pairs))  22.3 us
    all_to_all x1, starting transfers between devices, on_device(): landed = lax.all_to_all(pieces, others, 0, 0, tiled=True)  9.93 us
    ppermute x7, starting transfers between devices, on_device(): lax.ppermute(following, 'pipe', [(owner, (owner - 1) % npipe)])  6.74 us
  transfers between devices with their start and end apart: 24, of which 9 were waited for; matrix products, arithmetic and copies ran while one was open for 1% of the time, Pallas kernels for 4%

profile of v4, /device:TPU:1, one launch (start us, length us, event | category | flops | bytes accessed | tf_op | source)
XLA Modules:
  0.0 229.4 jit_solution(13647267207903360111)
XLA Ops:
  0.6 1.1 broadcast_in_dim.14
  1.7 0.0 copy-start.3
  1.7 0.0 copy-start.2
  1.7 35.4 %all_to_all.10.mine_ref = bf16[32,64,512]{2,1,0:T(8,128)(2,1)} all-to-all(bf16[32,64,512]{2,1,0:T(8,128)(2,1)S(1)} %broadcast_in_dim.14), channel_id=1, replica_groups=mesh['pipe'=4,'dp_0'=2,'dp_1'=4,'dp_2'=4,'dp_3'=2] {'dp_0','dp_1','dp_2'}, dimensions={0} | all-to-all | bytes 4194304 | tf_op jit(solution)/shard_map/all_to_all | solution.py:22
  37.2 2.5 %collective-permute-start = (bf16[32,64,512]{2,1,0:T(8,128)(2,1)}, bf16[32,64,512]{2,1,0:T(8,128)(2,1)}, u32[]{:S(2)}, u32[]{:S(2)}) collective-permute-start(bf16[32,64,512]{2,1,0:T(8,128)(2,1)} %all_to_all.10.mine_ref), channel_id=1, source_target_pairs={{0,1},{1,0},{2,3},{3,2},{4,5},{5,4},{6,7},{7,6},{8,9},{9,8},{10,11... | collective-permute-start | bytes 6291464 | tf_op jit(solution)/shard_map/ppermute | solution.py:251
  39.7 2.0 copy.7
  41.7 0.1 pad_add_fusion.where
  41.7 2.2 normalize.1
  43.9 4.8 %fold_weights.1 = (bf16[4096,512]{1,0:T(8,128)(2,1)S(1)}, bf16[2,512,512]{2,1,0:T(8,128)(2,1)S(1)}, f32[2,128,512]{2,1,0:T(8,128)S(1)}) custom-call(s32[3]{0:T(128)S(1)} %pad_add_fusion.where, bf16[32,64,512]{2,1,0:T(8,128)(2,1)} %all_to_all.10.mine_ref, bf16[32,64,512]{2,1,0:T(8,128)(2,1)} %collective-permute-done.other_ref, f32[4096,2]{1,0:T(8,128)S(1)} %bitcast.24, ...), custom_call_target="tpu_custom_call" | custom-call | tf_op jit(solution)/shard_map/fold_weights/pallas_call | solution.py:28
  48.8 0.6 chain.7.token_ref
  49.3 0.7 collective-permute-start.1
  50.0 0.2 slice_bitcast_fusion
  50.2 2.0 collective-permute-start.6
  52.2 0.5 collective-permute-start.5
  52.7 0.3 collective-permute-start.4
  53.0 0.0 collective-permute-done.1.dv_ref.refs_2_
  53.0 0.5 chain.8
  53.6 0.7 collective-permute-start.2
  54.3 0.6 chain.9
  54.8 1.3 collective-permute-start.3
  56.1 22.0 %collective-permute-done.3.refs_0_.dv_ref = bf16[128,512]{1,0:T(8,128)(2,1)S(1)} collective-permute-done((bf16[128,512]{1,0:T(8,128)(2,1)S(1)}, bf16[128,512]{1,0:T(8,128)(2,1)S(1)}, u32[]{:S(2)}, u32[]{:S(2)}) %collective-permute-start.3) | collective-permute-done | bytes 131104 | tf_op jit(solution)/shard_map/ppermute | solution.py:309
  78.1 0.9 chain.10
  79.0 1.3 collective-permute-start.10
  80.3 0.0 collective-permute-done.6.refs_6_.refs_3_
  80.3 0.0 collective-permute-done.4.refs_4_.refs_1_
  80.4 2.7 %changes.2 = (bf16[32,4096]{1,0:T(8,128)(2,1)S(1)}, bf16[32,4096]{1,0:T(8,128)(2,1)S(1)}, bf16[32,4096]{1,0:T(8,128)(2,1)S(1)}, bf16[32,4096]{1,0:T(8,128)(2,1)S(1)}, bf16[128,512]{1,0:T(8,128)(2,1)S(1)}) custom-call(s32[3]{0:T(128)S(1)} %pad_add_fusion.where, bf16[4096,512]{1,0:T(8,128)(2,1)S(1)} %get-tuple-element.24.w_ref, ...), custom_call_target="tpu_custom_call" | custom-call | tf_op jit(solution)/shard_map/changes/pallas_call | solution.py:28
  83.1 0.0 collective-permute-done.10.dv_ref.refs_3_
  83.1 0.6 chain.11
  83.6 0.7 collective-permute-start.11
  84.3 1.5 collective-permute-start.7
  85.8 7.6 %collective-permute-start.8 = (bf16[32,4096]{1,0:T(8,128)(2,1)S(1)}, bf16[32,4096]{1,0:T(8,128)(2,1)S(1)}, u32[]{:S(2)}, u32[]{:S(2)}) collective-permute-start(bf16[32,4096]{1,0:T(8,128)(2,1)S(1)} %get-tuple-element.32), channel_id=1, source_target_pairs={{0,128},{64,192},{128,0},{192,64},{1,129},{65,193},{129,1},{193,65... | collective-permute-start | bytes 786440 | tf_op jit(solution)/shard_map/ppermute | solution.py:236
  93.4 0.2 collective-permute-start.9
  93.6 0.0 collective-permute-done.11.dv_ref.refs_2_
  93.6 0.5 chain.12
  94.2 0.7 collective-permute-start.12
  94.9 5.7 %collective-permute-done.7.refs_0_.refs_1_ = bf16[32,4096]{1,0:T(8,128)(2,1)S(1)} collective-permute-done((bf16[32,4096]{1,0:T(8,128)(2,1)S(1)}, bf16[32,4096]{1,0:T(8,128)(2,1)S(1)}, u32[]{:S(2)}, u32[]{:S(2)}) %collective-permute-start.7) | collective-permute-done | bytes 262176 | tf_op jit(solution)/shard_map/ppermute | solution.py:236
  100.6 9.7 %collective-permute-done.8.refs_1_.refs_2_ = bf16[32,4096]{1,0:T(8,128)(2,1)S(1)} collective-permute-done((bf16[32,4096]{1,0:T(8,128)(2,1)S(1)}, bf16[32,4096]{1,0:T(8,128)(2,1)S(1)}, u32[]{:S(2)}, u32[]{:S(2)}) %collective-permute-start.8) | collective-permute-done | bytes 262176 | tf_op jit(solution)/shard_map/ppermute | solution.py:236
  110.3 6.8 %collective-permute-done.9.refs_2_.refs_3_ = bf16[32,4096]{1,0:T(8,128)(2,1)S(1)} collective-permute-done((bf16[32,4096]{1,0:T(8,128)(2,1)S(1)}, bf16[32,4096]{1,0:T(8,128)(2,1)S(1)}, u32[]{:S(2)}, u32[]{:S(2)}) %collective-permute-start.9) | collective-permute-done | bytes 262176 | tf_op jit(solution)/shard_map/ppermute | solution.py:236
  117.1 0.5 chain.13
  117.7 1.5 collective-permute-start.13
  119.1 9.7 %collective-permute-done.13.refs_0_ = bf16[128,512]{1,0:T(8,128)(2,1)S(1)} collective-permute-done((bf16[128,512]{1,0:T(8,128)(2,1)S(1)}, bf16[128,512]{1,0:T(8,128)(2,1)S(1)}, u32[]{:S(2)}, u32[]{:S(2)}) %collective-permute-start.13) | collective-permute-done | bytes 131104 | tf_op jit(solution)/shard_map/ppermute | solution.py:309
  128.9 2.7 %changes.3 = (bf16[32,4096]{1,0:T(8,128)(2,1)S(1)}, bf16[32,4096]{1,0:T(8,128)(2,1)S(1)}, bf16[32,4096]{1,0:T(8,128)(2,1)S(1)}, bf16[32,4096]{1,0:T(8,128)(2,1)S(1)}, bf16[256,512]{1,0:T(8,128)(2,1)S(1)}) custom-call(s32[3]{0:T(128)S(1)} %pad_add_fusion.where, bf16[4096,512]{1,0:T(8,128)(2,1)S(1)} %get-tuple-element.24.w_ref, ...), custom_call_target="tpu_custom_call" | custom-call | tf_op jit(solution)/shard_map/changes/pallas_call | solution.py:28
  131.6 0.1 collective-permute-start.14
  131.7 0.1 collective-permute-start.15
  131.8 3.5 %collective-permute-start.16 = (bf16[32,4096]{1,0:T(8,128)(2,1)S(1)}, bf16[32,4096]{1,0:T(8,128)(2,1)S(1)}, u32[]{:S(2)}, u32[]{:S(2)}) collective-permute-start(bf16[32,4096]{1,0:T(8,128)(2,1)S(1)} %get-tuple-element.38), channel_id=1, source_target_pairs={{0,192},{64,0},{128,64},{192,128},{1,193},{65,1},{129,65},{193,129... | collective-permute-start | bytes 786440 | tf_op jit(solution)/shard_map/ppermute | solution.py:236
  135.2 2.8 %collective-permute-start.21 = (bf16[256,512]{1,0:T(8,128)(2,1)S(1)}, bf16[256,512]{1,0:T(8,128)(2,1)S(1)}, u32[]{:S(2)}, u32[]{:S(2)}) collective-permute-start(bf16[256,512]{1,0:T(8,128)(2,1)S(1)} %get-tuple-element.43.refs_4_), channel_id=1, source_target_pairs={{0,16},{8,24},{16,0},{24,8},{1,17},{9,25},{17,1},{25,9},{2,18},{10... | collective-permute-start | bytes 786440 | tf_op jit(solution)/shard_map/ppermute | solution.py:236
  138.1 5.6 %collective-permute-done.14.refs_5_ = bf16[32,4096]{1,0:T(8,128)(2,1)S(1)} collective-permute-done((bf16[32,4096]{1,0:T(8,128)(2,1)S(1)}, bf16[32,4096]{1,0:T(8,128)(2,1)S(1)}, u32[]{:S(2)}, u32[]{:S(2)}) %collective-permute-start.14) | collective-permute-done | bytes 262176 | tf_op jit(solution)/shard_map/ppermute | solution.py:236
  143.7 0.0 collective-permute-start.20
  143.7 0.0 collective-permute-done.15.refs_6_
  143.7 12.0 %collective-permute-done.16.refs_7_ = bf16[32,4096]{1,0:T(8,128)(2,1)S(1)} collective-permute-done((bf16[32,4096]{1,0:T(8,128)(2,1)S(1)}, bf16[32,4096]{1,0:T(8,128)(2,1)S(1)}, u32[]{:S(2)}, u32[]{:S(2)}) %collective-permute-start.16) | collective-permute-done | bytes 262176 | tf_op jit(solution)/shard_map/ppermute | solution.py:236
  155.7 0.9 totals.1
  156.6 0.0 copy-start.4
  156.6 0.0 collective-permute-done.21.refs_6_
  156.7 0.0 collective-permute-done.20.refs_5_
  156.7 3.3 %part.1 = bf16[1024,512]{1,0:T(8,128)(2,1)} custom-call(bf16[2,128,1024]{2,1,0:T(8,128)(2,1)S(1)} %get-tuple-element.46.refs_0_, bf16[2,128,1024]{2,1,0:T(8,128)(2,1)S(1)} %collective-permute-done.4.refs_4_.refs_1_, bf16[2,128,1024]{2,1,0:T(8,128)(2,1)S(1)} %collective-permute-done.5.refs_5_.refs_2_, ...), custom_call_target="tpu_custom_call" | custom-call | tf_op jit(solution)/shard_map/part/pallas_call | solution.py:28
  160.0 9.9 %all-to-all-start.1 = ((bf16[16,64,512]{2,1,0:T(8,128)(2,1)}), bf16[16,64,512]{2,1,0:T(8,128)(2,1)S(1)}, u32[]{:S(2)}, u32[]{:S(2)}) async-start(bf16[16,64,512]{2,1,0:T(8,128)(2,1)} %bitcast.13), calls=%async_computation.1 | async-start | bytes 2097152 | tf_op jit(solution)/shard_map/all_to_all | solution.py:343
  169.9 0.1 collective-permute-start.17
  170.0 1.4 collective-permute-start.18
  171.4 2.2 collective-permute-start.19
  173.6 30.7 %collective-permute-done.17.refs_1_ = bf16[2,32,4096]{2,1,0:T(8,128)(2,1)S(1)} collective-permute-done((bf16[2,32,4096]{2,1,0:T(8,128)(2,1)S(1)}, bf16[2,32,4096]{2,1,0:T(8,128)(2,1)S(1)}, u32[]{:S(2)}, u32[]{:S(2)}) %collective-permute-start.17) | collective-permute-done | bytes 524320 | tf_op jit(solution)/shard_map/ppermute | solution.py:236
  204.4 22.3 %collective-permute-done.18.refs_2_ = bf16[2,32,4096]{2,1,0:T(8,128)(2,1)S(1)} collective-permute-done((bf16[2,32,4096]{2,1,0:T(8,128)(2,1)S(1)}, bf16[2,32,4096]{2,1,0:T(8,128)(2,1)S(1)}, u32[]{:S(2)}, u32[]{:S(2)}) %collective-permute-start.18) | collective-permute-done | bytes 524320 | tf_op jit(solution)/shard_map/ppermute | solution.py:236
  226.7 0.0 collective-permute-done.19.refs_3_
  226.7 1.9 collect_rows.1
  228.6 0.8 convert_reduce_fusion
  (17 shorter events, 0.0 us)
Async XLA Ops:
  1.7 38.0 %copy-start.3 = (f32[2,1,4096]{2,1,0:T(1,128)S(1)}, f32[2,1,4096]{2,1,0:T(1,128)}, u32[]{:S(2)}) copy-start(f32[2,1,4096]{2,1,0:T(1,128)} %g_ref.5) | copy-start | bytes 98308
  1.7 40.0 %copy-start.2 = (bf16[128,4096]{1,0:T(8,128)(2,1)S(1)}, bf16[128,4096]{1,0:T(8,128)(2,1)}, u32[]{:S(2)}) copy-start(bf16[128,4096]{1,0:T(8,128)(2,1)} %start_ref.1) | copy-start | bytes 3145732
  37.2 4.6 %copy-start = (bf16[2,1,128,4096]{3,2,1,0:T(8,128)(2,1)S(1)}, bf16[2,1,128,4096]{3,2,1,0:T(8,128)(2,1)}, u32[]{:S(2)}) copy-start(bf16[2,1,128,4096]{3,2,1,0:T(8,128)(2,1)} %param.4) | copy-start | bytes 6291460
  37.2 6.7 %collective-permute-start = (bf16[32,64,512]{2,1,0:T(8,128)(2,1)}, bf16[32,64,512]{2,1,0:T(8,128)(2,1)}, u32[]{:S(2)}, u32[]{:S(2)}) collective-permute-start(bf16[32,64,512]{2,1,0:T(8,128)(2,1)} %all_to_all.10.mine_ref), channel_id=1, source_target_pairs={{0,1},{1,0},{2,3},{3,2},{4,5},{5,4},{6,7},{7,6},{8,9},{9,8},{10,11... | collective-permute-start | bytes 6291464 | tf_op jit(solution)/shard_map/ppermute | solution.py:251
  41.7 2.3 copy-start.1
  49.3 3.7 %collective-permute-start.1 = (bf16[128,512]{1,0:T(8,128)(2,1)S(1)}, bf16[128,512]{1,0:T(8,128)(2,1)S(1)}, u32[]{:S(2)}, u32[]{:S(2)}) collective-permute-start(bf16[128,512]{1,0:T(8,128)(2,1)S(1)} %chain.7.token_ref), channel_id=1, source_target_pairs={{192,128},{193,129},{194,130},{195,131},{196,132},{197,133},{198,1... | collective-permute-start | bytes 393224 | tf_op jit(solution)/shard_map/ppermute | solution.py:309
  50.2 30.1 %collective-permute-start.6 = (bf16[2,128,1024]{2,1,0:T(8,128)(2,1)S(1)}, bf16[2,128,1024]{2,1,0:T(8,128)(2,1)S(1)}, u32[]{:S(2)}, u32[]{:S(2)}) collective-permute-start(bf16[2,128,1024]{2,1,0:T(8,128)(2,1)S(1)} %get-tuple-element.47), channel_id=1, source_target_pairs={{0,24},{8,0},{16,8},{24,16},{1,25},{9,1},{17,9},{25,17},{2,26},{10... | collective-permute-start | bytes 1572872 | tf_op jit(solution)/shard_map/ppermute | solution.py:236
  52.2 28.1 %collective-permute-start.5 = (bf16[2,128,1024]{2,1,0:T(8,128)(2,1)S(1)}, bf16[2,128,1024]{2,1,0:T(8,128)(2,1)S(1)}, u32[]{:S(2)}, u32[]{:S(2)}) collective-permute-start(bf16[2,128,1024]{2,1,0:T(8,128)(2,1)S(1)} %get-tuple-element.48), channel_id=1, source_target_pairs={{0,16},{8,24},{16,0},{24,8},{1,17},{9,25},{17,1},{25,9},{2,18},{10... | collective-permute-start | bytes 1572872 | tf_op jit(solution)/shard_map/ppermute | solution.py:236
  52.7 27.6 %collective-permute-start.4 = (bf16[2,128,1024]{2,1,0:T(8,128)(2,1)S(1)}, bf16[2,128,1024]{2,1,0:T(8,128)(2,1)S(1)}, u32[]{:S(2)}, u32[]{:S(2)}) collective-permute-start(bf16[2,128,1024]{2,1,0:T(8,128)(2,1)S(1)} %get-tuple-element.49), channel_id=1, source_target_pairs={{0,8},{8,16},{16,24},{24,0},{1,9},{9,17},{17,25},{25,1},{2,10},{10... | collective-permute-start | bytes 1572872 | tf_op jit(solution)/shard_map/ppermute | solution.py:236
  53.6 0.7 collective-permute-start.2
  54.8 23.3 %collective-permute-start.3 = (bf16[128,512]{1,0:T(8,128)(2,1)S(1)}, bf16[128,512]{1,0:T(8,128)(2,1)S(1)}, u32[]{:S(2)}, u32[]{:S(2)}) collective-permute-start(bf16[128,512]{1,0:T(8,128)(2,1)S(1)} %chain.9), channel_id=1, source_target_pairs={{64,0},{65,1},{66,2},{67,3},{68,4},{69,5},{70,6},{71,7},{72,8},{73... | collective-permute-start | bytes 393224 | tf_op jit(solution)/shard_map/ppermute | solution.py:309
  79.0 4.0 %collective-permute-start.10 = (bf16[128,512]{1,0:T(8,128)(2,1)S(1)}, bf16[128,512]{1,0:T(8,128)(2,1)S(1)}, u32[]{:S(2)}, u32[]{:S(2)}) collective-permute-start(bf16[128,512]{1,0:T(8,128)(2,1)S(1)} %chain.10), channel_id=1, source_target_pairs={{0,192},{1,193},{2,194},{3,195},{4,196},{5,197},{6,198},{7,199},{8... | collective-permute-start | bytes 393224 | tf_op jit(solution)/shard_map/ppermute | solution.py:309
  83.6 10.0 %collective-permute-start.11 = (bf16[128,512]{1,0:T(8,128)(2,1)S(1)}, bf16[128,512]{1,0:T(8,128)(2,1)S(1)}, u32[]{:S(2)}, u32[]{:S(2)}) collective-permute-start(bf16[128,512]{1,0:T(8,128)(2,1)S(1)} %chain.11), channel_id=1, source_target_pairs={{192,128},{193,129},{194,130},{195,131},{196,132},{197,133},{198,1... | collective-permute-start | bytes 393224 | tf_op jit(solution)/shard_map/ppermute | solution.py:309
  84.3 16.3 %collective-permute-start.7 = (bf16[32,4096]{1,0:T(8,128)(2,1)S(1)}, bf16[32,4096]{1,0:T(8,128)(2,1)S(1)}, u32[]{:S(2)}, u32[]{:S(2)}) collective-permute-start(bf16[32,4096]{1,0:T(8,128)(2,1)S(1)} %get-tuple-element.31), channel_id=1, source_target_pairs={{0,64},{64,128},{128,192},{192,0},{1,65},{65,129},{129,193},{193,1... | collective-permute-start | bytes 786440 | tf_op jit(solution)/shard_map/ppermute | solution.py:236
  85.8 24.5 %collective-permute-start.8 = (bf16[32,4096]{1,0:T(8,128)(2,1)S(1)}, bf16[32,4096]{1,0:T(8,128)(2,1)S(1)}, u32[]{:S(2)}, u32[]{:S(2)}) collective-permute-start(bf16[32,4096]{1,0:T(8,128)(2,1)S(1)} %get-tuple-element.32), channel_id=1, source_target_pairs={{0,128},{64,192},{128,0},{192,64},{1,129},{65,193},{129,1},{193,65... | collective-permute-start | bytes 786440 | tf_op jit(solution)/shard_map/ppermute | solution.py:236
  93.4 23.7 %collective-permute-start.9 = (bf16[32,4096]{1,0:T(8,128)(2,1)S(1)}, bf16[32,4096]{1,0:T(8,128)(2,1)S(1)}, u32[]{:S(2)}, u32[]{:S(2)}) collective-permute-start(bf16[32,4096]{1,0:T(8,128)(2,1)S(1)} %get-tuple-element.33), channel_id=1, source_target_pairs={{0,192},{64,0},{128,64},{192,128},{1,193},{65,1},{129,65},{193,129... | collective-permute-start | bytes 786440 | tf_op jit(solution)/shard_map/ppermute | solution.py:236
  94.2 0.7 collective-permute-start.12
  117.7 11.2 %collective-permute-start.13 = (bf16[128,512]{1,0:T(8,128)(2,1)S(1)}, bf16[128,512]{1,0:T(8,128)(2,1)S(1)}, u32[]{:S(2)}, u32[]{:S(2)}) collective-permute-start(bf16[128,512]{1,0:T(8,128)(2,1)S(1)} %chain.13), channel_id=1, source_target_pairs={{64,0},{65,1},{66,2},{67,3},{68,4},{69,5},{70,6},{71,7},{72,8},{73... | collective-permute-start | bytes 393224 | tf_op jit(solution)/shard_map/ppermute | solution.py:309
  131.6 12.1 %collective-permute-start.14 = (bf16[32,4096]{1,0:T(8,128)(2,1)S(1)}, bf16[32,4096]{1,0:T(8,128)(2,1)S(1)}, u32[]{:S(2)}, u32[]{:S(2)}) collective-permute-start(bf16[32,4096]{1,0:T(8,128)(2,1)S(1)} %get-tuple-element.36), channel_id=1, source_target_pairs={{0,64},{64,128},{128,192},{192,0},{1,65},{65,129},{129,193},{193,1... | collective-permute-start | bytes 786440 | tf_op jit(solution)/shard_map/ppermute | solution.py:236
  131.7 12.0 %collective-permute-start.15 = (bf16[32,4096]{1,0:T(8,128)(2,1)S(1)}, bf16[32,4096]{1,0:T(8,128)(2,1)S(1)}, u32[]{:S(2)}, u32[]{:S(2)}) collective-permute-start(bf16[32,4096]{1,0:T(8,128)(2,1)S(1)} %get-tuple-element.37), channel_id=1, source_target_pairs={{0,128},{64,192},{128,0},{192,64},{1,129},{65,193},{129,1},{193,65... | collective-permute-start | bytes 786440 | tf_op jit(solution)/shard_map/ppermute | solution.py:236
  131.8 23.9 %collective-permute-start.16 = (bf16[32,4096]{1,0:T(8,128)(2,1)S(1)}, bf16[32,4096]{1,0:T(8,128)(2,1)S(1)}, u32[]{:S(2)}, u32[]{:S(2)}) collective-permute-start(bf16[32,4096]{1,0:T(8,128)(2,1)S(1)} %get-tuple-element.38), channel_id=1, source_target_pairs={{0,192},{64,0},{128,64},{192,128},{1,193},{65,1},{129,65},{193,129... | collective-permute-start | bytes 786440 | tf_op jit(solution)/shard_map/ppermute | solution.py:236
  135.2 21.4 %collective-permute-start.22 = (bf16[256,512]{1,0:T(8,128)(2,1)S(1)}, bf16[256,512]{1,0:T(8,128)(2,1)S(1)}, u32[]{:S(2)}, u32[]{:S(2)}) collective-permute-start(bf16[256,512]{1,0:T(8,128)(2,1)S(1)} %get-tuple-element.43.refs_4_), channel_id=1, source_target_pairs={{0,24},{8,0},{16,8},{24,16},{1,25},{9,1},{17,9},{25,17},{2,26},{10... | collective-permute-start | bytes 786440 | tf_op jit(solution)/shard_map/ppermute | solution.py:236
  135.2 21.4 %collective-permute-start.21 = (bf16[256,512]{1,0:T(8,128)(2,1)S(1)}, bf16[256,512]{1,0:T(8,128)(2,1)S(1)}, u32[]{:S(2)}, u32[]{:S(2)}) collective-permute-start(bf16[256,512]{1,0:T(8,128)(2,1)S(1)} %get-tuple-element.43.refs_4_), channel_id=1, source_target_pairs={{0,16},{8,24},{16,0},{24,8},{1,17},{9,25},{17,1},{25,9},{2,18},{10... | collective-permute-start | bytes 786440 | tf_op jit(solution)/shard_map/ppermute | solution.py:236
  143.7 12.9 %collective-permute-start.20 = (bf16[256,512]{1,0:T(8,128)(2,1)S(1)}, bf16[256,512]{1,0:T(8,128)(2,1)S(1)}, u32[]{:S(2)}, u32[]{:S(2)}) collective-permute-start(bf16[256,512]{1,0:T(8,128)(2,1)S(1)} %get-tuple-element.43.refs_4_), channel_id=1, source_target_pairs={{0,8},{8,16},{16,24},{24,0},{1,9},{9,17},{17,25},{25,1},{2,10},{10... | collective-permute-start | bytes 786440 | tf_op jit(solution)/shard_map/ppermute | solution.py:236
  156.6 3.4 %copy-start.4 = (bf16[2,32,4096]{2,1,0:T(8,128)(2,1)}, bf16[2,32,4096]{2,1,0:T(8,128)(2,1)S(1)}, u32[]{:S(2)}) copy-start(bf16[2,32,4096]{2,1,0:T(8,128)(2,1)S(1)} %get-tuple-element.40) | copy-start | bytes 1572868
  160.0 9.9 %copy-start.5 = (bf16[2,32,4096]{2,1,0:T(8,128)(2,1)S(1)}, bf16[2,32,4096]{2,1,0:T(8,128)(2,1)}, u32[]{:S(2)}) copy-start(bf16[2,32,4096]{2,1,0:T(8,128)(2,1)} %copy-done.4) | copy-start | bytes 1572868
  160.0 68.6 %all-to-all-start.1 = ((bf16[16,64,512]{2,1,0:T(8,128)(2,1)}), bf16[16,64,512]{2,1,0:T(8,128)(2,1)S(1)}, u32[]{:S(2)}, u32[]{:S(2)}) async-start(bf16[16,64,512]{2,1,0:T(8,128)(2,1)} %bitcast.13), calls=%async_computation.1 | async-start | bytes 2097152 | tf_op jit(solution)/shard_map/all_to_all | solution.py:343
  169.9 34.4 %collective-permute-start.17 = (bf16[2,32,4096]{2,1,0:T(8,128)(2,1)S(1)}, bf16[2,32,4096]{2,1,0:T(8,128)(2,1)S(1)}, u32[]{:S(2)}, u32[]{:S(2)}) collective-permute-start(bf16[2,32,4096]{2,1,0:T(8,128)(2,1)S(1)} %copy-done.5), channel_id=1, source_target_pairs={{0,64},{64,128},{128,192},{192,0},{1,65},{65,129},{129,193},{193,1... | collective-permute-start | bytes 1572872 | tf_op jit(solution)/shard_map/ppermute | solution.py:236
  170.0 56.6 %collective-permute-start.18 = (bf16[2,32,4096]{2,1,0:T(8,128)(2,1)S(1)}, bf16[2,32,4096]{2,1,0:T(8,128)(2,1)S(1)}, u32[]{:S(2)}, u32[]{:S(2)}) collective-permute-start(bf16[2,32,4096]{2,1,0:T(8,128)(2,1)S(1)} %get-tuple-element.41), channel_id=1, source_target_pairs={{0,128},{64,192},{128,0},{192,64},{1,129},{65,193},{129,1},{193,65... | collective-permute-start | bytes 1572872 | tf_op jit(solution)/shard_map/ppermute | solution.py:236
  171.4 55.3 %collective-permute-start.19 = (bf16[2,32,4096]{2,1,0:T(8,128)(2,1)S(1)}, bf16[2,32,4096]{2,1,0:T(8,128)(2,1)S(1)}, u32[]{:S(2)}, u32[]{:S(2)}) collective-permute-start(bf16[2,32,4096]{2,1,0:T(8,128)(2,1)S(1)} %get-tuple-element.42), channel_id=1, source_target_pairs={{0,192},{64,0},{128,64},{192,128},{1,193},{65,1},{129,65},{193,129... | collective-permute-start | bytes 1572872 | tf_op jit(solution)/shard_map/ppermute | solution.py:236

commit v5 on v2

v5 whole, which is shorter than its diff:
```python
import functools

import jax
import jax.numpy as jnp
from jax import lax
from jax.experimental import pallas as pl
from jax.experimental.pallas import tpu as pltpu
from jax.sharding import Mesh
from jax.sharding import PartitionSpec as P

HEAD = 128
ROWS = 16
SLACK = 2
FAR = 2
HIDDEN_BY = 11
DP = ("dp_0", "dp_1", "dp_2", "dp_3")
IN_VMEM = pl.BlockSpec(memory_space=pltpu.VMEM)
IN_SMEM = pl.BlockSpec(memory_space=pltpu.SMEM)
ANYWHERE = pl.BlockSpec(memory_space=pl.ANY)
BF16, F32 = jnp.bfloat16, jnp.float32


def copy_for_each(array, axis):
    count = lax.axis_size(axis)
    return lax.all_to_all(
        jnp.broadcast_to(array[None], (count, *array.shape)), axis, 0, 0, tiled=True
    )


def kernel_call(kernel, name, out_shape, specs, operands, scratch=(), out_spec=IN_VMEM, room=8):
    return pl.pallas_call(
        kernel,
        out_shape=out_shape,
        in_specs=specs,
        out_specs=jax.tree.map(lambda _: out_spec, out_shape),
        scratch_shapes=list(scratch),
        compiler_params=pltpu.CompilerParams(vmem_limit_bytes=room * 2**20),
        name=name,
    )(*operands)


def held_until(value, token):
    return pl.pallas_call(
        lambda value_ref, token_ref, out_ref: None,
        out_shape=jax.ShapeDtypeStruct(value.shape, value.dtype),
        in_specs=[ANYWHERE, IN_VMEM],
        out_specs=ANYWHERE,
        input_output_aliases={0: 0},
        compiler_params=pltpu.CompilerParams(vmem_limit_bytes=2**20),
        name="held_until",
    )(value, token)


def norm_kernel(where, x_ref, g_ref, tiles_ref):
    _, tok, width = x_ref.shape
    across, _, _, part = tiles_ref.shape
    near = width // (across * FAR)

    def one(index, carry):
        rows = pl.ds(pl.multiple_of(index * ROWS, ROWS), ROWS)
        for loop in range(2):
            x = x_ref[loop, rows, :].astype(F32)
            rinv = lax.rsqrt(jnp.mean(x * x, axis=-1, keepdims=True) + 1e-05)
            hidden = (x * rinv * g_ref[loop]).astype(BF16)
            for place in range(across):
                for half in range(FAR):
                    at = (half * across + place) * near
                    tiles_ref[
                        lax.rem(place + across - where[1], across),
                        loop,
                        rows,
                        half * near : (half + 1) * near,
                    ] = hidden[:, at : at + near]
        return carry

    lax.fori_loop(0, tok // ROWS, one, 0)


def rows_kernel(where, mine_ref, other_ref, w_ref):
    count, piece, _ = mine_ref.shape
    for index in range(count):
        for ref, core in ((mine_ref, where[2]), (other_ref, 1 - where[2])):
            at = pl.multiple_of((2 * index + core) * piece, piece)
            w_ref[pl.ds(at, piece), :] = ref[index]


def part_kernel(*refs):
    part_ref = refs[-1]
    count = (len(refs) - 1) // 2
    total = None
    for tiles_ref, dv_ref in zip(refs[:count], refs[count:-1], strict=True):
        tok = tiles_ref.shape[1]
        for loop in range(2):
            at = 0 if loop == 0 else tok
            term = lax.dot_general(
                tiles_ref[loop],
                dv_ref[at : at + tok, :],
                (((0,), (0,)), ((), ())),
                preferred_element_type=F32,
            )
            total = term if total is None else total + term
    part_ref[...] = total.astype(BF16)


def task_of(step, section, npipe):
    return step - SLACK * (npipe - 1 - section)


def step_kernel(step, npipe, blocks, where, w_ref, x_ref, g_ref, fresh_ref, in_ref, *refs):
    dx_ref, dv_ref = refs[-2:]
    section = where[0]
    task = task_of(step, section, npipe)

    @pl.when((task >= 0) & (task < 2 * blocks))
    def _():
        later = task < blocks
        loop = jnp.where(later, 1, 0)
        block = jnp.where(later, task, task - blocks)
        row = pl.multiple_of(block * ROWS, ROWS)
        width = dx_ref.shape[1]
        kv_width = dv_ref.shape[1]
        heads = kv_width // HEAD
        group = width // kv_width
        take = later & (section == npipe - 1)
        dy = jnp.where(take, fresh_ref[pl.ds(row, ROWS), :], in_ref[...]).astype(F32)
        x = x_ref[loop, pl.ds(row, ROWS), :].astype(F32)
        sums = []
        for head in range(heads):
            base = head * group * HEAD
            total = dy[:, base : base + HEAD]
            for member in range(1, group):
                at = base + member * HEAD
                total = total + dy[:, at : at + HEAD]
            sums.append(total)
        dv = jnp.concatenate(sums, axis=1).astype(BF16)
        dv_ref[...] = dv
        dh = lax.dot_general(
            dv, w_ref[...], (((1,), (1,)), ((), ())), preferred_element_type=F32
        )
        dhg = dh * g_ref[loop]
        rinv = lax.rsqrt(jnp.mean(x * x, axis=-1, keepdims=True) + 1e-05)
        normed = x * rinv
        along = jnp.mean(dhg * normed, axis=-1, keepdims=True)
        dx_ref[...] = (dy + rinv * (dhg - normed * along)).astype(BF16)


def collect_kernel(npipe, blocks, where, *refs):
    *pieces, out_ref, sems = refs
    section = where[0]

    def each(act):
        for step, piece in enumerate(pieces):
            task = task_of(step, section, npipe)

            @pl.when((task >= 0) & (task < 2 * blocks))
            def _():
                later = task < blocks
                loop = jnp.where(later, 1, 0)
                row = pl.multiple_of((task - jnp.where(later, 0, blocks)) * ROWS, ROWS)
                target = out_ref.at[loop, pl.ds(row, ROWS), :]
                act(pltpu.make_async_copy(piece, target, sems.at[step]))

    each(lambda copy: copy.start())
    each(lambda copy: copy.wait())


def stack_kernel(npipe, blocks, where, *refs):
    *pieces, out_ref = refs
    section = where[0]
    for step, piece in enumerate(pieces):
        task = task_of(step, section, npipe)

        @pl.when((task >= 0) & (task < 2 * blocks))
        def _():
            place = task + jnp.where(task < blocks, blocks, -blocks)
            out_ref[pl.ds(pl.multiple_of(place * ROWS, ROWS), ROWS), :] = piece[...]


def exchanged(pieces, axis):
    count = lax.axis_size(axis)
    moved = [pieces[0]]
    for shift in range(1, count):
        pairs = [(source, (source + shift) % count) for source in range(count)]
        moved.append(lax.ppermute(pieces[shift], axis, pairs))
    return moved


def on_device(saved, grad_out, gain, w_value):
    npipe = lax.axis_size("pipe")
    where = jnp.stack([lax.axis_index(name) for name in ("pipe", "dp_1", "dp_3")]).astype(jnp.int32)
    x = saved[:, 0]
    _, tok, width = x.shape
    kv_width = w_value.shape[2]
    blocks = tok // ROWS
    across = lax.axis_size("dp_1")
    shape = jax.ShapeDtypeStruct

    mine = copy_for_each(w_value[0], DP[:3])
    other = lax.ppermute(mine, DP[3], [(0, 1), (1, 0)])
    tiles = kernel_call(
        norm_kernel,
        "normalize",
        shape((across, 2, tok, width // across), BF16),
        [IN_SMEM] + [IN_VMEM] * 2,
        (where, x, gain),
    )
    w_mat = kernel_call(
        rows_kernel,
        "rows",
        shape((width, kv_width), BF16),
        [IN_SMEM] + [IN_VMEM] * 2,
        (where, mine, other),
    )

    steps = 2 * blocks + SLACK * (npipe - 1)
    sent, gx_parts, gv_parts = {}, [], []
    for step in range(steps):
        incoming = sent.pop(step - SLACK, None)
        if incoming is None:
            incoming = jnp.zeros((ROWS, width), BF16)
        later = tuple(hidden[1:]) if step == HIDDEN_BY else ()
        dx, dv = kernel_call(
            functools.partial(step_kernel, step, npipe, blocks),
            "section_step",
            (shape((ROWS, width), BF16), shape((ROWS, kv_width), BF16)),
            [IN_SMEM] + [IN_VMEM] * (5 + min(step, 1)) + [ANYWHERE] * len(later),
            (where, w_mat, x, gain, grad_out, incoming, *gv_parts[-1:], *later),
        )
        gx_parts.append(dx)
        gv_parts.append(dv)
        pairs = []
        for source in range(npipe):
            task = task_of(step, source, npipe)
            if 0 <= task < (blocks if source == 0 else 2 * blocks):
                pairs.append((source, (source - 1) % npipe))
        if pairs:
            sent[step] = lax.ppermute(dx, "pipe", pairs)
        if step == 4:
            hidden = exchanged(held_until(tiles, dv), "dp_1")

    grad_x = kernel_call(
        functools.partial(collect_kernel, npipe, blocks),
        "collect_rows",
        shape((2, tok, width), BF16),
        [IN_SMEM] + [IN_VMEM] * steps,
        (where, *gx_parts),
        scratch=(pltpu.SemaphoreType.DMA((steps,)),),
        out_spec=ANYWHERE,
    )[:, None]
    dv_all = kernel_call(
        functools.partial(stack_kernel, npipe, blocks),
        "stack",
        shape((2 * tok, kv_width), BF16),
        [IN_SMEM] + [IN_VMEM] * steps,
        (where, *gv_parts),
    )
    spread = exchanged([dv_all] * across, "dp_1")
    part = kernel_call(
        part_kernel,
        "part",
        shape((width // across, kv_width), BF16),
        [IN_VMEM] * (2 * across),
        (*hidden, *spread),
    )
    others = ("dp_0", "dp_2", "dp_3")
    pieces = part.reshape(lax.axis_size(others), -1, kv_width)
    landed = lax.all_to_all(pieces, others, 0, 0, tiled=True)
    grad_w = landed.astype(F32).sum(axis=0)[None]
    return (grad_x, grad_w)


def solution(mesh):
    finer = Mesh(
        mesh.devices.reshape(mesh.shape["pipe"], 2, 4, 4, 2),
        ("pipe", "dp_0", "dp_1", "dp_2", "dp_3"),
    )
    placed = (P(None, "pipe", DP, None), P(DP, None), P(None, "pipe", None), P("pipe", DP, None))
    return jax.shard_map(
        on_device,
        mesh=finer,
        in_specs=placed,
        out_specs=(P(None, "pipe", DP, None), P("pipe", DP, None)),
        check_vma=False,
    )
```

time: 254 us -> 226 us (0.89)
  waiting for transfers between devices: 121 us -> 75.5 us
  blocking collectives: 10.7 us -> 35.2 us
  local copies, waits for them, and re-layouts: 23.2 us -> 1.3 us
  Pallas kernels: 24.7 us -> 43.7 us
  starting transfers between devices: 57.7 us -> 67.1 us
  other arithmetic: 9.5 us -> 2.11 us
  matrix products: 4.56 us -> 0 us
    ppermute x20, waiting for transfers between devices: 84.9 us -> 52.4 us  [on_device(): sent[step] = lax.ppermute(dx, 'pipe', pairs)]
    all_to_all x1, blocking collectives: 10.7 us -> 35.2 us  [copy_for_each(): lax.all_to_all(jnp.broadcast_to(array[None], (count, *array.shape)), axis...]
    all_to_all x5 -> x1, waiting for transfers between devices: 36.2 us -> 13.9 us  [on_device(): landed = lax.all_to_all(pieces, others, 0, 0, tiled=True)]
    all_to_all x5 -> x1, starting transfers between devices: 34.1 us -> 12 us  [on_device(): landed = lax.all_to_all(pieces, others, 0, 0, tiled=True)]
    pallas_call x23 -> x27, Pallas kernels: 24.7 us -> 43.7 us  [kernel_call(): pl.pallas_call(kernel, out_shape=out_shape, in_specs=specs, out_specs=jax...]
    ppermute x20, starting transfers between devices: 23.6 us -> 40 us  [on_device(): sent[step] = lax.ppermute(dx, 'pipe', pairs)]
    ppermute x0 -> x7, starting transfers between devices: none -> 15.1 us  [the longest x6 12.6 us: exchanged(): moved.append(lax.ppermute(pieces[shift], axis, pairs))]
    ppermute x0 -> x7, waiting for transfers between devices: none -> 9.29 us  [the longest x6 5.46 us: exchanged(): moved.append(lax.ppermute(pieces[shift], axis, pairs))]
  transfers between devices with their start and end apart: 25 -> 28, of which waited for: 18 -> 14; matrix products, arithmetic and copies ran while one was open for 8% -> 0% of each run, Pallas kernels for 9% -> 16%
where the time goes in v5:
time: 226 us
  waiting for transfers between devices  75.5 us (33%)
  starting transfers between devices  67.1 us (30%)
  Pallas kernels  43.7 us (19%)
  blocking collectives  35.2 us (16%)
    ppermute x20, waiting for transfers between devices, on_device(): sent[step] = lax.ppermute(dx, 'pipe', pairs)  52.4 us
    pallas_call x27, Pallas kernels, kernel_call(): pl.pallas_call(kernel, out_shape=out_shape, in_specs=specs, out_specs=jax...  43.7 us
    ppermute x20, starting transfers between devices, on_device(): sent[step] = lax.ppermute(dx, 'pipe', pairs)  40 us
    all_to_all x1, blocking collectives, copy_for_each(): lax.all_to_all(jnp.broadcast_to(array[None], (count, *array.shape)), axis...  35.2 us
    all_to_all x1, waiting for transfers between devices, on_device(): landed = lax.all_to_all(pieces, others, 0, 0, tiled=True)  13.9 us
    ppermute x6, starting transfers between devices, exchanged(): moved.append(lax.ppermute(pieces[shift], axis, pairs))  12.6 us
    all_to_all x1, starting transfers between devices, on_device(): landed = lax.all_to_all(pieces, others, 0, 0, tiled=True)  12 us
    ppermute x6, waiting for transfers between devices, exchanged(): moved.append(lax.ppermute(pieces[shift], axis, pairs))  5.46 us
  transfers between devices with their start and end apart: 28, of which 14 were waited for; matrix products, arithmetic and copies ran while one was open for 0% of the time, Pallas kernels for 16%

profile of v5, /device:TPU:1, one launch (start us, length us, event | category | flops | bytes accessed | tf_op | source)
XLA Modules:
  0.0 225.9 jit_solution(10575476659160012671)
XLA Ops:
  0.6 1.1 broadcast_in_dim.14
  1.7 35.2 %all_to_all.10.mine_ref = bf16[32,64,512]{2,1,0:T(8,128)(2,1)S(1)} all-to-all(bf16[32,64,512]{2,1,0:T(8,128)(2,1)S(1)} %broadcast_in_dim.14), channel_id=1, replica_groups=mesh['pipe'=4,'dp_0'=2,'dp_1'=4,'dp_2'=4,'dp_3'=2] {'dp_0','dp_1','dp_2'}, dimensions={0} | all-to-all | bytes 4194304 | tf_op jit(solution)/shard_map/all_to_all | solution.py:25
  36.9 2.5 %collective-permute-start = (bf16[32,64,512]{2,1,0:T(8,128)(2,1)S(1)}, bf16[32,64,512]{2,1,0:T(8,128)(2,1)}, u32[]{:S(2)}, u32[]{:S(2)}) collective-permute-start(bf16[32,64,512]{2,1,0:T(8,128)(2,1)S(1)} %all_to_all.10.mine_ref), channel_id=1, source_target_pairs={{0,1},{1,0},{2,3},{3,2},{4,5},{5,4},{6,7},{7,6},{8,9},{9,8},{10,11... | collective-permute-start | bytes 6291464 | tf_op jit(solution)/shard_map/ppermute | solution.py:199
  39.5 3.8 %collective-permute-done.other_ref = bf16[32,64,512]{2,1,0:T(8,128)(2,1)} collective-permute-done((bf16[32,64,512]{2,1,0:T(8,128)(2,1)S(1)}, bf16[32,64,512]{2,1,0:T(8,128)(2,1)}, u32[]{:S(2)}, u32[]{:S(2)}) %collective-permute-start) | collective-permute-done | bytes 2097184 | tf_op jit(solution)/shard_map/ppermute | solution.py:199
  43.3 1.9 rows.1.w_ref
  45.8 0.7 collective-permute-start.1
  47.1 0.7 collective-permute-start.2
  48.3 0.7 collective-permute-start.3
  49.0 2.0 normalize.1.value_ref
  53.1 0.7 collective-permute-start.11
  53.8 2.5 %collective-permute-start.12 = (bf16[2,128,1024]{2,1,0:T(8,128)(2,1)S(1)}, bf16[2,128,1024]{2,1,0:T(8,128)(2,1)S(1)}, u32[]{:S(2)}, u32[]{:S(2)}) collective-permute-start(bf16[2,128,1024]{2,1,0:T(8,128)(2,1)S(1)} %get-tuple-element.94), channel_id=1, source_target_pairs={{0,16},{8,24},{16,0},{24,8},{1,17},{9,25},{17,1},{25,9},{2,18},{10... | collective-permute-start | bytes 1572872 | tf_op jit(solution)/shard_map/ppermute | solution.py:184
  56.3 0.9 collective-permute-start.13
  57.1 1.3 collective-permute-start.5
  59.0 1.3 collective-permute-start.6
  60.3 28.8 %collective-permute-done.5.in_ref = bf16[16,4096]{1,0:T(8,128)(2,1)S(1)} collective-permute-done((bf16[16,4096]{1,0:T(8,128)(2,1)S(1)}, bf16[16,4096]{1,0:T(8,128)(2,1)S(1)}, u32[]{:S(2)}, u32[]{:S(2)}) %collective-permute-start.5) | collective-permute-done | bytes 131104 | tf_op jit(solution)/shard_map/ppermute | solution.py:237
  89.1 1.9 section_step.28
  90.9 4.6 %collective-permute-start.7 = (bf16[16,4096]{1,0:T(8,128)(2,1)S(1)}, bf16[16,4096]{1,0:T(8,128)(2,1)S(1)}, u32[]{:S(2)}, u32[]{:S(2)}) collective-permute-start(bf16[16,4096]{1,0:T(8,128)(2,1)S(1)} %get-tuple-element.58.refs_6_), channel_id=1, source_target_pairs={{0,192},{64,0},{128,64},{192,128},{1,193},{65,1},{129,65},{193,129... | collective-permute-start | bytes 393224 | tf_op jit(solution)/shard_map/ppermute | solution.py:237
  95.6 1.9 section_step.29
  97.5 4.6 %collective-permute-start.8 = (bf16[16,4096]{1,0:T(8,128)(2,1)S(1)}, bf16[16,4096]{1,0:T(8,128)(2,1)S(1)}, u32[]{:S(2)}, u32[]{:S(2)}) collective-permute-start(bf16[16,4096]{1,0:T(8,128)(2,1)S(1)} %get-tuple-element.60.refs_7_), channel_id=1, source_target_pairs={{0,192},{64,0},{128,64},{192,128},{1,193},{65,1},{129,65},{193,129... | collective-permute-start | bytes 393224 | tf_op jit(solution)/shard_map/ppermute | solution.py:237
  102.1 1.9 section_step.30
  103.9 3.5 %collective-permute-start.9 = (bf16[16,4096]{1,0:T(8,128)(2,1)S(1)}, bf16[16,4096]{1,0:T(8,128)(2,1)S(1)}, u32[]{:S(2)}, u32[]{:S(2)}) collective-permute-start(bf16[16,4096]{1,0:T(8,128)(2,1)S(1)} %get-tuple-element.62.refs_8_), channel_id=1, source_target_pairs={{0,192},{64,0},{128,64},{192,128},{1,193},{65,1},{129,65},{193,129... | collective-permute-start | bytes 393224 | tf_op jit(solution)/shard_map/ppermute | solution.py:237
  107.4 1.9 section_step.31
  109.3 2.2 collective-permute-start.10
  111.5 1.9 section_step.32
  113.3 5.7 %collective-permute-start.14 = (bf16[16,4096]{1,0:T(8,128)(2,1)S(1)}, bf16[16,4096]{1,0:T(8,128)(2,1)S(1)}, u32[]{:S(2)}, u32[]{:S(2)}) collective-permute-start(bf16[16,4096]{1,0:T(8,128)(2,1)S(1)} %get-tuple-element.66.refs_10_), channel_id=1, source_target_pairs={{0,192},{64,0},{128,64},{192,128},{1,193},{65,1},{129,65},{193,129... | collective-permute-start | bytes 393224 | tf_op jit(solution)/shard_map/ppermute | solution.py:237
  119.1 1.9 section_step.33
  121.0 0.7 collective-permute-start.15
  121.6 2.1 collective-permute-done.14.in_ref
  123.7 1.9 section_step.34
  125.6 3.2 %collective-permute-start.16 = (bf16[16,4096]{1,0:T(8,128)(2,1)S(1)}, bf16[16,4096]{1,0:T(8,128)(2,1)S(1)}, u32[]{:S(2)}, u32[]{:S(2)}) collective-permute-start(bf16[16,4096]{1,0:T(8,128)(2,1)S(1)} %get-tuple-element.70.refs_12_), channel_id=1, source_target_pairs={{0,192},{64,0},{128,64},{192,128},{1,193},{65,1},{129,65},{193,129... | collective-permute-start | bytes 393224 | tf_op jit(solution)/shard_map/ppermute | solution.py:237
  128.8 1.9 section_step.35
  130.7 2.7 %collective-permute-start.17 = (bf16[16,4096]{1,0:T(8,128)(2,1)S(1)}, bf16[16,4096]{1,0:T(8,128)(2,1)S(1)}, u32[]{:S(2)}, u32[]{:S(2)}) collective-permute-start(bf16[16,4096]{1,0:T(8,128)(2,1)S(1)} %get-tuple-element.72.refs_13_), channel_id=1, source_target_pairs={{0,192},{64,0},{128,64},{192,128},{1,193},{65,1},{129,65},{193,129... | collective-permute-start | bytes 393224 | tf_op jit(solution)/shard_map/ppermute | solution.py:237
  133.4 1.8 collective-permute-done.16.in_ref
  135.3 1.9 section_step.36
  137.2 1.3 collective-permute-start.18
  138.5 2.9 %collective-permute-done.17.in_ref = bf16[16,4096]{1,0:T(8,128)(2,1)S(1)} collective-permute-done((bf16[16,4096]{1,0:T(8,128)(2,1)S(1)}, bf16[16,4096]{1,0:T(8,128)(2,1)S(1)}, u32[]{:S(2)}, u32[]{:S(2)}) %collective-permute-start.17) | collective-permute-done | bytes 131104 | tf_op jit(solution)/shard_map/ppermute | solution.py:237
  141.3 1.9 section_step.37
  143.2 1.3 collective-permute-start.19
  144.5 2.1 collective-permute-done.18.in_ref
  146.6 1.9 section_step.38
  148.5 1.3 collective-permute-start.20
  149.8 5.8 %collective-permute-done.19.in_ref = bf16[16,4096]{1,0:T(8,128)(2,1)S(1)} collective-permute-done((bf16[16,4096]{1,0:T(8,128)(2,1)S(1)}, bf16[16,4096]{1,0:T(8,128)(2,1)S(1)}, u32[]{:S(2)}, u32[]{:S(2)}) %collective-permute-start.19) | collective-permute-done | bytes 131104 | tf_op jit(solution)/shard_map/ppermute | solution.py:237
  155.5 1.9 section_step.39
  157.4 1.3 collective-permute-start.21
  158.7 1.0 collective-permute-done.20.in_ref
  159.7 1.9 section_step.40
  161.6 1.3 collective-permute-start.22
  162.9 1.8 collective-permute-done.21.in_ref
  164.8 1.9 section_step.41
  166.7 1.3 collective-permute-start.23
  168.0 5.2 %collective-permute-done.22.in_ref = bf16[16,4096]{1,0:T(8,128)(2,1)S(1)} collective-permute-done((bf16[16,4096]{1,0:T(8,128)(2,1)S(1)}, bf16[16,4096]{1,0:T(8,128)(2,1)S(1)}, u32[]{:S(2)}, u32[]{:S(2)}) %collective-permute-start.22) | collective-permute-done | bytes 131104 | tf_op jit(solution)/shard_map/ppermute | solution.py:237
  173.2 1.9 section_step.42
  175.1 0.7 collective-permute-done.23.in_ref
  175.8 2.1 section_step.43
  177.9 0.7 stack.17.refs_4_
  178.6 2.6 %collective-permute-start.24 = (bf16[256,512]{1,0:T(8,128)(2,1)S(1)}, bf16[256,512]{1,0:T(8,128)(2,1)S(1)}, u32[]{:S(2)}, u32[]{:S(2)}) collective-permute-start(bf16[256,512]{1,0:T(8,128)(2,1)S(1)} %stack.17.refs_4_), channel_id=1, source_target_pairs={{0,8},{8,16},{16,24},{24,0},{1,9},{9,17},{17,25},{25,1},{2,10},{10... | collective-permute-start | bytes 786440 | tf_op jit(solution)/shard_map/ppermute | solution.py:184
  181.2 4.0 %collective-permute-start.25 = (bf16[256,512]{1,0:T(8,128)(2,1)S(1)}, bf16[256,512]{1,0:T(8,128)(2,1)S(1)}, u32[]{:S(2)}, u32[]{:S(2)}) collective-permute-start(bf16[256,512]{1,0:T(8,128)(2,1)S(1)} %stack.17.refs_4_), channel_id=1, source_target_pairs={{0,16},{8,24},{16,0},{24,8},{1,17},{9,25},{17,1},{25,9},{2,18},{10... | collective-permute-start | bytes 786440 | tf_op jit(solution)/shard_map/ppermute | solution.py:184
  185.2 2.0 collective-permute-start.26
  187.2 5.4 %collective-permute-done.25.refs_6_ = bf16[256,512]{1,0:T(8,128)(2,1)S(1)} collective-permute-done((bf16[256,512]{1,0:T(8,128)(2,1)S(1)}, bf16[256,512]{1,0:T(8,128)(2,1)S(1)}, u32[]{:S(2)}, u32[]{:S(2)}) %collective-permute-start.25) | collective-permute-done | bytes 262176 | tf_op jit(solution)/shard_map/ppermute | solution.py:184
  192.6 3.3 %part.1 = bf16[1024,512]{1,0:T(8,128)(2,1)} custom-call(bf16[2,128,1024]{2,1,0:T(8,128)(2,1)S(1)} %get-tuple-element.92.refs_0_, bf16[2,128,1024]{2,1,0:T(8,128)(2,1)S(1)} %collective-permute-done.11.refs_1_, bf16[2,128,1024]{2,1,0:T(8,128)(2,1)S(1)} %collective-permute-done.12.refs_2_, bf16[2,128,1024]{2,1,0:T(8,128)(2,1)S(1)} %collective-permute-done.13.refs_3_, ...), custom_call_target="tpu_custom_call" | custom-call | tf_op jit(solution)/shard_map/part/pallas_call | solution.py:31
  196.0 12.0 %all-to-all-start.1 = ((bf16[16,64,512]{2,1,0:T(8,128)(2,1)}), bf16[16,64,512]{2,1,0:T(8,128)(2,1)}, u32[]{:S(2)}, u32[]{:S(2)}) async-start(bf16[16,64,512]{2,1,0:T(8,128)(2,1)} %bitcast.11), calls=%async_computation.1 | async-start | bytes 2097152 | tf_op jit(solution)/shard_map/all_to_all | solution.py:267
  207.9 2.1 collect_rows.1
  210.0 13.9 %all-to-all-done.1 = bf16[16,64,512]{2,1,0:T(8,128)(2,1)} async-done(((bf16[16,64,512]{2,1,0:T(8,128)(2,1)}), bf16[16,64,512]{2,1,0:T(8,128)(2,1)}, u32[]{:S(2)}, u32[]{:S(2)}) %all-to-all-start.1) | async-done | bytes 1048608 | tf_op jit(solution)/shard_map/all_to_all | solution.py:267
  223.9 2.0 convert_reduce_fusion
  (32 shorter events, 4.5 us)
Async XLA Ops:
  36.9 6.4 %collective-permute-start = (bf16[32,64,512]{2,1,0:T(8,128)(2,1)S(1)}, bf16[32,64,512]{2,1,0:T(8,128)(2,1)}, u32[]{:S(2)}, u32[]{:S(2)}) collective-permute-start(bf16[32,64,512]{2,1,0:T(8,128)(2,1)S(1)} %all_to_all.10.mine_ref), channel_id=1, source_target_pairs={{0,1},{1,0},{2,3},{3,2},{4,5},{5,4},{6,7},{7,6},{8,9},{9,8},{10,11... | collective-permute-start | bytes 6291464 | tf_op jit(solution)/shard_map/ppermute | solution.py:199
  39.5 5.7 %copy-start = (bf16[2,1,128,4096]{3,2,1,0:T(8,128)(2,1)S(1)}, bf16[2,1,128,4096]{3,2,1,0:T(8,128)(2,1)}, u32[]{:S(2)}) copy-start(bf16[2,1,128,4096]{3,2,1,0:T(8,128)(2,1)} %param.4) | copy-start | bytes 6291460
  39.5 5.8 %copy-start.1 = (bf16[128,4096]{1,0:T(8,128)(2,1)S(1)}, bf16[128,4096]{1,0:T(8,128)(2,1)}, u32[]{:S(2)}) copy-start(bf16[128,4096]{1,0:T(8,128)(2,1)} %fresh_ref.43) | copy-start | bytes 3145732
  39.5 5.8 %copy-start.2 = (f32[2,1,4096]{2,1,0:T(1,128)S(1)}, f32[2,1,4096]{2,1,0:T(1,128)}, u32[]{:S(2)}) copy-start(f32[2,1,4096]{2,1,0:T(1,128)} %g_ref.45) | copy-start | bytes 98308
  45.8 1.9 collective-permute-start.1
  47.1 4.0 %collective-permute-start.2 = (bf16[16,4096]{1,0:T(8,128)(2,1)S(1)}, bf16[16,4096]{1,0:T(8,128)(2,1)S(1)}, u32[]{:S(2)}, u32[]{:S(2)}) collective-permute-start(bf16[16,4096]{1,0:T(8,128)(2,1)S(1)} %get-tuple-element.48.refs_1_), channel_id=1, source_target_pairs={{192,128},{193,129},{194,130},{195,131},{196,132},{197,133},{198,1... | collective-permute-start | bytes 393224 | tf_op jit(solution)/shard_map/ppermute | solution.py:237
  48.3 4.0 %collective-permute-start.3 = (bf16[16,4096]{1,0:T(8,128)(2,1)S(1)}, bf16[16,4096]{1,0:T(8,128)(2,1)S(1)}, u32[]{:S(2)}, u32[]{:S(2)}) collective-permute-start(bf16[16,4096]{1,0:T(8,128)(2,1)S(1)} %get-tuple-element.50.refs_2_), channel_id=1, source_target_pairs={{128,64},{192,128},{129,65},{193,129},{130,66},{194,130},{131,67},... | collective-permute-start | bytes 393224 | tf_op jit(solution)/shard_map/ppermute | solution.py:237
  51.6 6.8 %collective-permute-start.4 = (bf16[16,4096]{1,0:T(8,128)(2,1)S(1)}, bf16[16,4096]{1,0:T(8,128)(2,1)S(1)}, u32[]{:S(2)}, u32[]{:S(2)}) collective-permute-start(bf16[16,4096]{1,0:T(8,128)(2,1)S(1)} %get-tuple-element.52.refs_3_), channel_id=1, source_target_pairs={{128,64},{192,128},{129,65},{193,129},{130,66},{194,130},{131,67},... | collective-permute-start | bytes 393224 | tf_op jit(solution)/shard_map/ppermute | solution.py:237
  53.1 66.0 %collective-permute-start.11 = (bf16[2,128,1024]{2,1,0:T(8,128)(2,1)S(1)}, bf16[2,128,1024]{2,1,0:T(8,128)(2,1)S(1)}, u32[]{:S(2)}, u32[]{:S(2)}) collective-permute-start(bf16[2,128,1024]{2,1,0:T(8,128)(2,1)S(1)} %get-tuple-element.95), channel_id=1, source_target_pairs={{0,8},{8,16},{16,24},{24,0},{1,9},{9,17},{17,25},{25,1},{2,10},{10... | collective-permute-start | bytes 1572872 | tf_op jit(solution)/shard_map/ppermute | solution.py:184
  53.8 65.3 %collective-permute-start.12 = (bf16[2,128,1024]{2,1,0:T(8,128)(2,1)S(1)}, bf16[2,128,1024]{2,1,0:T(8,128)(2,1)S(1)}, u32[]{:S(2)}, u32[]{:S(2)}) collective-permute-start(bf16[2,128,1024]{2,1,0:T(8,128)(2,1)S(1)} %get-tuple-element.94), channel_id=1, source_target_pairs={{0,16},{8,24},{16,0},{24,8},{1,17},{9,25},{17,1},{25,9},{2,18},{10... | collective-permute-start | bytes 1572872 | tf_op jit(solution)/shard_map/ppermute | solution.py:184
  56.3 62.8 %collective-permute-start.13 = (bf16[2,128,1024]{2,1,0:T(8,128)(2,1)S(1)}, bf16[2,128,1024]{2,1,0:T(8,128)(2,1)S(1)}, u32[]{:S(2)}, u32[]{:S(2)}) collective-permute-start(bf16[2,128,1024]{2,1,0:T(8,128)(2,1)S(1)} %get-tuple-element.93), channel_id=1, source_target_pairs={{0,24},{8,0},{16,8},{24,16},{1,25},{9,1},{17,9},{25,17},{2,26},{10... | collective-permute-start | bytes 1572872 | tf_op jit(solution)/shard_map/ppermute | solution.py:184
  57.1 31.9 %collective-permute-start.5 = (bf16[16,4096]{1,0:T(8,128)(2,1)S(1)}, bf16[16,4096]{1,0:T(8,128)(2,1)S(1)}, u32[]{:S(2)}, u32[]{:S(2)}) collective-permute-start(bf16[16,4096]{1,0:T(8,128)(2,1)S(1)} %get-tuple-element.54.refs_4_), channel_id=1, source_target_pairs={{64,0},{128,64},{192,128},{65,1},{129,65},{193,129},{66,2},{130,66... | collective-permute-start | bytes 393224 | tf_op jit(solution)/shard_map/ppermute | solution.py:237
  59.0 36.6 %collective-permute-start.6 = (bf16[16,4096]{1,0:T(8,128)(2,1)S(1)}, bf16[16,4096]{1,0:T(8,128)(2,1)S(1)}, u32[]{:S(2)}, u32[]{:S(2)}) collective-permute-start(bf16[16,4096]{1,0:T(8,128)(2,1)S(1)} %get-tuple-element.56.refs_5_), channel_id=1, source_target_pairs={{64,0},{128,64},{192,128},{65,1},{129,65},{193,129},{66,2},{130,66... | collective-permute-start | bytes 393224 | tf_op jit(solution)/shard_map/ppermute | solution.py:237
  90.9 11.1 %collective-permute-start.7 = (bf16[16,4096]{1,0:T(8,128)(2,1)S(1)}, bf16[16,4096]{1,0:T(8,128)(2,1)S(1)}, u32[]{:S(2)}, u32[]{:S(2)}) collective-permute-start(bf16[16,4096]{1,0:T(8,128)(2,1)S(1)} %get-tuple-element.58.refs_6_), channel_id=1, source_target_pairs={{0,192},{64,0},{128,64},{192,128},{1,193},{65,1},{129,65},{193,129... | collective-permute-start | bytes 393224 | tf_op jit(solution)/shard_map/ppermute | solution.py:237
  97.5 9.9 %collective-permute-start.8 = (bf16[16,4096]{1,0:T(8,128)(2,1)S(1)}, bf16[16,4096]{1,0:T(8,128)(2,1)S(1)}, u32[]{:S(2)}, u32[]{:S(2)}) collective-permute-start(bf16[16,4096]{1,0:T(8,128)(2,1)S(1)} %get-tuple-element.60.refs_7_), channel_id=1, source_target_pairs={{0,192},{64,0},{128,64},{192,128},{1,193},{65,1},{129,65},{193,129... | collective-permute-start | bytes 393224 | tf_op jit(solution)/shard_map/ppermute | solution.py:237
  103.9 7.5 %collective-permute-start.9 = (bf16[16,4096]{1,0:T(8,128)(2,1)S(1)}, bf16[16,4096]{1,0:T(8,128)(2,1)S(1)}, u32[]{:S(2)}, u32[]{:S(2)}) collective-permute-start(bf16[16,4096]{1,0:T(8,128)(2,1)S(1)} %get-tuple-element.62.refs_8_), channel_id=1, source_target_pairs={{0,192},{64,0},{128,64},{192,128},{1,193},{65,1},{129,65},{193,129... | collective-permute-start | bytes 393224 | tf_op jit(solution)/shard_map/ppermute | solution.py:237
  109.3 9.8 %collective-permute-start.10 = (bf16[16,4096]{1,0:T(8,128)(2,1)S(1)}, bf16[16,4096]{1,0:T(8,128)(2,1)S(1)}, u32[]{:S(2)}, u32[]{:S(2)}) collective-permute-start(bf16[16,4096]{1,0:T(8,128)(2,1)S(1)} %get-tuple-element.64.refs_9_), channel_id=1, source_target_pairs={{0,192},{64,0},{128,64},{192,128},{1,193},{65,1},{129,65},{193,129... | collective-permute-start | bytes 393224 | tf_op jit(solution)/shard_map/ppermute | solution.py:237
  113.3 10.4 %collective-permute-start.14 = (bf16[16,4096]{1,0:T(8,128)(2,1)S(1)}, bf16[16,4096]{1,0:T(8,128)(2,1)S(1)}, u32[]{:S(2)}, u32[]{:S(2)}) collective-permute-start(bf16[16,4096]{1,0:T(8,128)(2,1)S(1)} %get-tuple-element.66.refs_10_), channel_id=1, source_target_pairs={{0,192},{64,0},{128,64},{192,128},{1,193},{65,1},{129,65},{193,129... | collective-permute-start | bytes 393224 | tf_op jit(solution)/shard_map/ppermute | solution.py:237
  121.0 7.8 %collective-permute-start.15 = (bf16[16,4096]{1,0:T(8,128)(2,1)S(1)}, bf16[16,4096]{1,0:T(8,128)(2,1)S(1)}, u32[]{:S(2)}, u32[]{:S(2)}) collective-permute-start(bf16[16,4096]{1,0:T(8,128)(2,1)S(1)} %get-tuple-element.68.refs_11_), channel_id=1, source_target_pairs={{0,192},{64,0},{128,64},{192,128},{1,193},{65,1},{129,65},{193,129... | collective-permute-start | bytes 393224 | tf_op jit(solution)/shard_map/ppermute | solution.py:237
  125.6 9.6 %collective-permute-start.16 = (bf16[16,4096]{1,0:T(8,128)(2,1)S(1)}, bf16[16,4096]{1,0:T(8,128)(2,1)S(1)}, u32[]{:S(2)}, u32[]{:S(2)}) collective-permute-start(bf16[16,4096]{1,0:T(8,128)(2,1)S(1)} %get-tuple-element.70.refs_12_), channel_id=1, source_target_pairs={{0,192},{64,0},{128,64},{192,128},{1,193},{65,1},{129,65},{193,129... | collective-permute-start | bytes 393224 | tf_op jit(solution)/shard_map/ppermute | solution.py:237
  130.7 10.6 %collective-permute-start.17 = (bf16[16,4096]{1,0:T(8,128)(2,1)S(1)}, bf16[16,4096]{1,0:T(8,128)(2,1)S(1)}, u32[]{:S(2)}, u32[]{:S(2)}) collective-permute-start(bf16[16,4096]{1,0:T(8,128)(2,1)S(1)} %get-tuple-element.72.refs_13_), channel_id=1, source_target_pairs={{0,192},{64,0},{128,64},{192,128},{1,193},{65,1},{129,65},{193,129... | collective-permute-start | bytes 393224 | tf_op jit(solution)/shard_map/ppermute | solution.py:237
  137.2 9.4 %collective-permute-start.18 = (bf16[16,4096]{1,0:T(8,128)(2,1)S(1)}, bf16[16,4096]{1,0:T(8,128)(2,1)S(1)}, u32[]{:S(2)}, u32[]{:S(2)}) collective-permute-start(bf16[16,4096]{1,0:T(8,128)(2,1)S(1)} %get-tuple-element.74.refs_14_), channel_id=1, source_target_pairs={{64,0},{128,64},{192,128},{65,1},{129,65},{193,129},{66,2},{130,66... | collective-permute-start | bytes 393224 | tf_op jit(solution)/shard_map/ppermute | solution.py:237
  143.2 12.3 %collective-permute-start.19 = (bf16[16,4096]{1,0:T(8,128)(2,1)S(1)}, bf16[16,4096]{1,0:T(8,128)(2,1)S(1)}, u32[]{:S(2)}, u32[]{:S(2)}) collective-permute-start(bf16[16,4096]{1,0:T(8,128)(2,1)S(1)} %get-tuple-element.76.refs_15_), channel_id=1, source_target_pairs={{64,0},{128,64},{192,128},{65,1},{129,65},{193,129},{66,2},{130,66... | collective-permute-start | bytes 393224 | tf_op jit(solution)/shard_map/ppermute | solution.py:237
  148.5 11.3 %collective-permute-start.20 = (bf16[16,4096]{1,0:T(8,128)(2,1)S(1)}, bf16[16,4096]{1,0:T(8,128)(2,1)S(1)}, u32[]{:S(2)}, u32[]{:S(2)}) collective-permute-start(bf16[16,4096]{1,0:T(8,128)(2,1)S(1)} %get-tuple-element.78.refs_16_), channel_id=1, source_target_pairs={{64,0},{128,64},{65,1},{129,65},{66,2},{130,66},{67,3},{131,67},{6... | collective-permute-start | bytes 393224 | tf_op jit(solution)/shard_map/ppermute | solution.py:237
  157.4 7.4 %collective-permute-start.21 = (bf16[16,4096]{1,0:T(8,128)(2,1)S(1)}, bf16[16,4096]{1,0:T(8,128)(2,1)S(1)}, u32[]{:S(2)}, u32[]{:S(2)}) collective-permute-start(bf16[16,4096]{1,0:T(8,128)(2,1)S(1)} %get-tuple-element.80.refs_17_), channel_id=1, source_target_pairs={{64,0},{128,64},{65,1},{129,65},{66,2},{130,66},{67,3},{131,67},{6... | collective-permute-start | bytes 393224 | tf_op jit(solution)/shard_map/ppermute | solution.py:237
  161.6 11.5 %collective-permute-start.22 = (bf16[16,4096]{1,0:T(8,128)(2,1)S(1)}, bf16[16,4096]{1,0:T(8,128)(2,1)S(1)}, u32[]{:S(2)}, u32[]{:S(2)}) collective-permute-start(bf16[16,4096]{1,0:T(8,128)(2,1)S(1)} %get-tuple-element.82.refs_18_), channel_id=1, source_target_pairs={{64,0},{65,1},{66,2},{67,3},{68,4},{69,5},{70,6},{71,7},{72,8},{73... | collective-permute-start | bytes 393224 | tf_op jit(solution)/shard_map/ppermute | solution.py:237
  166.7 9.1 %collective-permute-start.23 = (bf16[16,4096]{1,0:T(8,128)(2,1)S(1)}, bf16[16,4096]{1,0:T(8,128)(2,1)S(1)}, u32[]{:S(2)}, u32[]{:S(2)}) collective-permute-start(bf16[16,4096]{1,0:T(8,128)(2,1)S(1)} %get-tuple-element.84.refs_19_), channel_id=1, source_target_pairs={{64,0},{65,1},{66,2},{67,3},{68,4},{69,5},{70,6},{71,7},{72,8},{73... | collective-permute-start | bytes 393224 | tf_op jit(solution)/shard_map/ppermute | solution.py:237
  178.6 8.6 %collective-permute-start.24 = (bf16[256,512]{1,0:T(8,128)(2,1)S(1)}, bf16[256,512]{1,0:T(8,128)(2,1)S(1)}, u32[]{:S(2)}, u32[]{:S(2)}) collective-permute-start(bf16[256,512]{1,0:T(8,128)(2,1)S(1)} %stack.17.refs_4_), channel_id=1, source_target_pairs={{0,8},{8,16},{16,24},{24,0},{1,9},{9,17},{17,25},{25,1},{2,10},{10... | collective-permute-start | bytes 786440 | tf_op jit(solution)/shard_map/ppermute | solution.py:184
  181.2 11.5 %collective-permute-start.25 = (bf16[256,512]{1,0:T(8,128)(2,1)S(1)}, bf16[256,512]{1,0:T(8,128)(2,1)S(1)}, u32[]{:S(2)}, u32[]{:S(2)}) collective-permute-start(bf16[256,512]{1,0:T(8,128)(2,1)S(1)} %stack.17.refs_4_), channel_id=1, source_target_pairs={{0,16},{8,24},{16,0},{24,8},{1,17},{9,25},{17,1},{25,9},{2,18},{10... | collective-permute-start | bytes 786440 | tf_op jit(solution)/shard_map/ppermute | solution.py:184
  185.2 7.4 %collective-permute-start.26 = (bf16[256,512]{1,0:T(8,128)(2,1)S(1)}, bf16[256,512]{1,0:T(8,128)(2,1)S(1)}, u32[]{:S(2)}, u32[]{:S(2)}) collective-permute-start(bf16[256,512]{1,0:T(8,128)(2,1)S(1)} %stack.17.refs_4_), channel_id=1, source_target_pairs={{0,24},{8,0},{16,8},{24,16},{1,25},{9,1},{17,9},{25,17},{2,26},{10... | collective-permute-start | bytes 786440 | tf_op jit(solution)/shard_map/ppermute | solution.py:184
  196.0 27.9 %all-to-all-start.1 = ((bf16[16,64,512]{2,1,0:T(8,128)(2,1)}), bf16[16,64,512]{2,1,0:T(8,128)(2,1)}, u32[]{:S(2)}, u32[]{:S(2)}) async-start(bf16[16,64,512]{2,1,0:T(8,128)(2,1)} %bitcast.11), calls=%async_computation.1 | async-start | bytes 2097152 | tf_op jit(solution)/shard_map/all_to_all | solution.py:267

commit v6 on v5

--- a/solution.py
+++ b/solution.py
@@ -12,7 +12,9 @@
 ROWS = 16
 SLACK = 2
 FAR = 2
-HIDDEN_BY = 11
+HIDDEN_AT = 7
+HIDDEN_BY = 12
+PART_AT = 20
 DP = ("dp_0", "dp_1", "dp_2", "dp_3")
 IN_VMEM = pl.BlockSpec(memory_space=pltpu.VMEM)
 IN_SMEM = pl.BlockSpec(memory_space=pltpu.SMEM)
@@ -49,6 +51,19 @@
         compiler_params=pltpu.CompilerParams(vmem_limit_bytes=2**20),
         name="held_until",
     )(value, token)
+
+
+def folded(values, kv_width):
+    group = values.shape[1] // kv_width
+    sums = []
+    for head in range(kv_width // HEAD):
+        base = head * group * HEAD
+        total = values[:, base : base + HEAD]
+        for member in range(1, group):
+            at = base + member * HEAD
+            total = total + values[:, at : at + HEAD]
+        sums.append(total)
+    return jnp.concatenate(sums, axis=1)
 
 
 def norm_kernel(where, x_ref, g_ref, tiles_ref):
@@ -86,9 +101,9 @@
 
 def part_kernel(*refs):
     part_ref = refs[-1]
-    count = (len(refs) - 1) // 2
+    count = (len(refs) - 4) // 2
     total = None
-    for tiles_ref, dv_ref in zip(refs[:count], refs[count:-1], strict=True):
+    for tiles_ref, dv_ref in zip(refs[:count], refs[count:-4], strict=True):
         tok = tiles_ref.shape[1]
         for loop in range(2):
             at = 0 if loop == 0 else tok
@@ -106,42 +121,46 @@
     return step - SLACK * (npipe - 1 - section)
 
 
-def step_kernel(step, npipe, blocks, where, w_ref, x_ref, g_ref, fresh_ref, in_ref, *refs):
-    dx_ref, dv_ref = refs[-2:]
-    section = where[0]
-    task = task_of(step, section, npipe)
-
-    @pl.when((task >= 0) & (task < 2 * blocks))
+def change_kernel(owner, loop, first, where, w_ref, x_ref, g_ref, from_ref, *refs):
+    *outs, dh_ref = refs
+    change_ref, next_ref = outs[-3:-1] if first else outs[-2:]
+    dv_ref = outs[-1] if first else from_ref
+
+    @pl.when(where[0] == owner)
     def _():
-        later = task < blocks
-        loop = jnp.where(later, 1, 0)
-        block = jnp.where(later, task, task - blocks)
-        row = pl.multiple_of(block * ROWS, ROWS)
-        width = dx_ref.shape[1]
-        kv_width = dv_ref.shape[1]
-        heads = kv_width // HEAD
-        group = width // kv_width
-        take = later & (section == npipe - 1)
-        dy = jnp.where(take, fresh_ref[pl.ds(row, ROWS), :], in_ref[...]).astype(F32)
-        x = x_ref[loop, pl.ds(row, ROWS), :].astype(F32)
-        sums = []
-        for head in range(heads):
-            base = head * group * HEAD
-            total = dy[:, base : base + HEAD]
-            for member in range(1, group):
-                at = base + member * HEAD
-                total = total + dy[:, at : at + HEAD]
-            sums.append(total)
-        dv = jnp.concatenate(sums, axis=1).astype(BF16)
-        dv_ref[...] = dv
-        dh = lax.dot_general(
-            dv, w_ref[...], (((1,), (1,)), ((), ())), preferred_element_type=F32
+        tok, kv_width = next_ref.shape
+        if first:
+            for at in range(0, tok, ROWS):
+                rows = slice(at, at + ROWS)
+                dv_ref[rows, :] = folded(from_ref[rows, :].astype(F32), kv_width).astype(BF16)
+        dh_ref[...] = lax.dot_general(
+            dv_ref[...], w_ref[...], (((1,), (1,)), ((), ())), preferred_element_type=F32
         )
-        dhg = dh * g_ref[loop]
-        rinv = lax.rsqrt(jnp.mean(x * x, axis=-1, keepdims=True) + 1e-05)
-        normed = x * rinv
-        along = jnp.mean(dhg * normed, axis=-1, keepdims=True)
-        dx_ref[...] = (dy + rinv * (dhg - normed * along)).astype(BF16)
+        for at in range(0, tok, ROWS):
+            rows = slice(at, at + ROWS)
+            x = x_ref[loop, rows, :].astype(F32)
+            dhg = dh_ref[rows, :] * g_ref[loop]
+            rinv = lax.rsqrt(jnp.mean(x * x, axis=-1, keepdims=True) + 1e-05)
+            normed = x * rinv
+            along = jnp.mean(dhg * normed, axis=-1, keepdims=True)
+            change = rinv * (dhg - normed * along)
+            change_ref[rows, :] = change.astype(BF16)
+            next_ref[rows, :] = (dv_ref[rows, :].astype(F32) + folded(change, kv_width)).astype(BF16)
+
+
+def step_kernel(tasks, blocks, where, fresh_ref, in_ref, *refs):
+    dx_ref = refs[-1]
+    for place, task in enumerate(tasks):
+        if task is None:
+            continue
+
+        @pl.when(where[0] == place)
+        def _():
+            at = task % blocks * ROWS
+            rows = slice(at, at + ROWS)
+            fresh = place == len(tasks) - 1 and task < blocks
+            dy = fresh_ref[rows, :] if fresh else in_ref[...]
+            dx_ref[...] = (dy.astype(F32) + refs[place][rows, :].astype(F32)).astype(BF16)
 
 
 def collect_kernel(npipe, blocks, where, *refs):
@@ -164,16 +183,15 @@
     each(lambda copy: copy.wait())
 
 
-def stack_kernel(npipe, blocks, where, *refs):
-    *pieces, out_ref = refs
-    section = where[0]
-    for step, piece in enumerate(pieces):
-        task = task_of(step, section, npipe)
-
-        @pl.when((task >= 0) & (task < 2 * blocks))
+def stack_kernel(npipe, where, *refs):
+    out_ref = refs[-1]
+    tok = refs[0].shape[0]
+    for place in range(npipe):
+
+        @pl.when(where[0] == place)
         def _():
-            place = task + jnp.where(task < blocks, blocks, -blocks)
-            out_ref[pl.ds(pl.multiple_of(place * ROWS, ROWS), ROWS), :] = piece[...]
+            out_ref[tok:, :] = refs[npipe - 1 - place][...]
+            out_ref[:tok, :] = refs[2 * npipe - 1 - place][...]
 
 
 def exchanged(pieces, axis):
@@ -213,30 +231,75 @@
     )
 
     steps = 2 * blocks + SLACK * (npipe - 1)
-    sent, gx_parts, gv_parts = {}, [], []
+    sent, gx_parts, arrived, changes = {}, [], [], []
+    turn = []
     for step in range(steps):
+        hop, odd = divmod(step, SLACK)
+        if not odd and hop < 2 * npipe:
+            owner, loop, first = npipe - 1 - hop % npipe, 1 - hop // npipe, hop == 0
+            outs = (shape((tok, width), BF16), shape((tok, kv_width), BF16))
+            source = grad_out if first else arrived[hop]
+            out = kernel_call(
+                functools.partial(change_kernel, owner, loop, first),
+                "changes",
+                outs + outs[1:] * first,
+                [IN_SMEM] + [IN_VMEM] * (4 + len(turn)),
+                (where, w_mat, x, gain, source, *turn),
+                scratch=(pltpu.VMEM((tok, width), F32),),
+            )
+            changes.append(out[0])
+            turn = [out[1]]
+            if first:
+                arrived.append(out[2])
+            if hop < 2 * npipe - 1:
+                arrived.append(lax.ppermute(out[1], "pipe", [(owner, (owner - 1) % npipe)]))
+            else:
+                dv_all = kernel_call(
+                    functools.partial(stack_kernel, npipe),
+                    "stack",
+                    shape((2 * tok, kv_width), BF16),
+                    [IN_SMEM] + [IN_VMEM] * (2 * npipe),
+                    (where, *arrived),
+                )
+                spread = exchanged([dv_all] * across, "dp_1")
         incoming = sent.pop(step - SLACK, None)
         if incoming is None:
-            incoming = jnp.zeros((ROWS, width), BF16)
-        later = tuple(hidden[1:]) if step == HIDDEN_BY else ()
-        dx, dv = kernel_call(
-            functools.partial(step_kernel, step, npipe, blocks),
+            incoming = grad_out[:ROWS]
+        later = ()
+        if step == PART_AT - 1:
+            before = incoming
+        if step == HIDDEN_BY:
+            later = tuple(hidden[1:])
+        elif step == PART_AT:
+            part = kernel_call(
+                part_kernel,
+                "part",
+                shape((width // across, kv_width), BF16),
+                [IN_VMEM] * (2 * across + 3),
+                (*hidden, *spread, incoming, before, *turn),
+            )
+        tasks, pairs, mine_of = [], [], []
+        for place in range(npipe):
+            task = task_of(step, place, npipe)
+            valid = 0 <= task < 2 * blocks
+            tasks.append(task if valid else None)
+            source = npipe - 1 - place + (npipe if task >= blocks else 0)
+            mine_of.append(changes[source if valid else 0])
+            if valid and not (place == 0 and task >= blocks):
+                pairs.append((place, (place - 1) % npipe))
+        dx = kernel_call(
+            functools.partial(step_kernel, tuple(tasks), blocks),
             "section_step",
-            (shape((ROWS, width), BF16), shape((ROWS, kv_width), BF16)),
-            [IN_SMEM] + [IN_VMEM] * (5 + min(step, 1)) + [ANYWHERE] * len(later),
-            (where, w_mat, x, gain, grad_out, incoming, *gv_parts[-1:], *later),
+            shape((ROWS, width), BF16),
+            [IN_SMEM] + [IN_VMEM] * (2 + npipe + len(turn)) + [ANYWHERE] * len(later),
+            (where, grad_out, incoming, *mine_of, *turn, *later),
         )
         gx_parts.append(dx)
-        gv_parts.append(dv)
-        pairs = []
-        for source in range(npipe):
-            task = task_of(step, source, npipe)
-            if 0 <= task < (blocks if source == 0 else 2 * blocks):
-                pairs.append((source, (source - 1) % npipe))
+        turn = [dx]
         if pairs:
             sent[step] = lax.ppermute(dx, "pipe", pairs)
-        if step == 4:
-            hidden = exchanged(held_until(tiles, dv), "dp_1")
+        if step == HIDDEN_AT:
+            hidden = exchanged(held_until(tiles, dx), "dp_1")
 
     grad_x = kernel_call(
         functools.partial(collect_kernel, npipe, blocks),
@@ -247,21 +310,6 @@
         scratch=(pltpu.SemaphoreType.DMA((steps,)),),
         out_spec=ANYWHERE,
     )[:, None]
-    dv_all = kernel_call(
-        functools.partial(stack_kernel, npipe, blocks),
-        "stack",
-        shape((2 * tok, kv_width), BF16),
-        [IN_SMEM] + [IN_VMEM] * steps,
-        (where, *gv_parts),
-    )
-    spread = exchanged([dv_all] * across, "dp_1")
-    part = kernel_call(
-        part_kernel,
-        "part",
-        shape((width // across, kv_width), BF16),
-        [IN_VMEM] * (2 * across),
-        (*hidden, *spread),
-    )
     others = ("dp_0", "dp_2", "dp_3")
     pieces = part.reshape(lax.axis_size(others), -1, kv_width)
     landed = lax.all_to_all(pieces, others, 0, 0, tiled=True)

time: 226 us -> 226 us (level)
  waiting for transfers between devices: 75.5 us -> 89.6 us
  Pallas kernels: 43.7 us -> 31.1 us
  starting transfers between devices: 67.1 us -> 60.8 us
    ppermute x0 -> x7, waiting for transfers between devices: none -> 32.4 us  [on_device(): arrived.append(lax.ppermute(out[1], 'pipe', [(owner, (owner - 1) % npipe)]))]
    ppermute x20, starting transfers between devices: 40 us -> 25.6 us  [on_device(): sent[step] = lax.ppermute(dx, 'pipe', pairs)]
    ppermute x0 -> x7, starting transfers between devices: none -> 12.7 us  [on_device(): arrived.append(lax.ppermute(out[1], 'pipe', [(owner, (owner - 1) % npipe)]))]
    pallas_call x27 -> x35, Pallas kernels: 43.7 us -> 31.1 us  [kernel_call(): pl.pallas_call(kernel, out_shape=out_shape, in_specs=specs, out_specs=jax...]
    ppermute x20, waiting for transfers between devices: 52.4 us -> 44.9 us  [on_device(): sent[step] = lax.ppermute(dx, 'pipe', pairs)]
    all_to_all x1, waiting for transfers between devices: 13.9 us -> 8.18 us  [on_device(): landed = lax.all_to_all(pieces, others, 0, 0, tiled=True)]
    ppermute x6, waiting for transfers between devices: 5.46 us -> 0.02 us  [exchanged(): moved.append(lax.ppermute(pieces[shift], axis, pairs))]
    ppermute x6, starting transfers between devices: 12.6 us -> 9.68 us  [exchanged(): moved.append(lax.ppermute(pieces[shift], axis, pairs))]
  transfers between devices with their start and end apart: 28 -> 35, of which waited for: 14 -> 17; matrix products, arithmetic and copies ran while one was open for 0% -> 0% of each run, Pallas kernels for 16% -> 11%
where the time goes in v6:
time: 226 us; the launch traced here: 224 us
  waiting for transfers between devices  89.6 us (40%)
  starting transfers between devices  60.8 us (27%)
  blocking collectives  35.3 us (16%)
  Pallas kernels  31.1 us (14%)
  local copies, waits for them, and re-layouts  3.29 us (1%)
    ppermute x20, waiting for transfers between devices, on_device(): sent[step] = lax.ppermute(dx, 'pipe', pairs)  44.9 us
    all_to_all x1, blocking collectives, copy_for_each(): lax.all_to_all(jnp.broadcast_to(array[None], (count, *array.shape)), axis...  35.3 us
    ppermute x7, waiting for transfers between devices, on_device(): arrived.append(lax.ppermute(out[1], 'pipe', [(owner, (owner - 1) % npipe)]))  32.4 us
    pallas_call x35, Pallas kernels, kernel_call(): pl.pallas_call(kernel, out_shape=out_shape, in_specs=specs, out_specs=jax...  31.1 us
    ppermute x20, starting transfers between devices, on_device(): sent[step] = lax.ppermute(dx, 'pipe', pairs)  25.6 us
    ppermute x7, starting transfers between devices, on_device(): arrived.append(lax.ppermute(out[1], 'pipe', [(owner, (owner - 1) % npipe)]))  12.7 us
    all_to_all x1, starting transfers between devices, on_device(): landed = lax.all_to_all(pieces, others, 0, 0, tiled=True)  10.4 us
    ppermute x6, starting transfers between devices, exchanged(): moved.append(lax.ppermute(pieces[shift], axis, pairs))  9.68 us
  transfers between devices with their start and end apart: 35, of which 17 were waited for; matrix products, arithmetic and copies ran while one was open for 0% of the time, Pallas kernels for 11%

profile of v6, /device:TPU:1, one launch (start us, length us, event | category | flops | bytes accessed | tf_op | source)
XLA Modules:
  0.0 224.1 jit_solution(12293521271623991225)
XLA Ops:
  0.6 1.1 broadcast_in_dim.14
  1.7 35.3 %all_to_all.10.mine_ref = bf16[32,64,512]{2,1,0:T(8,128)(2,1)} all-to-all(bf16[32,64,512]{2,1,0:T(8,128)(2,1)S(1)} %broadcast_in_dim.14), channel_id=1, replica_groups=mesh['pipe'=4,'dp_0'=2,'dp_1'=4,'dp_2'=4,'dp_3'=2] {'dp_0','dp_1','dp_2'}, dimensions={0} | all-to-all | bytes 4194304 | tf_op jit(solution)/shard_map/all_to_all | solution.py:27
  37.0 2.5 %collective-permute-start = (bf16[32,64,512]{2,1,0:T(8,128)(2,1)}, bf16[32,64,512]{2,1,0:T(8,128)(2,1)}, u32[]{:S(2)}, u32[]{:S(2)}) collective-permute-start(bf16[32,64,512]{2,1,0:T(8,128)(2,1)} %all_to_all.10.mine_ref), channel_id=1, source_target_pairs={{0,1},{1,0},{2,3},{3,2},{4,5},{5,4},{6,7},{7,6},{8,9},{9,8},{10,11... | collective-permute-start | bytes 6291464 | tf_op jit(solution)/shard_map/ppermute | solution.py:217
  39.6 4.0 %collective-permute-done.other_ref = bf16[32,64,512]{2,1,0:T(8,128)(2,1)} collective-permute-done((bf16[32,64,512]{2,1,0:T(8,128)(2,1)}, bf16[32,64,512]{2,1,0:T(8,128)(2,1)}, u32[]{:S(2)}, u32[]{:S(2)}) %collective-permute-start) | collective-permute-done | bytes 2097184 | tf_op jit(solution)/shard_map/ppermute | solution.py:217
  43.7 2.5 %rows.1.w_ref = bf16[4096,512]{1,0:T(8,128)(2,1)S(1)} custom-call(s32[3]{0:T(128)S(1)} %pad_add_fusion.where, bf16[32,64,512]{2,1,0:T(8,128)(2,1)} %all_to_all.10.mine_ref, bf16[32,64,512]{2,1,0:T(8,128)(2,1)} %collective-permute-done.other_ref), custom_call_target="tpu_custom_call" | custom-call | tf_op jit(solution)/shard_map/rows/pallas_call | solution.py:33
  46.8 0.7 collective-permute-start.2
  48.0 0.7 collective-permute-start.1
  49.3 0.7 collective-permute-start.3
  50.5 0.7 collective-permute-start.5
  51.8 0.7 collective-permute-start.4
  53.1 0.7 collective-permute-start.6
  54.3 1.3 collective-permute-start.8
  56.2 1.3 collective-permute-start.7
  58.1 1.3 collective-permute-start.9
  59.4 2.0 normalize.1.value_ref
  61.5 26.4 %collective-permute-done.8.from_ref.refs_3_ = bf16[128,512]{1,0:T(8,128)(2,1)S(1)} collective-permute-done((bf16[128,512]{1,0:T(8,128)(2,1)S(1)}, bf16[128,512]{1,0:T(8,128)(2,1)S(1)}, u32[]{:S(2)}, u32[]{:S(2)}) %collective-permute-start.8) | collective-permute-done | bytes 131104 | tf_op jit(solution)/shard_map/ppermute | solution.py:255
  87.9 2.6 %changes.11 = (bf16[128,4096]{1,0:T(8,128)(2,1)S(1)}, bf16[128,512]{1,0:T(8,128)(2,1)S(1)}) custom-call(s32[3]{0:T(128)S(1)} %pad_add_fusion.where, bf16[4096,512]{1,0:T(8,128)(2,1)S(1)} %rows.1.w_ref, bf16[2,128,4096]{2,1,0:T(8,128)(2,1)S(1)} %bitcast.22, f32[2,1,4096]{2,1,0:T(1,128)S(1)} %copy-done.3, ...), custom_call_target="tpu_custom_call" | custom-call | tf_op jit(solution)/shard_map/changes/pallas_call | solution.py:33
  90.5 7.4 %collective-permute-start.11 = (bf16[128,512]{1,0:T(8,128)(2,1)S(1)}, bf16[128,512]{1,0:T(8,128)(2,1)S(1)}, u32[]{:S(2)}, u32[]{:S(2)}) collective-permute-start(bf16[128,512]{1,0:T(8,128)(2,1)S(1)} %get-tuple-element.26.refs_4_), channel_id=1, source_target_pairs={{0,192},{1,193},{2,194},{3,195},{4,196},{5,197},{6,198},{7,199},{8... | collective-permute-start | bytes 393224 | tf_op jit(solution)/shard_map/ppermute | solution.py:255
  97.9 0.6 section_step.28.refs_4_.refs_6_
  98.6 1.2 collective-permute-done.9.in_ref
  99.9 0.6 section_step.29.refs_0_.token_ref.refs_7_
  100.7 3.5 %collective-permute-start.20 = (bf16[2,128,1024]{2,1,0:T(8,128)(2,1)S(1)}, bf16[2,128,1024]{2,1,0:T(8,128)(2,1)S(1)}, u32[]{:S(2)}, u32[]{:S(2)}) collective-permute-start(bf16[2,128,1024]{2,1,0:T(8,128)(2,1)S(1)} %get-tuple-element.39), channel_id=1, source_target_pairs={{0,24},{8,0},{16,8},{24,16},{1,25},{9,1},{17,9},{25,17},{2,26},{10... | collective-permute-start | bytes 1572872 | tf_op jit(solution)/shard_map/ppermute | solution.py:202
  104.2 0.8 collective-permute-start.18
  106.1 0.7 collective-permute-start.14
  106.7 0.6 section_step.30.refs_4_.refs_8_
  107.3 8.7 %collective-permute-done.12.in_ref = bf16[16,4096]{1,0:T(8,128)(2,1)S(1)} collective-permute-done((bf16[16,4096]{1,0:T(8,128)(2,1)S(1)}, bf16[16,4096]{1,0:T(8,128)(2,1)S(1)}, u32[]{:S(2)}, u32[]{:S(2)}) %collective-permute-start.12) | collective-permute-done | bytes 131104 | tf_op jit(solution)/shard_map/ppermute | solution.py:300
  116.0 0.6 section_step.31.refs_0_.refs_9_
  116.7 4.2 %collective-permute-start.15 = (bf16[16,4096]{1,0:T(8,128)(2,1)S(1)}, bf16[16,4096]{1,0:T(8,128)(2,1)S(1)}, u32[]{:S(2)}, u32[]{:S(2)}) collective-permute-start(bf16[16,4096]{1,0:T(8,128)(2,1)S(1)} %section_step.31.refs_0_.refs_9_), channel_id=1, source_target_pairs={{0,192},{64,0},{128,64},{192,128},{1,193},{65,1},{129,65},{193,129... | collective-permute-start | bytes 393224 | tf_op jit(solution)/shard_map/ppermute | solution.py:300
  121.5 4.2 %collective-permute-done.13.in_ref = bf16[16,4096]{1,0:T(8,128)(2,1)S(1)} collective-permute-done((bf16[16,4096]{1,0:T(8,128)(2,1)S(1)}, bf16[16,4096]{1,0:T(8,128)(2,1)S(1)}, u32[]{:S(2)}, u32[]{:S(2)}) %collective-permute-start.13) | collective-permute-done | bytes 131104 | tf_op jit(solution)/shard_map/ppermute | solution.py:300
  125.7 0.7 collective-permute-start.17
  126.3 0.6 section_step.32.refs_4_.refs_10_
  126.9 2.6 %collective-permute-done.15.in_ref = bf16[16,4096]{1,0:T(8,128)(2,1)S(1)} collective-permute-done((bf16[16,4096]{1,0:T(8,128)(2,1)S(1)}, bf16[16,4096]{1,0:T(8,128)(2,1)S(1)}, u32[]{:S(2)}, u32[]{:S(2)}) %collective-permute-start.15) | collective-permute-done | bytes 131104 | tf_op jit(solution)/shard_map/ppermute | solution.py:300
  129.5 2.9 %collective-permute-start.16 = (bf16[16,4096]{1,0:T(8,128)(2,1)S(1)}, bf16[16,4096]{1,0:T(8,128)(2,1)S(1)}, u32[]{:S(2)}, u32[]{:S(2)}) collective-permute-start(bf16[16,4096]{1,0:T(8,128)(2,1)S(1)} %section_step.32.refs_4_.refs_10_), channel_id=1, source_target_pairs={{0,192},{64,0},{128,64},{192,128},{1,193},{65,1},{129,65},{193,129... | collective-permute-start | bytes 393224 | tf_op jit(solution)/shard_map/ppermute | solution.py:300
  133.0 3.5 %collective-permute-start.21 = (bf16[16,4096]{1,0:T(8,128)(2,1)S(1)}, bf16[16,4096]{1,0:T(8,128)(2,1)S(1)}, u32[]{:S(2)}, u32[]{:S(2)}) collective-permute-start(bf16[16,4096]{1,0:T(8,128)(2,1)S(1)} %section_step.33.refs_0_.refs_11_), channel_id=1, source_target_pairs={{0,192},{64,0},{128,64},{192,128},{1,193},{65,1},{129,65},{193,129... | collective-permute-start | bytes 393224 | tf_op jit(solution)/shard_map/ppermute | solution.py:300
  137.1 6.2 %collective-permute-done.16.in_ref = bf16[16,4096]{1,0:T(8,128)(2,1)S(1)} collective-permute-done((bf16[16,4096]{1,0:T(8,128)(2,1)S(1)}, bf16[16,4096]{1,0:T(8,128)(2,1)S(1)}, u32[]{:S(2)}, u32[]{:S(2)}) %collective-permute-start.16) | collective-permute-done | bytes 131104 | tf_op jit(solution)/shard_map/ppermute | solution.py:300
  143.2 1.3 collective-permute-start.23
  144.6 0.6 section_step.34.refs_4_.refs_12_
  145.3 2.8 %collective-permute-done.21.in_ref = bf16[16,4096]{1,0:T(8,128)(2,1)S(1)} collective-permute-done((bf16[16,4096]{1,0:T(8,128)(2,1)S(1)}, bf16[16,4096]{1,0:T(8,128)(2,1)S(1)}, u32[]{:S(2)}, u32[]{:S(2)}) %collective-permute-start.21) | collective-permute-done | bytes 131104 | tf_op jit(solution)/shard_map/ppermute | solution.py:300
  148.7 1.3 collective-permute-start.24
  149.9 6.0 %collective-permute-done.23.from_ref.refs_7_ = bf16[128,512]{1,0:T(8,128)(2,1)S(1)} collective-permute-done((bf16[128,512]{1,0:T(8,128)(2,1)S(1)}, bf16[128,512]{1,0:T(8,128)(2,1)S(1)}, u32[]{:S(2)}, u32[]{:S(2)}) %collective-permute-start.23) | collective-permute-done | bytes 131104 | tf_op jit(solution)/shard_map/ppermute | solution.py:255
  156.0 2.8 %changes.15 = (bf16[128,4096]{1,0:T(8,128)(2,1)S(1)}, bf16[128,512]{1,0:T(8,128)(2,1)S(1)}) custom-call(s32[3]{0:T(128)S(1)} %pad_add_fusion.where, bf16[4096,512]{1,0:T(8,128)(2,1)S(1)} %rows.1.w_ref, bf16[2,128,4096]{2,1,0:T(8,128)(2,1)S(1)} %bitcast.26, f32[2,1,4096]{2,1,0:T(1,128)S(1)} %copy-done.3, ...), custom_call_target="tpu_custom_call" | custom-call | tf_op jit(solution)/shard_map/changes/pallas_call | solution.py:33
  158.8 1.6 collective-permute-done.22.in_ref
  161.0 1.3 collective-permute-start.25
  162.3 1.9 collective-permute-done.24.in_ref
  164.2 0.6 section_step.37.refs_4_.refs_15_
  164.8 1.3 collective-permute-start.26
  166.8 1.7 collective-permute-done.25.in_ref
  169.1 1.3 collective-permute-start.27
  170.4 4.5 %collective-permute-start.32 = (bf16[256,512]{1,0:T(8,128)(2,1)S(1)}, bf16[256,512]{1,0:T(8,128)(2,1)S(1)}, u32[]{:S(2)}, u32[]{:S(2)}) collective-permute-start(bf16[256,512]{1,0:T(8,128)(2,1)S(1)} %stack.17.refs_4_), channel_id=1, source_target_pairs={{0,16},{8,24},{16,0},{24,8},{1,17},{9,25},{17,1},{25,9},{2,18},{10... | collective-permute-start | bytes 786440 | tf_op jit(solution)/shard_map/ppermute | solution.py:202
  174.9 0.8 collective-permute-start.31
  175.8 2.4 %collective-permute-done.26.in_ref = bf16[16,4096]{1,0:T(8,128)(2,1)S(1)} collective-permute-done((bf16[16,4096]{1,0:T(8,128)(2,1)S(1)}, bf16[16,4096]{1,0:T(8,128)(2,1)S(1)}, u32[]{:S(2)}, u32[]{:S(2)}) %collective-permute-start.26) | collective-permute-done | bytes 131104 | tf_op jit(solution)/shard_map/ppermute | solution.py:300
  178.8 1.3 collective-permute-start.28
  180.7 1.3 collective-permute-start.29
  182.0 5.2 %collective-permute-done.28.in_ref.refs_9_ = bf16[16,4096]{1,0:T(8,128)(2,1)S(1)} collective-permute-done((bf16[16,4096]{1,0:T(8,128)(2,1)S(1)}, bf16[16,4096]{1,0:T(8,128)(2,1)S(1)}, u32[]{:S(2)}, u32[]{:S(2)}) %collective-permute-start.28) | collective-permute-done | bytes 131104 | tf_op jit(solution)/shard_map/ppermute | solution.py:300
  187.9 1.6 collective-permute-done.29.in_ref.refs_8_
  189.5 2.3 %part.1 = bf16[1024,512]{1,0:T(8,128)(2,1)S(1)} custom-call(bf16[2,128,1024]{2,1,0:T(8,128)(2,1)S(1)} %get-tuple-element.38.refs_0_, bf16[2,128,1024]{2,1,0:T(8,128)(2,1)S(1)} %collective-permute-done.18.refs_5_.refs_1_, bf16[2,128,1024]{2,1,0:T(8,128)(2,1)S(1)} %collective-permute-done.19.refs_6_.refs_2_, ...), custom_call_target="tpu_custom_call" | custom-call | tf_op jit(solution)/shard_map/part/pallas_call | solution.py:33
  191.9 1.0 copy-done.2
  192.9 10.4 %all-to-all-start.1 = ((bf16[16,64,512]{2,1,0:T(8,128)(2,1)}), bf16[16,64,512]{2,1,0:T(8,128)(2,1)}, u32[]{:S(2)}, u32[]{:S(2)}) async-start(bf16[16,64,512]{2,1,0:T(8,128)(2,1)} %bitcast.27), calls=%async_computation.1 | async-start | bytes 2097152 | tf_op jit(solution)/shard_map/all_to_all | solution.py:315
  203.3 1.3 collective-permute-start.30
  204.6 0.9 copy-done.39
  206.2 4.8 %collective-permute-done.30.in_ref = bf16[16,4096]{1,0:T(8,128)(2,1)S(1)} collective-permute-done((bf16[16,4096]{1,0:T(8,128)(2,1)S(1)}, bf16[16,4096]{1,0:T(8,128)(2,1)S(1)}, u32[]{:S(2)}, u32[]{:S(2)}) %collective-permute-start.30) | collective-permute-done | bytes 131104 | tf_op jit(solution)/shard_map/ppermute | solution.py:300
  211.8 2.1 collect_rows.1
  213.9 8.2 %all-to-all-done.1 = bf16[16,64,512]{2,1,0:T(8,128)(2,1)} async-done(((bf16[16,64,512]{2,1,0:T(8,128)(2,1)}), bf16[16,64,512]{2,1,0:T(8,128)(2,1)}, u32[]{:S(2)}, u32[]{:S(2)}) %all-to-all-start.1) | async-done | bytes 1048608 | tf_op jit(solution)/shard_map/all_to_all | solution.py:315
  222.1 2.0 convert_reduce_fusion
  (128 shorter events, 13.9 us)
Async XLA Ops:
  37.0 6.7 %collective-permute-start = (bf16[32,64,512]{2,1,0:T(8,128)(2,1)}, bf16[32,64,512]{2,1,0:T(8,128)(2,1)}, u32[]{:S(2)}, u32[]{:S(2)}) collective-permute-start(bf16[32,64,512]{2,1,0:T(8,128)(2,1)} %all_to_all.10.mine_ref), channel_id=1, source_target_pairs={{0,1},{1,0},{2,3},{3,2},{4,5},{5,4},{6,7},{7,6},{8,9},{9,8},{10,11... | collective-permute-start | bytes 6291464 | tf_op jit(solution)/shard_map/ppermute | solution.py:217
  39.6 6.6 %copy-start = (bf16[128,4096]{1,0:T(8,128)(2,1)S(1)}, bf16[128,4096]{1,0:T(8,128)(2,1)}, u32[]{:S(2)}) copy-start(bf16[128,4096]{1,0:T(8,128)(2,1)} %fresh_ref.43) | copy-start | bytes 3145732
  39.6 6.6 %copy-start.1 = (bf16[2,1,128,4096]{3,2,1,0:T(8,128)(2,1)S(1)}, bf16[2,1,128,4096]{3,2,1,0:T(8,128)(2,1)}, u32[]{:S(2)}) copy-start(bf16[2,1,128,4096]{3,2,1,0:T(8,128)(2,1)} %param.4) | copy-start | bytes 6291460
  39.6 6.6 %copy-start.3 = (f32[2,1,4096]{2,1,0:T(1,128)S(1)}, f32[2,1,4096]{2,1,0:T(1,128)}, u32[]{:S(2)}) copy-start(f32[2,1,4096]{2,1,0:T(1,128)} %g_ref.17) | copy-start | bytes 98308
  46.8 3.2 %collective-permute-start.2 = (bf16[128,512]{1,0:T(8,128)(2,1)S(1)}, bf16[128,512]{1,0:T(8,128)(2,1)S(1)}, u32[]{:S(2)}, u32[]{:S(2)}) collective-permute-start(bf16[128,512]{1,0:T(8,128)(2,1)S(1)} %get-tuple-element.20.refs_4_), channel_id=1, source_target_pairs={{192,128},{193,129},{194,130},{195,131},{196,132},{197,133},{198,1... | collective-permute-start | bytes 393224 | tf_op jit(solution)/shard_map/ppermute | solution.py:255
  48.0 3.2 %collective-permute-start.1 = (bf16[16,4096]{1,0:T(8,128)(2,1)S(1)}, bf16[16,4096]{1,0:T(8,128)(2,1)S(1)}, u32[]{:S(2)}, u32[]{:S(2)}) collective-permute-start(bf16[16,4096]{1,0:T(8,128)(2,1)S(1)} %section_step.22.refs_4_.refs_0_), channel_id=1, source_target_pairs={{192,128},{193,129},{194,130},{195,131},{196,132},{197,133},{198,1... | collective-permute-start | bytes 393224 | tf_op jit(solution)/shard_map/ppermute | solution.py:300
  49.3 3.2 %collective-permute-start.3 = (bf16[16,4096]{1,0:T(8,128)(2,1)S(1)}, bf16[16,4096]{1,0:T(8,128)(2,1)S(1)}, u32[]{:S(2)}, u32[]{:S(2)}) collective-permute-start(bf16[16,4096]{1,0:T(8,128)(2,1)S(1)} %section_step.23.refs_0_.refs_1_), channel_id=1, source_target_pairs={{192,128},{193,129},{194,130},{195,131},{196,132},{197,133},{198,1... | collective-permute-start | bytes 393224 | tf_op jit(solution)/shard_map/ppermute | solution.py:300
  50.5 3.2 %collective-permute-start.5 = (bf16[128,512]{1,0:T(8,128)(2,1)S(1)}, bf16[128,512]{1,0:T(8,128)(2,1)S(1)}, u32[]{:S(2)}, u32[]{:S(2)}) collective-permute-start(bf16[128,512]{1,0:T(8,128)(2,1)S(1)} %get-tuple-element.22.refs_4_), channel_id=1, source_target_pairs={{128,64},{129,65},{130,66},{131,67},{132,68},{133,69},{134,70},{13... | collective-permute-start | bytes 393224 | tf_op jit(solution)/shard_map/ppermute | solution.py:255
  51.8 3.8 %collective-permute-start.4 = (bf16[16,4096]{1,0:T(8,128)(2,1)S(1)}, bf16[16,4096]{1,0:T(8,128)(2,1)S(1)}, u32[]{:S(2)}, u32[]{:S(2)}) collective-permute-start(bf16[16,4096]{1,0:T(8,128)(2,1)S(1)} %section_step.24.refs_4_.refs_2_), channel_id=1, source_target_pairs={{128,64},{192,128},{129,65},{193,129},{130,66},{194,130},{131,67},... | collective-permute-start | bytes 393224 | tf_op jit(solution)/shard_map/ppermute | solution.py:300
  53.1 4.5 %collective-permute-start.6 = (bf16[16,4096]{1,0:T(8,128)(2,1)S(1)}, bf16[16,4096]{1,0:T(8,128)(2,1)S(1)}, u32[]{:S(2)}, u32[]{:S(2)}) collective-permute-start(bf16[16,4096]{1,0:T(8,128)(2,1)S(1)} %section_step.25.refs_0_.refs_3_), channel_id=1, source_target_pairs={{128,64},{192,128},{129,65},{193,129},{130,66},{194,130},{131,67},... | collective-permute-start | bytes 393224 | tf_op jit(solution)/shard_map/ppermute | solution.py:300
  54.3 33.5 %collective-permute-start.8 = (bf16[128,512]{1,0:T(8,128)(2,1)S(1)}, bf16[128,512]{1,0:T(8,128)(2,1)S(1)}, u32[]{:S(2)}, u32[]{:S(2)}) collective-permute-start(bf16[128,512]{1,0:T(8,128)(2,1)S(1)} %get-tuple-element.24.refs_4_), channel_id=1, source_target_pairs={{64,0},{65,1},{66,2},{67,3},{68,4},{69,5},{70,6},{71,7},{72,8},{73... | collective-permute-start | bytes 393224 | tf_op jit(solution)/shard_map/ppermute | solution.py:255
  56.2 41.7 %collective-permute-start.7 = (bf16[16,4096]{1,0:T(8,128)(2,1)S(1)}, bf16[16,4096]{1,0:T(8,128)(2,1)S(1)}, u32[]{:S(2)}, u32[]{:S(2)}) collective-permute-start(bf16[16,4096]{1,0:T(8,128)(2,1)S(1)} %section_step.26.refs_4_), channel_id=1, source_target_pairs={{64,0},{128,64},{192,128},{65,1},{129,65},{193,129},{66,2},{130,66... | collective-permute-start | bytes 393224 | tf_op jit(solution)/shard_map/ppermute | solution.py:300
  58.1 29.7 %copy-start.30 = (bf16[16,4096]{1,0:T(8,128)(2,1)}, bf16[16,4096]{1,0:T(8,128)(2,1)S(1)}, u32[]{:S(2)}) copy-start(bf16[16,4096]{1,0:T(8,128)(2,1)S(1)} %section_step.27.refs_0_.refs_5_) | copy-start | bytes 393220
  58.1 41.7 %collective-permute-start.9 = (bf16[16,4096]{1,0:T(8,128)(2,1)S(1)}, bf16[16,4096]{1,0:T(8,128)(2,1)S(1)}, u32[]{:S(2)}, u32[]{:S(2)}) collective-permute-start(bf16[16,4096]{1,0:T(8,128)(2,1)S(1)} %section_step.27.refs_0_.refs_5_), channel_id=1, source_target_pairs={{64,0},{128,64},{192,128},{65,1},{129,65},{193,129},{66,2},{130,66... | collective-permute-start | bytes 393224 | tf_op jit(solution)/shard_map/ppermute | solution.py:300
  90.5 14.5 %collective-permute-start.11 = (bf16[128,512]{1,0:T(8,128)(2,1)S(1)}, bf16[128,512]{1,0:T(8,128)(2,1)S(1)}, u32[]{:S(2)}, u32[]{:S(2)}) collective-permute-start(bf16[128,512]{1,0:T(8,128)(2,1)S(1)} %get-tuple-element.26.refs_4_), channel_id=1, source_target_pairs={{0,192},{1,193},{2,194},{3,195},{4,196},{5,197},{6,198},{7,199},{8... | collective-permute-start | bytes 393224 | tf_op jit(solution)/shard_map/ppermute | solution.py:255
  98.5 7.5 %collective-permute-start.10 = (bf16[16,4096]{1,0:T(8,128)(2,1)S(1)}, bf16[16,4096]{1,0:T(8,128)(2,1)S(1)}, u32[]{:S(2)}, u32[]{:S(2)}) collective-permute-start(bf16[16,4096]{1,0:T(8,128)(2,1)S(1)} %section_step.28.refs_4_.refs_6_), channel_id=1, source_target_pairs={{0,192},{64,0},{128,64},{192,128},{1,193},{65,1},{129,65},{193,129... | collective-permute-start | bytes 393224 | tf_op jit(solution)/shard_map/ppermute | solution.py:300
  100.7 43.9 %collective-permute-start.20 = (bf16[2,128,1024]{2,1,0:T(8,128)(2,1)S(1)}, bf16[2,128,1024]{2,1,0:T(8,128)(2,1)S(1)}, u32[]{:S(2)}, u32[]{:S(2)}) collective-permute-start(bf16[2,128,1024]{2,1,0:T(8,128)(2,1)S(1)} %get-tuple-element.39), channel_id=1, source_target_pairs={{0,24},{8,0},{16,8},{24,16},{1,25},{9,1},{17,9},{25,17},{2,26},{10... | collective-permute-start | bytes 1572872 | tf_op jit(solution)/shard_map/ppermute | solution.py:202
  104.1 40.4 %collective-permute-start.19 = (bf16[2,128,1024]{2,1,0:T(8,128)(2,1)S(1)}, bf16[2,128,1024]{2,1,0:T(8,128)(2,1)S(1)}, u32[]{:S(2)}, u32[]{:S(2)}) collective-permute-start(bf16[2,128,1024]{2,1,0:T(8,128)(2,1)S(1)} %get-tuple-element.40), channel_id=1, source_target_pairs={{0,16},{8,24},{16,0},{24,8},{1,17},{9,25},{17,1},{25,9},{2,18},{10... | collective-permute-start | bytes 1572872 | tf_op jit(solution)/shard_map/ppermute | solution.py:202
  104.2 40.4 %collective-permute-start.18 = (bf16[2,128,1024]{2,1,0:T(8,128)(2,1)S(1)}, bf16[2,128,1024]{2,1,0:T(8,128)(2,1)S(1)}, u32[]{:S(2)}, u32[]{:S(2)}) collective-permute-start(bf16[2,128,1024]{2,1,0:T(8,128)(2,1)S(1)} %get-tuple-element.41), channel_id=1, source_target_pairs={{0,8},{8,16},{16,24},{24,0},{1,9},{9,17},{17,25},{25,1},{2,10},{10... | collective-permute-start | bytes 1572872 | tf_op jit(solution)/shard_map/ppermute | solution.py:202
  105.0 11.1 %collective-permute-start.12 = (bf16[16,4096]{1,0:T(8,128)(2,1)S(1)}, bf16[16,4096]{1,0:T(8,128)(2,1)S(1)}, u32[]{:S(2)}, u32[]{:S(2)}) collective-permute-start(bf16[16,4096]{1,0:T(8,128)(2,1)S(1)} %section_step.29.refs_0_.token_ref.refs_7_), channel_id=1, source_target_pairs={{0,192},{64,0},{128,64},{192,128},{1,193},{65,1},{129,65},{193,129... | collective-permute-start | bytes 393224 | tf_op jit(solution)/shard_map/ppermute | solution.py:300
  106.1 10.6 %collective-permute-start.14 = (bf16[128,512]{1,0:T(8,128)(2,1)S(1)}, bf16[128,512]{1,0:T(8,128)(2,1)S(1)}, u32[]{:S(2)}, u32[]{:S(2)}) collective-permute-start(bf16[128,512]{1,0:T(8,128)(2,1)S(1)} %get-tuple-element.28.refs_4_), channel_id=1, source_target_pairs={{192,128},{193,129},{194,130},{195,131},{196,132},{197,133},{198,1... | collective-permute-start | bytes 393224 | tf_op jit(solution)/shard_map/ppermute | solution.py:255
  107.3 9.3 %copy-start.12 = (bf16[16,4096]{1,0:T(8,128)(2,1)}, bf16[16,4096]{1,0:T(8,128)(2,1)S(1)}, u32[]{:S(2)}) copy-start(bf16[16,4096]{1,0:T(8,128)(2,1)S(1)} %section_step.30.refs_4_.refs_8_) | copy-start | bytes 393220
  116.0 9.6 %collective-permute-start.13 = (bf16[16,4096]{1,0:T(8,128)(2,1)S(1)}, bf16[16,4096]{1,0:T(8,128)(2,1)S(1)}, u32[]{:S(2)}, u32[]{:S(2)}) collective-permute-start(bf16[16,4096]{1,0:T(8,128)(2,1)S(1)} %section_step.30.refs_4_.refs_8_), channel_id=1, source_target_pairs={{0,192},{64,0},{128,64},{192,128},{1,193},{65,1},{129,65},{193,129... | collective-permute-start | bytes 393224 | tf_op jit(solution)/shard_map/ppermute | solution.py:300
  116.6 4.8 %copy-start.32 = (bf16[16,4096]{1,0:T(8,128)(2,1)}, bf16[16,4096]{1,0:T(8,128)(2,1)S(1)}, u32[]{:S(2)}) copy-start(bf16[16,4096]{1,0:T(8,128)(2,1)S(1)} %section_step.31.refs_0_.refs_9_) | copy-start | bytes 393220
  116.7 12.8 %collective-permute-start.15 = (bf16[16,4096]{1,0:T(8,128)(2,1)S(1)}, bf16[16,4096]{1,0:T(8,128)(2,1)S(1)}, u32[]{:S(2)}, u32[]{:S(2)}) collective-permute-start(bf16[16,4096]{1,0:T(8,128)(2,1)S(1)} %section_step.31.refs_0_.refs_9_), channel_id=1, source_target_pairs={{0,192},{64,0},{128,64},{192,128},{1,193},{65,1},{129,65},{193,129... | collective-permute-start | bytes 393224 | tf_op jit(solution)/shard_map/ppermute | solution.py:300
  125.7 7.4 %collective-permute-start.17 = (bf16[128,512]{1,0:T(8,128)(2,1)S(1)}, bf16[128,512]{1,0:T(8,128)(2,1)S(1)}, u32[]{:S(2)}, u32[]{:S(2)}) collective-permute-start(bf16[128,512]{1,0:T(8,128)(2,1)S(1)} %get-tuple-element.30.refs_4_), channel_id=1, source_target_pairs={{128,64},{129,65},{130,66},{131,67},{132,68},{133,69},{134,70},{13... | collective-permute-start | bytes 393224 | tf_op jit(solution)/shard_map/ppermute | solution.py:255
  126.9 6.1 %copy-start.14 = (bf16[16,4096]{1,0:T(8,128)(2,1)}, bf16[16,4096]{1,0:T(8,128)(2,1)S(1)}, u32[]{:S(2)}) copy-start(bf16[16,4096]{1,0:T(8,128)(2,1)S(1)} %section_step.32.refs_4_.refs_10_) | copy-start | bytes 393220
  129.5 13.7 %collective-permute-start.16 = (bf16[16,4096]{1,0:T(8,128)(2,1)S(1)}, bf16[16,4096]{1,0:T(8,128)(2,1)S(1)}, u32[]{:S(2)}, u32[]{:S(2)}) collective-permute-start(bf16[16,4096]{1,0:T(8,128)(2,1)S(1)} %section_step.32.refs_4_.refs_10_), channel_id=1, source_target_pairs={{0,192},{64,0},{128,64},{192,128},{1,193},{65,1},{129,65},{193,129... | collective-permute-start | bytes 393224 | tf_op jit(solution)/shard_map/ppermute | solution.py:300
  133.0 4.1 %copy-start.34 = (bf16[16,4096]{1,0:T(8,128)(2,1)}, bf16[16,4096]{1,0:T(8,128)(2,1)S(1)}, u32[]{:S(2)}) copy-start(bf16[16,4096]{1,0:T(8,128)(2,1)S(1)} %section_step.33.refs_0_.refs_11_) | copy-start | bytes 393220
  133.0 15.0 %collective-permute-start.21 = (bf16[16,4096]{1,0:T(8,128)(2,1)S(1)}, bf16[16,4096]{1,0:T(8,128)(2,1)S(1)}, u32[]{:S(2)}, u32[]{:S(2)}) collective-permute-start(bf16[16,4096]{1,0:T(8,128)(2,1)S(1)} %section_step.33.refs_0_.refs_11_), channel_id=1, source_target_pairs={{0,192},{64,0},{128,64},{192,128},{1,193},{65,1},{129,65},{193,129... | collective-permute-start | bytes 393224 | tf_op jit(solution)/shard_map/ppermute | solution.py:300
  143.2 12.7 %collective-permute-start.23 = (bf16[128,512]{1,0:T(8,128)(2,1)S(1)}, bf16[128,512]{1,0:T(8,128)(2,1)S(1)}, u32[]{:S(2)}, u32[]{:S(2)}) collective-permute-start(bf16[128,512]{1,0:T(8,128)(2,1)S(1)} %get-tuple-element.32.refs_4_), channel_id=1, source_target_pairs={{64,0},{65,1},{66,2},{67,3},{68,4},{69,5},{70,6},{71,7},{72,8},{73... | collective-permute-start | bytes 393224 | tf_op jit(solution)/shard_map/ppermute | solution.py:255
  145.2 15.2 %collective-permute-start.22 = (bf16[16,4096]{1,0:T(8,128)(2,1)S(1)}, bf16[16,4096]{1,0:T(8,128)(2,1)S(1)}, u32[]{:S(2)}, u32[]{:S(2)}) collective-permute-start(bf16[16,4096]{1,0:T(8,128)(2,1)S(1)} %section_step.34.refs_4_.refs_12_), channel_id=1, source_target_pairs={{0,192},{64,0},{128,64},{192,128},{1,193},{65,1},{129,65},{193,129... | collective-permute-start | bytes 393224 | tf_op jit(solution)/shard_map/ppermute | solution.py:300
  148.7 10.1 %copy-start.36 = (bf16[16,4096]{1,0:T(8,128)(2,1)}, bf16[16,4096]{1,0:T(8,128)(2,1)S(1)}, u32[]{:S(2)}) copy-start(bf16[16,4096]{1,0:T(8,128)(2,1)S(1)} %section_step.35.refs_0_.refs_13_) | copy-start | bytes 393220
  148.7 15.5 %collective-permute-start.24 = (bf16[16,4096]{1,0:T(8,128)(2,1)S(1)}, bf16[16,4096]{1,0:T(8,128)(2,1)S(1)}, u32[]{:S(2)}, u32[]{:S(2)}) collective-permute-start(bf16[16,4096]{1,0:T(8,128)(2,1)S(1)} %section_step.35.refs_0_.refs_13_), channel_id=1, source_target_pairs={{0,192},{64,0},{128,64},{192,128},{1,193},{65,1},{129,65},{193,129... | collective-permute-start | bytes 393224 | tf_op jit(solution)/shard_map/ppermute | solution.py:300
  161.0 7.6 %collective-permute-start.25 = (bf16[16,4096]{1,0:T(8,128)(2,1)S(1)}, bf16[16,4096]{1,0:T(8,128)(2,1)S(1)}, u32[]{:S(2)}, u32[]{:S(2)}) collective-permute-start(bf16[16,4096]{1,0:T(8,128)(2,1)S(1)} %section_step.36.refs_4_.refs_14_), channel_id=1, source_target_pairs={{64,0},{128,64},{192,128},{65,1},{129,65},{193,129},{66,2},{130,66... | collective-permute-start | bytes 393224 | tf_op jit(solution)/shard_map/ppermute | solution.py:300
  164.8 4.3 %copy-start.18 = (bf16[16,4096]{1,0:T(8,128)(2,1)}, bf16[16,4096]{1,0:T(8,128)(2,1)S(1)}, u32[]{:S(2)}) copy-start(bf16[16,4096]{1,0:T(8,128)(2,1)S(1)} %section_step.37.refs_4_.refs_15_) | copy-start | bytes 393220
  164.8 13.4 %collective-permute-start.26 = (bf16[16,4096]{1,0:T(8,128)(2,1)S(1)}, bf16[16,4096]{1,0:T(8,128)(2,1)S(1)}, u32[]{:S(2)}, u32[]{:S(2)}) collective-permute-start(bf16[16,4096]{1,0:T(8,128)(2,1)S(1)} %section_step.37.refs_4_.refs_15_), channel_id=1, source_target_pairs={{64,0},{128,64},{192,128},{65,1},{129,65},{193,129},{66,2},{130,66... | collective-permute-start | bytes 393224 | tf_op jit(solution)/shard_map/ppermute | solution.py:300
  166.7 21.2 %collective-permute-start.33 = (bf16[256,512]{1,0:T(8,128)(2,1)S(1)}, bf16[256,512]{1,0:T(8,128)(2,1)S(1)}, u32[]{:S(2)}, u32[]{:S(2)}) collective-permute-start(bf16[256,512]{1,0:T(8,128)(2,1)S(1)} %stack.17.refs_4_), channel_id=1, source_target_pairs={{0,24},{8,0},{16,8},{24,16},{1,25},{9,1},{17,9},{25,17},{2,26},{10... | collective-permute-start | bytes 786440 | tf_op jit(solution)/shard_map/ppermute | solution.py:202
  169.1 9.6 %copy-start.20 = (bf16[16,4096]{1,0:T(8,128)(2,1)}, bf16[16,4096]{1,0:T(8,128)(2,1)S(1)}, u32[]{:S(2)}) copy-start(bf16[16,4096]{1,0:T(8,128)(2,1)S(1)} %section_step.38.refs_4_.refs_16_) | copy-start | bytes 393220
  169.1 11.0 %collective-permute-start.27 = (bf16[16,4096]{1,0:T(8,128)(2,1)S(1)}, bf16[16,4096]{1,0:T(8,128)(2,1)S(1)}, u32[]{:S(2)}, u32[]{:S(2)}) collective-permute-start(bf16[16,4096]{1,0:T(8,128)(2,1)S(1)} %section_step.38.refs_4_.refs_16_), channel_id=1, source_target_pairs={{64,0},{128,64},{65,1},{129,65},{66,2},{130,66},{67,3},{131,67},{6... | collective-permute-start | bytes 393224 | tf_op jit(solution)/shard_map/ppermute | solution.py:300
  170.4 17.4 %collective-permute-start.32 = (bf16[256,512]{1,0:T(8,128)(2,1)S(1)}, bf16[256,512]{1,0:T(8,128)(2,1)S(1)}, u32[]{:S(2)}, u32[]{:S(2)}) collective-permute-start(bf16[256,512]{1,0:T(8,128)(2,1)S(1)} %stack.17.refs_4_), channel_id=1, source_target_pairs={{0,16},{8,24},{16,0},{24,8},{1,17},{9,25},{17,1},{25,9},{2,18},{10... | collective-permute-start | bytes 786440 | tf_op jit(solution)/shard_map/ppermute | solution.py:202
  174.9 13.0 %collective-permute-start.31 = (bf16[256,512]{1,0:T(8,128)(2,1)S(1)}, bf16[256,512]{1,0:T(8,128)(2,1)S(1)}, u32[]{:S(2)}, u32[]{:S(2)}) collective-permute-start(bf16[256,512]{1,0:T(8,128)(2,1)S(1)} %stack.17.refs_4_), channel_id=1, source_target_pairs={{0,8},{8,16},{16,24},{24,0},{1,9},{9,17},{17,25},{25,1},{2,10},{10... | collective-permute-start | bytes 786440 | tf_op jit(solution)/shard_map/ppermute | solution.py:202
  178.8 8.5 %collective-permute-start.28 = (bf16[16,4096]{1,0:T(8,128)(2,1)S(1)}, bf16[16,4096]{1,0:T(8,128)(2,1)S(1)}, u32[]{:S(2)}, u32[]{:S(2)}) collective-permute-start(bf16[16,4096]{1,0:T(8,128)(2,1)S(1)} %section_step.39.refs_4_.refs_17_), channel_id=1, source_target_pairs={{64,0},{128,64},{65,1},{129,65},{66,2},{130,66},{67,3},{131,67},{6... | collective-permute-start | bytes 393224 | tf_op jit(solution)/shard_map/ppermute | solution.py:300
  180.7 7.1 %copy-start.24 = (bf16[16,4096]{1,0:T(8,128)(2,1)}, bf16[16,4096]{1,0:T(8,128)(2,1)S(1)}, u32[]{:S(2)}) copy-start(bf16[16,4096]{1,0:T(8,128)(2,1)S(1)} %section_step.40.refs_4_.refs_18_) | copy-start | bytes 393220
  180.7 8.8 %collective-permute-start.29 = (bf16[16,4096]{1,0:T(8,128)(2,1)S(1)}, bf16[16,4096]{1,0:T(8,128)(2,1)S(1)}, u32[]{:S(2)}, u32[]{:S(2)}) collective-permute-start(bf16[16,4096]{1,0:T(8,128)(2,1)S(1)} %section_step.40.refs_4_.refs_18_), channel_id=1, source_target_pairs={{64,0},{65,1},{66,2},{67,3},{68,4},{69,5},{70,6},{71,7},{72,8},{73... | collective-permute-start | bytes 393224 | tf_op jit(solution)/shard_map/ppermute | solution.py:300
  192.9 29.2 %all-to-all-start.1 = ((bf16[16,64,512]{2,1,0:T(8,128)(2,1)}), bf16[16,64,512]{2,1,0:T(8,128)(2,1)}, u32[]{:S(2)}, u32[]{:S(2)}) async-start(bf16[16,64,512]{2,1,0:T(8,128)(2,1)} %bitcast.27), calls=%async_computation.1 | async-start | bytes 2097152 | tf_op jit(solution)/shard_map/all_to_all | solution.py:315
  203.3 7.7 %collective-permute-start.30 = (bf16[16,4096]{1,0:T(8,128)(2,1)S(1)}, bf16[16,4096]{1,0:T(8,128)(2,1)S(1)}, u32[]{:S(2)}, u32[]{:S(2)}) collective-permute-start(bf16[16,4096]{1,0:T(8,128)(2,1)S(1)} %section_step.41.refs_4_.refs_19_.refs_10_), channel_id=1, source_target_pairs={{64,0},{65,1},{66,2},{67,3},{68,4},{69,5},{70,6},{71,7},{72,8},{73... | collective-permute-start | bytes 393224 | tf_op jit(solution)/shard_map/ppermute | solution.py:300
  206.1 5.5 %copy-start.5 = (bf16[16,4096]{1,0:T(8,128)(2,1)S(1)}, bf16[16,4096]{1,0:T(8,128)(2,1)}, u32[]{:S(2)}) copy-start(bf16[16,4096]{1,0:T(8,128)(2,1)} %copy-done.4) | copy-start | bytes 393220
  206.1 5.5 %copy-start.7 = (bf16[16,4096]{1,0:T(8,128)(2,1)S(1)}, bf16[16,4096]{1,0:T(8,128)(2,1)}, u32[]{:S(2)}) copy-start(bf16[16,4096]{1,0:T(8,128)(2,1)} %copy-done.6) | copy-start | bytes 393220
  206.1 5.5 %copy-start.9 = (bf16[16,4096]{1,0:T(8,128)(2,1)S(1)}, bf16[16,4096]{1,0:T(8,128)(2,1)}, u32[]{:S(2)}) copy-start(bf16[16,4096]{1,0:T(8,128)(2,1)} %copy-done.8) | copy-start | bytes 393220
  206.1 5.5 %copy-start.11 = (bf16[16,4096]{1,0:T(8,128)(2,1)S(1)}, bf16[16,4096]{1,0:T(8,128)(2,1)}, u32[]{:S(2)}) copy-start(bf16[16,4096]{1,0:T(8,128)(2,1)} %copy-done.10) | copy-start | bytes 393220
  206.1 5.5 %copy-start.13 = (bf16[16,4096]{1,0:T(8,128)(2,1)S(1)}, bf16[16,4096]{1,0:T(8,128)(2,1)}, u32[]{:S(2)}) copy-start(bf16[16,4096]{1,0:T(8,128)(2,1)} %copy-done.12) | copy-start | bytes 393220
  206.1 5.5 %copy-start.15 = (bf16[16,4096]{1,0:T(8,128)(2,1)S(1)}, bf16[16,4096]{1,0:T(8,128)(2,1)}, u32[]{:S(2)}) copy-start(bf16[16,4096]{1,0:T(8,128)(2,1)} %copy-done.14) | copy-start | bytes 393220
  206.1 5.5 %copy-start.17 = (bf16[16,4096]{1,0:T(8,128)(2,1)S(1)}, bf16[16,4096]{1,0:T(8,128)(2,1)}, u32[]{:S(2)}) copy-start(bf16[16,4096]{1,0:T(8,128)(2,1)} %copy-done.16) | copy-start | bytes 393220
  206.1 5.5 %copy-start.19 = (bf16[16,4096]{1,0:T(8,128)(2,1)S(1)}, bf16[16,4096]{1,0:T(8,128)(2,1)}, u32[]{:S(2)}) copy-start(bf16[16,4096]{1,0:T(8,128)(2,1)} %copy-done.18) | copy-start | bytes 393220
  206.1 5.5 %copy-start.21 = (bf16[16,4096]{1,0:T(8,128)(2,1)S(1)}, bf16[16,4096]{1,0:T(8,128)(2,1)}, u32[]{:S(2)}) copy-start(bf16[16,4096]{1,0:T(8,128)(2,1)} %copy-done.20) | copy-start | bytes 393220
  206.2 5.5 %copy-start.23 = (bf16[16,4096]{1,0:T(8,128)(2,1)S(1)}, bf16[16,4096]{1,0:T(8,128)(2,1)}, u32[]{:S(2)}) copy-start(bf16[16,4096]{1,0:T(8,128)(2,1)} %copy-done.22) | copy-start | bytes 393220
  206.2 5.5 %copy-start.25 = (bf16[16,4096]{1,0:T(8,128)(2,1)S(1)}, bf16[16,4096]{1,0:T(8,128)(2,1)}, u32[]{:S(2)}) copy-start(bf16[16,4096]{1,0:T(8,128)(2,1)} %copy-done.24) | copy-start | bytes 393220
  206.2 5.5 %copy-start.27 = (bf16[16,4096]{1,0:T(8,128)(2,1)S(1)}, bf16[16,4096]{1,0:T(8,128)(2,1)}, u32[]{:S(2)}) copy-start(bf16[16,4096]{1,0:T(8,128)(2,1)} %copy-done.26) | copy-start | bytes 393220
  206.2 5.5 %copy-start.29 = (bf16[16,4096]{1,0:T(8,128)(2,1)S(1)}, bf16[16,4096]{1,0:T(8,128)(2,1)}, u32[]{:S(2)}) copy-start(bf16[16,4096]{1,0:T(8,128)(2,1)} %copy-done.28) | copy-start | bytes 393220
  206.2 5.5 %copy-start.31 = (bf16[16,4096]{1,0:T(8,128)(2,1)S(1)}, bf16[16,4096]{1,0:T(8,128)(2,1)}, u32[]{:S(2)}) copy-start(bf16[16,4096]{1,0:T(8,128)(2,1)} %copy-done.30) | copy-start | bytes 393220
  206.2 5.5 %copy-start.33 = (bf16[16,4096]{1,0:T(8,128)(2,1)S(1)}, bf16[16,4096]{1,0:T(8,128)(2,1)}, u32[]{:S(2)}) copy-start(bf16[16,4096]{1,0:T(8,128)(2,1)} %copy-done.32) | copy-start | bytes 393220
  206.2 5.5 %copy-start.35 = (bf16[16,4096]{1,0:T(8,128)(2,1)S(1)}, bf16[16,4096]{1,0:T(8,128)(2,1)}, u32[]{:S(2)}) copy-start(bf16[16,4096]{1,0:T(8,128)(2,1)} %copy-done.34) | copy-start | bytes 393220
  206.2 5.5 %copy-start.37 = (bf16[16,4096]{1,0:T(8,128)(2,1)S(1)}, bf16[16,4096]{1,0:T(8,128)(2,1)}, u32[]{:S(2)}) copy-start(bf16[16,4096]{1,0:T(8,128)(2,1)} %copy-done.36) | copy-start | bytes 393220
  (11 other events, 18.9 us)

commit v7 on v5

--- a/solution.py
+++ b/solution.py
@@ -12,7 +12,8 @@
 ROWS = 16
 SLACK = 2
 FAR = 2
-HIDDEN_BY = 11
+HIDDEN_AT = 5
+HIDDEN_BY = 12
 DP = ("dp_0", "dp_1", "dp_2", "dp_3")
 IN_VMEM = pl.BlockSpec(memory_space=pltpu.VMEM)
 IN_SMEM = pl.BlockSpec(memory_space=pltpu.SMEM)
@@ -39,19 +40,7 @@
     )(*operands)
 
 
-def held_until(value, token):
-    return pl.pallas_call(
-        lambda value_ref, token_ref, out_ref: None,
-        out_shape=jax.ShapeDtypeStruct(value.shape, value.dtype),
-        in_specs=[ANYWHERE, IN_VMEM],
-        out_specs=ANYWHERE,
-        input_output_aliases={0: 0},
-        compiler_params=pltpu.CompilerParams(vmem_limit_bytes=2**20),
-        name="held_until",
-    )(value, token)
-
-
-def norm_kernel(where, x_ref, g_ref, tiles_ref):
+def norm_kernel(where, x_ref, g_ref, turn_ref, tiles_ref):
     _, tok, width = x_ref.shape
     across, _, _, part = tiles_ref.shape
     near = width // (across * FAR)
@@ -197,13 +186,6 @@
 
     mine = copy_for_each(w_value[0], DP[:3])
     other = lax.ppermute(mine, DP[3], [(0, 1), (1, 0)])
-    tiles = kernel_call(
-        norm_kernel,
-        "normalize",
-        shape((across, 2, tok, width // across), BF16),
-        [IN_SMEM] + [IN_VMEM] * 2,
-        (where, x, gain),
-    )
     w_mat = kernel_call(
         rows_kernel,
         "rows",
@@ -219,12 +201,15 @@
         if incoming is None:
             incoming = jnp.zeros((ROWS, width), BF16)
         later = tuple(hidden[1:]) if step == HIDDEN_BY else ()
+        turn = gv_parts[-1:]
+        if step in (1, 3, 5):
+            turn = [*turn, sent[step - 1]]
         dx, dv = kernel_call(
             functools.partial(step_kernel, step, npipe, blocks),
             "section_step",
             (shape((ROWS, width), BF16), shape((ROWS, kv_width), BF16)),
-            [IN_SMEM] + [IN_VMEM] * (5 + min(step, 1)) + [ANYWHERE] * len(later),
-            (where, w_mat, x, gain, grad_out, incoming, *gv_parts[-1:], *later),
+            [IN_SMEM] + [IN_VMEM] * (5 + len(turn)) + [ANYWHERE] * len(later),
+            (where, w_mat, x, gain, grad_out, incoming, *turn, *later),
         )
         gx_parts.append(dx)
         gv_parts.append(dv)
@@ -235,8 +220,15 @@
                 pairs.append((source, (source - 1) % npipe))
         if pairs:
             sent[step] = lax.ppermute(dx, "pipe", pairs)
-        if step == 4:
-            hidden = exchanged(held_until(tiles, dv), "dp_1")
+        if step == HIDDEN_AT:
+            tiles = kernel_call(
+                norm_kernel,
+                "normalize",
+                shape((across, 2, tok, width // across), BF16),
+                [IN_SMEM] + [IN_VMEM] * 3,
+                (where, x, gain, dv),
+            )
+            hidden = exchanged(tiles, "dp_1")
 
     grad_x = kernel_call(
         functools.partial(collect_kernel, npipe, blocks),

time: 226 us -> 238 us (1.053)
  starting transfers between devices: 67.1 us -> 73.9 us
  waiting for transfers between devices: 75.5 us -> 79.5 us
    ppermute x20, starting transfers between devices: 40 us -> 46.5 us  [on_device(): sent[step] = lax.ppermute(dx, 'pipe', pairs)]
    ppermute x20, waiting for transfers between devices: 52.4 us -> 57.1 us  [on_device(): sent[step] = lax.ppermute(dx, 'pipe', pairs)]
  transfers between devices with their start and end apart: 28 -> 28, of which waited for: 14 -> 16; matrix products, arithmetic and copies ran while one was open for 0% -> 0% of each run, Pallas kernels for 16% -> 13%
where the time goes in v7:
time: 238 us; the launch traced here: 237 us
  waiting for transfers between devices  79.5 us (33%)
  starting transfers between devices  73.9 us (31%)
  Pallas kernels  43.6 us (18%)
  blocking collectives  35.2 us (15%)
    ppermute x20, waiting for transfers between devices, on_device(): sent[step] = lax.ppermute(dx, 'pipe', pairs)  57.1 us
    ppermute x20, starting transfers between devices, on_device(): sent[step] = lax.ppermute(dx, 'pipe', pairs)  46.5 us
    pallas_call x27, Pallas kernels, kernel_call(): pl.pallas_call(kernel, out_shape=out_shape, in_specs=specs, out_specs=jax...  43.6 us
    all_to_all x1, blocking collectives, copy_for_each(): lax.all_to_all(jnp.broadcast_to(array[None], (count, *array.shape)), axis...  35.2 us
    all_to_all x1, waiting for transfers between devices, on_device(): landed = lax.all_to_all(pieces, others, 0, 0, tiled=True)  13.9 us
    ppermute x6, starting transfers between devices, exchanged(): moved.append(lax.ppermute(pieces[shift], axis, pairs))  12.6 us
    all_to_all x1, starting transfers between devices, on_device(): landed = lax.all_to_all(pieces, others, 0, 0, tiled=True)  12.2 us
  transfers between devices with their start and end apart: 28, of which 16 were waited for; matrix products, arithmetic and copies ran while one was open for 0% of the time, Pallas kernels for 13%

profile of v7, /device:TPU:1, one launch (start us, length us, event | category | flops | bytes accessed | tf_op | source)
XLA Modules:
  0.0 236.6 jit_solution(10776865339159569140)
XLA Ops:
  0.6 1.1 broadcast_in_dim.14
  1.7 35.2 %all_to_all.10.mine_ref = bf16[32,64,512]{2,1,0:T(8,128)(2,1)S(1)} all-to-all(bf16[32,64,512]{2,1,0:T(8,128)(2,1)S(1)} %broadcast_in_dim.14), channel_id=1, replica_groups=mesh['pipe'=4,'dp_0'=2,'dp_1'=4,'dp_2'=4,'dp_3'=2] {'dp_0','dp_1','dp_2'}, dimensions={0} | all-to-all | bytes 4194304 | tf_op jit(solution)/shard_map/all_to_all | solution.py:26
  36.9 2.5 %collective-permute-start = (bf16[32,64,512]{2,1,0:T(8,128)(2,1)S(1)}, bf16[32,64,512]{2,1,0:T(8,128)(2,1)}, u32[]{:S(2)}, u32[]{:S(2)}) collective-permute-start(bf16[32,64,512]{2,1,0:T(8,128)(2,1)S(1)} %all_to_all.10.mine_ref), channel_id=1, source_target_pairs={{0,1},{1,0},{2,3},{3,2},{4,5},{5,4},{6,7},{7,6},{8,9},{9,8},{10,11... | collective-permute-start | bytes 6291464 | tf_op jit(solution)/shard_map/ppermute | solution.py:188
  39.5 3.8 %collective-permute-done.other_ref = bf16[32,64,512]{2,1,0:T(8,128)(2,1)} collective-permute-done((bf16[32,64,512]{2,1,0:T(8,128)(2,1)S(1)}, bf16[32,64,512]{2,1,0:T(8,128)(2,1)}, u32[]{:S(2)}, u32[]{:S(2)}) %collective-permute-start) | collective-permute-done | bytes 2097184 | tf_op jit(solution)/shard_map/ppermute | solution.py:188
  43.3 1.9 rows.1.w_ref
  45.8 0.7 collective-permute-start.1
  47.6 0.7 collective-permute-start.3
  50.1 1.3 collective-permute-start.5
  52.1 26.6 %collective-permute-done.5.refs_1_.in_ref = bf16[16,4096]{1,0:T(8,128)(2,1)S(1)} collective-permute-done((bf16[16,4096]{1,0:T(8,128)(2,1)S(1)}, bf16[16,4096]{1,0:T(8,128)(2,1)S(1)}, u32[]{:S(2)}, u32[]{:S(2)}) %collective-permute-start.5) | collective-permute-done | bytes 131104 | tf_op jit(solution)/shard_map/ppermute | solution.py:222
  79.3 2.0 normalize.1
  81.3 1.3 collective-permute-start.6
  82.8 0.8 collective-permute-start.12
  83.6 1.6 collective-permute-start.13
  85.2 0.9 collective-permute-start.14
  86.1 1.9 section_step.28
  88.0 17.8 %collective-permute-start.7 = (bf16[16,4096]{1,0:T(8,128)(2,1)S(1)}, bf16[16,4096]{1,0:T(8,128)(2,1)S(1)}, u32[]{:S(2)}, u32[]{:S(2)}) collective-permute-start(bf16[16,4096]{1,0:T(8,128)(2,1)S(1)} %get-tuple-element.58.refs_6_), channel_id=1, source_target_pairs={{0,192},{64,0},{128,64},{192,128},{1,193},{65,1},{129,65},{193,129... | collective-permute-start | bytes 393224 | tf_op jit(solution)/shard_map/ppermute | solution.py:222
  105.8 1.9 section_step.29
  107.6 2.2 collective-permute-start.8
  109.9 1.9 section_step.30
  111.8 3.5 %collective-permute-start.9 = (bf16[16,4096]{1,0:T(8,128)(2,1)S(1)}, bf16[16,4096]{1,0:T(8,128)(2,1)S(1)}, u32[]{:S(2)}, u32[]{:S(2)}) collective-permute-start(bf16[16,4096]{1,0:T(8,128)(2,1)S(1)} %get-tuple-element.62.refs_8_), channel_id=1, source_target_pairs={{0,192},{64,0},{128,64},{192,128},{1,193},{65,1},{129,65},{193,129... | collective-permute-start | bytes 393224 | tf_op jit(solution)/shard_map/ppermute | solution.py:222
  115.3 1.9 section_step.31
  117.2 3.1 %collective-permute-start.10 = (bf16[16,4096]{1,0:T(8,128)(2,1)S(1)}, bf16[16,4096]{1,0:T(8,128)(2,1)S(1)}, u32[]{:S(2)}, u32[]{:S(2)}) collective-permute-start(bf16[16,4096]{1,0:T(8,128)(2,1)S(1)} %get-tuple-element.64.refs_9_), channel_id=1, source_target_pairs={{0,192},{64,0},{128,64},{192,128},{1,193},{65,1},{129,65},{193,129... | collective-permute-start | bytes 393224 | tf_op jit(solution)/shard_map/ppermute | solution.py:222
  120.3 0.7 collective-permute-done.9.in_ref
  121.0 1.9 section_step.32
  122.9 2.5 %collective-permute-start.11 = (bf16[16,4096]{1,0:T(8,128)(2,1)S(1)}, bf16[16,4096]{1,0:T(8,128)(2,1)S(1)}, u32[]{:S(2)}, u32[]{:S(2)}) collective-permute-start(bf16[16,4096]{1,0:T(8,128)(2,1)S(1)} %get-tuple-element.66.refs_10_), channel_id=1, source_target_pairs={{0,192},{64,0},{128,64},{192,128},{1,193},{65,1},{129,65},{193,129... | collective-permute-start | bytes 393224 | tf_op jit(solution)/shard_map/ppermute | solution.py:222
  125.3 1.0 collective-permute-done.10.in_ref
  126.4 1.9 section_step.33
  128.2 2.2 collective-permute-start.15
  130.5 2.7 %collective-permute-done.11.in_ref = bf16[16,4096]{1,0:T(8,128)(2,1)S(1)} collective-permute-done((bf16[16,4096]{1,0:T(8,128)(2,1)S(1)}, bf16[16,4096]{1,0:T(8,128)(2,1)S(1)}, u32[]{:S(2)}, u32[]{:S(2)}) %collective-permute-start.11) | collective-permute-done | bytes 131104 | tf_op jit(solution)/shard_map/ppermute | solution.py:222
  133.2 1.9 section_step.34
  135.1 1.7 collective-permute-start.16
  136.8 1.6 collective-permute-done.15.in_ref
  138.4 1.9 section_step.35
  140.7 3.2 %collective-permute-done.16.in_ref = bf16[16,4096]{1,0:T(8,128)(2,1)S(1)} collective-permute-done((bf16[16,4096]{1,0:T(8,128)(2,1)S(1)}, bf16[16,4096]{1,0:T(8,128)(2,1)S(1)}, u32[]{:S(2)}, u32[]{:S(2)}) %collective-permute-start.16) | collective-permute-done | bytes 131104 | tf_op jit(solution)/shard_map/ppermute | solution.py:222
  143.9 1.9 section_step.36
  145.8 1.3 collective-permute-start.18
  147.1 2.0 collective-permute-done.17.in_ref
  149.1 1.9 section_step.37
  150.9 1.3 collective-permute-start.19
  152.2 1.9 collective-permute-done.18.in_ref
  154.2 1.9 section_step.38
  156.1 1.3 collective-permute-start.20
  157.6 1.9 section_step.39
  159.5 1.3 collective-permute-start.21
  160.8 8.5 %collective-permute-done.20.in_ref = bf16[16,4096]{1,0:T(8,128)(2,1)S(1)} collective-permute-done((bf16[16,4096]{1,0:T(8,128)(2,1)S(1)}, bf16[16,4096]{1,0:T(8,128)(2,1)S(1)}, u32[]{:S(2)}, u32[]{:S(2)}) %collective-permute-start.20) | collective-permute-done | bytes 131104 | tf_op jit(solution)/shard_map/ppermute | solution.py:222
  169.3 1.9 section_step.40
  171.2 1.3 collective-permute-start.22
  172.5 2.1 collective-permute-done.21.in_ref
  174.5 1.9 section_step.41
  176.4 1.3 collective-permute-start.23
  177.7 4.3 %collective-permute-done.22.in_ref = bf16[16,4096]{1,0:T(8,128)(2,1)S(1)} collective-permute-done((bf16[16,4096]{1,0:T(8,128)(2,1)S(1)}, bf16[16,4096]{1,0:T(8,128)(2,1)S(1)}, u32[]{:S(2)}, u32[]{:S(2)}) %collective-permute-start.22) | collective-permute-done | bytes 131104 | tf_op jit(solution)/shard_map/ppermute | solution.py:222
  182.0 1.9 section_step.42
  183.9 2.3 collective-permute-done.23.in_ref
  186.2 2.1 section_step.43
  188.3 0.7 stack.17.refs_4_
  189.0 2.2 collective-permute-start.24
  191.2 5.2 %collective-permute-start.25 = (bf16[256,512]{1,0:T(8,128)(2,1)S(1)}, bf16[256,512]{1,0:T(8,128)(2,1)S(1)}, u32[]{:S(2)}, u32[]{:S(2)}) collective-permute-start(bf16[256,512]{1,0:T(8,128)(2,1)S(1)} %stack.17.refs_4_), channel_id=1, source_target_pairs={{0,16},{8,24},{16,0},{24,8},{1,17},{9,25},{17,1},{25,9},{2,18},{10... | collective-permute-start | bytes 786440 | tf_op jit(solution)/shard_map/ppermute | solution.py:173
  196.4 2.0 collective-permute-start.26
  198.4 4.6 %collective-permute-done.25.refs_6_ = bf16[256,512]{1,0:T(8,128)(2,1)S(1)} collective-permute-done((bf16[256,512]{1,0:T(8,128)(2,1)S(1)}, bf16[256,512]{1,0:T(8,128)(2,1)S(1)}, u32[]{:S(2)}, u32[]{:S(2)}) %collective-permute-start.25) | collective-permute-done | bytes 262176 | tf_op jit(solution)/shard_map/ppermute | solution.py:173
  203.0 3.3 %part.1 = bf16[1024,512]{1,0:T(8,128)(2,1)} custom-call(bf16[2,128,1024]{2,1,0:T(8,128)(2,1)S(1)} %get-tuple-element.92.refs_0_, bf16[2,128,1024]{2,1,0:T(8,128)(2,1)S(1)} %collective-permute-done.12.refs_1_, bf16[2,128,1024]{2,1,0:T(8,128)(2,1)S(1)} %collective-permute-done.13.refs_2_, bf16[2,128,1024]{2,1,0:T(8,128)(2,1)S(1)} %collective-permute-done.14.refs_3_, ...), custom_call_target="tpu_custom_call" | custom-call | tf_op jit(solution)/shard_map/part/pallas_call | solution.py:32
  206.3 12.2 %all-to-all-start.1 = ((bf16[16,64,512]{2,1,0:T(8,128)(2,1)}), bf16[16,64,512]{2,1,0:T(8,128)(2,1)}, u32[]{:S(2)}, u32[]{:S(2)}) async-start(bf16[16,64,512]{2,1,0:T(8,128)(2,1)} %bitcast.11), calls=%async_computation.1 | async-start | bytes 2097152 | tf_op jit(solution)/shard_map/all_to_all | solution.py:259
  218.6 2.1 collect_rows.1
  220.7 13.9 %all-to-all-done.1 = bf16[16,64,512]{2,1,0:T(8,128)(2,1)} async-done(((bf16[16,64,512]{2,1,0:T(8,128)(2,1)}), bf16[16,64,512]{2,1,0:T(8,128)(2,1)}, u32[]{:S(2)}, u32[]{:S(2)}) %all-to-all-start.1) | async-done | bytes 1048608 | tf_op jit(solution)/shard_map/all_to_all | solution.py:259
  234.6 2.0 convert_reduce_fusion
  (31 shorter events, 5.7 us)
Async XLA Ops:
  36.9 6.4 %collective-permute-start = (bf16[32,64,512]{2,1,0:T(8,128)(2,1)S(1)}, bf16[32,64,512]{2,1,0:T(8,128)(2,1)}, u32[]{:S(2)}, u32[]{:S(2)}) collective-permute-start(bf16[32,64,512]{2,1,0:T(8,128)(2,1)S(1)} %all_to_all.10.mine_ref), channel_id=1, source_target_pairs={{0,1},{1,0},{2,3},{3,2},{4,5},{5,4},{6,7},{7,6},{8,9},{9,8},{10,11... | collective-permute-start | bytes 6291464 | tf_op jit(solution)/shard_map/ppermute | solution.py:188
  39.5 5.7 %copy-start = (bf16[2,1,128,4096]{3,2,1,0:T(8,128)(2,1)S(1)}, bf16[2,1,128,4096]{3,2,1,0:T(8,128)(2,1)}, u32[]{:S(2)}) copy-start(bf16[2,1,128,4096]{3,2,1,0:T(8,128)(2,1)} %param.4) | copy-start | bytes 6291460
  39.5 5.8 %copy-start.1 = (bf16[128,4096]{1,0:T(8,128)(2,1)S(1)}, bf16[128,4096]{1,0:T(8,128)(2,1)}, u32[]{:S(2)}) copy-start(bf16[128,4096]{1,0:T(8,128)(2,1)} %fresh_ref.43) | copy-start | bytes 3145732
  39.5 5.8 %copy-start.2 = (f32[2,1,4096]{2,1,0:T(1,128)S(1)}, f32[2,1,4096]{2,1,0:T(1,128)}, u32[]{:S(2)}) copy-start(f32[2,1,4096]{2,1,0:T(1,128)} %g_ref.45) | copy-start | bytes 98308
  45.8 0.7 collective-permute-start.1
  47.6 1.4 collective-permute-start.3
  48.3 0.7 collective-permute-start.2
  50.1 28.6 %collective-permute-start.5 = (bf16[16,4096]{1,0:T(8,128)(2,1)S(1)}, bf16[16,4096]{1,0:T(8,128)(2,1)S(1)}, u32[]{:S(2)}, u32[]{:S(2)}) collective-permute-start(bf16[16,4096]{1,0:T(8,128)(2,1)S(1)} %get-tuple-element.54.refs_4_), channel_id=1, source_target_pairs={{64,0},{128,64},{192,128},{65,1},{129,65},{193,129},{66,2},{130,66... | collective-permute-start | bytes 393224 | tf_op jit(solution)/shard_map/ppermute | solution.py:222
  51.4 27.3 %collective-permute-start.4 = (bf16[16,4096]{1,0:T(8,128)(2,1)S(1)}, bf16[16,4096]{1,0:T(8,128)(2,1)S(1)}, u32[]{:S(2)}, u32[]{:S(2)}) collective-permute-start(bf16[16,4096]{1,0:T(8,128)(2,1)S(1)} %get-tuple-element.52.refs_3_), channel_id=1, source_target_pairs={{128,64},{192,128},{129,65},{193,129},{130,66},{194,130},{131,67},... | collective-permute-start | bytes 393224 | tf_op jit(solution)/shard_map/ppermute | solution.py:222
  81.3 24.4 %collective-permute-start.6 = (bf16[16,4096]{1,0:T(8,128)(2,1)S(1)}, bf16[16,4096]{1,0:T(8,128)(2,1)S(1)}, u32[]{:S(2)}, u32[]{:S(2)}) collective-permute-start(bf16[16,4096]{1,0:T(8,128)(2,1)S(1)} %get-tuple-element.56.refs_5_), channel_id=1, source_target_pairs={{64,0},{128,64},{192,128},{65,1},{129,65},{193,129},{66,2},{130,66... | collective-permute-start | bytes 393224 | tf_op jit(solution)/shard_map/ppermute | solution.py:222
  82.8 50.4 %collective-permute-start.12 = (bf16[2,128,1024]{2,1,0:T(8,128)(2,1)S(1)}, bf16[2,128,1024]{2,1,0:T(8,128)(2,1)S(1)}, u32[]{:S(2)}, u32[]{:S(2)}) collective-permute-start(bf16[2,128,1024]{2,1,0:T(8,128)(2,1)S(1)} %get-tuple-element.95), channel_id=1, source_target_pairs={{0,8},{8,16},{16,24},{24,0},{1,9},{9,17},{17,25},{25,1},{2,10},{10... | collective-permute-start | bytes 1572872 | tf_op jit(solution)/shard_map/ppermute | solution.py:173
  83.6 49.6 %collective-permute-start.13 = (bf16[2,128,1024]{2,1,0:T(8,128)(2,1)S(1)}, bf16[2,128,1024]{2,1,0:T(8,128)(2,1)S(1)}, u32[]{:S(2)}, u32[]{:S(2)}) collective-permute-start(bf16[2,128,1024]{2,1,0:T(8,128)(2,1)S(1)} %get-tuple-element.94), channel_id=1, source_target_pairs={{0,16},{8,24},{16,0},{24,8},{1,17},{9,25},{17,1},{25,9},{2,18},{10... | collective-permute-start | bytes 1572872 | tf_op jit(solution)/shard_map/ppermute | solution.py:173
  85.2 48.0 %collective-permute-start.14 = (bf16[2,128,1024]{2,1,0:T(8,128)(2,1)S(1)}, bf16[2,128,1024]{2,1,0:T(8,128)(2,1)S(1)}, u32[]{:S(2)}, u32[]{:S(2)}) collective-permute-start(bf16[2,128,1024]{2,1,0:T(8,128)(2,1)S(1)} %get-tuple-element.93), channel_id=1, source_target_pairs={{0,24},{8,0},{16,8},{24,16},{1,25},{9,1},{17,9},{25,17},{2,26},{10... | collective-permute-start | bytes 1572872 | tf_op jit(solution)/shard_map/ppermute | solution.py:173
  88.0 21.9 %collective-permute-start.7 = (bf16[16,4096]{1,0:T(8,128)(2,1)S(1)}, bf16[16,4096]{1,0:T(8,128)(2,1)S(1)}, u32[]{:S(2)}, u32[]{:S(2)}) collective-permute-start(bf16[16,4096]{1,0:T(8,128)(2,1)S(1)} %get-tuple-element.58.refs_6_), channel_id=1, source_target_pairs={{0,192},{64,0},{128,64},{192,128},{1,193},{65,1},{129,65},{193,129... | collective-permute-start | bytes 393224 | tf_op jit(solution)/shard_map/ppermute | solution.py:222
  107.6 7.6 %collective-permute-start.8 = (bf16[16,4096]{1,0:T(8,128)(2,1)S(1)}, bf16[16,4096]{1,0:T(8,128)(2,1)S(1)}, u32[]{:S(2)}, u32[]{:S(2)}) collective-permute-start(bf16[16,4096]{1,0:T(8,128)(2,1)S(1)} %get-tuple-element.60.refs_7_), channel_id=1, source_target_pairs={{0,192},{64,0},{128,64},{192,128},{1,193},{65,1},{129,65},{193,129... | collective-permute-start | bytes 393224 | tf_op jit(solution)/shard_map/ppermute | solution.py:222
  111.8 9.2 %collective-permute-start.9 = (bf16[16,4096]{1,0:T(8,128)(2,1)S(1)}, bf16[16,4096]{1,0:T(8,128)(2,1)S(1)}, u32[]{:S(2)}, u32[]{:S(2)}) collective-permute-start(bf16[16,4096]{1,0:T(8,128)(2,1)S(1)} %get-tuple-element.62.refs_8_), channel_id=1, source_target_pairs={{0,192},{64,0},{128,64},{192,128},{1,193},{65,1},{129,65},{193,129... | collective-permute-start | bytes 393224 | tf_op jit(solution)/shard_map/ppermute | solution.py:222
  117.2 9.2 %collective-permute-start.10 = (bf16[16,4096]{1,0:T(8,128)(2,1)S(1)}, bf16[16,4096]{1,0:T(8,128)(2,1)S(1)}, u32[]{:S(2)}, u32[]{:S(2)}) collective-permute-start(bf16[16,4096]{1,0:T(8,128)(2,1)S(1)} %get-tuple-element.64.refs_9_), channel_id=1, source_target_pairs={{0,192},{64,0},{128,64},{192,128},{1,193},{65,1},{129,65},{193,129... | collective-permute-start | bytes 393224 | tf_op jit(solution)/shard_map/ppermute | solution.py:222
  122.9 10.3 %collective-permute-start.11 = (bf16[16,4096]{1,0:T(8,128)(2,1)S(1)}, bf16[16,4096]{1,0:T(8,128)(2,1)S(1)}, u32[]{:S(2)}, u32[]{:S(2)}) collective-permute-start(bf16[16,4096]{1,0:T(8,128)(2,1)S(1)} %get-tuple-element.66.refs_10_), channel_id=1, source_target_pairs={{0,192},{64,0},{128,64},{192,128},{1,193},{65,1},{129,65},{193,129... | collective-permute-start | bytes 393224 | tf_op jit(solution)/shard_map/ppermute | solution.py:222
  128.2 10.1 %collective-permute-start.15 = (bf16[16,4096]{1,0:T(8,128)(2,1)S(1)}, bf16[16,4096]{1,0:T(8,128)(2,1)S(1)}, u32[]{:S(2)}, u32[]{:S(2)}) collective-permute-start(bf16[16,4096]{1,0:T(8,128)(2,1)S(1)} %get-tuple-element.68.refs_11_), channel_id=1, source_target_pairs={{0,192},{64,0},{128,64},{192,128},{1,193},{65,1},{129,65},{193,129... | collective-permute-start | bytes 393224 | tf_op jit(solution)/shard_map/ppermute | solution.py:222
  135.1 8.8 %collective-permute-start.16 = (bf16[16,4096]{1,0:T(8,128)(2,1)S(1)}, bf16[16,4096]{1,0:T(8,128)(2,1)S(1)}, u32[]{:S(2)}, u32[]{:S(2)}) collective-permute-start(bf16[16,4096]{1,0:T(8,128)(2,1)S(1)} %get-tuple-element.70.refs_12_), channel_id=1, source_target_pairs={{0,192},{64,0},{128,64},{192,128},{1,193},{65,1},{129,65},{193,129... | collective-permute-start | bytes 393224 | tf_op jit(solution)/shard_map/ppermute | solution.py:222
  140.3 8.8 %collective-permute-start.17 = (bf16[16,4096]{1,0:T(8,128)(2,1)S(1)}, bf16[16,4096]{1,0:T(8,128)(2,1)S(1)}, u32[]{:S(2)}, u32[]{:S(2)}) collective-permute-start(bf16[16,4096]{1,0:T(8,128)(2,1)S(1)} %get-tuple-element.72.refs_13_), channel_id=1, source_target_pairs={{0,192},{64,0},{128,64},{192,128},{1,193},{65,1},{129,65},{193,129... | collective-permute-start | bytes 393224 | tf_op jit(solution)/shard_map/ppermute | solution.py:222
  145.8 8.4 %collective-permute-start.18 = (bf16[16,4096]{1,0:T(8,128)(2,1)S(1)}, bf16[16,4096]{1,0:T(8,128)(2,1)S(1)}, u32[]{:S(2)}, u32[]{:S(2)}) collective-permute-start(bf16[16,4096]{1,0:T(8,128)(2,1)S(1)} %get-tuple-element.74.refs_14_), channel_id=1, source_target_pairs={{64,0},{128,64},{192,128},{65,1},{129,65},{193,129},{66,2},{130,66... | collective-permute-start | bytes 393224 | tf_op jit(solution)/shard_map/ppermute | solution.py:222
  150.9 6.7 %collective-permute-start.19 = (bf16[16,4096]{1,0:T(8,128)(2,1)S(1)}, bf16[16,4096]{1,0:T(8,128)(2,1)S(1)}, u32[]{:S(2)}, u32[]{:S(2)}) collective-permute-start(bf16[16,4096]{1,0:T(8,128)(2,1)S(1)} %get-tuple-element.76.refs_15_), channel_id=1, source_target_pairs={{64,0},{128,64},{192,128},{65,1},{129,65},{193,129},{66,2},{130,66... | collective-permute-start | bytes 393224 | tf_op jit(solution)/shard_map/ppermute | solution.py:222
  156.1 13.2 %collective-permute-start.20 = (bf16[16,4096]{1,0:T(8,128)(2,1)S(1)}, bf16[16,4096]{1,0:T(8,128)(2,1)S(1)}, u32[]{:S(2)}, u32[]{:S(2)}) collective-permute-start(bf16[16,4096]{1,0:T(8,128)(2,1)S(1)} %get-tuple-element.78.refs_16_), channel_id=1, source_target_pairs={{64,0},{128,64},{65,1},{129,65},{66,2},{130,66},{67,3},{131,67},{6... | collective-permute-start | bytes 393224 | tf_op jit(solution)/shard_map/ppermute | solution.py:222
  159.5 15.0 %collective-permute-start.21 = (bf16[16,4096]{1,0:T(8,128)(2,1)S(1)}, bf16[16,4096]{1,0:T(8,128)(2,1)S(1)}, u32[]{:S(2)}, u32[]{:S(2)}) collective-permute-start(bf16[16,4096]{1,0:T(8,128)(2,1)S(1)} %get-tuple-element.80.refs_17_), channel_id=1, source_target_pairs={{64,0},{128,64},{65,1},{129,65},{66,2},{130,66},{67,3},{131,67},{6... | collective-permute-start | bytes 393224 | tf_op jit(solution)/shard_map/ppermute | solution.py:222
  171.2 10.8 %collective-permute-start.22 = (bf16[16,4096]{1,0:T(8,128)(2,1)S(1)}, bf16[16,4096]{1,0:T(8,128)(2,1)S(1)}, u32[]{:S(2)}, u32[]{:S(2)}) collective-permute-start(bf16[16,4096]{1,0:T(8,128)(2,1)S(1)} %get-tuple-element.82.refs_18_), channel_id=1, source_target_pairs={{64,0},{65,1},{66,2},{67,3},{68,4},{69,5},{70,6},{71,7},{72,8},{73... | collective-permute-start | bytes 393224 | tf_op jit(solution)/shard_map/ppermute | solution.py:222
  176.4 9.8 %collective-permute-start.23 = (bf16[16,4096]{1,0:T(8,128)(2,1)S(1)}, bf16[16,4096]{1,0:T(8,128)(2,1)S(1)}, u32[]{:S(2)}, u32[]{:S(2)}) collective-permute-start(bf16[16,4096]{1,0:T(8,128)(2,1)S(1)} %get-tuple-element.84.refs_19_), channel_id=1, source_target_pairs={{64,0},{65,1},{66,2},{67,3},{68,4},{69,5},{70,6},{71,7},{72,8},{73... | collective-permute-start | bytes 393224 | tf_op jit(solution)/shard_map/ppermute | solution.py:222
  189.0 9.4 %collective-permute-start.24 = (bf16[256,512]{1,0:T(8,128)(2,1)S(1)}, bf16[256,512]{1,0:T(8,128)(2,1)S(1)}, u32[]{:S(2)}, u32[]{:S(2)}) collective-permute-start(bf16[256,512]{1,0:T(8,128)(2,1)S(1)} %stack.17.refs_4_), channel_id=1, source_target_pairs={{0,8},{8,16},{16,24},{24,0},{1,9},{9,17},{17,25},{25,1},{2,10},{10... | collective-permute-start | bytes 786440 | tf_op jit(solution)/shard_map/ppermute | solution.py:173
  191.2 11.7 %collective-permute-start.25 = (bf16[256,512]{1,0:T(8,128)(2,1)S(1)}, bf16[256,512]{1,0:T(8,128)(2,1)S(1)}, u32[]{:S(2)}, u32[]{:S(2)}) collective-permute-start(bf16[256,512]{1,0:T(8,128)(2,1)S(1)} %stack.17.refs_4_), channel_id=1, source_target_pairs={{0,16},{8,24},{16,0},{24,8},{1,17},{9,25},{17,1},{25,9},{2,18},{10... | collective-permute-start | bytes 786440 | tf_op jit(solution)/shard_map/ppermute | solution.py:173
  196.4 6.6 %collective-permute-start.26 = (bf16[256,512]{1,0:T(8,128)(2,1)S(1)}, bf16[256,512]{1,0:T(8,128)(2,1)S(1)}, u32[]{:S(2)}, u32[]{:S(2)}) collective-permute-start(bf16[256,512]{1,0:T(8,128)(2,1)S(1)} %stack.17.refs_4_), channel_id=1, source_target_pairs={{0,24},{8,0},{16,8},{24,16},{1,25},{9,1},{17,9},{25,17},{2,26},{10... | collective-permute-start | bytes 786440 | tf_op jit(solution)/shard_map/ppermute | solution.py:173
  206.3 28.2 %all-to-all-start.1 = ((bf16[16,64,512]{2,1,0:T(8,128)(2,1)}), bf16[16,64,512]{2,1,0:T(8,128)(2,1)}, u32[]{:S(2)}, u32[]{:S(2)}) async-start(bf16[16,64,512]{2,1,0:T(8,128)(2,1)} %bitcast.11), calls=%async_computation.1 | async-start | bytes 2097152 | tf_op jit(solution)/shard_map/all_to_all | solution.py:259

commit v8 on v5

--- a/solution.py
+++ b/solution.py
@@ -12,7 +12,9 @@
 ROWS = 16
 SLACK = 2
 FAR = 2
-HIDDEN_BY = 11
+HIDDEN_BY = 6
+EARLY = 8
+EARLY_BY = 18
 DP = ("dp_0", "dp_1", "dp_2", "dp_3")
 IN_VMEM = pl.BlockSpec(memory_space=pltpu.VMEM)
 IN_SMEM = pl.BlockSpec(memory_space=pltpu.SMEM)
@@ -43,7 +45,7 @@
     return pl.pallas_call(
         lambda value_ref, token_ref, out_ref: None,
         out_shape=jax.ShapeDtypeStruct(value.shape, value.dtype),
-        in_specs=[ANYWHERE, IN_VMEM],
+        in_specs=[ANYWHERE, ANYWHERE],
         out_specs=ANYWHERE,
         input_output_aliases={0: 0},
         compiler_params=pltpu.CompilerParams(vmem_limit_bytes=2**20),
@@ -51,9 +53,10 @@
     )(value, token)
 
 
-def norm_kernel(where, x_ref, g_ref, tiles_ref):
+def norm_kernel(where, x_ref, g_ref, *refs):
+    *tiles, hidden_ref = refs
     _, tok, width = x_ref.shape
-    across, _, _, part = tiles_ref.shape
+    across = len(tiles)
     near = width // (across * FAR)
 
     def one(index, carry):
@@ -61,16 +64,14 @@
         for loop in range(2):
             x = x_ref[loop, rows, :].astype(F32)
             rinv = lax.rsqrt(jnp.mean(x * x, axis=-1, keepdims=True) + 1e-05)
-            hidden = (x * rinv * g_ref[loop]).astype(BF16)
-            for place in range(across):
+            hidden_ref[...] = (x * rinv * g_ref[loop]).astype(BF16)
+            for shift, tile_ref in enumerate(tiles):
+                place = lax.rem(where[1] + shift, across)
                 for half in range(FAR):
-                    at = (half * across + place) * near
-                    tiles_ref[
-                        lax.rem(place + across - where[1], across),
-                        loop,
-                        rows,
-                        half * near : (half + 1) * near,
-                    ] = hidden[:, at : at + near]
+                    at = pl.multiple_of((half * across + place) * near, near)
+                    tile_ref[loop, rows, half * near : (half + 1) * near] = hidden_ref[
+                        :, pl.ds(at, near)
+                    ]
         return carry
 
     lax.fori_loop(0, tok // ROWS, one, 0)
@@ -84,22 +85,24 @@
             w_ref[pl.ds(at, piece), :] = ref[index]
 
 
-def part_kernel(*refs):
+def part_kernel(start, across, *refs):
     part_ref = refs[-1]
-    count = (len(refs) - 1) // 2
-    total = None
-    for tiles_ref, dv_ref in zip(refs[:count], refs[count:-1], strict=True):
+    total = refs[2 * across][...] if start else None
+    for tiles_ref, dv_ref in zip(refs[:across], refs[across : 2 * across], strict=True):
         tok = tiles_ref.shape[1]
-        for loop in range(2):
-            at = 0 if loop == 0 else tok
+        done = 0
+        while done < dv_ref.shape[0]:
+            loop, row = 1 - (start + done) // tok, (start + done) % tok
+            count = min(tok - row, dv_ref.shape[0] - done)
             term = lax.dot_general(
-                tiles_ref[loop],
-                dv_ref[at : at + tok, :],
+                tiles_ref[loop, row : row + count, :],
+                dv_ref[done : done + count, :],
                 (((0,), (0,)), ((), ())),
                 preferred_element_type=F32,
             )
             total = term if total is None else total + term
-    part_ref[...] = total.astype(BF16)
+            done += count
+    part_ref[...] = total.astype(part_ref.dtype)
 
 
 def task_of(step, section, npipe):
@@ -164,15 +167,15 @@
     each(lambda copy: copy.wait())
 
 
-def stack_kernel(npipe, blocks, where, *refs):
+def stack_kernel(npipe, start, where, *refs):
     *pieces, out_ref = refs
     section = where[0]
+    count = out_ref.shape[0] // ROWS
     for step, piece in enumerate(pieces):
-        task = task_of(step, section, npipe)
-
-        @pl.when((task >= 0) & (task < 2 * blocks))
+        place = task_of(step, section, npipe) - start
+
+        @pl.when((place >= 0) & (place < count))
         def _():
-            place = task + jnp.where(task < blocks, blocks, -blocks)
             out_ref[pl.ds(pl.multiple_of(place * ROWS, ROWS), ROWS), :] = piece[...]
 
 
@@ -188,6 +191,7 @@
 def on_device(saved, grad_out, gain, w_value):
     npipe = lax.axis_size("pipe")
     where = jnp.stack([lax.axis_index(name) for name in ("pipe", "dp_1", "dp_3")]).astype(jnp.int32)
+    stage = lax.axis_index("pipe").astype(jnp.int32).reshape(1)
     x = saved[:, 0]
     _, tok, width = x.shape
     kv_width = w_value.shape[2]
@@ -195,15 +199,17 @@
     across = lax.axis_size("dp_1")
     shape = jax.ShapeDtypeStruct
 
-    mine = copy_for_each(w_value[0], DP[:3])
-    other = lax.ppermute(mine, DP[3], [(0, 1), (1, 0)])
     tiles = kernel_call(
         norm_kernel,
         "normalize",
-        shape((across, 2, tok, width // across), BF16),
+        (shape((2, tok, width // across), BF16),) * across,
         [IN_SMEM] + [IN_VMEM] * 2,
         (where, x, gain),
-    )
+        scratch=(pltpu.VMEM((ROWS, width), BF16),),
+    )
+    mine = held_until(copy_for_each(w_value[0], DP[:3]), tiles[0])
+    other = lax.ppermute(mine, DP[3], [(0, 1), (1, 0)])
+    hidden = exchanged(tiles, "dp_1")
     w_mat = kernel_call(
         rows_kernel,
         "rows",
@@ -212,19 +218,42 @@
         (where, mine, other),
     )
 
+    def partial_sum(start, end, extra, kind):
+        rows = (end - start) * ROWS
+        dv = kernel_call(
+            functools.partial(stack_kernel, npipe, start),
+            "stack",
+            shape((rows, kv_width), BF16),
+            [IN_SMEM] + [IN_VMEM] * len(gv_parts),
+            (stage, *gv_parts),
+        )
+        spread = exchanged([dv] * across, "dp_1")
+        return kernel_call(
+            functools.partial(part_kernel, start * ROWS, across),
+            "part",
+            shape((width // across, kv_width), kind),
+            [IN_VMEM] * (2 * across + len(extra)),
+            (*hidden, *spread, *extra),
+        )
+
     steps = 2 * blocks + SLACK * (npipe - 1)
     sent, gx_parts, gv_parts = {}, [], []
     for step in range(steps):
         incoming = sent.pop(step - SLACK, None)
         if incoming is None:
             incoming = jnp.zeros((ROWS, width), BF16)
-        later = tuple(hidden[1:]) if step == HIDDEN_BY else ()
+        later = ()
+        if step == HIDDEN_BY:
+            later = tuple(hidden[1:])
+        elif step == EARLY_BY:
+            later = (early,)
+        turn = gv_parts[-1:]
         dx, dv = kernel_call(
             functools.partial(step_kernel, step, npipe, blocks),
             "section_step",
             (shape((ROWS, width), BF16), shape((ROWS, kv_width), BF16)),
-            [IN_SMEM] + [IN_VMEM] * (5 + min(step, 1)) + [ANYWHERE] * len(later),
-            (where, w_mat, x, gain, grad_out, incoming, *gv_parts[-1:], *later),
+            [IN_SMEM] + [IN_VMEM] * (5 + len(turn)) + [ANYWHERE] * len(later),
+            (stage, w_mat, x, gain, grad_out, incoming, *turn, *later),
         )
         gx_parts.append(dx)
         gv_parts.append(dv)
@@ -235,33 +264,19 @@
                 pairs.append((source, (source - 1) % npipe))
         if pairs:
             sent[step] = lax.ppermute(dx, "pipe", pairs)
-        if step == 4:
-            hidden = exchanged(held_until(tiles, dv), "dp_1")
+        if step == EARLY + SLACK * (npipe - 1) - 1:
+            early = partial_sum(0, EARLY, (), F32)
 
     grad_x = kernel_call(
         functools.partial(collect_kernel, npipe, blocks),
         "collect_rows",
         shape((2, tok, width), BF16),
         [IN_SMEM] + [IN_VMEM] * steps,
-        (where, *gx_parts),
+        (stage, *gx_parts),
         scratch=(pltpu.SemaphoreType.DMA((steps,)),),
         out_spec=ANYWHERE,
     )[:, None]
-    dv_all = kernel_call(
-        functools.partial(stack_kernel, npipe, blocks),
-        "stack",
-        shape((2 * tok, kv_width), BF16),
-        [IN_SMEM] + [IN_VMEM] * steps,
-        (where, *gv_parts),
-    )
-    spread = exchanged([dv_all] * across, "dp_1")
-    part = kernel_call(
-        part_kernel,
-        "part",
-        shape((width // across, kv_width), BF16),
-        [IN_VMEM] * (2 * across),
-        (*hidden, *spread),
-    )
+    part = partial_sum(EARLY, 2 * blocks, (early,), BF16)
     others = ("dp_0", "dp_2", "dp_3")
     pieces = part.reshape(lax.axis_size(others), -1, kv_width)
     landed = lax.all_to_all(pieces, others, 0, 0, tiled=True)

time: 226 us -> 220 us (0.973)
  blocking collectives: 35.2 us -> 0 us
  waiting for transfers between devices: 75.5 us -> 100 us
  starting transfers between devices: 67.1 us -> 80.6 us
  Pallas kernels: 43.7 us -> 32.1 us
    all_to_all x1 -> x0, blocking collectives: 35.2 us -> none  [copy_for_each(): lax.all_to_all(jnp.broadcast_to(array[None], (count, *array.shape)), axis...]
    all_to_all x0 -> x1, waiting for transfers between devices: none -> 22.1 us  [copy_for_each(): lax.all_to_all(jnp.broadcast_to(array[None], (count, *array.shape)), axis...]
    ppermute x6 -> x9, waiting for transfers between devices: 5.46 us -> 17.1 us  [exchanged(): moved.append(lax.ppermute(pieces[shift], axis, pairs))]
    pallas_call x27 -> x29, Pallas kernels: 43.7 us -> 32.1 us  [kernel_call(): pl.pallas_call(kernel, out_shape=out_shape, in_specs=specs, out_specs=jax...]
    all_to_all x0 -> x1, starting transfers between devices: none -> 9.49 us  [copy_for_each(): lax.all_to_all(jnp.broadcast_to(array[None], (count, *array.shape)), axis...]
    ppermute x20, waiting for transfers between devices: 52.4 us -> 46.2 us  [on_device(): sent[step] = lax.ppermute(dx, 'pipe', pairs)]
    ppermute x1, waiting for transfers between devices: 3.84 us -> 0.4 us  [on_device(): other = lax.ppermute(mine, DP[3], [(0, 1), (1, 0)])]
    all_to_all x1, starting transfers between devices: 12 us -> 15.1 us  [on_device(): landed = lax.all_to_all(pieces, others, 0, 0, tiled=True)]
  transfers between devices with their start and end apart: 28 -> 32, of which waited for: 14 -> 16; matrix products, arithmetic and copies ran while one was open for 0% -> 0% of each run, Pallas kernels for 16% -> 13%
where the time goes in v8:
time: 220 us; the launch traced here: 219 us
  waiting for transfers between devices  100 us (45%)
  starting transfers between devices  80.6 us (37%)
  Pallas kernels  32.1 us (15%)
  local copies, waits for them, and re-layouts  2.56 us (1%)
    ppermute x20, waiting for transfers between devices, on_device(): sent[step] = lax.ppermute(dx, 'pipe', pairs)  46.2 us
    ppermute x20, starting transfers between devices, on_device(): sent[step] = lax.ppermute(dx, 'pipe', pairs)  37.6 us
    pallas_call x29, Pallas kernels, kernel_call(): pl.pallas_call(kernel, out_shape=out_shape, in_specs=specs, out_specs=jax...  32.1 us
    all_to_all x1, waiting for transfers between devices, copy_for_each(): lax.all_to_all(jnp.broadcast_to(array[None], (count, *array.shape)), axis...  22.1 us
    ppermute x9, waiting for transfers between devices, exchanged(): moved.append(lax.ppermute(pieces[shift], axis, pairs))  17.1 us
    all_to_all x1, starting transfers between devices, on_device(): landed = lax.all_to_all(pieces, others, 0, 0, tiled=True)  15.1 us
    ppermute x9, starting transfers between devices, exchanged(): moved.append(lax.ppermute(pieces[shift], axis, pairs))  14.4 us
    all_to_all x1, waiting for transfers between devices, on_device(): landed = lax.all_to_all(pieces, others, 0, 0, tiled=True)  14.3 us
  transfers between devices with their start and end apart: 32, of which 16 were waited for; matrix products, arithmetic and copies ran while one was open for 0% of the time, Pallas kernels for 13%

profile of v8, /device:TPU:1, one launch (start us, length us, event | category | flops | bytes accessed | tf_op | source)
XLA Modules:
  0.0 219.0 jit_solution(16944596253754486707)
XLA Ops:
  0.6 2.4 %broadcast_in_dim.14 = bf16[32,64,512]{2,1,0:T(8,128)(2,1)} broadcast(bf16[64,512]{1,0:T(8,128)(2,1)} %bitcast.35), dimensions={1,2} | broadcast | bytes 2162688 | tf_op jit(solution)/shard_map/broadcast_in_dim | solution.py:28
  3.0 9.5 %all-to-all-start = ((bf16[32,64,512]{2,1,0:T(8,128)(2,1)}), bf16[32,64,512]{2,1,0:T(8,128)(2,1)}, u32[]{:S(2)}, u32[]{:S(2)}) async-start(bf16[32,64,512]{2,1,0:T(8,128)(2,1)} %broadcast_in_dim.14), calls=%async_computation | async-start | bytes 4194304 | tf_op jit(solution)/shard_map/all_to_all | solution.py:27
  12.6 3.3 %normalize.1 = (bf16[2,128,1024]{2,1,0:T(8,128)(2,1)S(1)}, bf16[2,128,1024]{2,1,0:T(8,128)(2,1)}, bf16[2,128,1024]{2,1,0:T(8,128)(2,1)}, bf16[2,128,1024]{2,1,0:T(8,128)(2,1)}) custom-call(s32[3]{0:T(128)S(1)} %pad_add_fusion.where, bf16[2,128,4096]{2,1,0:T(8,128)(2,1)S(1)} %bitcast.10, f32[2,1,4096]{2,1,0:T(1,128)S(1)} %copy-done.2), custom_call_target="tpu_custom_call" | custom-call | tf_op jit(solution)/shard_map/normalize/pallas_call | solution.py:33
  15.9 22.1 %all-to-all-done.value_ref = bf16[32,64,512]{2,1,0:T(8,128)(2,1)} async-done(((bf16[32,64,512]{2,1,0:T(8,128)(2,1)}), bf16[32,64,512]{2,1,0:T(8,128)(2,1)}, u32[]{:S(2)}, u32[]{:S(2)}) %all-to-all-start) | async-done | bytes 2097184 | tf_op jit(solution)/shard_map/all_to_all | solution.py:27
  38.0 4.0 %collective-permute-start = (bf16[32,64,512]{2,1,0:T(8,128)(2,1)}, bf16[32,64,512]{2,1,0:T(8,128)(2,1)S(1)}, u32[]{:S(2)}, u32[]{:S(2)}) collective-permute-start(bf16[32,64,512]{2,1,0:T(8,128)(2,1)} %held_until.1.mine_ref), channel_id=1, source_target_pairs={{0,1},{1,0},{2,3},{3,2},{4,5},{5,4},{6,7},{7,6},{8,9},{9,8},{10,11... | collective-permute-start | bytes 6291464 | tf_op jit(solution)/shard_map/ppermute | solution.py:211
  42.5 1.7 collective-permute-start.7
  44.2 1.5 collective-permute-start.8
  46.0 1.9 rows.1.w_ref
  48.0 0.7 collective-permute-start.1
  48.6 0.7 collective-permute-start.2
  49.4 0.7 collective-permute-start.3
  50.8 1.3 collective-permute-start.5
  52.1 1.3 collective-permute-start.9
  53.4 14.8 %collective-permute-done.6.refs_1_ = bf16[2,128,1024]{2,1,0:T(8,128)(2,1)S(1)} collective-permute-done((bf16[2,128,1024]{2,1,0:T(8,128)(2,1)}, bf16[2,128,1024]{2,1,0:T(8,128)(2,1)S(1)}, u32[]{:S(2)}, u32[]{:S(2)}) %collective-permute-start.6) | collective-permute-done | bytes 524320 | tf_op jit(solution)/shard_map/ppermute | solution.py:187
  68.5 18.3 %collective-permute-done.5.in_ref = bf16[16,4096]{1,0:T(8,128)(2,1)S(1)} collective-permute-done((bf16[16,4096]{1,0:T(8,128)(2,1)S(1)}, bf16[16,4096]{1,0:T(8,128)(2,1)S(1)}, u32[]{:S(2)}, u32[]{:S(2)}) %collective-permute-start.5) | collective-permute-done | bytes 131104 | tf_op jit(solution)/shard_map/ppermute | solution.py:266
  86.8 1.3 section_step.28
  88.2 3.9 %collective-permute-start.10 = (bf16[16,4096]{1,0:T(8,128)(2,1)S(1)}, bf16[16,4096]{1,0:T(8,128)(2,1)S(1)}, u32[]{:S(2)}, u32[]{:S(2)}) collective-permute-start(bf16[16,4096]{1,0:T(8,128)(2,1)S(1)} %get-tuple-element.66.refs_6_), channel_id=1, source_target_pairs={{0,192},{64,0},{128,64},{192,128},{1,193},{65,1},{129,65},{193,129... | collective-permute-start | bytes 393224 | tf_op jit(solution)/shard_map/ppermute | solution.py:266
  92.1 1.3 section_step.29
  93.5 3.3 %collective-permute-start.11 = (bf16[16,4096]{1,0:T(8,128)(2,1)S(1)}, bf16[16,4096]{1,0:T(8,128)(2,1)S(1)}, u32[]{:S(2)}, u32[]{:S(2)}) collective-permute-start(bf16[16,4096]{1,0:T(8,128)(2,1)S(1)} %get-tuple-element.68.refs_7_), channel_id=1, source_target_pairs={{0,192},{64,0},{128,64},{192,128},{1,193},{65,1},{129,65},{193,129... | collective-permute-start | bytes 393224 | tf_op jit(solution)/shard_map/ppermute | solution.py:266
  96.8 3.8 %collective-permute-done.10.in_ref = bf16[16,4096]{1,0:T(8,128)(2,1)S(1)} collective-permute-done((bf16[16,4096]{1,0:T(8,128)(2,1)S(1)}, bf16[16,4096]{1,0:T(8,128)(2,1)S(1)}, u32[]{:S(2)}, u32[]{:S(2)}) %collective-permute-start.10) | collective-permute-done | bytes 131104 | tf_op jit(solution)/shard_map/ppermute | solution.py:266
  100.6 1.3 section_step.30
  101.9 0.8 collective-permute-start.12
  102.8 1.3 section_step.31
  104.1 2.0 collective-permute-start.13
  106.2 3.7 %collective-permute-done.12.in_ref = bf16[16,4096]{1,0:T(8,128)(2,1)S(1)} collective-permute-done((bf16[16,4096]{1,0:T(8,128)(2,1)S(1)}, bf16[16,4096]{1,0:T(8,128)(2,1)S(1)}, u32[]{:S(2)}, u32[]{:S(2)}) %collective-permute-start.12) | collective-permute-done | bytes 131104 | tf_op jit(solution)/shard_map/ppermute | solution.py:266
  109.9 1.3 section_step.32
  111.2 3.9 %collective-permute-start.14 = (bf16[16,4096]{1,0:T(8,128)(2,1)S(1)}, bf16[16,4096]{1,0:T(8,128)(2,1)S(1)}, u32[]{:S(2)}, u32[]{:S(2)}) collective-permute-start(bf16[16,4096]{1,0:T(8,128)(2,1)S(1)} %get-tuple-element.74.refs_10_), channel_id=1, source_target_pairs={{0,192},{64,0},{128,64},{192,128},{1,193},{65,1},{129,65},{193,129... | collective-permute-start | bytes 393224 | tf_op jit(solution)/shard_map/ppermute | solution.py:266
  115.1 1.3 section_step.33
  116.5 3.0 %collective-permute-start.15 = (bf16[16,4096]{1,0:T(8,128)(2,1)S(1)}, bf16[16,4096]{1,0:T(8,128)(2,1)S(1)}, u32[]{:S(2)}, u32[]{:S(2)}) collective-permute-start(bf16[16,4096]{1,0:T(8,128)(2,1)S(1)} %get-tuple-element.76.refs_11_), channel_id=1, source_target_pairs={{0,192},{64,0},{128,64},{192,128},{1,193},{65,1},{129,65},{193,129... | collective-permute-start | bytes 393224 | tf_op jit(solution)/shard_map/ppermute | solution.py:266
  119.5 1.3 section_step.34
  120.9 4.3 %collective-permute-start.16 = (bf16[16,4096]{1,0:T(8,128)(2,1)S(1)}, bf16[16,4096]{1,0:T(8,128)(2,1)S(1)}, u32[]{:S(2)}, u32[]{:S(2)}) collective-permute-start(bf16[16,4096]{1,0:T(8,128)(2,1)S(1)} %get-tuple-element.78.refs_12_), channel_id=1, source_target_pairs={{0,192},{64,0},{128,64},{192,128},{1,193},{65,1},{129,65},{193,129... | collective-permute-start | bytes 393224 | tf_op jit(solution)/shard_map/ppermute | solution.py:266
  125.2 1.3 section_step.35
  126.6 3.0 %collective-permute-start.17 = (bf16[16,4096]{1,0:T(8,128)(2,1)S(1)}, bf16[16,4096]{1,0:T(8,128)(2,1)S(1)}, u32[]{:S(2)}, u32[]{:S(2)}) collective-permute-start(bf16[16,4096]{1,0:T(8,128)(2,1)S(1)} %get-tuple-element.80.refs_13_), channel_id=1, source_target_pairs={{0,192},{64,0},{128,64},{192,128},{1,193},{65,1},{129,65},{193,129... | collective-permute-start | bytes 393224 | tf_op jit(solution)/shard_map/ppermute | solution.py:266
  129.7 1.4 collective-permute-done.16.in_ref
  131.1 1.3 section_step.36
  132.4 1.3 collective-permute-start.18
  133.7 2.8 %collective-permute-done.17.in_ref = bf16[16,4096]{1,0:T(8,128)(2,1)S(1)} collective-permute-done((bf16[16,4096]{1,0:T(8,128)(2,1)S(1)}, bf16[16,4096]{1,0:T(8,128)(2,1)S(1)}, u32[]{:S(2)}, u32[]{:S(2)}) %collective-permute-start.17) | collective-permute-done | bytes 131104 | tf_op jit(solution)/shard_map/ppermute | solution.py:266
  136.5 1.3 section_step.37
  137.9 1.3 collective-permute-start.19
  139.3 2.4 %collective-permute-start.21 = (bf16[128,512]{1,0:T(8,128)(2,1)S(1)}, bf16[128,512]{1,0:T(8,128)(2,1)S(1)}, u32[]{:S(2)}, u32[]{:S(2)}) collective-permute-start(bf16[128,512]{1,0:T(8,128)(2,1)S(1)} %stack.15.refs_4_), channel_id=1, source_target_pairs={{0,8},{8,16},{16,24},{24,0},{1,9},{9,17},{17,25},{25,1},{2,10},{10... | collective-permute-start | bytes 393224 | tf_op jit(solution)/shard_map/ppermute | solution.py:187
  142.0 2.3 %collective-permute-start.23 = (bf16[128,512]{1,0:T(8,128)(2,1)S(1)}, bf16[128,512]{1,0:T(8,128)(2,1)S(1)}, u32[]{:S(2)}, u32[]{:S(2)}) collective-permute-start(bf16[128,512]{1,0:T(8,128)(2,1)S(1)} %stack.15.refs_4_), channel_id=1, source_target_pairs={{0,24},{8,0},{16,8},{24,16},{1,25},{9,1},{17,9},{25,17},{2,26},{10... | collective-permute-start | bytes 393224 | tf_op jit(solution)/shard_map/ppermute | solution.py:187
  144.2 1.3 section_step.38
  145.6 1.3 collective-permute-start.20
  146.9 1.3 section_step.39
  148.3 1.5 collective-permute-start.24
  149.8 1.3 part.2.refs_1_.refs_8_
  151.1 4.6 %collective-permute-done.20.in_ref = bf16[16,4096]{1,0:T(8,128)(2,1)S(1)} collective-permute-done((bf16[16,4096]{1,0:T(8,128)(2,1)S(1)}, bf16[16,4096]{1,0:T(8,128)(2,1)S(1)}, u32[]{:S(2)}, u32[]{:S(2)}) %collective-permute-start.20) | collective-permute-done | bytes 131104 | tf_op jit(solution)/shard_map/ppermute | solution.py:266
  155.7 1.3 section_step.40
  157.1 1.3 collective-permute-start.25
  158.8 1.3 section_step.41
  160.1 1.3 collective-permute-start.26
  161.4 8.3 %collective-permute-done.25.in_ref = bf16[16,4096]{1,0:T(8,128)(2,1)S(1)} collective-permute-done((bf16[16,4096]{1,0:T(8,128)(2,1)S(1)}, bf16[16,4096]{1,0:T(8,128)(2,1)S(1)}, u32[]{:S(2)}, u32[]{:S(2)}) %collective-permute-start.25) | collective-permute-done | bytes 131104 | tf_op jit(solution)/shard_map/ppermute | solution.py:266
  169.8 1.3 section_step.42
  171.1 2.8 %collective-permute-done.26.in_ref = bf16[16,4096]{1,0:T(8,128)(2,1)S(1)} collective-permute-done((bf16[16,4096]{1,0:T(8,128)(2,1)S(1)}, bf16[16,4096]{1,0:T(8,128)(2,1)S(1)}, u32[]{:S(2)}, u32[]{:S(2)}) %collective-permute-start.26) | collective-permute-done | bytes 131104 | tf_op jit(solution)/shard_map/ppermute | solution.py:266
  174.0 1.3 section_step.43
  175.5 0.9 collective-permute-start.27
  176.4 3.0 %collective-permute-start.28 = (bf16[128,512]{1,0:T(8,128)(2,1)S(1)}, bf16[128,512]{1,0:T(8,128)(2,1)S(1)}, u32[]{:S(2)}, u32[]{:S(2)}) collective-permute-start(bf16[128,512]{1,0:T(8,128)(2,1)S(1)} %stack.16.refs_4_), channel_id=1, source_target_pairs={{0,16},{8,24},{16,0},{24,8},{1,17},{9,25},{17,1},{25,9},{2,18},{10... | collective-permute-start | bytes 393224 | tf_op jit(solution)/shard_map/ppermute | solution.py:187
  179.4 2.0 collective-permute-start.29
  181.4 1.7 collective-permute-done.28.refs_6_
  183.4 2.3 %part.3 = bf16[1024,512]{1,0:T(8,128)(2,1)} custom-call(bf16[2,128,1024]{2,1,0:T(8,128)(2,1)S(1)} %get-tuple-element.50.token_ref.refs_0_, bf16[2,128,1024]{2,1,0:T(8,128)(2,1)S(1)} %collective-permute-done.6.refs_1_, bf16[2,128,1024]{2,1,0:T(8,128)(2,1)S(1)} %collective-permute-done.7.refs_2_, bf16[2,128,1024]{2,1,0:T(8,128)(2,1)S(1)} %collective-permute-done.8.refs_3_, ...), custom_call_target="tpu_custom_call" | custom-call | tf_op jit(solution)/shard_map/part/pallas_call | solution.py:33
  185.8 15.1 %all-to-all-start.1 = ((bf16[16,64,512]{2,1,0:T(8,128)(2,1)}), bf16[16,64,512]{2,1,0:T(8,128)(2,1)}, u32[]{:S(2)}, u32[]{:S(2)}) async-start(bf16[16,64,512]{2,1,0:T(8,128)(2,1)} %bitcast.7), calls=%async_computation.1 | async-start | bytes 2097152 | tf_op jit(solution)/shard_map/all_to_all | solution.py:282
  201.1 1.5 collect_rows.1
  202.6 14.3 %all-to-all-done.1 = bf16[16,64,512]{2,1,0:T(8,128)(2,1)} async-done(((bf16[16,64,512]{2,1,0:T(8,128)(2,1)}), bf16[16,64,512]{2,1,0:T(8,128)(2,1)}, u32[]{:S(2)}, u32[]{:S(2)}) %all-to-all-start.1) | async-done | bytes 1048608 | tf_op jit(solution)/shard_map/all_to_all | solution.py:282
  216.9 2.0 convert_reduce_fusion
  (104 shorter events, 3.3 us)
Async XLA Ops:
  3.0 9.6 %copy-start = (bf16[2,1,128,4096]{3,2,1,0:T(8,128)(2,1)S(1)}, bf16[2,1,128,4096]{3,2,1,0:T(8,128)(2,1)}, u32[]{:S(2)}) copy-start(bf16[2,1,128,4096]{3,2,1,0:T(8,128)(2,1)} %param.4) | copy-start | bytes 6291460
  3.0 9.6 %copy-start.2 = (f32[2,1,4096]{2,1,0:T(1,128)S(1)}, f32[2,1,4096]{2,1,0:T(1,128)}, u32[]{:S(2)}) copy-start(f32[2,1,4096]{2,1,0:T(1,128)} %g_ref.45) | copy-start | bytes 98308
  3.0 35.0 %all-to-all-start = ((bf16[32,64,512]{2,1,0:T(8,128)(2,1)}), bf16[32,64,512]{2,1,0:T(8,128)(2,1)}, u32[]{:S(2)}, u32[]{:S(2)}) async-start(bf16[32,64,512]{2,1,0:T(8,128)(2,1)} %broadcast_in_dim.14), calls=%async_computation | async-start | bytes 4194304 | tf_op jit(solution)/shard_map/all_to_all | solution.py:27
  38.0 8.0 %collective-permute-start = (bf16[32,64,512]{2,1,0:T(8,128)(2,1)}, bf16[32,64,512]{2,1,0:T(8,128)(2,1)S(1)}, u32[]{:S(2)}, u32[]{:S(2)}) collective-permute-start(bf16[32,64,512]{2,1,0:T(8,128)(2,1)} %held_until.1.mine_ref), channel_id=1, source_target_pairs={{0,1},{1,0},{2,3},{3,2},{4,5},{5,4},{6,7},{7,6},{8,9},{9,8},{10,11... | collective-permute-start | bytes 6291464 | tf_op jit(solution)/shard_map/ppermute | solution.py:211
  42.0 26.2 %collective-permute-start.6 = (bf16[2,128,1024]{2,1,0:T(8,128)(2,1)}, bf16[2,128,1024]{2,1,0:T(8,128)(2,1)S(1)}, u32[]{:S(2)}, u32[]{:S(2)}) collective-permute-start(bf16[2,128,1024]{2,1,0:T(8,128)(2,1)} %get-tuple-element.63), channel_id=1, source_target_pairs={{0,8},{8,16},{16,24},{24,0},{1,9},{9,17},{17,25},{25,1},{2,10},{10... | collective-permute-start | bytes 1572872 | tf_op jit(solution)/shard_map/ppermute | solution.py:187
  42.5 25.8 %collective-permute-start.7 = (bf16[2,128,1024]{2,1,0:T(8,128)(2,1)}, bf16[2,128,1024]{2,1,0:T(8,128)(2,1)S(1)}, u32[]{:S(2)}, u32[]{:S(2)}) collective-permute-start(bf16[2,128,1024]{2,1,0:T(8,128)(2,1)} %get-tuple-element.64), channel_id=1, source_target_pairs={{0,16},{8,24},{16,0},{24,8},{1,17},{9,25},{17,1},{25,9},{2,18},{10... | collective-permute-start | bytes 1572872 | tf_op jit(solution)/shard_map/ppermute | solution.py:187
  44.2 3.8 %copy-start.1 = (bf16[128,4096]{1,0:T(8,128)(2,1)S(1)}, bf16[128,4096]{1,0:T(8,128)(2,1)}, u32[]{:S(2)}) copy-start(bf16[128,4096]{1,0:T(8,128)(2,1)} %fresh_ref.43) | copy-start | bytes 3145732
  44.2 24.4 %collective-permute-start.8 = (bf16[2,128,1024]{2,1,0:T(8,128)(2,1)}, bf16[2,128,1024]{2,1,0:T(8,128)(2,1)S(1)}, u32[]{:S(2)}, u32[]{:S(2)}) collective-permute-start(bf16[2,128,1024]{2,1,0:T(8,128)(2,1)} %get-tuple-element.65), channel_id=1, source_target_pairs={{0,24},{8,0},{16,8},{24,16},{1,25},{9,1},{17,9},{25,17},{2,26},{10... | collective-permute-start | bytes 1572872 | tf_op jit(solution)/shard_map/ppermute | solution.py:187
  48.0 1.4 collective-permute-start.1
  48.6 1.4 collective-permute-start.2
  49.4 1.4 collective-permute-start.3
  50.1 2.0 collective-permute-start.4
  50.8 36.0 %collective-permute-start.5 = (bf16[16,4096]{1,0:T(8,128)(2,1)S(1)}, bf16[16,4096]{1,0:T(8,128)(2,1)S(1)}, u32[]{:S(2)}, u32[]{:S(2)}) collective-permute-start(bf16[16,4096]{1,0:T(8,128)(2,1)S(1)} %get-tuple-element.59.refs_4_), channel_id=1, source_target_pairs={{64,0},{128,64},{192,128},{65,1},{129,65},{193,129},{66,2},{130,66... | collective-permute-start | bytes 393224 | tf_op jit(solution)/shard_map/ppermute | solution.py:266
  52.1 40.0 %collective-permute-start.9 = (bf16[16,4096]{1,0:T(8,128)(2,1)S(1)}, bf16[16,4096]{1,0:T(8,128)(2,1)S(1)}, u32[]{:S(2)}, u32[]{:S(2)}) collective-permute-start(bf16[16,4096]{1,0:T(8,128)(2,1)S(1)} %get-tuple-element.61.refs_5_), channel_id=1, source_target_pairs={{64,0},{128,64},{192,128},{65,1},{129,65},{193,129},{66,2},{130,66... | collective-permute-start | bytes 393224 | tf_op jit(solution)/shard_map/ppermute | solution.py:266
  88.2 5.3 %copy-start.3 = (bf16[16,4096]{1,0:T(8,128)(2,1)}, bf16[16,4096]{1,0:T(8,128)(2,1)S(1)}, u32[]{:S(2)}) copy-start(bf16[16,4096]{1,0:T(8,128)(2,1)S(1)} %get-tuple-element.66.refs_6_) | copy-start | bytes 393220
  88.2 12.4 %collective-permute-start.10 = (bf16[16,4096]{1,0:T(8,128)(2,1)S(1)}, bf16[16,4096]{1,0:T(8,128)(2,1)S(1)}, u32[]{:S(2)}, u32[]{:S(2)}) collective-permute-start(bf16[16,4096]{1,0:T(8,128)(2,1)S(1)} %get-tuple-element.66.refs_6_), channel_id=1, source_target_pairs={{0,192},{64,0},{128,64},{192,128},{1,193},{65,1},{129,65},{193,129... | collective-permute-start | bytes 393224 | tf_op jit(solution)/shard_map/ppermute | solution.py:266
  93.5 8.5 %copy-start.5 = (bf16[16,4096]{1,0:T(8,128)(2,1)}, bf16[16,4096]{1,0:T(8,128)(2,1)S(1)}, u32[]{:S(2)}) copy-start(bf16[16,4096]{1,0:T(8,128)(2,1)S(1)} %get-tuple-element.68.refs_7_) | copy-start | bytes 393220
  93.5 9.3 %collective-permute-start.11 = (bf16[16,4096]{1,0:T(8,128)(2,1)S(1)}, bf16[16,4096]{1,0:T(8,128)(2,1)S(1)}, u32[]{:S(2)}, u32[]{:S(2)}) collective-permute-start(bf16[16,4096]{1,0:T(8,128)(2,1)S(1)} %get-tuple-element.68.refs_7_), channel_id=1, source_target_pairs={{0,192},{64,0},{128,64},{192,128},{1,193},{65,1},{129,65},{193,129... | collective-permute-start | bytes 393224 | tf_op jit(solution)/shard_map/ppermute | solution.py:266
  101.9 7.9 %collective-permute-start.12 = (bf16[16,4096]{1,0:T(8,128)(2,1)S(1)}, bf16[16,4096]{1,0:T(8,128)(2,1)S(1)}, u32[]{:S(2)}, u32[]{:S(2)}) collective-permute-start(bf16[16,4096]{1,0:T(8,128)(2,1)S(1)} %get-tuple-element.70.refs_8_), channel_id=1, source_target_pairs={{0,192},{64,0},{128,64},{192,128},{1,193},{65,1},{129,65},{193,129... | collective-permute-start | bytes 393224 | tf_op jit(solution)/shard_map/ppermute | solution.py:266
  104.1 7.1 %copy-start.9 = (bf16[16,4096]{1,0:T(8,128)(2,1)}, bf16[16,4096]{1,0:T(8,128)(2,1)S(1)}, u32[]{:S(2)}) copy-start(bf16[16,4096]{1,0:T(8,128)(2,1)S(1)} %get-tuple-element.72.refs_9_) | copy-start | bytes 393220
  104.1 11.0 %collective-permute-start.13 = (bf16[16,4096]{1,0:T(8,128)(2,1)S(1)}, bf16[16,4096]{1,0:T(8,128)(2,1)S(1)}, u32[]{:S(2)}, u32[]{:S(2)}) collective-permute-start(bf16[16,4096]{1,0:T(8,128)(2,1)S(1)} %get-tuple-element.72.refs_9_), channel_id=1, source_target_pairs={{0,192},{64,0},{128,64},{192,128},{1,193},{65,1},{129,65},{193,129... | collective-permute-start | bytes 393224 | tf_op jit(solution)/shard_map/ppermute | solution.py:266
  111.2 5.3 %copy-start.11 = (bf16[16,4096]{1,0:T(8,128)(2,1)}, bf16[16,4096]{1,0:T(8,128)(2,1)S(1)}, u32[]{:S(2)}) copy-start(bf16[16,4096]{1,0:T(8,128)(2,1)S(1)} %get-tuple-element.74.refs_10_) | copy-start | bytes 393220
  111.2 8.3 %collective-permute-start.14 = (bf16[16,4096]{1,0:T(8,128)(2,1)S(1)}, bf16[16,4096]{1,0:T(8,128)(2,1)S(1)}, u32[]{:S(2)}, u32[]{:S(2)}) collective-permute-start(bf16[16,4096]{1,0:T(8,128)(2,1)S(1)} %get-tuple-element.74.refs_10_), channel_id=1, source_target_pairs={{0,192},{64,0},{128,64},{192,128},{1,193},{65,1},{129,65},{193,129... | collective-permute-start | bytes 393224 | tf_op jit(solution)/shard_map/ppermute | solution.py:266
  116.5 4.4 %copy-start.13 = (bf16[16,4096]{1,0:T(8,128)(2,1)}, bf16[16,4096]{1,0:T(8,128)(2,1)S(1)}, u32[]{:S(2)}) copy-start(bf16[16,4096]{1,0:T(8,128)(2,1)S(1)} %get-tuple-element.76.refs_11_) | copy-start | bytes 393220
  116.5 8.7 %collective-permute-start.15 = (bf16[16,4096]{1,0:T(8,128)(2,1)S(1)}, bf16[16,4096]{1,0:T(8,128)(2,1)S(1)}, u32[]{:S(2)}, u32[]{:S(2)}) collective-permute-start(bf16[16,4096]{1,0:T(8,128)(2,1)S(1)} %get-tuple-element.76.refs_11_), channel_id=1, source_target_pairs={{0,192},{64,0},{128,64},{192,128},{1,193},{65,1},{129,65},{193,129... | collective-permute-start | bytes 393224 | tf_op jit(solution)/shard_map/ppermute | solution.py:266
  120.9 5.7 %copy-start.15 = (bf16[16,4096]{1,0:T(8,128)(2,1)}, bf16[16,4096]{1,0:T(8,128)(2,1)S(1)}, u32[]{:S(2)}) copy-start(bf16[16,4096]{1,0:T(8,128)(2,1)S(1)} %get-tuple-element.78.refs_12_) | copy-start | bytes 393220
  120.9 10.2 %collective-permute-start.16 = (bf16[16,4096]{1,0:T(8,128)(2,1)S(1)}, bf16[16,4096]{1,0:T(8,128)(2,1)S(1)}, u32[]{:S(2)}, u32[]{:S(2)}) collective-permute-start(bf16[16,4096]{1,0:T(8,128)(2,1)S(1)} %get-tuple-element.78.refs_12_), channel_id=1, source_target_pairs={{0,192},{64,0},{128,64},{192,128},{1,193},{65,1},{129,65},{193,129... | collective-permute-start | bytes 393224 | tf_op jit(solution)/shard_map/ppermute | solution.py:266
  126.6 5.8 %copy-start.17 = (bf16[16,4096]{1,0:T(8,128)(2,1)}, bf16[16,4096]{1,0:T(8,128)(2,1)S(1)}, u32[]{:S(2)}) copy-start(bf16[16,4096]{1,0:T(8,128)(2,1)S(1)} %get-tuple-element.80.refs_13_) | copy-start | bytes 393220
  126.6 9.9 %collective-permute-start.17 = (bf16[16,4096]{1,0:T(8,128)(2,1)S(1)}, bf16[16,4096]{1,0:T(8,128)(2,1)S(1)}, u32[]{:S(2)}, u32[]{:S(2)}) collective-permute-start(bf16[16,4096]{1,0:T(8,128)(2,1)S(1)} %get-tuple-element.80.refs_13_), channel_id=1, source_target_pairs={{0,192},{64,0},{128,64},{192,128},{1,193},{65,1},{129,65},{193,129... | collective-permute-start | bytes 393224 | tf_op jit(solution)/shard_map/ppermute | solution.py:266
  132.4 5.5 %copy-start.19 = (bf16[16,4096]{1,0:T(8,128)(2,1)}, bf16[16,4096]{1,0:T(8,128)(2,1)S(1)}, u32[]{:S(2)}) copy-start(bf16[16,4096]{1,0:T(8,128)(2,1)S(1)} %get-tuple-element.82.refs_14_) | copy-start | bytes 393220
  132.4 11.8 %collective-permute-start.18 = (bf16[16,4096]{1,0:T(8,128)(2,1)S(1)}, bf16[16,4096]{1,0:T(8,128)(2,1)S(1)}, u32[]{:S(2)}, u32[]{:S(2)}) collective-permute-start(bf16[16,4096]{1,0:T(8,128)(2,1)S(1)} %get-tuple-element.82.refs_14_), channel_id=1, source_target_pairs={{64,0},{128,64},{192,128},{65,1},{129,65},{193,129},{66,2},{130,66... | collective-permute-start | bytes 393224 | tf_op jit(solution)/shard_map/ppermute | solution.py:266
  137.9 7.7 %copy-start.21 = (bf16[16,4096]{1,0:T(8,128)(2,1)}, bf16[16,4096]{1,0:T(8,128)(2,1)S(1)}, u32[]{:S(2)}) copy-start(bf16[16,4096]{1,0:T(8,128)(2,1)S(1)} %get-tuple-element.84.refs_15_) | copy-start | bytes 393220
  137.9 9.0 %collective-permute-start.19 = (bf16[16,4096]{1,0:T(8,128)(2,1)S(1)}, bf16[16,4096]{1,0:T(8,128)(2,1)S(1)}, u32[]{:S(2)}, u32[]{:S(2)}) collective-permute-start(bf16[16,4096]{1,0:T(8,128)(2,1)S(1)} %get-tuple-element.84.refs_15_), channel_id=1, source_target_pairs={{64,0},{128,64},{192,128},{65,1},{129,65},{193,129},{66,2},{130,66... | collective-permute-start | bytes 393224 | tf_op jit(solution)/shard_map/ppermute | solution.py:266
  139.3 10.5 %collective-permute-start.21 = (bf16[128,512]{1,0:T(8,128)(2,1)S(1)}, bf16[128,512]{1,0:T(8,128)(2,1)S(1)}, u32[]{:S(2)}, u32[]{:S(2)}) collective-permute-start(bf16[128,512]{1,0:T(8,128)(2,1)S(1)} %stack.15.refs_4_), channel_id=1, source_target_pairs={{0,8},{8,16},{16,24},{24,0},{1,9},{9,17},{17,25},{25,1},{2,10},{10... | collective-permute-start | bytes 393224 | tf_op jit(solution)/shard_map/ppermute | solution.py:187
  141.7 8.1 %collective-permute-start.22 = (bf16[128,512]{1,0:T(8,128)(2,1)S(1)}, bf16[128,512]{1,0:T(8,128)(2,1)S(1)}, u32[]{:S(2)}, u32[]{:S(2)}) collective-permute-start(bf16[128,512]{1,0:T(8,128)(2,1)S(1)} %stack.15.refs_4_), channel_id=1, source_target_pairs={{0,16},{8,24},{16,0},{24,8},{1,17},{9,25},{17,1},{25,9},{2,18},{10... | collective-permute-start | bytes 393224 | tf_op jit(solution)/shard_map/ppermute | solution.py:187
  142.0 7.9 %collective-permute-start.23 = (bf16[128,512]{1,0:T(8,128)(2,1)S(1)}, bf16[128,512]{1,0:T(8,128)(2,1)S(1)}, u32[]{:S(2)}, u32[]{:S(2)}) collective-permute-start(bf16[128,512]{1,0:T(8,128)(2,1)S(1)} %stack.15.refs_4_), channel_id=1, source_target_pairs={{0,24},{8,0},{16,8},{24,16},{1,25},{9,1},{17,9},{25,17},{2,26},{10... | collective-permute-start | bytes 393224 | tf_op jit(solution)/shard_map/ppermute | solution.py:187
  145.6 10.1 %collective-permute-start.20 = (bf16[16,4096]{1,0:T(8,128)(2,1)S(1)}, bf16[16,4096]{1,0:T(8,128)(2,1)S(1)}, u32[]{:S(2)}, u32[]{:S(2)}) collective-permute-start(bf16[16,4096]{1,0:T(8,128)(2,1)S(1)} %get-tuple-element.86.refs_16_), channel_id=1, source_target_pairs={{64,0},{128,64},{65,1},{129,65},{66,2},{130,66},{67,3},{131,67},{6... | collective-permute-start | bytes 393224 | tf_op jit(solution)/shard_map/ppermute | solution.py:266
  148.3 10.5 %collective-permute-start.24 = (bf16[16,4096]{1,0:T(8,128)(2,1)S(1)}, bf16[16,4096]{1,0:T(8,128)(2,1)S(1)}, u32[]{:S(2)}, u32[]{:S(2)}) collective-permute-start(bf16[16,4096]{1,0:T(8,128)(2,1)S(1)} %get-tuple-element.88.refs_17_), channel_id=1, source_target_pairs={{64,0},{128,64},{65,1},{129,65},{66,2},{130,66},{67,3},{131,67},{6... | collective-permute-start | bytes 393224 | tf_op jit(solution)/shard_map/ppermute | solution.py:266
  157.0 3.1 %copy-start.27 = (bf16[16,4096]{1,0:T(8,128)(2,1)}, bf16[16,4096]{1,0:T(8,128)(2,1)S(1)}, u32[]{:S(2)}) copy-start(bf16[16,4096]{1,0:T(8,128)(2,1)S(1)} %get-tuple-element.90.refs_18_) | copy-start | bytes 393220
  157.1 12.7 %collective-permute-start.25 = (bf16[16,4096]{1,0:T(8,128)(2,1)S(1)}, bf16[16,4096]{1,0:T(8,128)(2,1)S(1)}, u32[]{:S(2)}, u32[]{:S(2)}) collective-permute-start(bf16[16,4096]{1,0:T(8,128)(2,1)S(1)} %get-tuple-element.90.refs_18_), channel_id=1, source_target_pairs={{64,0},{65,1},{66,2},{67,3},{68,4},{69,5},{70,6},{71,7},{72,8},{73... | collective-permute-start | bytes 393224 | tf_op jit(solution)/shard_map/ppermute | solution.py:266
  160.1 11.0 %copy-start.29 = (bf16[16,4096]{1,0:T(8,128)(2,1)}, bf16[16,4096]{1,0:T(8,128)(2,1)S(1)}, u32[]{:S(2)}) copy-start(bf16[16,4096]{1,0:T(8,128)(2,1)S(1)} %get-tuple-element.92.refs_19_) | copy-start | bytes 393220
  160.1 13.8 %collective-permute-start.26 = (bf16[16,4096]{1,0:T(8,128)(2,1)S(1)}, bf16[16,4096]{1,0:T(8,128)(2,1)S(1)}, u32[]{:S(2)}, u32[]{:S(2)}) collective-permute-start(bf16[16,4096]{1,0:T(8,128)(2,1)S(1)} %get-tuple-element.92.refs_19_), channel_id=1, source_target_pairs={{64,0},{65,1},{66,2},{67,3},{68,4},{69,5},{70,6},{71,7},{72,8},{73... | collective-permute-start | bytes 393224 | tf_op jit(solution)/shard_map/ppermute | solution.py:266
  171.1 4.2 %copy-start.31 = (bf16[16,4096]{1,0:T(8,128)(2,1)}, bf16[16,4096]{1,0:T(8,128)(2,1)S(1)}, u32[]{:S(2)}) copy-start(bf16[16,4096]{1,0:T(8,128)(2,1)S(1)} %get-tuple-element.94.refs_20_) | copy-start | bytes 393220
  175.3 10.3 %copy-start.33 = (bf16[16,4096]{1,0:T(8,128)(2,1)}, bf16[16,4096]{1,0:T(8,128)(2,1)S(1)}, u32[]{:S(2)}) copy-start(bf16[16,4096]{1,0:T(8,128)(2,1)S(1)} %get-tuple-element.96.refs_21_) | copy-start | bytes 393220
  175.5 5.9 %collective-permute-start.27 = (bf16[128,512]{1,0:T(8,128)(2,1)S(1)}, bf16[128,512]{1,0:T(8,128)(2,1)S(1)}, u32[]{:S(2)}, u32[]{:S(2)}) collective-permute-start(bf16[128,512]{1,0:T(8,128)(2,1)S(1)} %stack.16.refs_4_), channel_id=1, source_target_pairs={{0,8},{8,16},{16,24},{24,0},{1,9},{9,17},{17,25},{25,1},{2,10},{10... | collective-permute-start | bytes 393224 | tf_op jit(solution)/shard_map/ppermute | solution.py:187
  176.4 6.7 %collective-permute-start.28 = (bf16[128,512]{1,0:T(8,128)(2,1)S(1)}, bf16[128,512]{1,0:T(8,128)(2,1)S(1)}, u32[]{:S(2)}, u32[]{:S(2)}) collective-permute-start(bf16[128,512]{1,0:T(8,128)(2,1)S(1)} %stack.16.refs_4_), channel_id=1, source_target_pairs={{0,16},{8,24},{16,0},{24,8},{1,17},{9,25},{17,1},{25,9},{2,18},{10... | collective-permute-start | bytes 393224 | tf_op jit(solution)/shard_map/ppermute | solution.py:187
  179.4 3.9 %collective-permute-start.29 = (bf16[128,512]{1,0:T(8,128)(2,1)S(1)}, bf16[128,512]{1,0:T(8,128)(2,1)S(1)}, u32[]{:S(2)}, u32[]{:S(2)}) collective-permute-start(bf16[128,512]{1,0:T(8,128)(2,1)S(1)} %stack.16.refs_4_), channel_id=1, source_target_pairs={{0,24},{8,0},{16,8},{24,16},{1,25},{9,1},{17,9},{25,17},{2,26},{10... | collective-permute-start | bytes 393224 | tf_op jit(solution)/shard_map/ppermute | solution.py:187
  185.6 15.3 %copy-start.4 = (bf16[16,4096]{1,0:T(8,128)(2,1)S(1)}, bf16[16,4096]{1,0:T(8,128)(2,1)}, u32[]{:S(2)}) copy-start(bf16[16,4096]{1,0:T(8,128)(2,1)} %copy-done.3) | copy-start | bytes 393220
  185.6 15.3 %copy-start.6 = (bf16[16,4096]{1,0:T(8,128)(2,1)S(1)}, bf16[16,4096]{1,0:T(8,128)(2,1)}, u32[]{:S(2)}) copy-start(bf16[16,4096]{1,0:T(8,128)(2,1)} %copy-done.5) | copy-start | bytes 393220
  185.6 15.3 %copy-start.8 = (bf16[16,4096]{1,0:T(8,128)(2,1)S(1)}, bf16[16,4096]{1,0:T(8,128)(2,1)}, u32[]{:S(2)}) copy-start(bf16[16,4096]{1,0:T(8,128)(2,1)} %copy-done.7) | copy-start | bytes 393220
  185.6 15.3 %copy-start.10 = (bf16[16,4096]{1,0:T(8,128)(2,1)S(1)}, bf16[16,4096]{1,0:T(8,128)(2,1)}, u32[]{:S(2)}) copy-start(bf16[16,4096]{1,0:T(8,128)(2,1)} %copy-done.9) | copy-start | bytes 393220
  185.6 15.3 %copy-start.12 = (bf16[16,4096]{1,0:T(8,128)(2,1)S(1)}, bf16[16,4096]{1,0:T(8,128)(2,1)}, u32[]{:S(2)}) copy-start(bf16[16,4096]{1,0:T(8,128)(2,1)} %copy-done.11) | copy-start | bytes 393220
  185.7 15.3 %copy-start.14 = (bf16[16,4096]{1,0:T(8,128)(2,1)S(1)}, bf16[16,4096]{1,0:T(8,128)(2,1)}, u32[]{:S(2)}) copy-start(bf16[16,4096]{1,0:T(8,128)(2,1)} %copy-done.13) | copy-start | bytes 393220
  185.7 15.3 %copy-start.16 = (bf16[16,4096]{1,0:T(8,128)(2,1)S(1)}, bf16[16,4096]{1,0:T(8,128)(2,1)}, u32[]{:S(2)}) copy-start(bf16[16,4096]{1,0:T(8,128)(2,1)} %copy-done.15) | copy-start | bytes 393220
  185.7 15.3 %copy-start.18 = (bf16[16,4096]{1,0:T(8,128)(2,1)S(1)}, bf16[16,4096]{1,0:T(8,128)(2,1)}, u32[]{:S(2)}) copy-start(bf16[16,4096]{1,0:T(8,128)(2,1)} %copy-done.17) | copy-start | bytes 393220
  185.7 15.3 %copy-start.20 = (bf16[16,4096]{1,0:T(8,128)(2,1)S(1)}, bf16[16,4096]{1,0:T(8,128)(2,1)}, u32[]{:S(2)}) copy-start(bf16[16,4096]{1,0:T(8,128)(2,1)} %copy-done.19) | copy-start | bytes 393220
  185.7 15.3 %copy-start.22 = (bf16[16,4096]{1,0:T(8,128)(2,1)S(1)}, bf16[16,4096]{1,0:T(8,128)(2,1)}, u32[]{:S(2)}) copy-start(bf16[16,4096]{1,0:T(8,128)(2,1)} %copy-done.21) | copy-start | bytes 393220
  185.7 15.3 %copy-start.24 = (bf16[16,4096]{1,0:T(8,128)(2,1)S(1)}, bf16[16,4096]{1,0:T(8,128)(2,1)}, u32[]{:S(2)}) copy-start(bf16[16,4096]{1,0:T(8,128)(2,1)} %copy-done.23) | copy-start | bytes 393220
  185.7 15.3 %copy-start.26 = (bf16[16,4096]{1,0:T(8,128)(2,1)S(1)}, bf16[16,4096]{1,0:T(8,128)(2,1)}, u32[]{:S(2)}) copy-start(bf16[16,4096]{1,0:T(8,128)(2,1)} %copy-done.25) | copy-start | bytes 393220
  185.7 15.3 %copy-start.28 = (bf16[16,4096]{1,0:T(8,128)(2,1)S(1)}, bf16[16,4096]{1,0:T(8,128)(2,1)}, u32[]{:S(2)}) copy-start(bf16[16,4096]{1,0:T(8,128)(2,1)} %copy-done.27) | copy-start | bytes 393220
  185.7 15.3 %copy-start.30 = (bf16[16,4096]{1,0:T(8,128)(2,1)S(1)}, bf16[16,4096]{1,0:T(8,128)(2,1)}, u32[]{:S(2)}) copy-start(bf16[16,4096]{1,0:T(8,128)(2,1)} %copy-done.29) | copy-start | bytes 393220
  185.7 15.3 %copy-start.32 = (bf16[16,4096]{1,0:T(8,128)(2,1)S(1)}, bf16[16,4096]{1,0:T(8,128)(2,1)}, u32[]{:S(2)}) copy-start(bf16[16,4096]{1,0:T(8,128)(2,1)} %copy-done.31) | copy-start | bytes 393220
  185.8 15.3 %copy-start.34 = (bf16[16,4096]{1,0:T(8,128)(2,1)S(1)}, bf16[16,4096]{1,0:T(8,128)(2,1)}, u32[]{:S(2)}) copy-start(bf16[16,4096]{1,0:T(8,128)(2,1)} %copy-done.33) | copy-start | bytes 393220
  185.8 31.2 %all-to-all-start.1 = ((bf16[16,64,512]{2,1,0:T(8,128)(2,1)}), bf16[16,64,512]{2,1,0:T(8,128)(2,1)}, u32[]{:S(2)}, u32[]{:S(2)}) async-start(bf16[16,64,512]{2,1,0:T(8,128)(2,1)} %bitcast.7), calls=%async_computation.1 | async-start | bytes 2097152 | tf_op jit(solution)/shard_map/all_to_all | solution.py:282
  (3 other events, 7.7 us)

commit v9 on v8

--- a/solution.py
+++ b/solution.py
@@ -85,8 +85,7 @@
             w_ref[pl.ds(at, piece), :] = ref[index]
 
 
-def part_kernel(start, across, *refs):
-    part_ref = refs[-1]
+def part_kernel(start, across, where, *refs):
     total = refs[2 * across][...] if start else None
     for tiles_ref, dv_ref in zip(refs[:across], refs[across : 2 * across], strict=True):
         tok = tiles_ref.shape[1]
@@ -102,7 +101,28 @@
             )
             total = term if total is None else total + term
             done += count
-    part_ref[...] = total.astype(part_ref.dtype)
+    if not start:
+        refs[-1][...] = total
+        return
+    keep_ref, give_ref, total_ref = refs[-3:]
+    total_ref[...] = total
+    count, piece, _ = keep_ref.shape
+    for index in range(count):
+        at = pl.multiple_of((2 * index + where[2]) * piece, piece)
+        keep_ref[index] = total_ref[pl.ds(at, piece), :]
+        at = pl.multiple_of((2 * index + 1 - where[2]) * piece, piece)
+        give_ref[index] = total_ref[pl.ds(at, piece), :].astype(BF16)
+
+
+def pair_kernel(keep_ref, got_ref, out_ref):
+    out_ref[...] = (keep_ref[...] + got_ref[...].astype(F32)).astype(BF16)
+
+
+def sum_kernel(pieces_ref, out_ref):
+    total = pieces_ref[0].astype(F32)
+    for index in range(1, pieces_ref.shape[0]):
+        total = total + pieces_ref[index].astype(F32)
+    out_ref[...] = total
 
 
 def task_of(step, section, npipe):
@@ -218,8 +238,8 @@
         (where, mine, other),
     )
 
-    def partial_sum(start, end, extra, kind):
-        rows = (end - start) * ROWS
+    def partial_sum(start, end, extra):
+        rows, whole = (end - start) * ROWS, width // across
         dv = kernel_call(
             functools.partial(stack_kernel, npipe, start),
             "stack",
@@ -228,14 +248,19 @@
             (stage, *gv_parts),
         )
         spread = exchanged([dv] * across, "dp_1")
+        kinds = (shape(halves, F32), shape(halves, BF16)) if start else shape((whole, kv_width), F32)
         return kernel_call(
             functools.partial(part_kernel, start * ROWS, across),
             "part",
-            shape((width // across, kv_width), kind),
-            [IN_VMEM] * (2 * across + len(extra)),
-            (*hidden, *spread, *extra),
+            kinds,
+            [IN_SMEM] + [IN_VMEM] * (2 * across + len(extra)),
+            (where, *hidden, *spread, *extra),
+            scratch=(pltpu.VMEM((whole, kv_width), F32),) if start else (),
         )
 
+    others = ("dp_0", "dp_2")
+    count = lax.axis_size(others)
+    halves = (count, w_value.shape[1], kv_width)
     steps = 2 * blocks + SLACK * (npipe - 1)
     sent, gx_parts, gv_parts = {}, [], []
     for step in range(steps):
@@ -265,7 +290,7 @@
         if pairs:
             sent[step] = lax.ppermute(dx, "pipe", pairs)
         if step == EARLY + SLACK * (npipe - 1) - 1:
-            early = partial_sum(0, EARLY, (), F32)
+            early = partial_sum(0, EARLY, ())
 
     grad_x = kernel_call(
         functools.partial(collect_kernel, npipe, blocks),
@@ -276,11 +301,11 @@
         scratch=(pltpu.SemaphoreType.DMA((steps,)),),
         out_spec=ANYWHERE,
     )[:, None]
-    part = partial_sum(EARLY, 2 * blocks, (early,), BF16)
-    others = ("dp_0", "dp_2", "dp_3")
-    pieces = part.reshape(lax.axis_size(others), -1, kv_width)
-    landed = lax.all_to_all(pieces, others, 0, 0, tiled=True)
-    grad_w = landed.astype(F32).sum(axis=0)[None]
+    keep, give = partial_sum(EARLY, 2 * blocks, (early,))
+    got = lax.ppermute(give, DP[3], [(0, 1), (1, 0)])
+    paired = kernel_call(pair_kernel, "pair", shape(halves, BF16), [IN_VMEM] * 2, (keep, got))
+    landed = lax.all_to_all(paired, others, 0, 0, tiled=True)
+    grad_w = kernel_call(sum_kernel, "sum", shape(halves[1:], F32), [IN_VMEM], (landed,))[None]
     return (grad_x, grad_w)
 
 

time: 220 us -> 213 us (0.968)
  starting transfers between devices: 80.6 us -> 73.2 us
    all_to_all x1, starting transfers between devices: 15.1 us -> 3.49 us  [on_device(): landed = lax.all_to_all(paired, others, 0, 0, tiled=True)]
    ppermute x0 -> x1, starting transfers between devices: none -> 10.7 us  [on_device(): got = lax.ppermute(give, DP[3], [(0, 1), (1, 0)])]
    all_to_all x1, waiting for transfers between devices: 14.3 us -> 6.53 us  [on_device(): landed = lax.all_to_all(paired, others, 0, 0, tiled=True)]
    ppermute x9, starting transfers between devices: 14.4 us -> 9.47 us  [exchanged(): moved.append(lax.ppermute(pieces[shift], axis, pairs))]
    ppermute x20, waiting for transfers between devices: 46.2 us -> 50 us  [on_device(): sent[step] = lax.ppermute(dx, 'pipe', pairs)]
    ppermute x9, waiting for transfers between devices: 17.1 us -> 19.6 us  [exchanged(): moved.append(lax.ppermute(pieces[shift], axis, pairs))]
    pallas_call x29 -> x31, Pallas kernels: 32.1 us -> 33.9 us  [kernel_call(): pl.pallas_call(kernel, out_shape=out_shape, in_specs=specs, out_specs=jax...]
  transfers between devices with their start and end apart: 32 -> 33, of which waited for: 16 -> 19; matrix products, arithmetic and copies ran while one was open for 0% -> 0% of each run, Pallas kernels for 13% -> 14%
where the time goes in v9:
time: 213 us; the launch traced here: 212 us
  waiting for transfers between devices  100 us (47%)
  starting transfers between devices  73.2 us (34%)
  Pallas kernels  33.9 us (16%)
  local copies, waits for them, and re-layouts  3.19 us (1%)
    ppermute x20, waiting for transfers between devices, on_device(): sent[step] = lax.ppermute(dx, 'pipe', pairs)  50 us
    ppermute x20, starting transfers between devices, on_device(): sent[step] = lax.ppermute(dx, 'pipe', pairs)  36 us
    pallas_call x31, Pallas kernels, kernel_call(): pl.pallas_call(kernel, out_shape=out_shape, in_specs=specs, out_specs=jax...  33.9 us
    all_to_all x1, waiting for transfers between devices, copy_for_each(): lax.all_to_all(jnp.broadcast_to(array[None], (count, *array.shape)), axis...  22.1 us
    ppermute x9, waiting for transfers between devices, exchanged(): moved.append(lax.ppermute(pieces[shift], axis, pairs))  19.6 us
    ppermute x1, starting transfers between devices, on_device(): got = lax.ppermute(give, DP[3], [(0, 1), (1, 0)])  10.7 us
    all_to_all x1, starting transfers between devices, copy_for_each(): lax.all_to_all(jnp.broadcast_to(array[None], (count, *array.shape)), axis...  9.49 us
    ppermute x9, starting transfers between devices, exchanged(): moved.append(lax.ppermute(pieces[shift], axis, pairs))  9.47 us
  transfers between devices with their start and end apart: 33, of which 19 were waited for; matrix products, arithmetic and copies ran while one was open for 0% of the time, Pallas kernels for 14%

profile of v9, /device:TPU:1, one launch (start us, length us, event | category | flops | bytes accessed | tf_op | source)
XLA Modules:
  0.0 212.0 jit_solution(11629083511899001801)
XLA Ops:
  0.6 2.4 %broadcast_in_dim.14 = bf16[32,64,512]{2,1,0:T(8,128)(2,1)} broadcast(bf16[64,512]{1,0:T(8,128)(2,1)} %bitcast.34), dimensions={1,2} | broadcast | bytes 2162688 | tf_op jit(solution)/shard_map/broadcast_in_dim | solution.py:28
  3.0 9.5 %all-to-all-start = ((bf16[32,64,512]{2,1,0:T(8,128)(2,1)}), bf16[32,64,512]{2,1,0:T(8,128)(2,1)}, u32[]{:S(2)}, u32[]{:S(2)}) async-start(bf16[32,64,512]{2,1,0:T(8,128)(2,1)} %broadcast_in_dim.14), calls=%async_computation | async-start | bytes 4194304 | tf_op jit(solution)/shard_map/all_to_all | solution.py:27
  12.6 3.4 %normalize.1 = (bf16[2,128,1024]{2,1,0:T(8,128)(2,1)S(1)}, bf16[2,128,1024]{2,1,0:T(8,128)(2,1)}, bf16[2,128,1024]{2,1,0:T(8,128)(2,1)}, bf16[2,128,1024]{2,1,0:T(8,128)(2,1)}) custom-call(s32[3]{0:T(128)S(1)} %pad_add_fusion.where, bf16[2,128,4096]{2,1,0:T(8,128)(2,1)S(1)} %bitcast.9, f32[2,1,4096]{2,1,0:T(1,128)S(1)} %copy-done.2), custom_call_target="tpu_custom_call" | custom-call | tf_op jit(solution)/shard_map/normalize/pallas_call | solution.py:33
  16.0 22.1 %all-to-all-done.value_ref = bf16[32,64,512]{2,1,0:T(8,128)(2,1)} async-done(((bf16[32,64,512]{2,1,0:T(8,128)(2,1)}), bf16[32,64,512]{2,1,0:T(8,128)(2,1)}, u32[]{:S(2)}, u32[]{:S(2)}) %all-to-all-start) | async-done | bytes 2097184 | tf_op jit(solution)/shard_map/all_to_all | solution.py:27
  38.0 4.0 %collective-permute-start = (bf16[32,64,512]{2,1,0:T(8,128)(2,1)}, bf16[32,64,512]{2,1,0:T(8,128)(2,1)S(1)}, u32[]{:S(2)}, u32[]{:S(2)}) collective-permute-start(bf16[32,64,512]{2,1,0:T(8,128)(2,1)} %held_until.1.mine_ref), channel_id=1, source_target_pairs={{0,1},{1,0},{2,3},{3,2},{4,5},{5,4},{6,7},{7,6},{8,9},{9,8},{10,11... | collective-permute-start | bytes 6291464 | tf_op jit(solution)/shard_map/ppermute | solution.py:231
  42.5 1.7 collective-permute-start.7
  44.2 1.5 collective-permute-start.8
  46.0 1.9 rows.1.w_ref
  50.8 1.3 collective-permute-start.5
  52.1 1.3 collective-permute-start.9
  53.4 14.8 %collective-permute-done.6.refs_1_ = bf16[2,128,1024]{2,1,0:T(8,128)(2,1)S(1)} collective-permute-done((bf16[2,128,1024]{2,1,0:T(8,128)(2,1)}, bf16[2,128,1024]{2,1,0:T(8,128)(2,1)S(1)}, u32[]{:S(2)}, u32[]{:S(2)}) %collective-permute-start.6) | collective-permute-done | bytes 524320 | tf_op jit(solution)/shard_map/ppermute | solution.py:207
  68.5 18.3 %collective-permute-done.5.in_ref = bf16[16,4096]{1,0:T(8,128)(2,1)S(1)} collective-permute-done((bf16[16,4096]{1,0:T(8,128)(2,1)S(1)}, bf16[16,4096]{1,0:T(8,128)(2,1)S(1)}, u32[]{:S(2)}, u32[]{:S(2)}) %collective-permute-start.5) | collective-permute-done | bytes 131104 | tf_op jit(solution)/shard_map/ppermute | solution.py:291
  86.8 1.3 section_step.28
  88.2 3.9 %collective-permute-start.10 = (bf16[16,4096]{1,0:T(8,128)(2,1)S(1)}, bf16[16,4096]{1,0:T(8,128)(2,1)S(1)}, u32[]{:S(2)}, u32[]{:S(2)}) collective-permute-start(bf16[16,4096]{1,0:T(8,128)(2,1)S(1)} %get-tuple-element.68.refs_6_), channel_id=1, source_target_pairs={{0,192},{64,0},{128,64},{192,128},{1,193},{65,1},{129,65},{193,129... | collective-permute-start | bytes 393224 | tf_op jit(solution)/shard_map/ppermute | solution.py:291
  92.1 1.3 section_step.29
  93.5 4.7 %collective-permute-start.11 = (bf16[16,4096]{1,0:T(8,128)(2,1)S(1)}, bf16[16,4096]{1,0:T(8,128)(2,1)S(1)}, u32[]{:S(2)}, u32[]{:S(2)}) collective-permute-start(bf16[16,4096]{1,0:T(8,128)(2,1)S(1)} %get-tuple-element.70.refs_7_), channel_id=1, source_target_pairs={{0,192},{64,0},{128,64},{192,128},{1,193},{65,1},{129,65},{193,129... | collective-permute-start | bytes 393224 | tf_op jit(solution)/shard_map/ppermute | solution.py:291
  98.2 2.3 %collective-permute-done.10.in_ref = bf16[16,4096]{1,0:T(8,128)(2,1)S(1)} collective-permute-done((bf16[16,4096]{1,0:T(8,128)(2,1)S(1)}, bf16[16,4096]{1,0:T(8,128)(2,1)S(1)}, u32[]{:S(2)}, u32[]{:S(2)}) %collective-permute-start.10) | collective-permute-done | bytes 131104 | tf_op jit(solution)/shard_map/ppermute | solution.py:291
  100.5 1.3 section_step.30
  101.9 0.9 collective-permute-start.12
  102.8 1.3 section_step.31
  104.1 5.9 %collective-permute-start.13 = (bf16[16,4096]{1,0:T(8,128)(2,1)S(1)}, bf16[16,4096]{1,0:T(8,128)(2,1)S(1)}, u32[]{:S(2)}, u32[]{:S(2)}) collective-permute-start(bf16[16,4096]{1,0:T(8,128)(2,1)S(1)} %get-tuple-element.74.refs_9_), channel_id=1, source_target_pairs={{0,192},{64,0},{128,64},{192,128},{1,193},{65,1},{129,65},{193,129... | collective-permute-start | bytes 393224 | tf_op jit(solution)/shard_map/ppermute | solution.py:291
  110.0 1.3 section_step.32
  111.4 3.0 %collective-permute-start.14 = (bf16[16,4096]{1,0:T(8,128)(2,1)S(1)}, bf16[16,4096]{1,0:T(8,128)(2,1)S(1)}, u32[]{:S(2)}, u32[]{:S(2)}) collective-permute-start(bf16[16,4096]{1,0:T(8,128)(2,1)S(1)} %get-tuple-element.76.refs_10_), channel_id=1, source_target_pairs={{0,192},{64,0},{128,64},{192,128},{1,193},{65,1},{129,65},{193,129... | collective-permute-start | bytes 393224 | tf_op jit(solution)/shard_map/ppermute | solution.py:291
  114.4 1.3 collective-permute-done.13.in_ref
  115.7 1.3 section_step.33
  117.1 4.1 %collective-permute-start.15 = (bf16[16,4096]{1,0:T(8,128)(2,1)S(1)}, bf16[16,4096]{1,0:T(8,128)(2,1)S(1)}, u32[]{:S(2)}, u32[]{:S(2)}) collective-permute-start(bf16[16,4096]{1,0:T(8,128)(2,1)S(1)} %get-tuple-element.78.refs_11_), channel_id=1, source_target_pairs={{0,192},{64,0},{128,64},{192,128},{1,193},{65,1},{129,65},{193,129... | collective-permute-start | bytes 393224 | tf_op jit(solution)/shard_map/ppermute | solution.py:291
  121.2 2.0 collective-permute-done.14.in_ref
  123.2 1.3 section_step.34
  124.7 4.3 %collective-permute-done.15.in_ref = bf16[16,4096]{1,0:T(8,128)(2,1)S(1)} collective-permute-done((bf16[16,4096]{1,0:T(8,128)(2,1)S(1)}, bf16[16,4096]{1,0:T(8,128)(2,1)S(1)}, u32[]{:S(2)}, u32[]{:S(2)}) %collective-permute-start.15) | collective-permute-done | bytes 131104 | tf_op jit(solution)/shard_map/ppermute | solution.py:291
  128.9 1.3 section_step.35
  130.5 3.5 %collective-permute-done.16.in_ref = bf16[16,4096]{1,0:T(8,128)(2,1)S(1)} collective-permute-done((bf16[16,4096]{1,0:T(8,128)(2,1)S(1)}, bf16[16,4096]{1,0:T(8,128)(2,1)S(1)}, u32[]{:S(2)}, u32[]{:S(2)}) %collective-permute-start.16) | collective-permute-done | bytes 131104 | tf_op jit(solution)/shard_map/ppermute | solution.py:291
  134.0 1.3 section_step.36
  135.3 1.3 collective-permute-start.18
  136.6 1.7 collective-permute-done.17.in_ref
  138.3 1.3 section_step.37
  139.7 1.3 collective-permute-start.19
  141.9 2.1 collective-permute-start.23
  144.0 1.3 section_step.38
  145.4 1.3 collective-permute-start.20
  146.7 1.9 collective-permute-done.19.in_ref
  148.6 1.3 section_step.39
  150.0 1.5 collective-permute-start.24
  151.5 1.8 part.2.refs_1_.refs_8_
  153.3 3.4 %collective-permute-done.20.in_ref = bf16[16,4096]{1,0:T(8,128)(2,1)S(1)} collective-permute-done((bf16[16,4096]{1,0:T(8,128)(2,1)S(1)}, bf16[16,4096]{1,0:T(8,128)(2,1)S(1)}, u32[]{:S(2)}, u32[]{:S(2)}) %collective-permute-start.20) | collective-permute-done | bytes 131104 | tf_op jit(solution)/shard_map/ppermute | solution.py:291
  156.8 1.3 section_step.40
  158.1 1.3 collective-permute-start.25
  159.4 1.3 section_step.41
  160.8 1.3 collective-permute-start.26
  162.1 7.8 %collective-permute-done.25.in_ref = bf16[16,4096]{1,0:T(8,128)(2,1)S(1)} collective-permute-done((bf16[16,4096]{1,0:T(8,128)(2,1)S(1)}, bf16[16,4096]{1,0:T(8,128)(2,1)S(1)}, u32[]{:S(2)}, u32[]{:S(2)}) %collective-permute-start.25) | collective-permute-done | bytes 131104 | tf_op jit(solution)/shard_map/ppermute | solution.py:291
  169.9 1.3 section_step.42
  171.9 3.4 %collective-permute-done.26.in_ref = bf16[16,4096]{1,0:T(8,128)(2,1)S(1)} collective-permute-done((bf16[16,4096]{1,0:T(8,128)(2,1)S(1)}, bf16[16,4096]{1,0:T(8,128)(2,1)S(1)}, u32[]{:S(2)}, u32[]{:S(2)}) %collective-permute-start.26) | collective-permute-done | bytes 131104 | tf_op jit(solution)/shard_map/ppermute | solution.py:291
  175.3 1.3 section_step.43
  176.9 1.9 collective-permute-start.28
  178.8 1.0 collective-permute-start.29
  179.8 3.6 %collective-permute-done.27.refs_5_ = bf16[128,512]{1,0:T(8,128)(2,1)S(1)} collective-permute-done((bf16[128,512]{1,0:T(8,128)(2,1)S(1)}, bf16[128,512]{1,0:T(8,128)(2,1)S(1)}, u32[]{:S(2)}, u32[]{:S(2)}) %collective-permute-start.27) | collective-permute-done | bytes 131104 | tf_op jit(solution)/shard_map/ppermute | solution.py:207
  183.5 0.8 collective-permute-done.29.refs_7_
  184.3 1.9 part.3
  186.4 10.7 %collective-permute-start.30 = (bf16[8,64,512]{2,1,0:T(8,128)(2,1)S(1)}, bf16[8,64,512]{2,1,0:T(8,128)(2,1)S(1)}, u32[]{:S(2)}, u32[]{:S(2)}) collective-permute-start(bf16[8,64,512]{2,1,0:T(8,128)(2,1)S(1)} %get-tuple-element.101), channel_id=1, source_target_pairs={{0,1},{1,0},{2,3},{3,2},{4,5},{5,4},{6,7},{7,6},{8,9},{9,8},{10,11... | collective-permute-start | bytes 1572872 | tf_op jit(solution)/shard_map/ppermute | solution.py:305
  197.1 1.5 collective-permute-done.30.got_ref
  198.6 0.9 pair.1
  199.5 3.5 %all-to-all-start.1 = ((bf16[8,64,512]{2,1,0:T(8,128)(2,1)}), bf16[8,64,512]{2,1,0:T(8,128)(2,1)S(1)}, u32[]{:S(2)}, u32[]{:S(2)}) async-start(bf16[8,64,512]{2,1,0:T(8,128)(2,1)} %pair.1), calls=%async_computation.1 | async-start | bytes 1048576 | tf_op jit(solution)/shard_map/all_to_all | solution.py:307
  203.2 1.5 collect_rows.1
  204.7 6.5 %all-to-all-done.1.pieces_ref = bf16[8,64,512]{2,1,0:T(8,128)(2,1)S(1)} async-done(((bf16[8,64,512]{2,1,0:T(8,128)(2,1)}), bf16[8,64,512]{2,1,0:T(8,128)(2,1)S(1)}, u32[]{:S(2)}, u32[]{:S(2)}) %all-to-all-start.1) | async-done | bytes 524320 | tf_op jit(solution)/shard_map/all_to_all | solution.py:307
  211.3 0.7 sum.1
  (107 shorter events, 6.2 us)
Async XLA Ops:
  3.0 9.6 %copy-start = (bf16[2,1,128,4096]{3,2,1,0:T(8,128)(2,1)S(1)}, bf16[2,1,128,4096]{3,2,1,0:T(8,128)(2,1)}, u32[]{:S(2)}) copy-start(bf16[2,1,128,4096]{3,2,1,0:T(8,128)(2,1)} %param.4) | copy-start | bytes 6291460
  3.0 9.6 %copy-start.2 = (f32[2,1,4096]{2,1,0:T(1,128)S(1)}, f32[2,1,4096]{2,1,0:T(1,128)}, u32[]{:S(2)}) copy-start(f32[2,1,4096]{2,1,0:T(1,128)} %g_ref.45) | copy-start | bytes 98308
  3.0 35.0 %all-to-all-start = ((bf16[32,64,512]{2,1,0:T(8,128)(2,1)}), bf16[32,64,512]{2,1,0:T(8,128)(2,1)}, u32[]{:S(2)}, u32[]{:S(2)}) async-start(bf16[32,64,512]{2,1,0:T(8,128)(2,1)} %broadcast_in_dim.14), calls=%async_computation | async-start | bytes 4194304 | tf_op jit(solution)/shard_map/all_to_all | solution.py:27
  38.0 8.0 %collective-permute-start = (bf16[32,64,512]{2,1,0:T(8,128)(2,1)}, bf16[32,64,512]{2,1,0:T(8,128)(2,1)S(1)}, u32[]{:S(2)}, u32[]{:S(2)}) collective-permute-start(bf16[32,64,512]{2,1,0:T(8,128)(2,1)} %held_until.1.mine_ref), channel_id=1, source_target_pairs={{0,1},{1,0},{2,3},{3,2},{4,5},{5,4},{6,7},{7,6},{8,9},{9,8},{10,11... | collective-permute-start | bytes 6291464 | tf_op jit(solution)/shard_map/ppermute | solution.py:231
  42.0 26.2 %collective-permute-start.6 = (bf16[2,128,1024]{2,1,0:T(8,128)(2,1)}, bf16[2,128,1024]{2,1,0:T(8,128)(2,1)S(1)}, u32[]{:S(2)}, u32[]{:S(2)}) collective-permute-start(bf16[2,128,1024]{2,1,0:T(8,128)(2,1)} %get-tuple-element.65), channel_id=1, source_target_pairs={{0,8},{8,16},{16,24},{24,0},{1,9},{9,17},{17,25},{25,1},{2,10},{10... | collective-permute-start | bytes 1572872 | tf_op jit(solution)/shard_map/ppermute | solution.py:207
  42.5 25.8 %collective-permute-start.7 = (bf16[2,128,1024]{2,1,0:T(8,128)(2,1)}, bf16[2,128,1024]{2,1,0:T(8,128)(2,1)S(1)}, u32[]{:S(2)}, u32[]{:S(2)}) collective-permute-start(bf16[2,128,1024]{2,1,0:T(8,128)(2,1)} %get-tuple-element.66), channel_id=1, source_target_pairs={{0,16},{8,24},{16,0},{24,8},{1,17},{9,25},{17,1},{25,9},{2,18},{10... | collective-permute-start | bytes 1572872 | tf_op jit(solution)/shard_map/ppermute | solution.py:207
  44.2 3.8 %copy-start.1 = (bf16[128,4096]{1,0:T(8,128)(2,1)S(1)}, bf16[128,4096]{1,0:T(8,128)(2,1)}, u32[]{:S(2)}) copy-start(bf16[128,4096]{1,0:T(8,128)(2,1)} %fresh_ref.43) | copy-start | bytes 3145732
  44.2 24.4 %collective-permute-start.8 = (bf16[2,128,1024]{2,1,0:T(8,128)(2,1)}, bf16[2,128,1024]{2,1,0:T(8,128)(2,1)S(1)}, u32[]{:S(2)}, u32[]{:S(2)}) collective-permute-start(bf16[2,128,1024]{2,1,0:T(8,128)(2,1)} %get-tuple-element.67), channel_id=1, source_target_pairs={{0,24},{8,0},{16,8},{24,16},{1,25},{9,1},{17,9},{25,17},{2,26},{10... | collective-permute-start | bytes 1572872 | tf_op jit(solution)/shard_map/ppermute | solution.py:207
  48.0 1.4 collective-permute-start.1
  48.6 1.4 collective-permute-start.2
  49.4 1.4 collective-permute-start.3
  50.1 2.0 collective-permute-start.4
  50.8 36.0 %collective-permute-start.5 = (bf16[16,4096]{1,0:T(8,128)(2,1)S(1)}, bf16[16,4096]{1,0:T(8,128)(2,1)S(1)}, u32[]{:S(2)}, u32[]{:S(2)}) collective-permute-start(bf16[16,4096]{1,0:T(8,128)(2,1)S(1)} %get-tuple-element.61.refs_4_), channel_id=1, source_target_pairs={{64,0},{128,64},{192,128},{65,1},{129,65},{193,129},{66,2},{130,66... | collective-permute-start | bytes 393224 | tf_op jit(solution)/shard_map/ppermute | solution.py:291
  52.1 40.0 %collective-permute-start.9 = (bf16[16,4096]{1,0:T(8,128)(2,1)S(1)}, bf16[16,4096]{1,0:T(8,128)(2,1)S(1)}, u32[]{:S(2)}, u32[]{:S(2)}) collective-permute-start(bf16[16,4096]{1,0:T(8,128)(2,1)S(1)} %get-tuple-element.63.refs_5_), channel_id=1, source_target_pairs={{64,0},{128,64},{192,128},{65,1},{129,65},{193,129},{66,2},{130,66... | collective-permute-start | bytes 393224 | tf_op jit(solution)/shard_map/ppermute | solution.py:291
  88.2 5.3 %copy-start.3 = (bf16[16,4096]{1,0:T(8,128)(2,1)}, bf16[16,4096]{1,0:T(8,128)(2,1)S(1)}, u32[]{:S(2)}) copy-start(bf16[16,4096]{1,0:T(8,128)(2,1)S(1)} %get-tuple-element.68.refs_6_) | copy-start | bytes 393220
  88.2 12.3 %collective-permute-start.10 = (bf16[16,4096]{1,0:T(8,128)(2,1)S(1)}, bf16[16,4096]{1,0:T(8,128)(2,1)S(1)}, u32[]{:S(2)}, u32[]{:S(2)}) collective-permute-start(bf16[16,4096]{1,0:T(8,128)(2,1)S(1)} %get-tuple-element.68.refs_6_), channel_id=1, source_target_pairs={{0,192},{64,0},{128,64},{192,128},{1,193},{65,1},{129,65},{193,129... | collective-permute-start | bytes 393224 | tf_op jit(solution)/shard_map/ppermute | solution.py:291
  93.5 8.4 %copy-start.5 = (bf16[16,4096]{1,0:T(8,128)(2,1)}, bf16[16,4096]{1,0:T(8,128)(2,1)S(1)}, u32[]{:S(2)}) copy-start(bf16[16,4096]{1,0:T(8,128)(2,1)S(1)} %get-tuple-element.70.refs_7_) | copy-start | bytes 393220
  93.5 9.3 %collective-permute-start.11 = (bf16[16,4096]{1,0:T(8,128)(2,1)S(1)}, bf16[16,4096]{1,0:T(8,128)(2,1)S(1)}, u32[]{:S(2)}, u32[]{:S(2)}) collective-permute-start(bf16[16,4096]{1,0:T(8,128)(2,1)S(1)} %get-tuple-element.70.refs_7_), channel_id=1, source_target_pairs={{0,192},{64,0},{128,64},{192,128},{1,193},{65,1},{129,65},{193,129... | collective-permute-start | bytes 393224 | tf_op jit(solution)/shard_map/ppermute | solution.py:291
  101.9 8.1 %collective-permute-start.12 = (bf16[16,4096]{1,0:T(8,128)(2,1)S(1)}, bf16[16,4096]{1,0:T(8,128)(2,1)S(1)}, u32[]{:S(2)}, u32[]{:S(2)}) collective-permute-start(bf16[16,4096]{1,0:T(8,128)(2,1)S(1)} %get-tuple-element.72.refs_8_), channel_id=1, source_target_pairs={{0,192},{64,0},{128,64},{192,128},{1,193},{65,1},{129,65},{193,129... | collective-permute-start | bytes 393224 | tf_op jit(solution)/shard_map/ppermute | solution.py:291
  104.1 7.2 %copy-start.9 = (bf16[16,4096]{1,0:T(8,128)(2,1)}, bf16[16,4096]{1,0:T(8,128)(2,1)S(1)}, u32[]{:S(2)}) copy-start(bf16[16,4096]{1,0:T(8,128)(2,1)S(1)} %get-tuple-element.74.refs_9_) | copy-start | bytes 393220
  104.1 11.6 %collective-permute-start.13 = (bf16[16,4096]{1,0:T(8,128)(2,1)S(1)}, bf16[16,4096]{1,0:T(8,128)(2,1)S(1)}, u32[]{:S(2)}, u32[]{:S(2)}) collective-permute-start(bf16[16,4096]{1,0:T(8,128)(2,1)S(1)} %get-tuple-element.74.refs_9_), channel_id=1, source_target_pairs={{0,192},{64,0},{128,64},{192,128},{1,193},{65,1},{129,65},{193,129... | collective-permute-start | bytes 393224 | tf_op jit(solution)/shard_map/ppermute | solution.py:291
  111.4 5.7 %copy-start.11 = (bf16[16,4096]{1,0:T(8,128)(2,1)}, bf16[16,4096]{1,0:T(8,128)(2,1)S(1)}, u32[]{:S(2)}) copy-start(bf16[16,4096]{1,0:T(8,128)(2,1)S(1)} %get-tuple-element.76.refs_10_) | copy-start | bytes 393220
  111.4 11.9 %collective-permute-start.14 = (bf16[16,4096]{1,0:T(8,128)(2,1)S(1)}, bf16[16,4096]{1,0:T(8,128)(2,1)S(1)}, u32[]{:S(2)}, u32[]{:S(2)}) collective-permute-start(bf16[16,4096]{1,0:T(8,128)(2,1)S(1)} %get-tuple-element.76.refs_10_), channel_id=1, source_target_pairs={{0,192},{64,0},{128,64},{192,128},{1,193},{65,1},{129,65},{193,129... | collective-permute-start | bytes 393224 | tf_op jit(solution)/shard_map/ppermute | solution.py:291
  117.1 7.5 %copy-start.13 = (bf16[16,4096]{1,0:T(8,128)(2,1)}, bf16[16,4096]{1,0:T(8,128)(2,1)S(1)}, u32[]{:S(2)}) copy-start(bf16[16,4096]{1,0:T(8,128)(2,1)S(1)} %get-tuple-element.78.refs_11_) | copy-start | bytes 393220
  117.1 11.9 %collective-permute-start.15 = (bf16[16,4096]{1,0:T(8,128)(2,1)S(1)}, bf16[16,4096]{1,0:T(8,128)(2,1)S(1)}, u32[]{:S(2)}, u32[]{:S(2)}) collective-permute-start(bf16[16,4096]{1,0:T(8,128)(2,1)S(1)} %get-tuple-element.78.refs_11_), channel_id=1, source_target_pairs={{0,192},{64,0},{128,64},{192,128},{1,193},{65,1},{129,65},{193,129... | collective-permute-start | bytes 393224 | tf_op jit(solution)/shard_map/ppermute | solution.py:291
  124.6 5.7 %copy-start.15 = (bf16[16,4096]{1,0:T(8,128)(2,1)}, bf16[16,4096]{1,0:T(8,128)(2,1)S(1)}, u32[]{:S(2)}) copy-start(bf16[16,4096]{1,0:T(8,128)(2,1)S(1)} %get-tuple-element.80.refs_12_) | copy-start | bytes 393220
  124.6 9.4 %collective-permute-start.16 = (bf16[16,4096]{1,0:T(8,128)(2,1)S(1)}, bf16[16,4096]{1,0:T(8,128)(2,1)S(1)}, u32[]{:S(2)}, u32[]{:S(2)}) collective-permute-start(bf16[16,4096]{1,0:T(8,128)(2,1)S(1)} %get-tuple-element.80.refs_12_), channel_id=1, source_target_pairs={{0,192},{64,0},{128,64},{192,128},{1,193},{65,1},{129,65},{193,129... | collective-permute-start | bytes 393224 | tf_op jit(solution)/shard_map/ppermute | solution.py:291
  130.3 5.0 %copy-start.17 = (bf16[16,4096]{1,0:T(8,128)(2,1)}, bf16[16,4096]{1,0:T(8,128)(2,1)S(1)}, u32[]{:S(2)}) copy-start(bf16[16,4096]{1,0:T(8,128)(2,1)S(1)} %get-tuple-element.82.refs_13_) | copy-start | bytes 393220
  130.3 8.0 %collective-permute-start.17 = (bf16[16,4096]{1,0:T(8,128)(2,1)S(1)}, bf16[16,4096]{1,0:T(8,128)(2,1)S(1)}, u32[]{:S(2)}, u32[]{:S(2)}) collective-permute-start(bf16[16,4096]{1,0:T(8,128)(2,1)S(1)} %get-tuple-element.82.refs_13_), channel_id=1, source_target_pairs={{0,192},{64,0},{128,64},{192,128},{1,193},{65,1},{129,65},{193,129... | collective-permute-start | bytes 393224 | tf_op jit(solution)/shard_map/ppermute | solution.py:291
  135.3 4.4 %copy-start.19 = (bf16[16,4096]{1,0:T(8,128)(2,1)}, bf16[16,4096]{1,0:T(8,128)(2,1)S(1)}, u32[]{:S(2)}) copy-start(bf16[16,4096]{1,0:T(8,128)(2,1)S(1)} %get-tuple-element.84.refs_14_) | copy-start | bytes 393220
  135.3 8.7 %collective-permute-start.18 = (bf16[16,4096]{1,0:T(8,128)(2,1)S(1)}, bf16[16,4096]{1,0:T(8,128)(2,1)S(1)}, u32[]{:S(2)}, u32[]{:S(2)}) collective-permute-start(bf16[16,4096]{1,0:T(8,128)(2,1)S(1)} %get-tuple-element.84.refs_14_), channel_id=1, source_target_pairs={{64,0},{128,64},{192,128},{65,1},{129,65},{193,129},{66,2},{130,66... | collective-permute-start | bytes 393224 | tf_op jit(solution)/shard_map/ppermute | solution.py:291
  139.7 5.6 %copy-start.21 = (bf16[16,4096]{1,0:T(8,128)(2,1)}, bf16[16,4096]{1,0:T(8,128)(2,1)S(1)}, u32[]{:S(2)}) copy-start(bf16[16,4096]{1,0:T(8,128)(2,1)S(1)} %get-tuple-element.86.refs_15_) | copy-start | bytes 393220
  139.7 8.9 %collective-permute-start.19 = (bf16[16,4096]{1,0:T(8,128)(2,1)S(1)}, bf16[16,4096]{1,0:T(8,128)(2,1)S(1)}, u32[]{:S(2)}, u32[]{:S(2)}) collective-permute-start(bf16[16,4096]{1,0:T(8,128)(2,1)S(1)} %get-tuple-element.86.refs_15_), channel_id=1, source_target_pairs={{64,0},{128,64},{192,128},{65,1},{129,65},{193,129},{66,2},{130,66... | collective-permute-start | bytes 393224 | tf_op jit(solution)/shard_map/ppermute | solution.py:291
  141.1 10.4 %collective-permute-start.21 = (bf16[128,512]{1,0:T(8,128)(2,1)S(1)}, bf16[128,512]{1,0:T(8,128)(2,1)S(1)}, u32[]{:S(2)}, u32[]{:S(2)}) collective-permute-start(bf16[128,512]{1,0:T(8,128)(2,1)S(1)} %stack.15.refs_4_), channel_id=1, source_target_pairs={{0,8},{8,16},{16,24},{24,0},{1,9},{9,17},{17,25},{25,1},{2,10},{10... | collective-permute-start | bytes 393224 | tf_op jit(solution)/shard_map/ppermute | solution.py:207
  141.5 10.0 %collective-permute-start.22 = (bf16[128,512]{1,0:T(8,128)(2,1)S(1)}, bf16[128,512]{1,0:T(8,128)(2,1)S(1)}, u32[]{:S(2)}, u32[]{:S(2)}) collective-permute-start(bf16[128,512]{1,0:T(8,128)(2,1)S(1)} %stack.15.refs_4_), channel_id=1, source_target_pairs={{0,16},{8,24},{16,0},{24,8},{1,17},{9,25},{17,1},{25,9},{2,18},{10... | collective-permute-start | bytes 393224 | tf_op jit(solution)/shard_map/ppermute | solution.py:207
  141.9 9.6 %collective-permute-start.23 = (bf16[128,512]{1,0:T(8,128)(2,1)S(1)}, bf16[128,512]{1,0:T(8,128)(2,1)S(1)}, u32[]{:S(2)}, u32[]{:S(2)}) collective-permute-start(bf16[128,512]{1,0:T(8,128)(2,1)S(1)} %stack.15.refs_4_), channel_id=1, source_target_pairs={{0,24},{8,0},{16,8},{24,16},{1,25},{9,1},{17,9},{25,17},{2,26},{10... | collective-permute-start | bytes 393224 | tf_op jit(solution)/shard_map/ppermute | solution.py:207
  145.3 4.6 %copy-start.23 = (bf16[16,4096]{1,0:T(8,128)(2,1)}, bf16[16,4096]{1,0:T(8,128)(2,1)S(1)}, u32[]{:S(2)}) copy-start(bf16[16,4096]{1,0:T(8,128)(2,1)S(1)} %get-tuple-element.88.refs_16_) | copy-start | bytes 393220
  145.4 11.4 %collective-permute-start.20 = (bf16[16,4096]{1,0:T(8,128)(2,1)S(1)}, bf16[16,4096]{1,0:T(8,128)(2,1)S(1)}, u32[]{:S(2)}, u32[]{:S(2)}) collective-permute-start(bf16[16,4096]{1,0:T(8,128)(2,1)S(1)} %get-tuple-element.88.refs_16_), channel_id=1, source_target_pairs={{64,0},{128,64},{65,1},{129,65},{66,2},{130,66},{67,3},{131,67},{6... | collective-permute-start | bytes 393224 | tf_op jit(solution)/shard_map/ppermute | solution.py:291
  150.0 9.5 %collective-permute-start.24 = (bf16[16,4096]{1,0:T(8,128)(2,1)S(1)}, bf16[16,4096]{1,0:T(8,128)(2,1)S(1)}, u32[]{:S(2)}, u32[]{:S(2)}) collective-permute-start(bf16[16,4096]{1,0:T(8,128)(2,1)S(1)} %get-tuple-element.90.refs_17_), channel_id=1, source_target_pairs={{64,0},{128,64},{65,1},{129,65},{66,2},{130,66},{67,3},{131,67},{6... | collective-permute-start | bytes 393224 | tf_op jit(solution)/shard_map/ppermute | solution.py:291
  158.1 11.8 %collective-permute-start.25 = (bf16[16,4096]{1,0:T(8,128)(2,1)S(1)}, bf16[16,4096]{1,0:T(8,128)(2,1)S(1)}, u32[]{:S(2)}, u32[]{:S(2)}) collective-permute-start(bf16[16,4096]{1,0:T(8,128)(2,1)S(1)} %get-tuple-element.92.refs_18_), channel_id=1, source_target_pairs={{64,0},{65,1},{66,2},{67,3},{68,4},{69,5},{70,6},{71,7},{72,8},{73... | collective-permute-start | bytes 393224 | tf_op jit(solution)/shard_map/ppermute | solution.py:291
  160.8 10.4 %copy-start.29 = (bf16[16,4096]{1,0:T(8,128)(2,1)}, bf16[16,4096]{1,0:T(8,128)(2,1)S(1)}, u32[]{:S(2)}) copy-start(bf16[16,4096]{1,0:T(8,128)(2,1)S(1)} %get-tuple-element.94.refs_19_) | copy-start | bytes 393220
  160.8 14.5 %collective-permute-start.26 = (bf16[16,4096]{1,0:T(8,128)(2,1)S(1)}, bf16[16,4096]{1,0:T(8,128)(2,1)S(1)}, u32[]{:S(2)}, u32[]{:S(2)}) collective-permute-start(bf16[16,4096]{1,0:T(8,128)(2,1)S(1)} %get-tuple-element.94.refs_19_), channel_id=1, source_target_pairs={{64,0},{65,1},{66,2},{67,3},{68,4},{69,5},{70,6},{71,7},{72,8},{73... | collective-permute-start | bytes 393224 | tf_op jit(solution)/shard_map/ppermute | solution.py:291
  176.6 9.5 %copy-start.33 = (bf16[16,4096]{1,0:T(8,128)(2,1)}, bf16[16,4096]{1,0:T(8,128)(2,1)S(1)}, u32[]{:S(2)}) copy-start(bf16[16,4096]{1,0:T(8,128)(2,1)S(1)} %get-tuple-element.98.refs_21_) | copy-start | bytes 393220
  176.8 6.6 %collective-permute-start.27 = (bf16[128,512]{1,0:T(8,128)(2,1)S(1)}, bf16[128,512]{1,0:T(8,128)(2,1)S(1)}, u32[]{:S(2)}, u32[]{:S(2)}) collective-permute-start(bf16[128,512]{1,0:T(8,128)(2,1)S(1)} %stack.16.refs_4_), channel_id=1, source_target_pairs={{0,8},{8,16},{16,24},{24,0},{1,9},{9,17},{17,25},{25,1},{2,10},{10... | collective-permute-start | bytes 393224 | tf_op jit(solution)/shard_map/ppermute | solution.py:207
  176.9 6.6 %collective-permute-start.28 = (bf16[128,512]{1,0:T(8,128)(2,1)S(1)}, bf16[128,512]{1,0:T(8,128)(2,1)S(1)}, u32[]{:S(2)}, u32[]{:S(2)}) collective-permute-start(bf16[128,512]{1,0:T(8,128)(2,1)S(1)} %stack.16.refs_4_), channel_id=1, source_target_pairs={{0,16},{8,24},{16,0},{24,8},{1,17},{9,25},{17,1},{25,9},{2,18},{10... | collective-permute-start | bytes 393224 | tf_op jit(solution)/shard_map/ppermute | solution.py:207
  178.8 5.5 %collective-permute-start.29 = (bf16[128,512]{1,0:T(8,128)(2,1)S(1)}, bf16[128,512]{1,0:T(8,128)(2,1)S(1)}, u32[]{:S(2)}, u32[]{:S(2)}) collective-permute-start(bf16[128,512]{1,0:T(8,128)(2,1)S(1)} %stack.16.refs_4_), channel_id=1, source_target_pairs={{0,24},{8,0},{16,8},{24,16},{1,25},{9,1},{17,9},{25,17},{2,26},{10... | collective-permute-start | bytes 393224 | tf_op jit(solution)/shard_map/ppermute | solution.py:207
  186.2 16.8 %copy-start.4 = (bf16[16,4096]{1,0:T(8,128)(2,1)S(1)}, bf16[16,4096]{1,0:T(8,128)(2,1)}, u32[]{:S(2)}) copy-start(bf16[16,4096]{1,0:T(8,128)(2,1)} %copy-done.3) | copy-start | bytes 393220
  186.2 16.8 %copy-start.6 = (bf16[16,4096]{1,0:T(8,128)(2,1)S(1)}, bf16[16,4096]{1,0:T(8,128)(2,1)}, u32[]{:S(2)}) copy-start(bf16[16,4096]{1,0:T(8,128)(2,1)} %copy-done.5) | copy-start | bytes 393220
  186.2 16.8 %copy-start.8 = (bf16[16,4096]{1,0:T(8,128)(2,1)S(1)}, bf16[16,4096]{1,0:T(8,128)(2,1)}, u32[]{:S(2)}) copy-start(bf16[16,4096]{1,0:T(8,128)(2,1)} %copy-done.7) | copy-start | bytes 393220
  186.2 16.8 %copy-start.10 = (bf16[16,4096]{1,0:T(8,128)(2,1)S(1)}, bf16[16,4096]{1,0:T(8,128)(2,1)}, u32[]{:S(2)}) copy-start(bf16[16,4096]{1,0:T(8,128)(2,1)} %copy-done.9) | copy-start | bytes 393220
  186.2 16.8 %copy-start.12 = (bf16[16,4096]{1,0:T(8,128)(2,1)S(1)}, bf16[16,4096]{1,0:T(8,128)(2,1)}, u32[]{:S(2)}) copy-start(bf16[16,4096]{1,0:T(8,128)(2,1)} %copy-done.11) | copy-start | bytes 393220
  186.3 16.8 %copy-start.14 = (bf16[16,4096]{1,0:T(8,128)(2,1)S(1)}, bf16[16,4096]{1,0:T(8,128)(2,1)}, u32[]{:S(2)}) copy-start(bf16[16,4096]{1,0:T(8,128)(2,1)} %copy-done.13) | copy-start | bytes 393220
  186.3 16.8 %copy-start.16 = (bf16[16,4096]{1,0:T(8,128)(2,1)S(1)}, bf16[16,4096]{1,0:T(8,128)(2,1)}, u32[]{:S(2)}) copy-start(bf16[16,4096]{1,0:T(8,128)(2,1)} %copy-done.15) | copy-start | bytes 393220
  186.3 16.8 %copy-start.18 = (bf16[16,4096]{1,0:T(8,128)(2,1)S(1)}, bf16[16,4096]{1,0:T(8,128)(2,1)}, u32[]{:S(2)}) copy-start(bf16[16,4096]{1,0:T(8,128)(2,1)} %copy-done.17) | copy-start | bytes 393220
  186.3 16.8 %copy-start.20 = (bf16[16,4096]{1,0:T(8,128)(2,1)S(1)}, bf16[16,4096]{1,0:T(8,128)(2,1)}, u32[]{:S(2)}) copy-start(bf16[16,4096]{1,0:T(8,128)(2,1)} %copy-done.19) | copy-start | bytes 393220
  186.3 16.8 %copy-start.22 = (bf16[16,4096]{1,0:T(8,128)(2,1)S(1)}, bf16[16,4096]{1,0:T(8,128)(2,1)}, u32[]{:S(2)}) copy-start(bf16[16,4096]{1,0:T(8,128)(2,1)} %copy-done.21) | copy-start | bytes 393220
  186.3 16.8 %copy-start.24 = (bf16[16,4096]{1,0:T(8,128)(2,1)S(1)}, bf16[16,4096]{1,0:T(8,128)(2,1)}, u32[]{:S(2)}) copy-start(bf16[16,4096]{1,0:T(8,128)(2,1)} %copy-done.23) | copy-start | bytes 393220
  186.3 16.8 %copy-start.26 = (bf16[16,4096]{1,0:T(8,128)(2,1)S(1)}, bf16[16,4096]{1,0:T(8,128)(2,1)}, u32[]{:S(2)}) copy-start(bf16[16,4096]{1,0:T(8,128)(2,1)} %copy-done.25) | copy-start | bytes 393220
  186.3 16.8 %copy-start.28 = (bf16[16,4096]{1,0:T(8,128)(2,1)S(1)}, bf16[16,4096]{1,0:T(8,128)(2,1)}, u32[]{:S(2)}) copy-start(bf16[16,4096]{1,0:T(8,128)(2,1)} %copy-done.27) | copy-start | bytes 393220
  186.3 16.8 %copy-start.30 = (bf16[16,4096]{1,0:T(8,128)(2,1)S(1)}, bf16[16,4096]{1,0:T(8,128)(2,1)}, u32[]{:S(2)}) copy-start(bf16[16,4096]{1,0:T(8,128)(2,1)} %copy-done.29) | copy-start | bytes 393220
  186.3 16.8 %copy-start.32 = (bf16[16,4096]{1,0:T(8,128)(2,1)S(1)}, bf16[16,4096]{1,0:T(8,128)(2,1)}, u32[]{:S(2)}) copy-start(bf16[16,4096]{1,0:T(8,128)(2,1)} %copy-done.31) | copy-start | bytes 393220
  186.4 16.8 %copy-start.34 = (bf16[16,4096]{1,0:T(8,128)(2,1)S(1)}, bf16[16,4096]{1,0:T(8,128)(2,1)}, u32[]{:S(2)}) copy-start(bf16[16,4096]{1,0:T(8,128)(2,1)} %copy-done.33) | copy-start | bytes 393220
  186.4 12.2 %collective-permute-start.30 = (bf16[8,64,512]{2,1,0:T(8,128)(2,1)S(1)}, bf16[8,64,512]{2,1,0:T(8,128)(2,1)S(1)}, u32[]{:S(2)}, u32[]{:S(2)}) collective-permute-start(bf16[8,64,512]{2,1,0:T(8,128)(2,1)S(1)} %get-tuple-element.101), channel_id=1, source_target_pairs={{0,1},{1,0},{2,3},{3,2},{4,5},{5,4},{6,7},{7,6},{8,9},{9,8},{10,11... | collective-permute-start | bytes 1572872 | tf_op jit(solution)/shard_map/ppermute | solution.py:305
  199.5 11.7 %all-to-all-start.1 = ((bf16[8,64,512]{2,1,0:T(8,128)(2,1)}), bf16[8,64,512]{2,1,0:T(8,128)(2,1)S(1)}, u32[]{:S(2)}, u32[]{:S(2)}) async-start(bf16[8,64,512]{2,1,0:T(8,128)(2,1)} %pair.1), calls=%async_computation.1 | async-start | bytes 1048576 | tf_op jit(solution)/shard_map/all_to_all | solution.py:307
  (4 other events, 8.9 us)

commit v10 on v9

--- a/solution.py
+++ b/solution.py
@@ -14,7 +14,7 @@
 FAR = 2
 HIDDEN_BY = 6
 EARLY = 8
-EARLY_BY = 18
+EARLY_BY = 19
 DP = ("dp_0", "dp_1", "dp_2", "dp_3")
 IN_VMEM = pl.BlockSpec(memory_space=pltpu.VMEM)
 IN_SMEM = pl.BlockSpec(memory_space=pltpu.SMEM)
@@ -238,16 +238,18 @@
         (where, mine, other),
     )
 
-    def partial_sum(start, end, extra):
-        rows, whole = (end - start) * ROWS, width // across
+    def spread_rows(start, end):
         dv = kernel_call(
             functools.partial(stack_kernel, npipe, start),
             "stack",
-            shape((rows, kv_width), BF16),
+            shape(((end - start) * ROWS, kv_width), BF16),
             [IN_SMEM] + [IN_VMEM] * len(gv_parts),
             (stage, *gv_parts),
         )
-        spread = exchanged([dv] * across, "dp_1")
+        return exchanged([dv] * across, "dp_1")
+
+    def partial_sum(start, spread, extra):
+        whole = width // across
         kinds = (shape(halves, F32), shape(halves, BF16)) if start else shape((whole, kv_width), F32)
         return kernel_call(
             functools.partial(part_kernel, start * ROWS, across),
@@ -271,7 +273,7 @@
         if step == HIDDEN_BY:
             later = tuple(hidden[1:])
         elif step == EARLY_BY:
-            later = (early,)
+            later = tuple(early[1:])
         turn = gv_parts[-1:]
         dx, dv = kernel_call(
             functools.partial(step_kernel, step, npipe, blocks),
@@ -290,7 +292,7 @@
         if pairs:
             sent[step] = lax.ppermute(dx, "pipe", pairs)
         if step == EARLY + SLACK * (npipe - 1) - 1:
-            early = partial_sum(0, EARLY, ())
+            early = spread_rows(0, EARLY)
 
     grad_x = kernel_call(
         functools.partial(collect_kernel, npipe, blocks),
@@ -301,7 +303,9 @@
         scratch=(pltpu.SemaphoreType.DMA((steps,)),),
         out_spec=ANYWHERE,
     )[:, None]
-    keep, give = partial_sum(EARLY, 2 * blocks, (early,))
+    late = spread_rows(EARLY, 2 * blocks)
+    first = partial_sum(0, early, (late[0],))
+    keep, give = partial_sum(EARLY, late, (first,))
     got = lax.ppermute(give, DP[3], [(0, 1), (1, 0)])
     paired = kernel_call(pair_kernel, "pair", shape(halves, BF16), [IN_VMEM] * 2, (keep, got))
     landed = lax.all_to_all(paired, others, 0, 0, tiled=True)

time: 213 us -> 213 us (level)
  waiting for transfers between devices: 100 us -> 96.7 us
  starting transfers between devices: 73.2 us -> 76.4 us
    ppermute x9, starting transfers between devices: 9.47 us -> 14 us  [exchanged(): moved.append(lax.ppermute(pieces[shift], axis, pairs))]
    ppermute x9, waiting for transfers between devices: 19.6 us -> 17.3 us  [exchanged(): moved.append(lax.ppermute(pieces[shift], axis, pairs))]
  transfers between devices with their start and end apart: 33 -> 33, of which waited for: 19 -> 18; matrix products, arithmetic and copies ran while one was open for 0% -> 0% of each run, Pallas kernels for 14% -> 14%
where the time goes in v10:
time: 213 us; the launch traced here: 212 us
  waiting for transfers between devices  96.7 us (45%)
  starting transfers between devices  76.4 us (36%)
  Pallas kernels  34.1 us (16%)
  local copies, waits for them, and re-layouts  3.19 us (1%)
    ppermute x20, waiting for transfers between devices, on_device(): sent[step] = lax.ppermute(dx, 'pipe', pairs)  48.7 us
    ppermute x20, starting transfers between devices, on_device(): sent[step] = lax.ppermute(dx, 'pipe', pairs)  35.8 us
    pallas_call x31, Pallas kernels, kernel_call(): pl.pallas_call(kernel, out_shape=out_shape, in_specs=specs, out_specs=jax...  34.1 us
    all_to_all x1, waiting for transfers between devices, copy_for_each(): lax.all_to_all(jnp.broadcast_to(array[None], (count, *array.shape)), axis...  22.1 us
    ppermute x9, waiting for transfers between devices, exchanged(): moved.append(lax.ppermute(pieces[shift], axis, pairs))  17.3 us
    ppermute x9, starting transfers between devices, exchanged(): moved.append(lax.ppermute(pieces[shift], axis, pairs))  14 us
    ppermute x1, starting transfers between devices, on_device(): got = lax.ppermute(give, DP[3], [(0, 1), (1, 0)])  9.57 us
    all_to_all x1, starting transfers between devices, copy_for_each(): lax.all_to_all(jnp.broadcast_to(array[None], (count, *array.shape)), axis...  9.49 us
  transfers between devices with their start and end apart: 33, of which 18 were waited for; matrix products, arithmetic and copies ran while one was open for 0% of the time, Pallas kernels for 14%

profile of v10, /device:TPU:1, one launch (start us, length us, event | category | flops | bytes accessed | tf_op | source)
XLA Modules:
  0.0 212.0 jit_solution(10632035558154844183)
XLA Ops:
  0.6 2.4 %broadcast_in_dim.14 = bf16[32,64,512]{2,1,0:T(8,128)(2,1)} broadcast(bf16[64,512]{1,0:T(8,128)(2,1)} %bitcast.34), dimensions={1,2} | broadcast | bytes 2162688 | tf_op jit(solution)/shard_map/broadcast_in_dim | solution.py:28
  3.0 9.5 %all-to-all-start = ((bf16[32,64,512]{2,1,0:T(8,128)(2,1)}), bf16[32,64,512]{2,1,0:T(8,128)(2,1)}, u32[]{:S(2)}, u32[]{:S(2)}) async-start(bf16[32,64,512]{2,1,0:T(8,128)(2,1)} %broadcast_in_dim.14), calls=%async_computation | async-start | bytes 4194304 | tf_op jit(solution)/shard_map/all_to_all | solution.py:27
  12.6 3.4 %normalize.1 = (bf16[2,128,1024]{2,1,0:T(8,128)(2,1)S(1)}, bf16[2,128,1024]{2,1,0:T(8,128)(2,1)}, bf16[2,128,1024]{2,1,0:T(8,128)(2,1)}, bf16[2,128,1024]{2,1,0:T(8,128)(2,1)}) custom-call(s32[3]{0:T(128)S(1)} %pad_add_fusion.where, bf16[2,128,4096]{2,1,0:T(8,128)(2,1)S(1)} %bitcast.9, f32[2,1,4096]{2,1,0:T(1,128)S(1)} %copy-done.2), custom_call_target="tpu_custom_call" | custom-call | tf_op jit(solution)/shard_map/normalize/pallas_call | solution.py:33
  16.0 22.1 %all-to-all-done.value_ref = bf16[32,64,512]{2,1,0:T(8,128)(2,1)} async-done(((bf16[32,64,512]{2,1,0:T(8,128)(2,1)}), bf16[32,64,512]{2,1,0:T(8,128)(2,1)}, u32[]{:S(2)}, u32[]{:S(2)}) %all-to-all-start) | async-done | bytes 2097184 | tf_op jit(solution)/shard_map/all_to_all | solution.py:27
  38.0 4.0 %collective-permute-start = (bf16[32,64,512]{2,1,0:T(8,128)(2,1)}, bf16[32,64,512]{2,1,0:T(8,128)(2,1)S(1)}, u32[]{:S(2)}, u32[]{:S(2)}) collective-permute-start(bf16[32,64,512]{2,1,0:T(8,128)(2,1)} %held_until.1.mine_ref), channel_id=1, source_target_pairs={{0,1},{1,0},{2,3},{3,2},{4,5},{5,4},{6,7},{7,6},{8,9},{9,8},{10,11... | collective-permute-start | bytes 6291464 | tf_op jit(solution)/shard_map/ppermute | solution.py:231
  42.5 1.7 collective-permute-start.7
  44.2 1.5 collective-permute-start.8
  46.0 1.9 rows.1.w_ref
  48.0 0.7 collective-permute-start.1
  50.8 1.3 collective-permute-start.5
  52.1 1.3 collective-permute-start.9
  53.4 14.8 %collective-permute-done.6.refs_1_ = bf16[2,128,1024]{2,1,0:T(8,128)(2,1)S(1)} collective-permute-done((bf16[2,128,1024]{2,1,0:T(8,128)(2,1)}, bf16[2,128,1024]{2,1,0:T(8,128)(2,1)S(1)}, u32[]{:S(2)}, u32[]{:S(2)}) %collective-permute-start.6) | collective-permute-done | bytes 524320 | tf_op jit(solution)/shard_map/ppermute | solution.py:207
  68.5 18.3 %collective-permute-done.5.in_ref = bf16[16,4096]{1,0:T(8,128)(2,1)S(1)} collective-permute-done((bf16[16,4096]{1,0:T(8,128)(2,1)S(1)}, bf16[16,4096]{1,0:T(8,128)(2,1)S(1)}, u32[]{:S(2)}, u32[]{:S(2)}) %collective-permute-start.5) | collective-permute-done | bytes 131104 | tf_op jit(solution)/shard_map/ppermute | solution.py:293
  86.8 1.3 section_step.28
  88.2 3.9 %collective-permute-start.10 = (bf16[16,4096]{1,0:T(8,128)(2,1)S(1)}, bf16[16,4096]{1,0:T(8,128)(2,1)S(1)}, u32[]{:S(2)}, u32[]{:S(2)}) collective-permute-start(bf16[16,4096]{1,0:T(8,128)(2,1)S(1)} %get-tuple-element.68.refs_6_), channel_id=1, source_target_pairs={{0,192},{64,0},{128,64},{192,128},{1,193},{65,1},{129,65},{193,129... | collective-permute-start | bytes 393224 | tf_op jit(solution)/shard_map/ppermute | solution.py:293
  92.1 1.3 section_step.29
  93.5 4.7 %collective-permute-start.11 = (bf16[16,4096]{1,0:T(8,128)(2,1)S(1)}, bf16[16,4096]{1,0:T(8,128)(2,1)S(1)}, u32[]{:S(2)}, u32[]{:S(2)}) collective-permute-start(bf16[16,4096]{1,0:T(8,128)(2,1)S(1)} %get-tuple-element.70.refs_7_), channel_id=1, source_target_pairs={{0,192},{64,0},{128,64},{192,128},{1,193},{65,1},{129,65},{193,129... | collective-permute-start | bytes 393224 | tf_op jit(solution)/shard_map/ppermute | solution.py:293
  98.2 2.3 %collective-permute-done.10.in_ref = bf16[16,4096]{1,0:T(8,128)(2,1)S(1)} collective-permute-done((bf16[16,4096]{1,0:T(8,128)(2,1)S(1)}, bf16[16,4096]{1,0:T(8,128)(2,1)S(1)}, u32[]{:S(2)}, u32[]{:S(2)}) %collective-permute-start.10) | collective-permute-done | bytes 131104 | tf_op jit(solution)/shard_map/ppermute | solution.py:293
  100.5 1.3 section_step.30
  101.9 0.9 collective-permute-start.12
  102.8 1.3 section_step.31
  104.1 5.9 %collective-permute-start.13 = (bf16[16,4096]{1,0:T(8,128)(2,1)S(1)}, bf16[16,4096]{1,0:T(8,128)(2,1)S(1)}, u32[]{:S(2)}, u32[]{:S(2)}) collective-permute-start(bf16[16,4096]{1,0:T(8,128)(2,1)S(1)} %get-tuple-element.74.refs_9_), channel_id=1, source_target_pairs={{0,192},{64,0},{128,64},{192,128},{1,193},{65,1},{129,65},{193,129... | collective-permute-start | bytes 393224 | tf_op jit(solution)/shard_map/ppermute | solution.py:293
  110.0 1.3 section_step.32
  111.4 3.0 %collective-permute-start.14 = (bf16[16,4096]{1,0:T(8,128)(2,1)S(1)}, bf16[16,4096]{1,0:T(8,128)(2,1)S(1)}, u32[]{:S(2)}, u32[]{:S(2)}) collective-permute-start(bf16[16,4096]{1,0:T(8,128)(2,1)S(1)} %get-tuple-element.76.refs_10_), channel_id=1, source_target_pairs={{0,192},{64,0},{128,64},{192,128},{1,193},{65,1},{129,65},{193,129... | collective-permute-start | bytes 393224 | tf_op jit(solution)/shard_map/ppermute | solution.py:293
  114.4 1.3 collective-permute-done.13.in_ref
  115.7 1.3 section_step.33
  117.1 4.1 %collective-permute-start.15 = (bf16[16,4096]{1,0:T(8,128)(2,1)S(1)}, bf16[16,4096]{1,0:T(8,128)(2,1)S(1)}, u32[]{:S(2)}, u32[]{:S(2)}) collective-permute-start(bf16[16,4096]{1,0:T(8,128)(2,1)S(1)} %get-tuple-element.78.refs_11_), channel_id=1, source_target_pairs={{0,192},{64,0},{128,64},{192,128},{1,193},{65,1},{129,65},{193,129... | collective-permute-start | bytes 393224 | tf_op jit(solution)/shard_map/ppermute | solution.py:293
  121.2 2.0 collective-permute-done.14.in_ref
  123.2 1.3 section_step.34
  124.7 4.3 %collective-permute-done.15.in_ref = bf16[16,4096]{1,0:T(8,128)(2,1)S(1)} collective-permute-done((bf16[16,4096]{1,0:T(8,128)(2,1)S(1)}, bf16[16,4096]{1,0:T(8,128)(2,1)S(1)}, u32[]{:S(2)}, u32[]{:S(2)}) %collective-permute-start.15) | collective-permute-done | bytes 131104 | tf_op jit(solution)/shard_map/ppermute | solution.py:293
  128.9 1.3 section_step.35
  130.5 3.5 %collective-permute-done.16.in_ref = bf16[16,4096]{1,0:T(8,128)(2,1)S(1)} collective-permute-done((bf16[16,4096]{1,0:T(8,128)(2,1)S(1)}, bf16[16,4096]{1,0:T(8,128)(2,1)S(1)}, u32[]{:S(2)}, u32[]{:S(2)}) %collective-permute-start.16) | collective-permute-done | bytes 131104 | tf_op jit(solution)/shard_map/ppermute | solution.py:293
  134.0 1.3 section_step.36
  135.3 1.3 collective-permute-start.18
  136.6 1.7 collective-permute-done.17.in_ref
  138.3 1.3 section_step.37
  139.7 1.3 collective-permute-start.19
  141.1 2.8 %collective-permute-done.18.in_ref = bf16[16,4096]{1,0:T(8,128)(2,1)S(1)} collective-permute-done((bf16[16,4096]{1,0:T(8,128)(2,1)S(1)}, bf16[16,4096]{1,0:T(8,128)(2,1)S(1)}, u32[]{:S(2)}, u32[]{:S(2)}) %collective-permute-start.18) | collective-permute-done | bytes 131104 | tf_op jit(solution)/shard_map/ppermute | solution.py:293
  143.9 1.3 section_step.38
  145.3 1.3 collective-permute-start.20
  146.6 4.8 %collective-permute-start.22 = (bf16[128,512]{1,0:T(8,128)(2,1)S(1)}, bf16[128,512]{1,0:T(8,128)(2,1)S(1)}, u32[]{:S(2)}, u32[]{:S(2)}) collective-permute-start(bf16[128,512]{1,0:T(8,128)(2,1)S(1)} %stack.15.refs_4_), channel_id=1, source_target_pairs={{0,8},{8,16},{16,24},{24,0},{1,9},{9,17},{17,25},{25,1},{2,10},{10... | collective-permute-start | bytes 393224 | tf_op jit(solution)/shard_map/ppermute | solution.py:207
  151.5 2.5 %collective-permute-start.24 = (bf16[128,512]{1,0:T(8,128)(2,1)S(1)}, bf16[128,512]{1,0:T(8,128)(2,1)S(1)}, u32[]{:S(2)}, u32[]{:S(2)}) collective-permute-start(bf16[128,512]{1,0:T(8,128)(2,1)S(1)} %stack.15.refs_4_), channel_id=1, source_target_pairs={{0,24},{8,0},{16,8},{24,16},{1,25},{9,1},{17,9},{25,17},{2,26},{10... | collective-permute-start | bytes 393224 | tf_op jit(solution)/shard_map/ppermute | solution.py:207
  153.9 1.3 section_step.39
  155.3 1.3 collective-permute-start.21
  156.6 1.6 section_step.40
  158.2 1.3 collective-permute-start.25
  159.5 7.3 %collective-permute-done.21.in_ref = bf16[16,4096]{1,0:T(8,128)(2,1)S(1)} collective-permute-done((bf16[16,4096]{1,0:T(8,128)(2,1)S(1)}, bf16[16,4096]{1,0:T(8,128)(2,1)S(1)}, u32[]{:S(2)}, u32[]{:S(2)}) %collective-permute-start.21) | collective-permute-done | bytes 131104 | tf_op jit(solution)/shard_map/ppermute | solution.py:293
  166.9 1.3 section_step.41
  168.2 1.3 collective-permute-start.26
  169.6 1.3 section_step.42
  171.6 5.1 %collective-permute-done.26.in_ref = bf16[16,4096]{1,0:T(8,128)(2,1)S(1)} collective-permute-done((bf16[16,4096]{1,0:T(8,128)(2,1)S(1)}, bf16[16,4096]{1,0:T(8,128)(2,1)S(1)}, u32[]{:S(2)}, u32[]{:S(2)}) %collective-permute-start.26) | collective-permute-done | bytes 131104 | tf_op jit(solution)/shard_map/ppermute | solution.py:293
  176.6 1.3 section_step.43
  178.2 1.1 collective-permute-start.28
  179.3 2.0 collective-permute-start.29
  181.2 1.8 part.2.refs_8_
  183.1 1.6 collective-permute-done.27.refs_5_
  185.2 1.9 part.3
  187.3 9.6 %collective-permute-start.30 = (bf16[8,64,512]{2,1,0:T(8,128)(2,1)S(1)}, bf16[8,64,512]{2,1,0:T(8,128)(2,1)S(1)}, u32[]{:S(2)}, u32[]{:S(2)}) collective-permute-start(bf16[8,64,512]{2,1,0:T(8,128)(2,1)S(1)} %get-tuple-element.101), channel_id=1, source_target_pairs={{0,1},{1,0},{2,3},{3,2},{4,5},{5,4},{6,7},{7,6},{8,9},{9,8},{10,11... | collective-permute-start | bytes 1572872 | tf_op jit(solution)/shard_map/ppermute | solution.py:309
  196.9 1.5 collective-permute-done.30.got_ref
  198.4 0.9 pair.1
  199.4 3.5 %all-to-all-start.1 = ((bf16[8,64,512]{2,1,0:T(8,128)(2,1)}), bf16[8,64,512]{2,1,0:T(8,128)(2,1)S(1)}, u32[]{:S(2)}, u32[]{:S(2)}) async-start(bf16[8,64,512]{2,1,0:T(8,128)(2,1)} %pair.1), calls=%async_computation.1 | async-start | bytes 1048576 | tf_op jit(solution)/shard_map/all_to_all | solution.py:311
  203.0 1.5 collect_rows.1
  204.6 6.7 %all-to-all-done.1.pieces_ref = bf16[8,64,512]{2,1,0:T(8,128)(2,1)S(1)} async-done(((bf16[8,64,512]{2,1,0:T(8,128)(2,1)}), bf16[8,64,512]{2,1,0:T(8,128)(2,1)S(1)}, u32[]{:S(2)}, u32[]{:S(2)}) %all-to-all-start.1) | async-done | bytes 524320 | tf_op jit(solution)/shard_map/all_to_all | solution.py:311
  211.3 0.7 sum.1
  (107 shorter events, 5.3 us)
Async XLA Ops:
  3.0 9.6 %copy-start = (bf16[2,1,128,4096]{3,2,1,0:T(8,128)(2,1)S(1)}, bf16[2,1,128,4096]{3,2,1,0:T(8,128)(2,1)}, u32[]{:S(2)}) copy-start(bf16[2,1,128,4096]{3,2,1,0:T(8,128)(2,1)} %param.4) | copy-start | bytes 6291460
  3.0 9.6 %copy-start.2 = (f32[2,1,4096]{2,1,0:T(1,128)S(1)}, f32[2,1,4096]{2,1,0:T(1,128)}, u32[]{:S(2)}) copy-start(f32[2,1,4096]{2,1,0:T(1,128)} %g_ref.45) | copy-start | bytes 98308
  3.0 35.0 %all-to-all-start = ((bf16[32,64,512]{2,1,0:T(8,128)(2,1)}), bf16[32,64,512]{2,1,0:T(8,128)(2,1)}, u32[]{:S(2)}, u32[]{:S(2)}) async-start(bf16[32,64,512]{2,1,0:T(8,128)(2,1)} %broadcast_in_dim.14), calls=%async_computation | async-start | bytes 4194304 | tf_op jit(solution)/shard_map/all_to_all | solution.py:27
  38.0 8.0 %collective-permute-start = (bf16[32,64,512]{2,1,0:T(8,128)(2,1)}, bf16[32,64,512]{2,1,0:T(8,128)(2,1)S(1)}, u32[]{:S(2)}, u32[]{:S(2)}) collective-permute-start(bf16[32,64,512]{2,1,0:T(8,128)(2,1)} %held_until.1.mine_ref), channel_id=1, source_target_pairs={{0,1},{1,0},{2,3},{3,2},{4,5},{5,4},{6,7},{7,6},{8,9},{9,8},{10,11... | collective-permute-start | bytes 6291464 | tf_op jit(solution)/shard_map/ppermute | solution.py:231
  42.0 26.2 %collective-permute-start.6 = (bf16[2,128,1024]{2,1,0:T(8,128)(2,1)}, bf16[2,128,1024]{2,1,0:T(8,128)(2,1)S(1)}, u32[]{:S(2)}, u32[]{:S(2)}) collective-permute-start(bf16[2,128,1024]{2,1,0:T(8,128)(2,1)} %get-tuple-element.65), channel_id=1, source_target_pairs={{0,8},{8,16},{16,24},{24,0},{1,9},{9,17},{17,25},{25,1},{2,10},{10... | collective-permute-start | bytes 1572872 | tf_op jit(solution)/shard_map/ppermute | solution.py:207
  42.5 25.8 %collective-permute-start.7 = (bf16[2,128,1024]{2,1,0:T(8,128)(2,1)}, bf16[2,128,1024]{2,1,0:T(8,128)(2,1)S(1)}, u32[]{:S(2)}, u32[]{:S(2)}) collective-permute-start(bf16[2,128,1024]{2,1,0:T(8,128)(2,1)} %get-tuple-element.66), channel_id=1, source_target_pairs={{0,16},{8,24},{16,0},{24,8},{1,17},{9,25},{17,1},{25,9},{2,18},{10... | collective-permute-start | bytes 1572872 | tf_op jit(solution)/shard_map/ppermute | solution.py:207
  44.2 3.8 %copy-start.1 = (bf16[128,4096]{1,0:T(8,128)(2,1)S(1)}, bf16[128,4096]{1,0:T(8,128)(2,1)}, u32[]{:S(2)}) copy-start(bf16[128,4096]{1,0:T(8,128)(2,1)} %fresh_ref.43) | copy-start | bytes 3145732
  44.2 24.4 %collective-permute-start.8 = (bf16[2,128,1024]{2,1,0:T(8,128)(2,1)}, bf16[2,128,1024]{2,1,0:T(8,128)(2,1)S(1)}, u32[]{:S(2)}, u32[]{:S(2)}) collective-permute-start(bf16[2,128,1024]{2,1,0:T(8,128)(2,1)} %get-tuple-element.67), channel_id=1, source_target_pairs={{0,24},{8,0},{16,8},{24,16},{1,25},{9,1},{17,9},{25,17},{2,26},{10... | collective-permute-start | bytes 1572872 | tf_op jit(solution)/shard_map/ppermute | solution.py:207
  48.0 1.4 collective-permute-start.1
  48.6 1.4 collective-permute-start.2
  49.4 1.4 collective-permute-start.3
  50.1 2.0 collective-permute-start.4
  50.8 36.0 %collective-permute-start.5 = (bf16[16,4096]{1,0:T(8,128)(2,1)S(1)}, bf16[16,4096]{1,0:T(8,128)(2,1)S(1)}, u32[]{:S(2)}, u32[]{:S(2)}) collective-permute-start(bf16[16,4096]{1,0:T(8,128)(2,1)S(1)} %get-tuple-element.61.refs_4_), channel_id=1, source_target_pairs={{64,0},{128,64},{192,128},{65,1},{129,65},{193,129},{66,2},{130,66... | collective-permute-start | bytes 393224 | tf_op jit(solution)/shard_map/ppermute | solution.py:293
  52.1 40.0 %collective-permute-start.9 = (bf16[16,4096]{1,0:T(8,128)(2,1)S(1)}, bf16[16,4096]{1,0:T(8,128)(2,1)S(1)}, u32[]{:S(2)}, u32[]{:S(2)}) collective-permute-start(bf16[16,4096]{1,0:T(8,128)(2,1)S(1)} %get-tuple-element.63.refs_5_), channel_id=1, source_target_pairs={{64,0},{128,64},{192,128},{65,1},{129,65},{193,129},{66,2},{130,66... | collective-permute-start | bytes 393224 | tf_op jit(solution)/shard_map/ppermute | solution.py:293
  88.2 5.3 %copy-start.3 = (bf16[16,4096]{1,0:T(8,128)(2,1)}, bf16[16,4096]{1,0:T(8,128)(2,1)S(1)}, u32[]{:S(2)}) copy-start(bf16[16,4096]{1,0:T(8,128)(2,1)S(1)} %get-tuple-element.68.refs_6_) | copy-start | bytes 393220
  88.2 12.3 %collective-permute-start.10 = (bf16[16,4096]{1,0:T(8,128)(2,1)S(1)}, bf16[16,4096]{1,0:T(8,128)(2,1)S(1)}, u32[]{:S(2)}, u32[]{:S(2)}) collective-permute-start(bf16[16,4096]{1,0:T(8,128)(2,1)S(1)} %get-tuple-element.68.refs_6_), channel_id=1, source_target_pairs={{0,192},{64,0},{128,64},{192,128},{1,193},{65,1},{129,65},{193,129... | collective-permute-start | bytes 393224 | tf_op jit(solution)/shard_map/ppermute | solution.py:293
  93.5 8.4 %copy-start.5 = (bf16[16,4096]{1,0:T(8,128)(2,1)}, bf16[16,4096]{1,0:T(8,128)(2,1)S(1)}, u32[]{:S(2)}) copy-start(bf16[16,4096]{1,0:T(8,128)(2,1)S(1)} %get-tuple-element.70.refs_7_) | copy-start | bytes 393220
  93.5 9.3 %collective-permute-start.11 = (bf16[16,4096]{1,0:T(8,128)(2,1)S(1)}, bf16[16,4096]{1,0:T(8,128)(2,1)S(1)}, u32[]{:S(2)}, u32[]{:S(2)}) collective-permute-start(bf16[16,4096]{1,0:T(8,128)(2,1)S(1)} %get-tuple-element.70.refs_7_), channel_id=1, source_target_pairs={{0,192},{64,0},{128,64},{192,128},{1,193},{65,1},{129,65},{193,129... | collective-permute-start | bytes 393224 | tf_op jit(solution)/shard_map/ppermute | solution.py:293
  101.9 8.1 %collective-permute-start.12 = (bf16[16,4096]{1,0:T(8,128)(2,1)S(1)}, bf16[16,4096]{1,0:T(8,128)(2,1)S(1)}, u32[]{:S(2)}, u32[]{:S(2)}) collective-permute-start(bf16[16,4096]{1,0:T(8,128)(2,1)S(1)} %get-tuple-element.72.refs_8_), channel_id=1, source_target_pairs={{0,192},{64,0},{128,64},{192,128},{1,193},{65,1},{129,65},{193,129... | collective-permute-start | bytes 393224 | tf_op jit(solution)/shard_map/ppermute | solution.py:293
  104.1 7.2 %copy-start.9 = (bf16[16,4096]{1,0:T(8,128)(2,1)}, bf16[16,4096]{1,0:T(8,128)(2,1)S(1)}, u32[]{:S(2)}) copy-start(bf16[16,4096]{1,0:T(8,128)(2,1)S(1)} %get-tuple-element.74.refs_9_) | copy-start | bytes 393220
  104.1 11.6 %collective-permute-start.13 = (bf16[16,4096]{1,0:T(8,128)(2,1)S(1)}, bf16[16,4096]{1,0:T(8,128)(2,1)S(1)}, u32[]{:S(2)}, u32[]{:S(2)}) collective-permute-start(bf16[16,4096]{1,0:T(8,128)(2,1)S(1)} %get-tuple-element.74.refs_9_), channel_id=1, source_target_pairs={{0,192},{64,0},{128,64},{192,128},{1,193},{65,1},{129,65},{193,129... | collective-permute-start | bytes 393224 | tf_op jit(solution)/shard_map/ppermute | solution.py:293
  111.4 5.7 %copy-start.11 = (bf16[16,4096]{1,0:T(8,128)(2,1)}, bf16[16,4096]{1,0:T(8,128)(2,1)S(1)}, u32[]{:S(2)}) copy-start(bf16[16,4096]{1,0:T(8,128)(2,1)S(1)} %get-tuple-element.76.refs_10_) | copy-start | bytes 393220
  111.4 11.9 %collective-permute-start.14 = (bf16[16,4096]{1,0:T(8,128)(2,1)S(1)}, bf16[16,4096]{1,0:T(8,128)(2,1)S(1)}, u32[]{:S(2)}, u32[]{:S(2)}) collective-permute-start(bf16[16,4096]{1,0:T(8,128)(2,1)S(1)} %get-tuple-element.76.refs_10_), channel_id=1, source_target_pairs={{0,192},{64,0},{128,64},{192,128},{1,193},{65,1},{129,65},{193,129... | collective-permute-start | bytes 393224 | tf_op jit(solution)/shard_map/ppermute | solution.py:293
  117.1 7.5 %copy-start.13 = (bf16[16,4096]{1,0:T(8,128)(2,1)}, bf16[16,4096]{1,0:T(8,128)(2,1)S(1)}, u32[]{:S(2)}) copy-start(bf16[16,4096]{1,0:T(8,128)(2,1)S(1)} %get-tuple-element.78.refs_11_) | copy-start | bytes 393220
  117.1 11.9 %collective-permute-start.15 = (bf16[16,4096]{1,0:T(8,128)(2,1)S(1)}, bf16[16,4096]{1,0:T(8,128)(2,1)S(1)}, u32[]{:S(2)}, u32[]{:S(2)}) collective-permute-start(bf16[16,4096]{1,0:T(8,128)(2,1)S(1)} %get-tuple-element.78.refs_11_), channel_id=1, source_target_pairs={{0,192},{64,0},{128,64},{192,128},{1,193},{65,1},{129,65},{193,129... | collective-permute-start | bytes 393224 | tf_op jit(solution)/shard_map/ppermute | solution.py:293
  124.6 5.7 %copy-start.15 = (bf16[16,4096]{1,0:T(8,128)(2,1)}, bf16[16,4096]{1,0:T(8,128)(2,1)S(1)}, u32[]{:S(2)}) copy-start(bf16[16,4096]{1,0:T(8,128)(2,1)S(1)} %get-tuple-element.80.refs_12_) | copy-start | bytes 393220
  124.6 9.4 %collective-permute-start.16 = (bf16[16,4096]{1,0:T(8,128)(2,1)S(1)}, bf16[16,4096]{1,0:T(8,128)(2,1)S(1)}, u32[]{:S(2)}, u32[]{:S(2)}) collective-permute-start(bf16[16,4096]{1,0:T(8,128)(2,1)S(1)} %get-tuple-element.80.refs_12_), channel_id=1, source_target_pairs={{0,192},{64,0},{128,64},{192,128},{1,193},{65,1},{129,65},{193,129... | collective-permute-start | bytes 393224 | tf_op jit(solution)/shard_map/ppermute | solution.py:293
  130.3 5.0 %copy-start.17 = (bf16[16,4096]{1,0:T(8,128)(2,1)}, bf16[16,4096]{1,0:T(8,128)(2,1)S(1)}, u32[]{:S(2)}) copy-start(bf16[16,4096]{1,0:T(8,128)(2,1)S(1)} %get-tuple-element.82.refs_13_) | copy-start | bytes 393220
  130.3 8.0 %collective-permute-start.17 = (bf16[16,4096]{1,0:T(8,128)(2,1)S(1)}, bf16[16,4096]{1,0:T(8,128)(2,1)S(1)}, u32[]{:S(2)}, u32[]{:S(2)}) collective-permute-start(bf16[16,4096]{1,0:T(8,128)(2,1)S(1)} %get-tuple-element.82.refs_13_), channel_id=1, source_target_pairs={{0,192},{64,0},{128,64},{192,128},{1,193},{65,1},{129,65},{193,129... | collective-permute-start | bytes 393224 | tf_op jit(solution)/shard_map/ppermute | solution.py:293
  135.3 4.4 %copy-start.19 = (bf16[16,4096]{1,0:T(8,128)(2,1)}, bf16[16,4096]{1,0:T(8,128)(2,1)S(1)}, u32[]{:S(2)}) copy-start(bf16[16,4096]{1,0:T(8,128)(2,1)S(1)} %get-tuple-element.84.refs_14_) | copy-start | bytes 393220
  135.3 8.6 %collective-permute-start.18 = (bf16[16,4096]{1,0:T(8,128)(2,1)S(1)}, bf16[16,4096]{1,0:T(8,128)(2,1)S(1)}, u32[]{:S(2)}, u32[]{:S(2)}) collective-permute-start(bf16[16,4096]{1,0:T(8,128)(2,1)S(1)} %get-tuple-element.84.refs_14_), channel_id=1, source_target_pairs={{64,0},{128,64},{192,128},{65,1},{129,65},{193,129},{66,2},{130,66... | collective-permute-start | bytes 393224 | tf_op jit(solution)/shard_map/ppermute | solution.py:293
  139.7 5.6 %copy-start.21 = (bf16[16,4096]{1,0:T(8,128)(2,1)}, bf16[16,4096]{1,0:T(8,128)(2,1)S(1)}, u32[]{:S(2)}) copy-start(bf16[16,4096]{1,0:T(8,128)(2,1)S(1)} %get-tuple-element.86.refs_15_) | copy-start | bytes 393220
  139.7 14.2 %collective-permute-start.19 = (bf16[16,4096]{1,0:T(8,128)(2,1)S(1)}, bf16[16,4096]{1,0:T(8,128)(2,1)S(1)}, u32[]{:S(2)}, u32[]{:S(2)}) collective-permute-start(bf16[16,4096]{1,0:T(8,128)(2,1)S(1)} %get-tuple-element.86.refs_15_), channel_id=1, source_target_pairs={{64,0},{128,64},{192,128},{65,1},{129,65},{193,129},{66,2},{130,66... | collective-permute-start | bytes 393224 | tf_op jit(solution)/shard_map/ppermute | solution.py:293
  145.3 10.0 %copy-start.23 = (bf16[16,4096]{1,0:T(8,128)(2,1)}, bf16[16,4096]{1,0:T(8,128)(2,1)S(1)}, u32[]{:S(2)}) copy-start(bf16[16,4096]{1,0:T(8,128)(2,1)S(1)} %get-tuple-element.88.refs_16_) | copy-start | bytes 393220
  145.3 11.3 %collective-permute-start.20 = (bf16[16,4096]{1,0:T(8,128)(2,1)S(1)}, bf16[16,4096]{1,0:T(8,128)(2,1)S(1)}, u32[]{:S(2)}, u32[]{:S(2)}) collective-permute-start(bf16[16,4096]{1,0:T(8,128)(2,1)S(1)} %get-tuple-element.88.refs_16_), channel_id=1, source_target_pairs={{64,0},{128,64},{65,1},{129,65},{66,2},{130,66},{67,3},{131,67},{6... | collective-permute-start | bytes 393224 | tf_op jit(solution)/shard_map/ppermute | solution.py:293
  146.6 12.9 %collective-permute-start.22 = (bf16[128,512]{1,0:T(8,128)(2,1)S(1)}, bf16[128,512]{1,0:T(8,128)(2,1)S(1)}, u32[]{:S(2)}, u32[]{:S(2)}) collective-permute-start(bf16[128,512]{1,0:T(8,128)(2,1)S(1)} %stack.15.refs_4_), channel_id=1, source_target_pairs={{0,8},{8,16},{16,24},{24,0},{1,9},{9,17},{17,25},{25,1},{2,10},{10... | collective-permute-start | bytes 393224 | tf_op jit(solution)/shard_map/ppermute | solution.py:207
  151.4 8.1 %collective-permute-start.23 = (bf16[128,512]{1,0:T(8,128)(2,1)S(1)}, bf16[128,512]{1,0:T(8,128)(2,1)S(1)}, u32[]{:S(2)}, u32[]{:S(2)}) collective-permute-start(bf16[128,512]{1,0:T(8,128)(2,1)S(1)} %stack.15.refs_4_), channel_id=1, source_target_pairs={{0,16},{8,24},{16,0},{24,8},{1,17},{9,25},{17,1},{25,9},{2,18},{10... | collective-permute-start | bytes 393224 | tf_op jit(solution)/shard_map/ppermute | solution.py:207
  151.5 8.1 %collective-permute-start.24 = (bf16[128,512]{1,0:T(8,128)(2,1)S(1)}, bf16[128,512]{1,0:T(8,128)(2,1)S(1)}, u32[]{:S(2)}, u32[]{:S(2)}) collective-permute-start(bf16[128,512]{1,0:T(8,128)(2,1)S(1)} %stack.15.refs_4_), channel_id=1, source_target_pairs={{0,24},{8,0},{16,8},{24,16},{1,25},{9,1},{17,9},{25,17},{2,26},{10... | collective-permute-start | bytes 393224 | tf_op jit(solution)/shard_map/ppermute | solution.py:207
  155.3 2.9 %copy-start.25 = (bf16[16,4096]{1,0:T(8,128)(2,1)}, bf16[16,4096]{1,0:T(8,128)(2,1)S(1)}, u32[]{:S(2)}) copy-start(bf16[16,4096]{1,0:T(8,128)(2,1)S(1)} %get-tuple-element.90.refs_17_) | copy-start | bytes 393220
  155.3 11.6 %collective-permute-start.21 = (bf16[16,4096]{1,0:T(8,128)(2,1)S(1)}, bf16[16,4096]{1,0:T(8,128)(2,1)S(1)}, u32[]{:S(2)}, u32[]{:S(2)}) collective-permute-start(bf16[16,4096]{1,0:T(8,128)(2,1)S(1)} %get-tuple-element.90.refs_17_), channel_id=1, source_target_pairs={{64,0},{128,64},{65,1},{129,65},{66,2},{130,66},{67,3},{131,67},{6... | collective-permute-start | bytes 393224 | tf_op jit(solution)/shard_map/ppermute | solution.py:293
  158.2 10.0 %copy-start.27 = (bf16[16,4096]{1,0:T(8,128)(2,1)}, bf16[16,4096]{1,0:T(8,128)(2,1)S(1)}, u32[]{:S(2)}) copy-start(bf16[16,4096]{1,0:T(8,128)(2,1)S(1)} %get-tuple-element.92.refs_18_) | copy-start | bytes 393220
  158.2 11.3 %collective-permute-start.25 = (bf16[16,4096]{1,0:T(8,128)(2,1)S(1)}, bf16[16,4096]{1,0:T(8,128)(2,1)S(1)}, u32[]{:S(2)}, u32[]{:S(2)}) collective-permute-start(bf16[16,4096]{1,0:T(8,128)(2,1)S(1)} %get-tuple-element.92.refs_18_), channel_id=1, source_target_pairs={{64,0},{65,1},{66,2},{67,3},{68,4},{69,5},{70,6},{71,7},{72,8},{73... | collective-permute-start | bytes 393224 | tf_op jit(solution)/shard_map/ppermute | solution.py:293
  168.2 8.4 %collective-permute-start.26 = (bf16[16,4096]{1,0:T(8,128)(2,1)S(1)}, bf16[16,4096]{1,0:T(8,128)(2,1)S(1)}, u32[]{:S(2)}, u32[]{:S(2)}) collective-permute-start(bf16[16,4096]{1,0:T(8,128)(2,1)S(1)} %get-tuple-element.94.refs_19_), channel_id=1, source_target_pairs={{64,0},{65,1},{66,2},{67,3},{68,4},{69,5},{70,6},{71,7},{72,8},{73... | collective-permute-start | bytes 393224 | tf_op jit(solution)/shard_map/ppermute | solution.py:293
  178.1 6.5 %collective-permute-start.27 = (bf16[128,512]{1,0:T(8,128)(2,1)S(1)}, bf16[128,512]{1,0:T(8,128)(2,1)S(1)}, u32[]{:S(2)}, u32[]{:S(2)}) collective-permute-start(bf16[128,512]{1,0:T(8,128)(2,1)S(1)} %stack.16.refs_8_.refs_4_), channel_id=1, source_target_pairs={{0,8},{8,16},{16,24},{24,0},{1,9},{9,17},{17,25},{25,1},{2,10},{10... | collective-permute-start | bytes 393224 | tf_op jit(solution)/shard_map/ppermute | solution.py:207
  178.2 6.4 %collective-permute-start.28 = (bf16[128,512]{1,0:T(8,128)(2,1)S(1)}, bf16[128,512]{1,0:T(8,128)(2,1)S(1)}, u32[]{:S(2)}, u32[]{:S(2)}) collective-permute-start(bf16[128,512]{1,0:T(8,128)(2,1)S(1)} %stack.16.refs_8_.refs_4_), channel_id=1, source_target_pairs={{0,16},{8,24},{16,0},{24,8},{1,17},{9,25},{17,1},{25,9},{2,18},{10... | collective-permute-start | bytes 393224 | tf_op jit(solution)/shard_map/ppermute | solution.py:207
  179.3 5.9 %collective-permute-start.29 = (bf16[128,512]{1,0:T(8,128)(2,1)S(1)}, bf16[128,512]{1,0:T(8,128)(2,1)S(1)}, u32[]{:S(2)}, u32[]{:S(2)}) collective-permute-start(bf16[128,512]{1,0:T(8,128)(2,1)S(1)} %stack.16.refs_8_.refs_4_), channel_id=1, source_target_pairs={{0,24},{8,0},{16,8},{24,16},{1,25},{9,1},{17,9},{25,17},{2,26},{10... | collective-permute-start | bytes 393224 | tf_op jit(solution)/shard_map/ppermute | solution.py:207
  187.2 15.7 %copy-start.4 = (bf16[16,4096]{1,0:T(8,128)(2,1)S(1)}, bf16[16,4096]{1,0:T(8,128)(2,1)}, u32[]{:S(2)}) copy-start(bf16[16,4096]{1,0:T(8,128)(2,1)} %copy-done.3) | copy-start | bytes 393220
  187.2 15.7 %copy-start.6 = (bf16[16,4096]{1,0:T(8,128)(2,1)S(1)}, bf16[16,4096]{1,0:T(8,128)(2,1)}, u32[]{:S(2)}) copy-start(bf16[16,4096]{1,0:T(8,128)(2,1)} %copy-done.5) | copy-start | bytes 393220
  187.2 15.7 %copy-start.8 = (bf16[16,4096]{1,0:T(8,128)(2,1)S(1)}, bf16[16,4096]{1,0:T(8,128)(2,1)}, u32[]{:S(2)}) copy-start(bf16[16,4096]{1,0:T(8,128)(2,1)} %copy-done.7) | copy-start | bytes 393220
  187.2 15.7 %copy-start.10 = (bf16[16,4096]{1,0:T(8,128)(2,1)S(1)}, bf16[16,4096]{1,0:T(8,128)(2,1)}, u32[]{:S(2)}) copy-start(bf16[16,4096]{1,0:T(8,128)(2,1)} %copy-done.9) | copy-start | bytes 393220
  187.2 15.7 %copy-start.12 = (bf16[16,4096]{1,0:T(8,128)(2,1)S(1)}, bf16[16,4096]{1,0:T(8,128)(2,1)}, u32[]{:S(2)}) copy-start(bf16[16,4096]{1,0:T(8,128)(2,1)} %copy-done.11) | copy-start | bytes 393220
  187.2 15.7 %copy-start.14 = (bf16[16,4096]{1,0:T(8,128)(2,1)S(1)}, bf16[16,4096]{1,0:T(8,128)(2,1)}, u32[]{:S(2)}) copy-start(bf16[16,4096]{1,0:T(8,128)(2,1)} %copy-done.13) | copy-start | bytes 393220
  187.2 15.7 %copy-start.16 = (bf16[16,4096]{1,0:T(8,128)(2,1)S(1)}, bf16[16,4096]{1,0:T(8,128)(2,1)}, u32[]{:S(2)}) copy-start(bf16[16,4096]{1,0:T(8,128)(2,1)} %copy-done.15) | copy-start | bytes 393220
  187.2 15.7 %copy-start.18 = (bf16[16,4096]{1,0:T(8,128)(2,1)S(1)}, bf16[16,4096]{1,0:T(8,128)(2,1)}, u32[]{:S(2)}) copy-start(bf16[16,4096]{1,0:T(8,128)(2,1)} %copy-done.17) | copy-start | bytes 393220
  187.2 15.7 %copy-start.20 = (bf16[16,4096]{1,0:T(8,128)(2,1)S(1)}, bf16[16,4096]{1,0:T(8,128)(2,1)}, u32[]{:S(2)}) copy-start(bf16[16,4096]{1,0:T(8,128)(2,1)} %copy-done.19) | copy-start | bytes 393220
  187.3 15.7 %copy-start.22 = (bf16[16,4096]{1,0:T(8,128)(2,1)S(1)}, bf16[16,4096]{1,0:T(8,128)(2,1)}, u32[]{:S(2)}) copy-start(bf16[16,4096]{1,0:T(8,128)(2,1)} %copy-done.21) | copy-start | bytes 393220
  187.3 15.7 %copy-start.24 = (bf16[16,4096]{1,0:T(8,128)(2,1)S(1)}, bf16[16,4096]{1,0:T(8,128)(2,1)}, u32[]{:S(2)}) copy-start(bf16[16,4096]{1,0:T(8,128)(2,1)} %copy-done.23) | copy-start | bytes 393220
  187.3 15.7 %copy-start.26 = (bf16[16,4096]{1,0:T(8,128)(2,1)S(1)}, bf16[16,4096]{1,0:T(8,128)(2,1)}, u32[]{:S(2)}) copy-start(bf16[16,4096]{1,0:T(8,128)(2,1)} %copy-done.25) | copy-start | bytes 393220
  187.3 15.7 %copy-start.28 = (bf16[16,4096]{1,0:T(8,128)(2,1)S(1)}, bf16[16,4096]{1,0:T(8,128)(2,1)}, u32[]{:S(2)}) copy-start(bf16[16,4096]{1,0:T(8,128)(2,1)} %copy-done.27) | copy-start | bytes 393220
  187.3 15.7 %copy-start.30 = (bf16[16,4096]{1,0:T(8,128)(2,1)S(1)}, bf16[16,4096]{1,0:T(8,128)(2,1)}, u32[]{:S(2)}) copy-start(bf16[16,4096]{1,0:T(8,128)(2,1)} %copy-done.29) | copy-start | bytes 393220
  187.3 15.7 %copy-start.32 = (bf16[16,4096]{1,0:T(8,128)(2,1)S(1)}, bf16[16,4096]{1,0:T(8,128)(2,1)}, u32[]{:S(2)}) copy-start(bf16[16,4096]{1,0:T(8,128)(2,1)} %copy-done.31) | copy-start | bytes 393220
  187.3 15.7 %copy-start.34 = (bf16[16,4096]{1,0:T(8,128)(2,1)S(1)}, bf16[16,4096]{1,0:T(8,128)(2,1)}, u32[]{:S(2)}) copy-start(bf16[16,4096]{1,0:T(8,128)(2,1)} %copy-done.33) | copy-start | bytes 393220
  187.3 11.1 %collective-permute-start.30 = (bf16[8,64,512]{2,1,0:T(8,128)(2,1)S(1)}, bf16[8,64,512]{2,1,0:T(8,128)(2,1)S(1)}, u32[]{:S(2)}, u32[]{:S(2)}) collective-permute-start(bf16[8,64,512]{2,1,0:T(8,128)(2,1)S(1)} %get-tuple-element.101), channel_id=1, source_target_pairs={{0,1},{1,0},{2,3},{3,2},{4,5},{5,4},{6,7},{7,6},{8,9},{9,8},{10,11... | collective-permute-start | bytes 1572872 | tf_op jit(solution)/shard_map/ppermute | solution.py:309
  199.4 11.9 %all-to-all-start.1 = ((bf16[8,64,512]{2,1,0:T(8,128)(2,1)}), bf16[8,64,512]{2,1,0:T(8,128)(2,1)S(1)}, u32[]{:S(2)}, u32[]{:S(2)}) async-start(bf16[8,64,512]{2,1,0:T(8,128)(2,1)} %pair.1), calls=%async_computation.1 | async-start | bytes 1048576 | tf_op jit(solution)/shard_map/all_to_all | solution.py:311
  (4 other events, 6.9 us)

commit v11 on v10

--- a/solution.py
+++ b/solution.py
@@ -13,8 +13,8 @@
 SLACK = 2
 FAR = 2
 HIDDEN_BY = 6
-EARLY = 8
-EARLY_BY = 19
+EARLY = 13
+EARLY_BY = 21
 DP = ("dp_0", "dp_1", "dp_2", "dp_3")
 IN_VMEM = pl.BlockSpec(memory_space=pltpu.VMEM)
 IN_SMEM = pl.BlockSpec(memory_space=pltpu.SMEM)

time: 213 us -> 213 us (level)
  waiting for transfers between devices: 96.7 us -> 94.5 us
  starting transfers between devices: 76.4 us -> 78.6 us
    ppermute x1, starting transfers between devices: 9.57 us -> 13 us  [on_device(): got = lax.ppermute(give, DP[3], [(0, 1), (1, 0)])]
  transfers between devices with their start and end apart: 33 -> 33, of which waited for: 18 -> 19; matrix products, arithmetic and copies ran while one was open for 0% -> 0% of each run, Pallas kernels for 14% -> 14%
where the time goes in v11:
time: 213 us; the launch traced here: 212 us
  waiting for transfers between devices  94.5 us (44%)
  starting transfers between devices  78.6 us (37%)
  Pallas kernels  35 us (16%)
  local copies, waits for them, and re-layouts  2.56 us (1%)
    ppermute x20, waiting for transfers between devices, on_device(): sent[step] = lax.ppermute(dx, 'pipe', pairs)  48.4 us
    ppermute x20, starting transfers between devices, on_device(): sent[step] = lax.ppermute(dx, 'pipe', pairs)  35.8 us
    pallas_call x31, Pallas kernels, kernel_call(): pl.pallas_call(kernel, out_shape=out_shape, in_specs=specs, out_specs=jax...  35 us
    all_to_all x1, waiting for transfers between devices, copy_for_each(): lax.all_to_all(jnp.broadcast_to(array[None], (count, *array.shape)), axis...  22.1 us
    ppermute x9, waiting for transfers between devices, exchanged(): moved.append(lax.ppermute(pieces[shift], axis, pairs))  15.3 us
    ppermute x1, starting transfers between devices, on_device(): got = lax.ppermute(give, DP[3], [(0, 1), (1, 0)])  13 us
    ppermute x9, starting transfers between devices, exchanged(): moved.append(lax.ppermute(pieces[shift], axis, pairs))  12.8 us
    all_to_all x1, starting transfers between devices, copy_for_each(): lax.all_to_all(jnp.broadcast_to(array[None], (count, *array.shape)), axis...  9.49 us
  transfers between devices with their start and end apart: 33, of which 19 were waited for; matrix products, arithmetic and copies ran while one was open for 0% of the time, Pallas kernels for 14%

profile of v11, /device:TPU:1, one launch (start us, length us, event | category | flops | bytes accessed | tf_op | source)
XLA Modules:
  0.0 212.3 jit_solution(12261184291202055490)
XLA Ops:
  0.6 2.4 %broadcast_in_dim.14 = bf16[32,64,512]{2,1,0:T(8,128)(2,1)} broadcast(bf16[64,512]{1,0:T(8,128)(2,1)} %bitcast.34), dimensions={1,2} | broadcast | bytes 2162688 | tf_op jit(solution)/shard_map/broadcast_in_dim | solution.py:28
  3.0 9.5 %all-to-all-start = ((bf16[32,64,512]{2,1,0:T(8,128)(2,1)}), bf16[32,64,512]{2,1,0:T(8,128)(2,1)}, u32[]{:S(2)}, u32[]{:S(2)}) async-start(bf16[32,64,512]{2,1,0:T(8,128)(2,1)} %broadcast_in_dim.14), calls=%async_computation | async-start | bytes 4194304 | tf_op jit(solution)/shard_map/all_to_all | solution.py:27
  12.6 3.4 %normalize.1 = (bf16[2,128,1024]{2,1,0:T(8,128)(2,1)S(1)}, bf16[2,128,1024]{2,1,0:T(8,128)(2,1)}, bf16[2,128,1024]{2,1,0:T(8,128)(2,1)}, bf16[2,128,1024]{2,1,0:T(8,128)(2,1)}) custom-call(s32[3]{0:T(128)S(1)} %pad_add_fusion.where, bf16[2,128,4096]{2,1,0:T(8,128)(2,1)S(1)} %bitcast.9, f32[2,1,4096]{2,1,0:T(1,128)S(1)} %copy-done.2), custom_call_target="tpu_custom_call" | custom-call | tf_op jit(solution)/shard_map/normalize/pallas_call | solution.py:33
  16.0 22.1 %all-to-all-done.value_ref = bf16[32,64,512]{2,1,0:T(8,128)(2,1)} async-done(((bf16[32,64,512]{2,1,0:T(8,128)(2,1)}), bf16[32,64,512]{2,1,0:T(8,128)(2,1)}, u32[]{:S(2)}, u32[]{:S(2)}) %all-to-all-start) | async-done | bytes 2097184 | tf_op jit(solution)/shard_map/all_to_all | solution.py:27
  38.0 4.0 %collective-permute-start = (bf16[32,64,512]{2,1,0:T(8,128)(2,1)}, bf16[32,64,512]{2,1,0:T(8,128)(2,1)S(1)}, u32[]{:S(2)}, u32[]{:S(2)}) collective-permute-start(bf16[32,64,512]{2,1,0:T(8,128)(2,1)} %held_until.1.mine_ref), channel_id=1, source_target_pairs={{0,1},{1,0},{2,3},{3,2},{4,5},{5,4},{6,7},{7,6},{8,9},{9,8},{10,11... | collective-permute-start | bytes 6291464 | tf_op jit(solution)/shard_map/ppermute | solution.py:231
  42.5 1.7 collective-permute-start.7
  44.2 1.5 collective-permute-start.8
  46.0 1.9 rows.1.w_ref
  48.0 0.7 collective-permute-start.1
  50.8 1.3 collective-permute-start.5
  52.1 1.3 collective-permute-start.9
  53.4 14.8 %collective-permute-done.6.refs_1_ = bf16[2,128,1024]{2,1,0:T(8,128)(2,1)S(1)} collective-permute-done((bf16[2,128,1024]{2,1,0:T(8,128)(2,1)}, bf16[2,128,1024]{2,1,0:T(8,128)(2,1)S(1)}, u32[]{:S(2)}, u32[]{:S(2)}) %collective-permute-start.6) | collective-permute-done | bytes 524320 | tf_op jit(solution)/shard_map/ppermute | solution.py:207
  68.5 18.3 %collective-permute-done.5.in_ref = bf16[16,4096]{1,0:T(8,128)(2,1)S(1)} collective-permute-done((bf16[16,4096]{1,0:T(8,128)(2,1)S(1)}, bf16[16,4096]{1,0:T(8,128)(2,1)S(1)}, u32[]{:S(2)}, u32[]{:S(2)}) %collective-permute-start.5) | collective-permute-done | bytes 131104 | tf_op jit(solution)/shard_map/ppermute | solution.py:293
  86.8 1.3 section_step.28
  88.2 3.9 %collective-permute-start.10 = (bf16[16,4096]{1,0:T(8,128)(2,1)S(1)}, bf16[16,4096]{1,0:T(8,128)(2,1)S(1)}, u32[]{:S(2)}, u32[]{:S(2)}) collective-permute-start(bf16[16,4096]{1,0:T(8,128)(2,1)S(1)} %get-tuple-element.68.refs_6_), channel_id=1, source_target_pairs={{0,192},{64,0},{128,64},{192,128},{1,193},{65,1},{129,65},{193,129... | collective-permute-start | bytes 393224 | tf_op jit(solution)/shard_map/ppermute | solution.py:293
  92.1 1.3 section_step.29
  93.5 4.7 %collective-permute-start.11 = (bf16[16,4096]{1,0:T(8,128)(2,1)S(1)}, bf16[16,4096]{1,0:T(8,128)(2,1)S(1)}, u32[]{:S(2)}, u32[]{:S(2)}) collective-permute-start(bf16[16,4096]{1,0:T(8,128)(2,1)S(1)} %get-tuple-element.70.refs_7_), channel_id=1, source_target_pairs={{0,192},{64,0},{128,64},{192,128},{1,193},{65,1},{129,65},{193,129... | collective-permute-start | bytes 393224 | tf_op jit(solution)/shard_map/ppermute | solution.py:293
  98.2 2.3 %collective-permute-done.10.in_ref = bf16[16,4096]{1,0:T(8,128)(2,1)S(1)} collective-permute-done((bf16[16,4096]{1,0:T(8,128)(2,1)S(1)}, bf16[16,4096]{1,0:T(8,128)(2,1)S(1)}, u32[]{:S(2)}, u32[]{:S(2)}) %collective-permute-start.10) | collective-permute-done | bytes 131104 | tf_op jit(solution)/shard_map/ppermute | solution.py:293
  100.5 1.3 section_step.30
  101.9 0.9 collective-permute-start.12
  102.8 1.3 section_step.31
  104.1 5.9 %collective-permute-start.13 = (bf16[16,4096]{1,0:T(8,128)(2,1)S(1)}, bf16[16,4096]{1,0:T(8,128)(2,1)S(1)}, u32[]{:S(2)}, u32[]{:S(2)}) collective-permute-start(bf16[16,4096]{1,0:T(8,128)(2,1)S(1)} %get-tuple-element.74.refs_9_), channel_id=1, source_target_pairs={{0,192},{64,0},{128,64},{192,128},{1,193},{65,1},{129,65},{193,129... | collective-permute-start | bytes 393224 | tf_op jit(solution)/shard_map/ppermute | solution.py:293
  110.0 1.3 section_step.32
  111.4 3.0 %collective-permute-start.14 = (bf16[16,4096]{1,0:T(8,128)(2,1)S(1)}, bf16[16,4096]{1,0:T(8,128)(2,1)S(1)}, u32[]{:S(2)}, u32[]{:S(2)}) collective-permute-start(bf16[16,4096]{1,0:T(8,128)(2,1)S(1)} %get-tuple-element.76.refs_10_), channel_id=1, source_target_pairs={{0,192},{64,0},{128,64},{192,128},{1,193},{65,1},{129,65},{193,129... | collective-permute-start | bytes 393224 | tf_op jit(solution)/shard_map/ppermute | solution.py:293
  114.4 1.3 collective-permute-done.13.in_ref
  115.7 1.3 section_step.33
  117.1 4.1 %collective-permute-start.15 = (bf16[16,4096]{1,0:T(8,128)(2,1)S(1)}, bf16[16,4096]{1,0:T(8,128)(2,1)S(1)}, u32[]{:S(2)}, u32[]{:S(2)}) collective-permute-start(bf16[16,4096]{1,0:T(8,128)(2,1)S(1)} %get-tuple-element.78.refs_11_), channel_id=1, source_target_pairs={{0,192},{64,0},{128,64},{192,128},{1,193},{65,1},{129,65},{193,129... | collective-permute-start | bytes 393224 | tf_op jit(solution)/shard_map/ppermute | solution.py:293
  121.2 2.0 collective-permute-done.14.in_ref
  123.2 1.3 section_step.34
  124.7 4.3 %collective-permute-done.15.in_ref = bf16[16,4096]{1,0:T(8,128)(2,1)S(1)} collective-permute-done((bf16[16,4096]{1,0:T(8,128)(2,1)S(1)}, bf16[16,4096]{1,0:T(8,128)(2,1)S(1)}, u32[]{:S(2)}, u32[]{:S(2)}) %collective-permute-start.15) | collective-permute-done | bytes 131104 | tf_op jit(solution)/shard_map/ppermute | solution.py:293
  128.9 1.3 section_step.35
  130.5 3.5 %collective-permute-done.16.in_ref = bf16[16,4096]{1,0:T(8,128)(2,1)S(1)} collective-permute-done((bf16[16,4096]{1,0:T(8,128)(2,1)S(1)}, bf16[16,4096]{1,0:T(8,128)(2,1)S(1)}, u32[]{:S(2)}, u32[]{:S(2)}) %collective-permute-start.16) | collective-permute-done | bytes 131104 | tf_op jit(solution)/shard_map/ppermute | solution.py:293
  134.0 1.3 section_step.36
  135.3 1.3 collective-permute-start.18
  136.6 1.7 collective-permute-done.17.in_ref
  138.3 1.3 section_step.37
  139.7 1.3 collective-permute-start.19
  141.0 2.9 %collective-permute-done.18.in_ref = bf16[16,4096]{1,0:T(8,128)(2,1)S(1)} collective-permute-done((bf16[16,4096]{1,0:T(8,128)(2,1)S(1)}, bf16[16,4096]{1,0:T(8,128)(2,1)S(1)}, u32[]{:S(2)}, u32[]{:S(2)}) %collective-permute-start.18) | collective-permute-done | bytes 131104 | tf_op jit(solution)/shard_map/ppermute | solution.py:293
  143.9 1.3 section_step.38
  145.3 1.3 collective-permute-start.20
  146.6 2.0 collective-permute-done.19.in_ref
  148.6 1.3 section_step.39
  150.0 1.3 collective-permute-start.21
  151.3 5.0 %collective-permute-done.20.in_ref = bf16[16,4096]{1,0:T(8,128)(2,1)S(1)} collective-permute-done((bf16[16,4096]{1,0:T(8,128)(2,1)S(1)}, bf16[16,4096]{1,0:T(8,128)(2,1)S(1)}, u32[]{:S(2)}, u32[]{:S(2)}) %collective-permute-start.20) | collective-permute-done | bytes 131104 | tf_op jit(solution)/shard_map/ppermute | solution.py:293
  156.3 1.3 section_step.40
  157.8 3.9 %collective-permute-start.24 = (bf16[208,512]{1,0:T(8,128)(2,1)S(1)}, bf16[208,512]{1,0:T(8,128)(2,1)S(1)}, u32[]{:S(2)}, u32[]{:S(2)}) collective-permute-start(bf16[208,512]{1,0:T(8,128)(2,1)S(1)} %stack.15.refs_4_), channel_id=1, source_target_pairs={{0,8},{8,16},{16,24},{24,0},{1,9},{9,17},{17,25},{25,1},{2,10},{10... | collective-permute-start | bytes 638984 | tf_op jit(solution)/shard_map/ppermute | solution.py:207
  161.6 2.5 %collective-permute-start.26 = (bf16[208,512]{1,0:T(8,128)(2,1)S(1)}, bf16[208,512]{1,0:T(8,128)(2,1)S(1)}, u32[]{:S(2)}, u32[]{:S(2)}) collective-permute-start(bf16[208,512]{1,0:T(8,128)(2,1)S(1)} %stack.15.refs_4_), channel_id=1, source_target_pairs={{0,24},{8,0},{16,8},{24,16},{1,25},{9,1},{17,9},{25,17},{2,26},{10... | collective-permute-start | bytes 638984 | tf_op jit(solution)/shard_map/ppermute | solution.py:207
  164.1 1.3 collective-permute-start.22
  165.4 1.3 section_step.41
  166.8 1.3 collective-permute-start.23
  168.1 4.8 %collective-permute-done.22.in_ref = bf16[16,4096]{1,0:T(8,128)(2,1)S(1)} collective-permute-done((bf16[16,4096]{1,0:T(8,128)(2,1)S(1)}, bf16[16,4096]{1,0:T(8,128)(2,1)S(1)}, u32[]{:S(2)}, u32[]{:S(2)}) %collective-permute-start.22) | collective-permute-done | bytes 131104 | tf_op jit(solution)/shard_map/ppermute | solution.py:293
  172.9 1.3 section_step.42
  174.5 1.3 section_step.43
  176.2 0.8 collective-permute-start.28
  177.0 2.0 collective-permute-start.29
  179.0 2.9 %part.2.refs_8_ = f32[1024,512]{1,0:T(8,128)S(1)} custom-call(s32[3]{0:T(128)S(1)} %pad_add_fusion.where, bf16[2,128,1024]{2,1,0:T(8,128)(2,1)S(1)} %get-tuple-element.52.token_ref.refs_0_, bf16[2,128,1024]{2,1,0:T(8,128)(2,1)S(1)} %collective-permute-done.6.refs_1_, bf16[2,128,1024]{2,1,0:T(8,128)(2,1)S(1)} %collective-permute-done.7.refs_2_, ...), custom_call_target="tpu_custom_call" | custom-call | tf_op jit(solution)/shard_map/part/pallas_call | solution.py:33
  182.1 1.9 part.3
  184.2 13.0 %collective-permute-start.30 = (bf16[8,64,512]{2,1,0:T(8,128)(2,1)S(1)}, bf16[8,64,512]{2,1,0:T(8,128)(2,1)S(1)}, u32[]{:S(2)}, u32[]{:S(2)}) collective-permute-start(bf16[8,64,512]{2,1,0:T(8,128)(2,1)S(1)} %get-tuple-element.101), channel_id=1, source_target_pairs={{0,1},{1,0},{2,3},{3,2},{4,5},{5,4},{6,7},{7,6},{8,9},{9,8},{10,11... | collective-permute-start | bytes 1572872 | tf_op jit(solution)/shard_map/ppermute | solution.py:309
  197.2 1.5 collective-permute-done.30.got_ref
  198.7 0.9 pair.1
  199.6 3.5 %all-to-all-start.1 = ((bf16[8,64,512]{2,1,0:T(8,128)(2,1)}), bf16[8,64,512]{2,1,0:T(8,128)(2,1)S(1)}, u32[]{:S(2)}, u32[]{:S(2)}) async-start(bf16[8,64,512]{2,1,0:T(8,128)(2,1)} %pair.1), calls=%async_computation.1 | async-start | bytes 1048576 | tf_op jit(solution)/shard_map/all_to_all | solution.py:311
  203.3 1.5 collect_rows.1
  204.8 6.7 %all-to-all-done.1.pieces_ref = bf16[8,64,512]{2,1,0:T(8,128)(2,1)S(1)} async-done(((bf16[8,64,512]{2,1,0:T(8,128)(2,1)}), bf16[8,64,512]{2,1,0:T(8,128)(2,1)S(1)}, u32[]{:S(2)}, u32[]{:S(2)}) %all-to-all-start.1) | async-done | bytes 524320 | tf_op jit(solution)/shard_map/all_to_all | solution.py:311
  211.5 0.7 sum.1
  (107 shorter events, 4.6 us)
Async XLA Ops:
  3.0 9.6 %copy-start = (bf16[2,1,128,4096]{3,2,1,0:T(8,128)(2,1)S(1)}, bf16[2,1,128,4096]{3,2,1,0:T(8,128)(2,1)}, u32[]{:S(2)}) copy-start(bf16[2,1,128,4096]{3,2,1,0:T(8,128)(2,1)} %param.4) | copy-start | bytes 6291460
  3.0 9.6 %copy-start.2 = (f32[2,1,4096]{2,1,0:T(1,128)S(1)}, f32[2,1,4096]{2,1,0:T(1,128)}, u32[]{:S(2)}) copy-start(f32[2,1,4096]{2,1,0:T(1,128)} %g_ref.45) | copy-start | bytes 98308
  3.0 35.0 %all-to-all-start = ((bf16[32,64,512]{2,1,0:T(8,128)(2,1)}), bf16[32,64,512]{2,1,0:T(8,128)(2,1)}, u32[]{:S(2)}, u32[]{:S(2)}) async-start(bf16[32,64,512]{2,1,0:T(8,128)(2,1)} %broadcast_in_dim.14), calls=%async_computation | async-start | bytes 4194304 | tf_op jit(solution)/shard_map/all_to_all | solution.py:27
  38.0 8.0 %collective-permute-start = (bf16[32,64,512]{2,1,0:T(8,128)(2,1)}, bf16[32,64,512]{2,1,0:T(8,128)(2,1)S(1)}, u32[]{:S(2)}, u32[]{:S(2)}) collective-permute-start(bf16[32,64,512]{2,1,0:T(8,128)(2,1)} %held_until.1.mine_ref), channel_id=1, source_target_pairs={{0,1},{1,0},{2,3},{3,2},{4,5},{5,4},{6,7},{7,6},{8,9},{9,8},{10,11... | collective-permute-start | bytes 6291464 | tf_op jit(solution)/shard_map/ppermute | solution.py:231
  42.0 26.2 %collective-permute-start.6 = (bf16[2,128,1024]{2,1,0:T(8,128)(2,1)}, bf16[2,128,1024]{2,1,0:T(8,128)(2,1)S(1)}, u32[]{:S(2)}, u32[]{:S(2)}) collective-permute-start(bf16[2,128,1024]{2,1,0:T(8,128)(2,1)} %get-tuple-element.65), channel_id=1, source_target_pairs={{0,8},{8,16},{16,24},{24,0},{1,9},{9,17},{17,25},{25,1},{2,10},{10... | collective-permute-start | bytes 1572872 | tf_op jit(solution)/shard_map/ppermute | solution.py:207
  42.5 25.8 %collective-permute-start.7 = (bf16[2,128,1024]{2,1,0:T(8,128)(2,1)}, bf16[2,128,1024]{2,1,0:T(8,128)(2,1)S(1)}, u32[]{:S(2)}, u32[]{:S(2)}) collective-permute-start(bf16[2,128,1024]{2,1,0:T(8,128)(2,1)} %get-tuple-element.66), channel_id=1, source_target_pairs={{0,16},{8,24},{16,0},{24,8},{1,17},{9,25},{17,1},{25,9},{2,18},{10... | collective-permute-start | bytes 1572872 | tf_op jit(solution)/shard_map/ppermute | solution.py:207
  44.2 24.4 %collective-permute-start.8 = (bf16[2,128,1024]{2,1,0:T(8,128)(2,1)}, bf16[2,128,1024]{2,1,0:T(8,128)(2,1)S(1)}, u32[]{:S(2)}, u32[]{:S(2)}) collective-permute-start(bf16[2,128,1024]{2,1,0:T(8,128)(2,1)} %get-tuple-element.67), channel_id=1, source_target_pairs={{0,24},{8,0},{16,8},{24,16},{1,25},{9,1},{17,9},{25,17},{2,26},{10... | collective-permute-start | bytes 1572872 | tf_op jit(solution)/shard_map/ppermute | solution.py:207
  48.0 1.4 collective-permute-start.1
  48.6 1.4 collective-permute-start.2
  49.4 1.4 collective-permute-start.3
  50.1 2.0 collective-permute-start.4
  50.8 36.0 %collective-permute-start.5 = (bf16[16,4096]{1,0:T(8,128)(2,1)S(1)}, bf16[16,4096]{1,0:T(8,128)(2,1)S(1)}, u32[]{:S(2)}, u32[]{:S(2)}) collective-permute-start(bf16[16,4096]{1,0:T(8,128)(2,1)S(1)} %get-tuple-element.61.refs_4_), channel_id=1, source_target_pairs={{64,0},{128,64},{192,128},{65,1},{129,65},{193,129},{66,2},{130,66... | collective-permute-start | bytes 393224 | tf_op jit(solution)/shard_map/ppermute | solution.py:293
  52.1 40.0 %collective-permute-start.9 = (bf16[16,4096]{1,0:T(8,128)(2,1)S(1)}, bf16[16,4096]{1,0:T(8,128)(2,1)S(1)}, u32[]{:S(2)}, u32[]{:S(2)}) collective-permute-start(bf16[16,4096]{1,0:T(8,128)(2,1)S(1)} %get-tuple-element.63.refs_5_), channel_id=1, source_target_pairs={{64,0},{128,64},{192,128},{65,1},{129,65},{193,129},{66,2},{130,66... | collective-permute-start | bytes 393224 | tf_op jit(solution)/shard_map/ppermute | solution.py:293
  88.2 5.3 %copy-start.3 = (bf16[16,4096]{1,0:T(8,128)(2,1)}, bf16[16,4096]{1,0:T(8,128)(2,1)S(1)}, u32[]{:S(2)}) copy-start(bf16[16,4096]{1,0:T(8,128)(2,1)S(1)} %get-tuple-element.68.refs_6_) | copy-start | bytes 393220
  88.2 12.3 %collective-permute-start.10 = (bf16[16,4096]{1,0:T(8,128)(2,1)S(1)}, bf16[16,4096]{1,0:T(8,128)(2,1)S(1)}, u32[]{:S(2)}, u32[]{:S(2)}) collective-permute-start(bf16[16,4096]{1,0:T(8,128)(2,1)S(1)} %get-tuple-element.68.refs_6_), channel_id=1, source_target_pairs={{0,192},{64,0},{128,64},{192,128},{1,193},{65,1},{129,65},{193,129... | collective-permute-start | bytes 393224 | tf_op jit(solution)/shard_map/ppermute | solution.py:293
  93.5 8.4 %copy-start.5 = (bf16[16,4096]{1,0:T(8,128)(2,1)}, bf16[16,4096]{1,0:T(8,128)(2,1)S(1)}, u32[]{:S(2)}) copy-start(bf16[16,4096]{1,0:T(8,128)(2,1)S(1)} %get-tuple-element.70.refs_7_) | copy-start | bytes 393220
  93.5 9.3 %collective-permute-start.11 = (bf16[16,4096]{1,0:T(8,128)(2,1)S(1)}, bf16[16,4096]{1,0:T(8,128)(2,1)S(1)}, u32[]{:S(2)}, u32[]{:S(2)}) collective-permute-start(bf16[16,4096]{1,0:T(8,128)(2,1)S(1)} %get-tuple-element.70.refs_7_), channel_id=1, source_target_pairs={{0,192},{64,0},{128,64},{192,128},{1,193},{65,1},{129,65},{193,129... | collective-permute-start | bytes 393224 | tf_op jit(solution)/shard_map/ppermute | solution.py:293
  101.9 8.1 %collective-permute-start.12 = (bf16[16,4096]{1,0:T(8,128)(2,1)S(1)}, bf16[16,4096]{1,0:T(8,128)(2,1)S(1)}, u32[]{:S(2)}, u32[]{:S(2)}) collective-permute-start(bf16[16,4096]{1,0:T(8,128)(2,1)S(1)} %get-tuple-element.72.refs_8_), channel_id=1, source_target_pairs={{0,192},{64,0},{128,64},{192,128},{1,193},{65,1},{129,65},{193,129... | collective-permute-start | bytes 393224 | tf_op jit(solution)/shard_map/ppermute | solution.py:293
  104.1 7.2 %copy-start.9 = (bf16[16,4096]{1,0:T(8,128)(2,1)}, bf16[16,4096]{1,0:T(8,128)(2,1)S(1)}, u32[]{:S(2)}) copy-start(bf16[16,4096]{1,0:T(8,128)(2,1)S(1)} %get-tuple-element.74.refs_9_) | copy-start | bytes 393220
  104.1 11.6 %collective-permute-start.13 = (bf16[16,4096]{1,0:T(8,128)(2,1)S(1)}, bf16[16,4096]{1,0:T(8,128)(2,1)S(1)}, u32[]{:S(2)}, u32[]{:S(2)}) collective-permute-start(bf16[16,4096]{1,0:T(8,128)(2,1)S(1)} %get-tuple-element.74.refs_9_), channel_id=1, source_target_pairs={{0,192},{64,0},{128,64},{192,128},{1,193},{65,1},{129,65},{193,129... | collective-permute-start | bytes 393224 | tf_op jit(solution)/shard_map/ppermute | solution.py:293
  111.4 5.7 %copy-start.11 = (bf16[16,4096]{1,0:T(8,128)(2,1)}, bf16[16,4096]{1,0:T(8,128)(2,1)S(1)}, u32[]{:S(2)}) copy-start(bf16[16,4096]{1,0:T(8,128)(2,1)S(1)} %get-tuple-element.76.refs_10_) | copy-start | bytes 393220
  111.4 11.9 %collective-permute-start.14 = (bf16[16,4096]{1,0:T(8,128)(2,1)S(1)}, bf16[16,4096]{1,0:T(8,128)(2,1)S(1)}, u32[]{:S(2)}, u32[]{:S(2)}) collective-permute-start(bf16[16,4096]{1,0:T(8,128)(2,1)S(1)} %get-tuple-element.76.refs_10_), channel_id=1, source_target_pairs={{0,192},{64,0},{128,64},{192,128},{1,193},{65,1},{129,65},{193,129... | collective-permute-start | bytes 393224 | tf_op jit(solution)/shard_map/ppermute | solution.py:293
  117.1 7.5 %copy-start.13 = (bf16[16,4096]{1,0:T(8,128)(2,1)}, bf16[16,4096]{1,0:T(8,128)(2,1)S(1)}, u32[]{:S(2)}) copy-start(bf16[16,4096]{1,0:T(8,128)(2,1)S(1)} %get-tuple-element.78.refs_11_) | copy-start | bytes 393220
  117.1 11.9 %collective-permute-start.15 = (bf16[16,4096]{1,0:T(8,128)(2,1)S(1)}, bf16[16,4096]{1,0:T(8,128)(2,1)S(1)}, u32[]{:S(2)}, u32[]{:S(2)}) collective-permute-start(bf16[16,4096]{1,0:T(8,128)(2,1)S(1)} %get-tuple-element.78.refs_11_), channel_id=1, source_target_pairs={{0,192},{64,0},{128,64},{192,128},{1,193},{65,1},{129,65},{193,129... | collective-permute-start | bytes 393224 | tf_op jit(solution)/shard_map/ppermute | solution.py:293
  124.6 5.7 %copy-start.15 = (bf16[16,4096]{1,0:T(8,128)(2,1)}, bf16[16,4096]{1,0:T(8,128)(2,1)S(1)}, u32[]{:S(2)}) copy-start(bf16[16,4096]{1,0:T(8,128)(2,1)S(1)} %get-tuple-element.80.refs_12_) | copy-start | bytes 393220
  124.6 9.4 %collective-permute-start.16 = (bf16[16,4096]{1,0:T(8,128)(2,1)S(1)}, bf16[16,4096]{1,0:T(8,128)(2,1)S(1)}, u32[]{:S(2)}, u32[]{:S(2)}) collective-permute-start(bf16[16,4096]{1,0:T(8,128)(2,1)S(1)} %get-tuple-element.80.refs_12_), channel_id=1, source_target_pairs={{0,192},{64,0},{128,64},{192,128},{1,193},{65,1},{129,65},{193,129... | collective-permute-start | bytes 393224 | tf_op jit(solution)/shard_map/ppermute | solution.py:293
  130.3 5.0 %copy-start.17 = (bf16[16,4096]{1,0:T(8,128)(2,1)}, bf16[16,4096]{1,0:T(8,128)(2,1)S(1)}, u32[]{:S(2)}) copy-start(bf16[16,4096]{1,0:T(8,128)(2,1)S(1)} %get-tuple-element.82.refs_13_) | copy-start | bytes 393220
  130.3 8.0 %collective-permute-start.17 = (bf16[16,4096]{1,0:T(8,128)(2,1)S(1)}, bf16[16,4096]{1,0:T(8,128)(2,1)S(1)}, u32[]{:S(2)}, u32[]{:S(2)}) collective-permute-start(bf16[16,4096]{1,0:T(8,128)(2,1)S(1)} %get-tuple-element.82.refs_13_), channel_id=1, source_target_pairs={{0,192},{64,0},{128,64},{192,128},{1,193},{65,1},{129,65},{193,129... | collective-permute-start | bytes 393224 | tf_op jit(solution)/shard_map/ppermute | solution.py:293
  135.3 4.4 %copy-start.19 = (bf16[16,4096]{1,0:T(8,128)(2,1)}, bf16[16,4096]{1,0:T(8,128)(2,1)S(1)}, u32[]{:S(2)}) copy-start(bf16[16,4096]{1,0:T(8,128)(2,1)S(1)} %get-tuple-element.84.refs_14_) | copy-start | bytes 393220
  135.3 8.6 %collective-permute-start.18 = (bf16[16,4096]{1,0:T(8,128)(2,1)S(1)}, bf16[16,4096]{1,0:T(8,128)(2,1)S(1)}, u32[]{:S(2)}, u32[]{:S(2)}) collective-permute-start(bf16[16,4096]{1,0:T(8,128)(2,1)S(1)} %get-tuple-element.84.refs_14_), channel_id=1, source_target_pairs={{64,0},{128,64},{192,128},{65,1},{129,65},{193,129},{66,2},{130,66... | collective-permute-start | bytes 393224 | tf_op jit(solution)/shard_map/ppermute | solution.py:293
  139.7 5.6 %copy-start.21 = (bf16[16,4096]{1,0:T(8,128)(2,1)}, bf16[16,4096]{1,0:T(8,128)(2,1)S(1)}, u32[]{:S(2)}) copy-start(bf16[16,4096]{1,0:T(8,128)(2,1)S(1)} %get-tuple-element.86.refs_15_) | copy-start | bytes 393220
  139.7 8.9 %collective-permute-start.19 = (bf16[16,4096]{1,0:T(8,128)(2,1)S(1)}, bf16[16,4096]{1,0:T(8,128)(2,1)S(1)}, u32[]{:S(2)}, u32[]{:S(2)}) collective-permute-start(bf16[16,4096]{1,0:T(8,128)(2,1)S(1)} %get-tuple-element.86.refs_15_), channel_id=1, source_target_pairs={{64,0},{128,64},{192,128},{65,1},{129,65},{193,129},{66,2},{130,66... | collective-permute-start | bytes 393224 | tf_op jit(solution)/shard_map/ppermute | solution.py:293
  145.3 4.6 %copy-start.23 = (bf16[16,4096]{1,0:T(8,128)(2,1)}, bf16[16,4096]{1,0:T(8,128)(2,1)S(1)}, u32[]{:S(2)}) copy-start(bf16[16,4096]{1,0:T(8,128)(2,1)S(1)} %get-tuple-element.88.refs_16_) | copy-start | bytes 393220
  145.3 10.9 %collective-permute-start.20 = (bf16[16,4096]{1,0:T(8,128)(2,1)S(1)}, bf16[16,4096]{1,0:T(8,128)(2,1)S(1)}, u32[]{:S(2)}, u32[]{:S(2)}) collective-permute-start(bf16[16,4096]{1,0:T(8,128)(2,1)S(1)} %get-tuple-element.88.refs_16_), channel_id=1, source_target_pairs={{64,0},{128,64},{65,1},{129,65},{66,2},{130,66},{67,3},{131,67},{6... | collective-permute-start | bytes 393224 | tf_op jit(solution)/shard_map/ppermute | solution.py:293
  149.9 7.7 %copy-start.25 = (bf16[16,4096]{1,0:T(8,128)(2,1)}, bf16[16,4096]{1,0:T(8,128)(2,1)S(1)}, u32[]{:S(2)}) copy-start(bf16[16,4096]{1,0:T(8,128)(2,1)S(1)} %get-tuple-element.90.refs_17_) | copy-start | bytes 393220
  150.0 15.4 %collective-permute-start.21 = (bf16[16,4096]{1,0:T(8,128)(2,1)S(1)}, bf16[16,4096]{1,0:T(8,128)(2,1)S(1)}, u32[]{:S(2)}, u32[]{:S(2)}) collective-permute-start(bf16[16,4096]{1,0:T(8,128)(2,1)S(1)} %get-tuple-element.90.refs_17_), channel_id=1, source_target_pairs={{64,0},{128,64},{65,1},{129,65},{66,2},{130,66},{67,3},{131,67},{6... | collective-permute-start | bytes 393224 | tf_op jit(solution)/shard_map/ppermute | solution.py:293
  157.6 9.2 %copy-start.27 = (bf16[16,4096]{1,0:T(8,128)(2,1)}, bf16[16,4096]{1,0:T(8,128)(2,1)S(1)}, u32[]{:S(2)}) copy-start(bf16[16,4096]{1,0:T(8,128)(2,1)S(1)} %get-tuple-element.92.refs_18_) | copy-start | bytes 393220
  157.8 16.8 %collective-permute-start.24 = (bf16[208,512]{1,0:T(8,128)(2,1)S(1)}, bf16[208,512]{1,0:T(8,128)(2,1)S(1)}, u32[]{:S(2)}, u32[]{:S(2)}) collective-permute-start(bf16[208,512]{1,0:T(8,128)(2,1)S(1)} %stack.15.refs_4_), channel_id=1, source_target_pairs={{0,8},{8,16},{16,24},{24,0},{1,9},{9,17},{17,25},{25,1},{2,10},{10... | collective-permute-start | bytes 638984 | tf_op jit(solution)/shard_map/ppermute | solution.py:207
  161.6 12.9 %collective-permute-start.25 = (bf16[208,512]{1,0:T(8,128)(2,1)S(1)}, bf16[208,512]{1,0:T(8,128)(2,1)S(1)}, u32[]{:S(2)}, u32[]{:S(2)}) collective-permute-start(bf16[208,512]{1,0:T(8,128)(2,1)S(1)} %stack.15.refs_4_), channel_id=1, source_target_pairs={{0,16},{8,24},{16,0},{24,8},{1,17},{9,25},{17,1},{25,9},{2,18},{10... | collective-permute-start | bytes 638984 | tf_op jit(solution)/shard_map/ppermute | solution.py:207
  161.6 12.9 %collective-permute-start.26 = (bf16[208,512]{1,0:T(8,128)(2,1)S(1)}, bf16[208,512]{1,0:T(8,128)(2,1)S(1)}, u32[]{:S(2)}, u32[]{:S(2)}) collective-permute-start(bf16[208,512]{1,0:T(8,128)(2,1)S(1)} %stack.15.refs_4_), channel_id=1, source_target_pairs={{0,24},{8,0},{16,8},{24,16},{1,25},{9,1},{17,9},{25,17},{2,26},{10... | collective-permute-start | bytes 638984 | tf_op jit(solution)/shard_map/ppermute | solution.py:207
  164.1 8.8 %collective-permute-start.22 = (bf16[16,4096]{1,0:T(8,128)(2,1)S(1)}, bf16[16,4096]{1,0:T(8,128)(2,1)S(1)}, u32[]{:S(2)}, u32[]{:S(2)}) collective-permute-start(bf16[16,4096]{1,0:T(8,128)(2,1)S(1)} %get-tuple-element.92.refs_18_), channel_id=1, source_target_pairs={{64,0},{65,1},{66,2},{67,3},{68,4},{69,5},{70,6},{71,7},{72,8},{73... | collective-permute-start | bytes 393224 | tf_op jit(solution)/shard_map/ppermute | solution.py:293
  166.8 7.5 %copy-start.29 = (bf16[16,4096]{1,0:T(8,128)(2,1)}, bf16[16,4096]{1,0:T(8,128)(2,1)S(1)}, u32[]{:S(2)}) copy-start(bf16[16,4096]{1,0:T(8,128)(2,1)S(1)} %get-tuple-element.94.refs_19_) | copy-start | bytes 393220
  166.8 7.7 %collective-permute-start.23 = (bf16[16,4096]{1,0:T(8,128)(2,1)S(1)}, bf16[16,4096]{1,0:T(8,128)(2,1)S(1)}, u32[]{:S(2)}, u32[]{:S(2)}) collective-permute-start(bf16[16,4096]{1,0:T(8,128)(2,1)S(1)} %get-tuple-element.94.refs_19_), channel_id=1, source_target_pairs={{64,0},{65,1},{66,2},{67,3},{68,4},{69,5},{70,6},{71,7},{72,8},{73... | collective-permute-start | bytes 393224 | tf_op jit(solution)/shard_map/ppermute | solution.py:293
  176.1 5.8 %collective-permute-start.27 = (bf16[48,512]{1,0:T(8,128)(2,1)S(1)}, bf16[48,512]{1,0:T(8,128)(2,1)S(1)}, u32[]{:S(2)}, u32[]{:S(2)}) collective-permute-start(bf16[48,512]{1,0:T(8,128)(2,1)S(1)} %stack.16.refs_8_.refs_4_), channel_id=1, source_target_pairs={{0,8},{8,16},{16,24},{24,0},{1,9},{9,17},{17,25},{25,1},{2,10},{10... | collective-permute-start | bytes 147464 | tf_op jit(solution)/shard_map/ppermute | solution.py:207
  176.2 5.7 %collective-permute-start.28 = (bf16[48,512]{1,0:T(8,128)(2,1)S(1)}, bf16[48,512]{1,0:T(8,128)(2,1)S(1)}, u32[]{:S(2)}, u32[]{:S(2)}) collective-permute-start(bf16[48,512]{1,0:T(8,128)(2,1)S(1)} %stack.16.refs_8_.refs_4_), channel_id=1, source_target_pairs={{0,16},{8,24},{16,0},{24,8},{1,17},{9,25},{17,1},{25,9},{2,18},{10... | collective-permute-start | bytes 147464 | tf_op jit(solution)/shard_map/ppermute | solution.py:207
  177.0 5.1 %collective-permute-start.29 = (bf16[48,512]{1,0:T(8,128)(2,1)S(1)}, bf16[48,512]{1,0:T(8,128)(2,1)S(1)}, u32[]{:S(2)}, u32[]{:S(2)}) collective-permute-start(bf16[48,512]{1,0:T(8,128)(2,1)S(1)} %stack.16.refs_8_.refs_4_), channel_id=1, source_target_pairs={{0,24},{8,0},{16,8},{24,16},{1,25},{9,1},{17,9},{25,17},{2,26},{10... | collective-permute-start | bytes 147464 | tf_op jit(solution)/shard_map/ppermute | solution.py:207
  184.0 19.1 %copy-start.4 = (bf16[16,4096]{1,0:T(8,128)(2,1)S(1)}, bf16[16,4096]{1,0:T(8,128)(2,1)}, u32[]{:S(2)}) copy-start(bf16[16,4096]{1,0:T(8,128)(2,1)} %copy-done.3) | copy-start | bytes 393220
  184.0 19.1 %copy-start.6 = (bf16[16,4096]{1,0:T(8,128)(2,1)S(1)}, bf16[16,4096]{1,0:T(8,128)(2,1)}, u32[]{:S(2)}) copy-start(bf16[16,4096]{1,0:T(8,128)(2,1)} %copy-done.5) | copy-start | bytes 393220
  184.1 19.1 %copy-start.8 = (bf16[16,4096]{1,0:T(8,128)(2,1)S(1)}, bf16[16,4096]{1,0:T(8,128)(2,1)}, u32[]{:S(2)}) copy-start(bf16[16,4096]{1,0:T(8,128)(2,1)} %copy-done.7) | copy-start | bytes 393220
  184.1 19.1 %copy-start.10 = (bf16[16,4096]{1,0:T(8,128)(2,1)S(1)}, bf16[16,4096]{1,0:T(8,128)(2,1)}, u32[]{:S(2)}) copy-start(bf16[16,4096]{1,0:T(8,128)(2,1)} %copy-done.9) | copy-start | bytes 393220
  184.1 19.1 %copy-start.12 = (bf16[16,4096]{1,0:T(8,128)(2,1)S(1)}, bf16[16,4096]{1,0:T(8,128)(2,1)}, u32[]{:S(2)}) copy-start(bf16[16,4096]{1,0:T(8,128)(2,1)} %copy-done.11) | copy-start | bytes 393220
  184.1 19.1 %copy-start.14 = (bf16[16,4096]{1,0:T(8,128)(2,1)S(1)}, bf16[16,4096]{1,0:T(8,128)(2,1)}, u32[]{:S(2)}) copy-start(bf16[16,4096]{1,0:T(8,128)(2,1)} %copy-done.13) | copy-start | bytes 393220
  184.1 19.1 %copy-start.16 = (bf16[16,4096]{1,0:T(8,128)(2,1)S(1)}, bf16[16,4096]{1,0:T(8,128)(2,1)}, u32[]{:S(2)}) copy-start(bf16[16,4096]{1,0:T(8,128)(2,1)} %copy-done.15) | copy-start | bytes 393220
  184.1 19.1 %copy-start.18 = (bf16[16,4096]{1,0:T(8,128)(2,1)S(1)}, bf16[16,4096]{1,0:T(8,128)(2,1)}, u32[]{:S(2)}) copy-start(bf16[16,4096]{1,0:T(8,128)(2,1)} %copy-done.17) | copy-start | bytes 393220
  184.1 19.1 %copy-start.20 = (bf16[16,4096]{1,0:T(8,128)(2,1)S(1)}, bf16[16,4096]{1,0:T(8,128)(2,1)}, u32[]{:S(2)}) copy-start(bf16[16,4096]{1,0:T(8,128)(2,1)} %copy-done.19) | copy-start | bytes 393220
  184.1 19.1 %copy-start.22 = (bf16[16,4096]{1,0:T(8,128)(2,1)S(1)}, bf16[16,4096]{1,0:T(8,128)(2,1)}, u32[]{:S(2)}) copy-start(bf16[16,4096]{1,0:T(8,128)(2,1)} %copy-done.21) | copy-start | bytes 393220
  184.1 19.1 %copy-start.24 = (bf16[16,4096]{1,0:T(8,128)(2,1)S(1)}, bf16[16,4096]{1,0:T(8,128)(2,1)}, u32[]{:S(2)}) copy-start(bf16[16,4096]{1,0:T(8,128)(2,1)} %copy-done.23) | copy-start | bytes 393220
  184.1 19.1 %copy-start.26 = (bf16[16,4096]{1,0:T(8,128)(2,1)S(1)}, bf16[16,4096]{1,0:T(8,128)(2,1)}, u32[]{:S(2)}) copy-start(bf16[16,4096]{1,0:T(8,128)(2,1)} %copy-done.25) | copy-start | bytes 393220
  184.2 19.1 %copy-start.28 = (bf16[16,4096]{1,0:T(8,128)(2,1)S(1)}, bf16[16,4096]{1,0:T(8,128)(2,1)}, u32[]{:S(2)}) copy-start(bf16[16,4096]{1,0:T(8,128)(2,1)} %copy-done.27) | copy-start | bytes 393220
  184.2 19.1 %copy-start.30 = (bf16[16,4096]{1,0:T(8,128)(2,1)S(1)}, bf16[16,4096]{1,0:T(8,128)(2,1)}, u32[]{:S(2)}) copy-start(bf16[16,4096]{1,0:T(8,128)(2,1)} %copy-done.29) | copy-start | bytes 393220
  184.2 19.1 %copy-start.32 = (bf16[16,4096]{1,0:T(8,128)(2,1)S(1)}, bf16[16,4096]{1,0:T(8,128)(2,1)}, u32[]{:S(2)}) copy-start(bf16[16,4096]{1,0:T(8,128)(2,1)} %copy-done.31) | copy-start | bytes 393220
  184.2 19.1 %copy-start.34 = (bf16[16,4096]{1,0:T(8,128)(2,1)S(1)}, bf16[16,4096]{1,0:T(8,128)(2,1)}, u32[]{:S(2)}) copy-start(bf16[16,4096]{1,0:T(8,128)(2,1)} %copy-done.33) | copy-start | bytes 393220
  184.2 14.5 %collective-permute-start.30 = (bf16[8,64,512]{2,1,0:T(8,128)(2,1)S(1)}, bf16[8,64,512]{2,1,0:T(8,128)(2,1)S(1)}, u32[]{:S(2)}, u32[]{:S(2)}) collective-permute-start(bf16[8,64,512]{2,1,0:T(8,128)(2,1)S(1)} %get-tuple-element.101), channel_id=1, source_target_pairs={{0,1},{1,0},{2,3},{3,2},{4,5},{5,4},{6,7},{7,6},{8,9},{9,8},{10,11... | collective-permute-start | bytes 1572872 | tf_op jit(solution)/shard_map/ppermute | solution.py:309
  199.6 11.9 %all-to-all-start.1 = ((bf16[8,64,512]{2,1,0:T(8,128)(2,1)}), bf16[8,64,512]{2,1,0:T(8,128)(2,1)S(1)}, u32[]{:S(2)}, u32[]{:S(2)}) async-start(bf16[8,64,512]{2,1,0:T(8,128)(2,1)} %pair.1), calls=%async_computation.1 | async-start | bytes 1048576 | tf_op jit(solution)/shard_map/all_to_all | solution.py:311
  (4 other events, 8.8 us)
